TPU v7x, 512 devices: a whole 4x4x16 slice. The times are simulated.
512 devices in a mesh: row: 32 (over z, x_lo), col: 16 (over x_hi, y, core).
Axes of the slice: x: 4 (x_hi: 2, x_lo: 2; x = x_hi * 2 + x_lo), y: 4, z: 16, core: 2. Of those that a mesh axis runs over, the one named last changes fastest.
Arguments:
- amplitudes: bfloat16 [2048, 16384], P('col', 'row'), may hold values from -6 to 6
- integrals: bfloat16 [2048, 16384], P('row', 'col'), may hold values from -0.125 to 0.125
- tile_mask: int32 [16, 128], P('col', 'row'), may hold values from 0 to 1, as said below
Outputs:
- residual: bfloat16 [16384, 16384], P('row', 'col')
Inputs may be any that keep to these rules, and one draw needn't show every extreme that they name: tile_mask is 0 or 1 for each tile.
All inputs are finite; a program needn't handle non-finite values.
Results may differ from a plain program's by a relative error of at most 0.001.
Values may be sent and summed in bfloat16 or wider, within the bound.
No kernel may reach another device: no remote copies, remote signals or barrier semaphores. Data moves between devices by JAX's collectives and lax.ppermute only.
A program may use at most 64 MiB of HBM per device.

v0:
```python
import jax
import jax.numpy as jnp
from jax import lax
from jax.sharding import PartitionSpec as P

OI = 4


def mask_tiles(amplitudes, tile_mask):
    virt_rows, pair_count = amplitudes.shape
    tile_rows, tile_cols = tile_mask.shape
    blocks = amplitudes.reshape(
        tile_rows, virt_rows // tile_rows, tile_cols, pair_count // tile_cols
    )
    scaled = blocks * tile_mask.astype(jnp.bfloat16)[:, None, :, None]
    return scaled.reshape(virt_rows, pair_count)


def product(left, right):
    return lax.dot_general(
        left, right, (((0,), (0,)), ((), ())), preferred_element_type=jnp.float32
    )


def on_device(amplitudes, integrals, tile_mask):
    row_count = lax.axis_size("row")
    masked = mask_tiles(amplitudes, tile_mask)
    whole_ints = lax.all_gather(integrals, "row", axis=0, tiled=True)
    arranged = masked.reshape(masked.shape[0], OI, row_count, OI).transpose(0, 3, 2, 1)
    swapped = lax.all_to_all(arranged, "row", split_axis=2, concat_axis=2, tiled=True).reshape(
        masked.shape
    )
    own_rows = lax.all_gather(masked, "col", axis=0, tiled=True)
    swap_rows = lax.all_gather(swapped, "col", axis=0, tiled=True)
    difference = product(own_rows, whole_ints) - product(swap_rows, whole_ints)
    return difference.astype(jnp.bfloat16)


def solution(mesh):
    in_specs = (P("col", "row"), P("row", "col"), P("col", "row"))
    out_specs = P("row", "col")
    return jax.shard_map(
        on_device, mesh=mesh, in_specs=in_specs, out_specs=out_specs, check_vma=False
    )
```

profile of v0, /device:TPU:1, one launch (start us, length us, event | category | flops | bytes accessed | tf_op | source)
XLA Modules:
  0.0 295.7 jit_solution(5210928227185118666)
XLA Ops:
  6.5 0.0 all-gather.4.cloned.1.call-start
  6.5 0.7 convert_bitcast_fusion
  7.2 0.1 broadcast_bitcast_fusion
  7.3 1.6 broadcast_multiply_fusion
  8.8 0.0 all-gather.4.cloned.1.call-update
  8.9 0.0 all-gather.6.cloned.1.call-start
  8.9 0.7 all-gather.6.cloned.1.call-update
  9.6 0.0 all-gather.8.cloned.1.call-start
  9.7 1.0 copy.6
  10.7 0.1 multiply_bitcast_fusion
  10.9 30.8 %all_to_all.5 = bf16[128,4,32,4]{0,1,3,2:T(4,128)(2,1)S(1)} all-to-all(bf16[128,4,32,4]{0,1,3,2:T(4,128)(2,1)S(1)} %copy.7), channel_id=1, replica_groups=mesh['row'=32,'col'=16] {'row'}, dimensions={2} | all-to-all | bytes 262144 | tf_op jit(solution)/shard_map/all_to_all | solution.py:30
  41.7 0.7 copy.8
  42.4 0.0 all-gather.8.cloned.1.call-update
  42.5 36.9 %all-gather.4.cloned.1.call-done = bf16[2048,512]{1,0:T(8,128)(2,1)} async-done(((bf16[128,512]{1,0:T(8,128)(2,1)}), bf16[2048,512]{1,0:T(8,128)(2,1)}) %all-gather.4.cloned.1.call-update) | async-done | bytes 2097168 | tf_op jit(solution)/shard_map/all_gather | solution.py:33
  79.3 122.6 %all-gather.6.cloned.1.call-done = bf16[2048,1024]{1,0:T(8,128)(2,1)} async-done(((bf16[64,1024]{1,0:T(8,128)(2,1)}), bf16[2048,1024]{1,0:T(8,128)(2,1)}) %all-gather.6.cloned.1.call-update) | async-done | bytes 4194320 | tf_op jit(solution)/shard_map/all_gather | solution.py:28
  201.9 5.2 %fusion = f32[512,1024]{1,0:T(8,128)S(1)} fusion(bf16[2048,512]{1,0:T(8,128)(2,1)} %all-gather.4.cloned.1.call-done, bf16[2048,1024]{1,0:T(8,128)(2,1)} %all-gather.6.cloned.1.call-done), kind=kOutput, calls=%fused_computation.5 | convolution fusion | flops 2147483648 | bytes 8388608 | tf_op jit(solution)/shard_map/dot_general | solution.py:20
  207.1 76.0 %all-gather.8.cloned.1.call-done = bf16[2048,512]{0,1:T(8,128)(2,1)} async-done(((bf16[128,512]{0,1:T(8,128)(2,1)}), bf16[2048,512]{0,1:T(8,128)(2,1)}) %all-gather.8.cloned.1.call-update) | async-done | bytes 2097168 | tf_op jit(solution)/shard_map/all_gather | solution.py:34
  283.1 6.1 %subtract_convert_fusion = bf16[512,1024]{1,0:T(8,128)(2,1)} fusion(f32[512,1024]{1,0:T(8,128)S(1)} %fusion, bf16[2048,512]{0,1:T(8,128)(2,1)} %all-gather.8.cloned.1.call-done, bf16[2048,1024]{1,0:T(8,128)(2,1)} %all-gather.6.cloned.1.call-done), kind=kOutput, calls=%fused_computation | convolution fusion | flops 2148532224 | bytes 9437184 | tf_op jit(solution)/shard_map/dot_general | solution.py:20
  (1 shorter events, 0.0 us)
Async XLA Ops:
  6.5 72.8 %all-gather.4.cloned.1.call-start = ((), (), s32[]{:S(2)}) async-start(), calls=%async_computation.1 | async-start | bytes 2228224 | tf_op jit(solution)/shard_map/all_gather | solution.py:33
  8.9 193.0 %all-gather.6.cloned.1.call-start = ((), (), s32[]{:S(2)}) async-start(), calls=%async_computation.2 | async-start | bytes 4325376 | tf_op jit(solution)/shard_map/all_gather | solution.py:28
  9.6 273.4 %all-gather.8.cloned.1.call-start = ((), (), s32[]{:S(2)}) async-start(), calls=%async_computation.3 | async-start | bytes 2228224 | tf_op jit(solution)/shard_map/all_gather | solution.py:34
Sparse Core Ops, SparseCore 0:
  10.7 68.5 all-gather.3
  81.4 120.4 all-gather.5
  205.1 77.9 all-gather.7
where the time goes:
time: 296 us
  waiting for transfers between devices  236 us (80%)
  blocking collectives  30.8 us (10%)
  between operations  13.1 us (4%)
  matrix products  11.3 us (4%)
    all_gather x1, waiting for transfers between devices, on_device(): whole_ints = lax.all_gather(integrals, 'row', axis=0, tiled=True)  123 us
    all_gather x1, waiting for transfers between devices, on_device(): swap_rows = lax.all_gather(swapped, 'col', axis=0, tiled=True)  76 us
    all_gather x1, waiting for transfers between devices, on_device(): own_rows = lax.all_gather(masked, 'col', axis=0, tiled=True)  36.9 us
    all_to_all x1, blocking collectives, on_device(): lax.all_to_all(arranged, 'row', split_axis=2, concat_axis=2, tiled=True)  30.8 us
    dot_general x2, matrix products, product(): lax.dot_general(left, right, (((0,), (0,)), ((), ())), preferred_element_...  11.3 us
  transfers between devices with their start and end apart: 3, of which 3 were waited for; matrix products, arithmetic and copies ran while one was open for 2% of the time, Pallas kernels for 0%

commit v1 on v0

--- a/solution.py
+++ b/solution.py
@@ -4,6 +4,7 @@
 from jax.sharding import PartitionSpec as P
 
 OI = 4
+ZN = 16
 
 
 def mask_tiles(amplitudes, tile_mask):
@@ -22,17 +23,88 @@
     )
 
 
+def z_shift(x, d):
+    return lax.ppermute(x, "row", [(r, (r + 2 * d) % 32) for r in range(32)])
+
+
+def x_swap(x):
+    return lax.ppermute(x, "row", [(r, r ^ 1) for r in range(32)])
+
+
+def core_swap(x):
+    return lax.ppermute(x, "col", [(c, c ^ 1) for c in range(16)])
+
+
+CORE_GROUPS = [list(range(c, 16, 2)) for c in range(2)]
+
+
+def gather_half(x):
+    return lax.all_gather(x, "col", axis=0, tiled=True, axis_index_groups=CORE_GROUPS)
+
+
+def put(whole, block, *starts):
+    zero = jnp.int32(0)
+    starts = starts + (zero,) * (whole.ndim - len(starts))
+    return lax.dynamic_update_slice(whole, block, starts)
+
+
 def on_device(amplitudes, integrals, tile_mask):
     row_count = lax.axis_size("row")
+    row = lax.axis_index("row")
+    core = lax.axis_index("col") % 2
+    z = row // 2
+    xl = row % 2
+    rows, cols = integrals.shape
+
     masked = mask_tiles(amplitudes, tile_mask)
-    whole_ints = lax.all_gather(integrals, "row", axis=0, tiled=True)
     arranged = masked.reshape(masked.shape[0], OI, row_count, OI).transpose(0, 3, 2, 1)
+
+    up4 = z_shift(integrals, 4)
+    down4 = z_shift(integrals, -4)
+    far = z_shift(integrals, 8)
+
     swapped = lax.all_to_all(arranged, "row", split_axis=2, concat_axis=2, tiled=True).reshape(
         masked.shape
     )
-    own_rows = lax.all_gather(masked, "col", axis=0, tiled=True)
-    swap_rows = lax.all_gather(swapped, "col", axis=0, tiled=True)
-    difference = product(own_rows, whole_ints) - product(swap_rows, whole_ints)
+    own_half = gather_half(masked)
+    swap_half = gather_half(swapped)
+    own_other = core_swap(own_half)
+    swap_other = core_swap(swap_half)
+
+    q = z // 4
+    block = jnp.zeros((4, rows, cols), integrals.dtype)
+    block = put(block, integrals[None], q)
+    block = put(block, up4[None], (q + 3) % 4)
+    block = put(block, down4[None], (q + 1) % 4)
+    block = put(block, far[None], (q + 2) % 4)
+
+    partner = x_swap(block)
+    two = z_shift(block, 2)
+    two_partner = x_swap(two)
+    up = z_shift(block, 1)
+    down = z_shift(block, -1)
+    up_partner = z_shift(partner, 1)
+    down_partner = z_shift(partner, -1)
+
+    whole = jnp.zeros((2, 4, 2, 2, rows, cols), integrals.dtype)
+    for got, got_partner, shift in (
+        (block, partner, 0),
+        (two, two_partner, 2),
+        (up, up_partner, 3),
+        (down, down_partner, 1),
+    ):
+        m = (z + shift) % 4
+        side = (m % 2 + core) % 2
+        for part, x_index in ((got, xl), (got_partner, 1 - xl)):
+            whole = put(whole, part[None, :, None, None], side, jnp.int32(0), m // 2, x_index)
+    same = whole[0].reshape(-1, cols)
+    other = whole[1].reshape(-1, cols)
+    difference = (
+        product(own_half, same)
+        - product(swap_half, same)
+        + product(own_other, other)
+        - product(swap_other, other)
+    )
     return difference.astype(jnp.bfloat16)
 
 

time: 296 us -> 166 us (0.56)
  waiting for transfers between devices: 236 us -> 56.6 us
  starting transfers between devices: 0.08 us -> 70.8 us
  blocking collectives: 30.8 us -> 0 us
  local copies, waits for them, and re-layouts: 1.87 us -> 15.6 us
  matrix products: 11.3 us -> 6.08 us
    all_gather x3 -> x2, waiting for transfers between devices: 235 us -> 30.5 us  [gather_half(): lax.all_gather(x, 'col', axis=0, tiled=True, axis_index_groups=CORE_GROUPS)]
    ppermute x0 -> x12, starting transfers between devices: none -> 59.4 us  [the longest x8 44.3 us: z_shift(): return lax.ppermute(x, 'row', [(r, (r + 2 * d) % 32) for r in range(32)])]
    all_to_all x1 -> x0, blocking collectives: 30.8 us -> none  [on_device(): lax.all_to_all(arranged, 'row', split_axis=2, concat_axis=2, tiled=True)]
    all_to_all x0 -> x1, waiting for transfers between devices: none -> 13.2 us  [on_device(): lax.all_to_all(arranged, 'row', split_axis=2, concat_axis=2, tiled=True)]
    ppermute x0 -> x12, waiting for transfers between devices: none -> 12.8 us  [the longest x8 12.8 us: z_shift(): return lax.ppermute(x, 'row', [(r, (r + 2 * d) % 32) for r in range(32)])]
    all_to_all x0 -> x1, starting transfers between devices: none -> 11.4 us  [on_device(): lax.all_to_all(arranged, 'row', split_axis=2, concat_axis=2, tiled=True)]
    dynamic_update_slice x0 -> x12, local copies, waits for them, and re-layouts: none -> 7.82 us  [put(): return lax.dynamic_update_slice(whole, block, starts)]
    dot_general x2 -> x4, matrix products: 11.3 us -> 6.08 us  [product(): lax.dot_general(left, right, (((0,), (0,)), ((), ())), preferred_element_...]
  transfers between devices with their start and end apart: 3 -> 15, of which waited for: 3 -> 5; matrix products, arithmetic and copies ran while one was open for 2% -> 11% of each run, Pallas kernels for 0% -> 0%
where the time goes in v1:
time: 166 us; the launch traced here: 165 us
  starting transfers between devices  70.8 us (43%)
  waiting for transfers between devices  56.6 us (34%)
  local copies, waits for them, and re-layouts  15.6 us (9%)
  between operations  14 us (8%)
  matrix products  6.08 us (4%)
  other arithmetic  2.35 us (1%)
    ppermute x8, starting transfers between devices, z_shift(): return lax.ppermute(x, 'row', [(r, (r + 2 * d) % 32) for r in range(32)])  44.3 us
    all_gather x2, waiting for transfers between devices, gather_half(): lax.all_gather(x, 'col', axis=0, tiled=True, axis_index_groups=CORE_GROUPS)  30.5 us
    all_to_all x1, waiting for transfers between devices, on_device(): lax.all_to_all(arranged, 'row', split_axis=2, concat_axis=2, tiled=True)  13.2 us
    ppermute x8, waiting for transfers between devices, z_shift(): return lax.ppermute(x, 'row', [(r, (r + 2 * d) % 32) for r in range(32)])  12.8 us
    all_to_all x1, starting transfers between devices, on_device(): lax.all_to_all(arranged, 'row', split_axis=2, concat_axis=2, tiled=True)  11.4 us
    ppermute x2, starting transfers between devices, core_swap(): return lax.ppermute(x, 'col', [(c, c ^ 1) for c in range(16)])  10.1 us
    dynamic_update_slice x12, local copies, waits for them, and re-layouts, put(): return lax.dynamic_update_slice(whole, block, starts)  7.82 us
    dot_general x4, matrix products, product(): lax.dot_general(left, right, (((0,), (0,)), ((), ())), preferred_element_...  6.08 us
  transfers between devices with their start and end apart: 15, of which 5 were waited for; matrix products, arithmetic and copies ran while one was open for 11% of the time, Pallas kernels for 0%

profile of v1, /device:TPU:1, one launch (start us, length us, event | category | flops | bytes accessed | tf_op | source)
XLA Modules:
  0.0 165.5 jit_solution(4363983666931814427)
XLA Ops:
  6.5 0.0 all-gather.3.cloned.1.call-start
  6.5 0.7 convert_bitcast_fusion
  7.2 0.1 broadcast_bitcast_fusion
  7.3 1.6 broadcast_multiply_fusion
  8.8 0.0 all-gather.3.cloned.1.call-update
  8.9 9.6 %collective-permute-start = (bf16[64,1024]{1,0:T(8,128)(2,1)}, bf16[64,1024]{1,0:T(8,128)(2,1)S(1)}, u32[]{:S(2)}, u32[]{:S(2)}) collective-permute-start(bf16[64,1024]{1,0:T(8,128)(2,1)} %param.4), channel_id=1, source_target_pairs={{0,128},{16,144},{32,160},{48,176},{64,192},{80,208},{96,224},{112... | collective-permute-start | bytes 393224 | tf_op jit(solution)/shard_map/ppermute | solution.py:27
  18.5 5.6 %collective-permute-start.1 = (bf16[64,1024]{1,0:T(8,128)(2,1)}, bf16[64,1024]{1,0:T(8,128)(2,1)S(1)}, u32[]{:S(2)}, u32[]{:S(2)}) collective-permute-start(bf16[64,1024]{1,0:T(8,128)(2,1)} %param.4), channel_id=1, source_target_pairs={{0,384},{16,400},{32,416},{48,432},{64,448},{80,464},{96,480},{112... | collective-permute-start | bytes 393224 | tf_op jit(solution)/shard_map/ppermute | solution.py:27
  24.1 10.3 %collective-permute-start.2 = (bf16[64,1024]{1,0:T(8,128)(2,1)}, bf16[64,1024]{1,0:T(8,128)(2,1)S(1)}, u32[]{:S(2)}, u32[]{:S(2)}) collective-permute-start(bf16[64,1024]{1,0:T(8,128)(2,1)} %param.4), channel_id=1, source_target_pairs={{0,256},{16,272},{32,288},{48,304},{64,320},{80,336},{96,352},{112... | collective-permute-start | bytes 393224 | tf_op jit(solution)/shard_map/ppermute | solution.py:27
  34.4 1.0 copy.20
  35.5 0.1 broadcast_in_dim.44
  35.5 0.9 bitcast_dynamic-update-slice_fusion.11
  36.5 0.0 collective-permute-done
  36.5 7.1 %collective-permute-done.1 = bf16[64,1024]{1,0:T(8,128)(2,1)S(1)} collective-permute-done((bf16[64,1024]{1,0:T(8,128)(2,1)}, bf16[64,1024]{1,0:T(8,128)(2,1)S(1)}, u32[]{:S(2)}, u32[]{:S(2)}) %collective-permute-start.1) | collective-permute-done | bytes 131104 | tf_op jit(solution)/shard_map/ppermute | solution.py:27
  43.6 2.9 %collective-permute-done.2 = bf16[64,1024]{1,0:T(8,128)(2,1)S(1)} collective-permute-done((bf16[64,1024]{1,0:T(8,128)(2,1)}, bf16[64,1024]{1,0:T(8,128)(2,1)S(1)}, u32[]{:S(2)}, u32[]{:S(2)}) %collective-permute-start.2) | collective-permute-done | bytes 131104 | tf_op jit(solution)/shard_map/ppermute | solution.py:27
  46.5 5.8 %collective-permute-start.4 = (bf16[4,64,1024]{2,1,0:T(8,128)(2,1)S(1)}, bf16[4,64,1024]{2,1,0:T(8,128)(2,1)S(1)}, u32[]{:S(2)}, u32[]{:S(2)}) collective-permute-start(bf16[4,64,1024]{2,1,0:T(8,128)(2,1)S(1)} %bitcast_dynamic-update-slice_fusion.8), channel_id=1, source_target_pairs={{0,64},{16,80},{32,96},{48,112},{64,128},{80,144},{96,160},{112,17... | collective-permute-start | bytes 1572872 | tf_op jit(solution)/shard_map/ppermute | solution.py:27
  52.3 0.1 multiply_bitcast_fusion
  52.5 0.7 copy.21
  53.2 11.4 %all-to-all-start = ((bf16[128,4,32,4]{0,1,3,2:T(4,128)(2,1)}), bf16[128,4,32,4]{0,1,3,2:T(4,128)(2,1)S(1)}, u32[]{:S(2)}, u32[]{:S(2)}) async-start(bf16[128,4,32,4]{0,1,3,2:T(4,128)(2,1)} %copy.21), calls=%async_computation | async-start | bytes 262144 | tf_op jit(solution)/shard_map/all_to_all | solution.py:66
  64.6 0.0 all-gather.5.cloned.1.call-start
  64.6 3.1 %collective-permute-start.3 = (bf16[4,64,1024]{2,1,0:T(8,128)(2,1)S(1)}, bf16[4,64,1024]{2,1,0:T(8,128)(2,1)S(1)}, u32[]{:S(2)}, u32[]{:S(2)}) collective-permute-start(bf16[4,64,1024]{2,1,0:T(8,128)(2,1)S(1)} %bitcast_dynamic-update-slice_fusion.8), channel_id=1, source_target_pairs={{0,16},{16,0},{32,48},{48,32},{64,80},{80,64},{96,112},{112,96},{1... | collective-permute-start | bytes 1572872 | tf_op jit(solution)/shard_map/ppermute | solution.py:31
  68.1 3.1 %collective-permute-start.6 = (bf16[4,64,1024]{2,1,0:T(8,128)(2,1)S(1)}, bf16[4,64,1024]{2,1,0:T(8,128)(2,1)S(1)}, u32[]{:S(2)}, u32[]{:S(2)}) collective-permute-start(bf16[4,64,1024]{2,1,0:T(8,128)(2,1)S(1)} %bitcast_dynamic-update-slice_fusion.8), channel_id=1, source_target_pairs={{0,32},{16,48},{32,64},{48,80},{64,96},{80,112},{96,128},{112,144}... | collective-permute-start | bytes 1572872 | tf_op jit(solution)/shard_map/ppermute | solution.py:27
  71.2 3.4 %collective-permute-start.8 = (bf16[4,64,1024]{2,1,0:T(8,128)(2,1)S(1)}, bf16[4,64,1024]{2,1,0:T(8,128)(2,1)S(1)}, u32[]{:S(2)}, u32[]{:S(2)}) collective-permute-start(bf16[4,64,1024]{2,1,0:T(8,128)(2,1)S(1)} %bitcast_dynamic-update-slice_fusion.8), channel_id=1, source_target_pairs={{0,480},{16,496},{32,0},{48,16},{64,32},{80,48},{96,64},{112,80},{... | collective-permute-start | bytes 1572872 | tf_op jit(solution)/shard_map/ppermute | solution.py:27
  74.6 13.2 %all-to-all-done = bf16[128,4,32,4]{0,1,3,2:T(4,128)(2,1)S(1)} async-done(((bf16[128,4,32,4]{0,1,3,2:T(4,128)(2,1)}), bf16[128,4,32,4]{0,1,3,2:T(4,128)(2,1)S(1)}, u32[]{:S(2)}, u32[]{:S(2)}) %all-to-all-start) | async-done | bytes 131104 | tf_op jit(solution)/shard_map/all_to_all | solution.py:66
  87.8 0.7 copy.22
  88.5 0.0 all-gather.5.cloned.1.call-update
  88.5 0.0 collective-permute-done.4
  88.5 1.9 %collective-permute-start.5 = (bf16[4,64,1024]{2,1,0:T(8,128)(2,1)S(1)}, bf16[4,64,1024]{2,1,0:T(8,128)(2,1)S(1)}, u32[]{:S(2)}, u32[]{:S(2)}) collective-permute-start(bf16[4,64,1024]{2,1,0:T(8,128)(2,1)S(1)} %collective-permute-done.4), channel_id=1, source_target_pairs={{0,16},{16,0},{32,48},{48,32},{64,80},{80,64},{96,112},{112,96},{1... | collective-permute-start | bytes 1572872 | tf_op jit(solution)/shard_map/ppermute | solution.py:31
  90.5 2.5 %broadcast_in_dim.43 = bf16[2,4,2,2,64,1024]{5,4,3,2,1,0:T(8,128)(2,1)} broadcast(bf16[]{:T(256)} %constant.144.clone.1), dimensions={} | broadcast | bytes 4194306 | tf_op jit(solution)/shard_map/broadcast_in_dim | solution.py:89
  92.9 0.9 bitcast_dynamic-update-slice_fusion.6
  93.8 0.0 collective-permute-done.3
  93.8 1.9 %collective-permute-start.7 = (bf16[4,64,1024]{2,1,0:T(8,128)(2,1)S(1)}, bf16[4,64,1024]{2,1,0:T(8,128)(2,1)S(1)}, u32[]{:S(2)}, u32[]{:S(2)}) collective-permute-start(bf16[4,64,1024]{2,1,0:T(8,128)(2,1)S(1)} %collective-permute-done.3), channel_id=1, source_target_pairs={{0,32},{16,48},{32,64},{48,80},{64,96},{80,112},{96,128},{112,144}... | collective-permute-start | bytes 1572872 | tf_op jit(solution)/shard_map/ppermute | solution.py:27
  95.7 4.6 %collective-permute-start.9 = (bf16[4,64,1024]{2,1,0:T(8,128)(2,1)S(1)}, bf16[4,64,1024]{2,1,0:T(8,128)(2,1)S(1)}, u32[]{:S(2)}, u32[]{:S(2)}) collective-permute-start(bf16[4,64,1024]{2,1,0:T(8,128)(2,1)S(1)} %collective-permute-done.3), channel_id=1, source_target_pairs={{0,480},{16,496},{32,0},{48,16},{64,32},{80,48},{96,64},{112,80},{... | collective-permute-start | bytes 1572872 | tf_op jit(solution)/shard_map/ppermute | solution.py:27
  100.3 0.9 bitcast_dynamic-update-slice_fusion.5
  101.1 0.9 bitcast_dynamic-update-slice_fusion.4
  102.0 0.0 collective-permute-done.5
  102.0 0.9 bitcast_dynamic-update-slice_fusion.3
  102.9 0.0 collective-permute-done.6
  102.9 0.9 bitcast_dynamic-update-slice_fusion.2
  103.7 2.8 %collective-permute-done.7 = bf16[4,64,1024]{2,1,0:T(8,128)(2,1)S(1)} collective-permute-done((bf16[4,64,1024]{2,1,0:T(8,128)(2,1)S(1)}, bf16[4,64,1024]{2,1,0:T(8,128)(2,1)S(1)}, u32[]{:S(2)}, u32[]{:S(2)}) %collective-permute-start.7) | collective-permute-done | bytes 524320 | tf_op jit(solution)/shard_map/ppermute | solution.py:27
  106.6 0.9 bitcast_dynamic-update-slice_fusion.1
  107.5 0.0 all-gather.3.cloned.1.call-done
  107.5 6.5 %collective-permute-start.10 = (bf16[1024,512]{1,0:T(8,128)(2,1)}, bf16[1024,512]{1,0:T(8,128)(2,1)S(1)}, u32[]{:S(2)}, u32[]{:S(2)}) collective-permute-start(bf16[1024,512]{1,0:T(8,128)(2,1)} %all-gather.3.cloned.1.call-done), channel_id=1, source_target_pairs={{0,1},{1,0},{2,3},{3,2},{4,5},{5,4},{6,7},{7,6},{8,9},{9,8},{10,11... | collective-permute-start | bytes 3145736 | tf_op jit(solution)/shard_map/ppermute | solution.py:35
  114.0 0.0 collective-permute-done.8
  114.0 0.9 bitcast_dynamic-update-slice_fusion
  114.9 0.0 collective-permute-done.9
  114.9 0.8 bitcast_dynamic-update-slice_fusion.7
  115.7 30.5 %all-gather.5.cloned.1.call-done = bf16[1024,512]{0,1:T(8,128)(2,1)} async-done(((bf16[128,512]{0,1:T(8,128)(2,1)}), bf16[1024,512]{0,1:T(8,128)(2,1)}) %all-gather.5.cloned.1.call-update) | async-done | bytes 1048592 | tf_op jit(solution)/shard_map/all_gather | solution.py:42
  146.2 0.0 copy-start.1
  146.2 3.5 %collective-permute-start.11 = (bf16[1024,512]{0,1:T(8,128)(2,1)}, bf16[1024,512]{0,1:T(8,128)(2,1)S(1)}, u32[]{:S(2)}, u32[]{:S(2)}) collective-permute-start(bf16[1024,512]{0,1:T(8,128)(2,1)} %all-gather.5.cloned.1.call-done), channel_id=1, source_target_pairs={{0,1},{1,0},{2,3},{3,2},{4,5},{5,4},{6,7},{7,6},{8,9},{9,8},{10,11... | collective-permute-start | bytes 3145736 | tf_op jit(solution)/shard_map/ppermute | solution.py:35
  149.7 2.7 %fusion = (bf16[1,4,2,2,64,1024]{5,4,3,2,1,0:T(8,128)(2,1)S(1)}, bf16[1,4,2,2,64,1024]{5,4,3,2,1,0:T(8,128)(2,1)S(1)}) fusion(bf16[2,4,2,2,64,1024]{5,4,3,2,1,0:T(8,128)(2,1)} %bitcast_dynamic-update-slice_fusion.7), kind=kLoop, calls=%fused_computation.17 | loop fusion | bytes 8388608 | tf_op jit(solution)/shard_map/slice | solution.py:100
  152.5 0.0 copy-done.1
  152.5 1.3 fusion.1
  153.8 0.0 collective-permute-done.10
  153.8 1.3 fusion.2
  155.1 0.0 copy-start
  155.1 0.0 collective-permute-done.11
  155.1 1.3 fusion.3
  156.4 0.0 copy-done
  156.4 2.3 %subtract_convert_fusion = bf16[512,1024]{1,0:T(8,128)(2,1)} fusion(f32[512,1024]{1,0:T(8,128)S(1)} %fusion.3, f32[512,1024]{1,0:T(8,128)S(1)} %fusion.2, f32[512,1024]{1,0:T(8,128)S(1)} %fusion.1, bf16[1024,512]{1,0:T(8,128)(2,1)S(1)} %copy-done, bf16[1024,1024]{1,0:T(8,128)(2,1)S(1)} %bitcast.57), kind=kOutput, calls=%fused_computation | convolution fusion | flops 1075838976 | bytes 10485760 | tf_op jit(solution)/shard_map/dot_general | solution.py:21
  (3 shorter events, 0.0 us)
Async XLA Ops:
  6.5 100.9 %all-gather.3.cloned.1.call-start = ((), (), s32[]{:S(2)}) async-start(), calls=%async_computation.1 | async-start | bytes 1179648 | tf_op jit(solution)/shard_map/all_gather | solution.py:42
  8.9 27.6 %collective-permute-start = (bf16[64,1024]{1,0:T(8,128)(2,1)}, bf16[64,1024]{1,0:T(8,128)(2,1)S(1)}, u32[]{:S(2)}, u32[]{:S(2)}) collective-permute-start(bf16[64,1024]{1,0:T(8,128)(2,1)} %param.4), channel_id=1, source_target_pairs={{0,128},{16,144},{32,160},{48,176},{64,192},{80,208},{96,224},{112... | collective-permute-start | bytes 393224 | tf_op jit(solution)/shard_map/ppermute | solution.py:27
  18.5 25.1 %collective-permute-start.1 = (bf16[64,1024]{1,0:T(8,128)(2,1)}, bf16[64,1024]{1,0:T(8,128)(2,1)S(1)}, u32[]{:S(2)}, u32[]{:S(2)}) collective-permute-start(bf16[64,1024]{1,0:T(8,128)(2,1)} %param.4), channel_id=1, source_target_pairs={{0,384},{16,400},{32,416},{48,432},{64,448},{80,464},{96,480},{112... | collective-permute-start | bytes 393224 | tf_op jit(solution)/shard_map/ppermute | solution.py:27
  24.1 22.4 %collective-permute-start.2 = (bf16[64,1024]{1,0:T(8,128)(2,1)}, bf16[64,1024]{1,0:T(8,128)(2,1)S(1)}, u32[]{:S(2)}, u32[]{:S(2)}) collective-permute-start(bf16[64,1024]{1,0:T(8,128)(2,1)} %param.4), channel_id=1, source_target_pairs={{0,256},{16,272},{32,288},{48,304},{64,320},{80,336},{96,352},{112... | collective-permute-start | bytes 393224 | tf_op jit(solution)/shard_map/ppermute | solution.py:27
  46.5 42.0 %collective-permute-start.4 = (bf16[4,64,1024]{2,1,0:T(8,128)(2,1)S(1)}, bf16[4,64,1024]{2,1,0:T(8,128)(2,1)S(1)}, u32[]{:S(2)}, u32[]{:S(2)}) collective-permute-start(bf16[4,64,1024]{2,1,0:T(8,128)(2,1)S(1)} %bitcast_dynamic-update-slice_fusion.8), channel_id=1, source_target_pairs={{0,64},{16,80},{32,96},{48,112},{64,128},{80,144},{96,160},{112,17... | collective-permute-start | bytes 1572872 | tf_op jit(solution)/shard_map/ppermute | solution.py:27
  53.2 34.6 %all-to-all-start = ((bf16[128,4,32,4]{0,1,3,2:T(4,128)(2,1)}), bf16[128,4,32,4]{0,1,3,2:T(4,128)(2,1)S(1)}, u32[]{:S(2)}, u32[]{:S(2)}) async-start(bf16[128,4,32,4]{0,1,3,2:T(4,128)(2,1)} %copy.21), calls=%async_computation | async-start | bytes 262144 | tf_op jit(solution)/shard_map/all_to_all | solution.py:66
  64.6 81.6 %all-gather.5.cloned.1.call-start = ((), (), s32[]{:S(2)}) async-start(), calls=%async_computation.2 | async-start | bytes 1179648 | tf_op jit(solution)/shard_map/all_gather | solution.py:42
  64.6 29.1 %collective-permute-start.3 = (bf16[4,64,1024]{2,1,0:T(8,128)(2,1)S(1)}, bf16[4,64,1024]{2,1,0:T(8,128)(2,1)S(1)}, u32[]{:S(2)}, u32[]{:S(2)}) collective-permute-start(bf16[4,64,1024]{2,1,0:T(8,128)(2,1)S(1)} %bitcast_dynamic-update-slice_fusion.8), channel_id=1, source_target_pairs={{0,16},{16,0},{32,48},{48,32},{64,80},{80,64},{96,112},{112,96},{1... | collective-permute-start | bytes 1572872 | tf_op jit(solution)/shard_map/ppermute | solution.py:31
  68.1 34.8 %collective-permute-start.6 = (bf16[4,64,1024]{2,1,0:T(8,128)(2,1)S(1)}, bf16[4,64,1024]{2,1,0:T(8,128)(2,1)S(1)}, u32[]{:S(2)}, u32[]{:S(2)}) collective-permute-start(bf16[4,64,1024]{2,1,0:T(8,128)(2,1)S(1)} %bitcast_dynamic-update-slice_fusion.8), channel_id=1, source_target_pairs={{0,32},{16,48},{32,64},{48,80},{64,96},{80,112},{96,128},{112,144}... | collective-permute-start | bytes 1572872 | tf_op jit(solution)/shard_map/ppermute | solution.py:27
  71.2 42.8 %collective-permute-start.8 = (bf16[4,64,1024]{2,1,0:T(8,128)(2,1)S(1)}, bf16[4,64,1024]{2,1,0:T(8,128)(2,1)S(1)}, u32[]{:S(2)}, u32[]{:S(2)}) collective-permute-start(bf16[4,64,1024]{2,1,0:T(8,128)(2,1)S(1)} %bitcast_dynamic-update-slice_fusion.8), channel_id=1, source_target_pairs={{0,480},{16,496},{32,0},{48,16},{64,32},{80,48},{96,64},{112,80},{... | collective-permute-start | bytes 1572872 | tf_op jit(solution)/shard_map/ppermute | solution.py:27
  88.5 13.5 %collective-permute-start.5 = (bf16[4,64,1024]{2,1,0:T(8,128)(2,1)S(1)}, bf16[4,64,1024]{2,1,0:T(8,128)(2,1)S(1)}, u32[]{:S(2)}, u32[]{:S(2)}) collective-permute-start(bf16[4,64,1024]{2,1,0:T(8,128)(2,1)S(1)} %collective-permute-done.4), channel_id=1, source_target_pairs={{0,16},{16,0},{32,48},{48,32},{64,80},{80,64},{96,112},{112,96},{1... | collective-permute-start | bytes 1572872 | tf_op jit(solution)/shard_map/ppermute | solution.py:31
  93.8 12.8 %collective-permute-start.7 = (bf16[4,64,1024]{2,1,0:T(8,128)(2,1)S(1)}, bf16[4,64,1024]{2,1,0:T(8,128)(2,1)S(1)}, u32[]{:S(2)}, u32[]{:S(2)}) collective-permute-start(bf16[4,64,1024]{2,1,0:T(8,128)(2,1)S(1)} %collective-permute-done.3), channel_id=1, source_target_pairs={{0,32},{16,48},{32,64},{48,80},{64,96},{80,112},{96,128},{112,144}... | collective-permute-start | bytes 1572872 | tf_op jit(solution)/shard_map/ppermute | solution.py:27
  95.7 19.2 %collective-permute-start.9 = (bf16[4,64,1024]{2,1,0:T(8,128)(2,1)S(1)}, bf16[4,64,1024]{2,1,0:T(8,128)(2,1)S(1)}, u32[]{:S(2)}, u32[]{:S(2)}) collective-permute-start(bf16[4,64,1024]{2,1,0:T(8,128)(2,1)S(1)} %collective-permute-done.3), channel_id=1, source_target_pairs={{0,480},{16,496},{32,0},{48,16},{64,32},{80,48},{96,64},{112,80},{... | collective-permute-start | bytes 1572872 | tf_op jit(solution)/shard_map/ppermute | solution.py:27
  107.5 46.3 %collective-permute-start.10 = (bf16[1024,512]{1,0:T(8,128)(2,1)}, bf16[1024,512]{1,0:T(8,128)(2,1)S(1)}, u32[]{:S(2)}, u32[]{:S(2)}) collective-permute-start(bf16[1024,512]{1,0:T(8,128)(2,1)} %all-gather.3.cloned.1.call-done), channel_id=1, source_target_pairs={{0,1},{1,0},{2,3},{3,2},{4,5},{5,4},{6,7},{7,6},{8,9},{9,8},{10,11... | collective-permute-start | bytes 3145736 | tf_op jit(solution)/shard_map/ppermute | solution.py:35
  146.2 6.3 %copy-start.1 = (bf16[1024,512]{0,1:T(8,128)(2,1)S(1)}, bf16[1024,512]{0,1:T(8,128)(2,1)}, u32[]{:S(2)}) copy-start(bf16[1024,512]{0,1:T(8,128)(2,1)} %all-gather.5.cloned.1.call-done) | copy-start | bytes 3145732
  146.2 8.9 %collective-permute-start.11 = (bf16[1024,512]{0,1:T(8,128)(2,1)}, bf16[1024,512]{0,1:T(8,128)(2,1)S(1)}, u32[]{:S(2)}, u32[]{:S(2)}) collective-permute-start(bf16[1024,512]{0,1:T(8,128)(2,1)} %all-gather.5.cloned.1.call-done), channel_id=1, source_target_pairs={{0,1},{1,0},{2,3},{3,2},{4,5},{5,4},{6,7},{7,6},{8,9},{9,8},{10,11... | collective-permute-start | bytes 3145736 | tf_op jit(solution)/shard_map/ppermute | solution.py:35
  155.1 1.3 copy-start
Sparse Core Ops, SparseCore 0:
  10.6 65.7 all-gather.2
  88.6 57.5 all-gather.4

commit v2 on v0

v2 whole, which is shorter than its diff:
```python
import jax
import jax.numpy as jnp
from jax import lax
from jax.sharding import PartitionSpec as P

OI = 4
CORE_GROUPS = [list(range(c, 16, 2)) for c in range(2)]


def z_shift(x, d):
    return lax.ppermute(x, "row", [(r, (r + 2 * d) % 32) for r in range(32)])


def x_swap(x):
    return lax.ppermute(x, "row", [(r, r ^ 1) for r in range(32)])


def core_swap(x):
    return lax.ppermute(x, "col", [(c, c ^ 1) for c in range(16)])


def put(whole, block, *starts):
    starts = tuple(jnp.int32(s) for s in starts)
    starts = starts + (jnp.int32(0),) * (whole.ndim - len(starts))
    return lax.dynamic_update_slice(whole, block, starts)


def product(left, right):
    return lax.dot_general(
        left, right, (((0, 2), (0, 1)), ((), ())), preferred_element_type=jnp.float32
    )


def on_device(amplitudes, integrals, tile_mask):
    row = lax.axis_index("row")
    core = lax.axis_index("col") % 2
    z = row // 2
    xl = row % 2
    rows, cols = integrals.shape
    depth, pairs = amplitudes.shape

    far = z_shift(integrals, 8)
    up4 = z_shift(integrals, 4)
    down4 = z_shift(integrals, -4)

    scale = jnp.repeat(tile_mask.astype(jnp.bfloat16).reshape(-1), pairs // OI)
    masked = (amplitudes * scale[None, :]).T
    sent = masked.reshape(OI, 32, OI, depth).transpose(1, 2, 0, 3)
    got = lax.all_to_all(sent, "row", split_axis=0, concat_axis=0, tiled=True)
    swapped = got.transpose(1, 0, 2, 3).reshape(pairs, depth)

    both = jnp.stack([masked, swapped])
    copies = jnp.broadcast_to(both[None], (8,) + both.shape)
    own = lax.all_to_all(
        copies, "col", split_axis=0, concat_axis=0, tiled=True, axis_index_groups=CORE_GROUPS
    )
    other = core_swap(own)

    block = jnp.stack([integrals, up4, down4, far])
    two = z_shift(block, 2)
    partner = x_swap(block)
    up = z_shift(block, 1)
    down = z_shift(block, -1)
    up_partner = z_shift(partner, 1)
    down_partner = z_shift(partner, -1)
    two_partner = x_swap(two)

    whole = jnp.zeros((2, 8, 2, rows, cols), integrals.dtype)
    for mine, theirs, shift in (
        (block, partner, 0),
        (two, two_partner, -2),
        (up, up_partner, -1),
        (down, down_partner, 1),
    ):
        for slot, offset in enumerate((0, -4, 4, 8)):
            zz = (z + shift + offset + 32) % 16
            for part, x_index in ((mine, xl), (theirs, 1 - xl)):
                whole = put(
                    whole, part[slot][None, None, None], (zz + core) % 2, zz // 2, x_index
                )
    same = whole[0].reshape(8, -1, cols)
    across = whole[1].reshape(8, -1, cols)
    difference = (
        product(own[:, 0], same)
        - product(own[:, 1], same)
        + product(other[:, 0], across)
        - product(other[:, 1], across)
    )
    return difference.astype(jnp.bfloat16)


def solution(mesh):
    in_specs = (P("col", "row"), P("row", "col"), P("col", "row"))
    out_specs = P("row", "col")
    return jax.shard_map(
        on_device, mesh=mesh, in_specs=in_specs, out_specs=out_specs, check_vma=False
    )
```

time: 296 us -> 139 us (0.47)
  waiting for transfers between devices: 236 us -> 16.9 us
  starting transfers between devices: 0.08 us -> 73.6 us
  local copies, waits for them, and re-layouts: 1.87 us -> 37.6 us
  blocking collectives: 30.8 us -> 0 us
  between operations: 13.1 us -> 1.31 us
  matrix products: 11.3 us -> 6.09 us
    all_gather x3 -> x0, waiting for transfers between devices: 235 us -> none  [the longest x1 123 us: on_device(): whole_ints = lax.all_gather(integrals, 'row', axis=0, tiled=True)]
    ppermute x0 -> x11, starting transfers between devices: none -> 61.2 us  [the longest x8 48 us: z_shift(): return lax.ppermute(x, 'row', [(r, (r + 2 * d) % 32) for r in range(32)])]
    all_to_all x1 -> x0, blocking collectives: 30.8 us -> none  [on_device(): lax.all_to_all(arranged, 'row', split_axis=2, concat_axis=2, tiled=True)]
    dynamic_update_slice x0 -> x32, local copies, waits for them, and re-layouts: none -> 28.4 us  [put(): return lax.dynamic_update_slice(whole, block, starts)]
    ppermute x0 -> x11, waiting for transfers between devices: none -> 16.9 us  [the longest x2 14.5 us: x_swap(): return lax.ppermute(x, 'row', [(r, r ^ 1) for r in range(32)])]
    all_to_all x0 -> x2, starting transfers between devices: none -> 12.4 us  [the longest x1 6.36 us: on_device(): lax.all_to_all(copies, 'col', split_axis=0, concat_axis=0, tiled=True, ax...]
    dot_general x2 -> x4, matrix products: 11.3 us -> 6.09 us  [product(): lax.dot_general(left, right, (((0, 2), (0, 1)), ((), ())), preferred_elem...]
    broadcast_in_dim x0 -> x2, local copies, waits for them, and re-layouts: none -> 4.26 us  [the longest x1 2.49 us: on_device(): whole = jnp.zeros((2, 8, 2, rows, cols), integrals.dtype)]
  transfers between devices with their start and end apart: 3 -> 13, of which waited for: 3 -> 2; matrix products, arithmetic and copies ran while one was open for 2% -> 31% of each run, Pallas kernels for 0% -> 0%
where the time goes in v2:
time: 139 us; the launch traced here: 138 us
  starting transfers between devices  73.6 us (53%)
  local copies, waits for them, and re-layouts  37.6 us (27%)
  waiting for transfers between devices  16.9 us (12%)
  matrix products  6.09 us (4%)
  other arithmetic  2.72 us (2%)
    ppermute x8, starting transfers between devices, z_shift(): return lax.ppermute(x, 'row', [(r, (r + 2 * d) % 32) for r in range(32)])  48 us
    dynamic_update_slice x32, local copies, waits for them, and re-layouts, put(): return lax.dynamic_update_slice(whole, block, starts)  28.4 us
    ppermute x2, waiting for transfers between devices, x_swap(): return lax.ppermute(x, 'row', [(r, r ^ 1) for r in range(32)])  14.5 us
    ppermute x1, starting transfers between devices, core_swap(): return lax.ppermute(x, 'col', [(c, c ^ 1) for c in range(16)])  8.14 us
    all_to_all x1, starting transfers between devices, on_device(): lax.all_to_all(copies, 'col', split_axis=0, concat_axis=0, tiled=True, ax...  6.36 us
    dot_general x4, matrix products, product(): lax.dot_general(left, right, (((0, 2), (0, 1)), ((), ())), preferred_elem...  6.09 us
    all_to_all x1, starting transfers between devices, on_device(): got = lax.all_to_all(sent, 'row', split_axis=0, concat_axis=0, tiled=True)  6.06 us
    ppermute x2, starting transfers between devices, x_swap(): return lax.ppermute(x, 'row', [(r, r ^ 1) for r in range(32)])  5.02 us
  transfers between devices with their start and end apart: 13, of which 2 were waited for; matrix products, arithmetic and copies ran while one was open for 31% of the time, Pallas kernels for 0%

profile of v2, /device:TPU:1, one launch (start us, length us, event | category | flops | bytes accessed | tf_op | source)
XLA Modules:
  0.0 138.2 jit_solution(1233221275569905670)
XLA Ops:
  0.0 9.8 %collective-permute-start = (bf16[64,1024]{1,0:T(8,128)(2,1)}, bf16[64,1024]{1,0:T(8,128)(2,1)S(1)}, u32[]{:S(2)}, u32[]{:S(2)}) collective-permute-start(bf16[64,1024]{1,0:T(8,128)(2,1)} %param.4), channel_id=1, source_target_pairs={{0,128},{16,144},{32,160},{48,176},{64,192},{80,208},{96,224},{112... | collective-permute-start | bytes 393224 | tf_op jit(solution)/shard_map/ppermute | solution.py:11
  9.8 5.6 %collective-permute-start.1 = (bf16[64,1024]{1,0:T(8,128)(2,1)}, bf16[64,1024]{1,0:T(8,128)(2,1)S(1)}, u32[]{:S(2)}, u32[]{:S(2)}) collective-permute-start(bf16[64,1024]{1,0:T(8,128)(2,1)} %param.4), channel_id=1, source_target_pairs={{0,384},{16,400},{32,416},{48,432},{64,448},{80,464},{96,480},{112... | collective-permute-start | bytes 393224 | tf_op jit(solution)/shard_map/ppermute | solution.py:11
  15.3 10.3 %collective-permute-start.2 = (bf16[64,1024]{1,0:T(8,128)(2,1)}, bf16[64,1024]{1,0:T(8,128)(2,1)S(1)}, u32[]{:S(2)}, u32[]{:S(2)}) collective-permute-start(bf16[64,1024]{1,0:T(8,128)(2,1)} %param.4), channel_id=1, source_target_pairs={{0,256},{16,272},{32,288},{48,304},{64,320},{80,336},{96,352},{112... | collective-permute-start | bytes 393224 | tf_op jit(solution)/shard_map/ppermute | solution.py:11
  25.6 1.0 copy.8
  26.6 0.7 convert_bitcast_fusion
  27.3 0.1 broadcast_bitcast_fusion
  27.4 0.1 broadcast_multiply_fusion
  27.5 0.7 copy.9
  28.2 6.1 %all-to-all-start = ((bf16[32,4,4,128]{3,1,2,0:T(4,128)(2,1)}), bf16[32,4,4,128]{3,1,2,0:T(4,128)(2,1)S(1)}, u32[]{:S(2)}, u32[]{:S(2)}) async-start(bf16[32,4,4,128]{3,1,2,0:T(4,128)(2,1)} %copy.9), calls=%async_computation | async-start | bytes 262144 | tf_op jit(solution)/shard_map/all_to_all | solution.py:49
  35.4 2.4 %collective-permute-done.2 = bf16[64,1024]{1,0:T(8,128)(2,1)S(1)} collective-permute-done((bf16[64,1024]{1,0:T(8,128)(2,1)}, bf16[64,1024]{1,0:T(8,128)(2,1)S(1)}, u32[]{:S(2)}, u32[]{:S(2)}) %collective-permute-start.2) | collective-permute-done | bytes 131104 | tf_op jit(solution)/shard_map/ppermute | solution.py:11
  37.7 1.8 %pad_maximum_fusion = bf16[4,64,1024]{2,1,0:T(8,128)(2,1)} fusion(bf16[1,64,1024]{2,1,0:T(8,128)(2,1)S(1)} %bitcast.178, bf16[1,64,1024]{2,1,0:T(8,128)(2,1)S(1)} %bitcast.179, bf16[1,64,1024]{2,1,0:T(8,128)(2,1)S(1)} %bitcast.180, bf16[1,64,1024]{2,1,0:T(8,128)(2,1)} %bitcast.177), kind=kLoop, calls=%fused_computation.11 | loop fusion | flops 786432 | bytes 1048576 | tf_op jit(solution)/shard_map/stack | solution.py:59
  39.5 3.1 %collective-permute-start.3 = (bf16[4,64,1024]{2,1,0:T(8,128)(2,1)}, bf16[4,64,1024]{2,1,0:T(8,128)(2,1)S(1)}, u32[]{:S(2)}, u32[]{:S(2)}) collective-permute-start(bf16[4,64,1024]{2,1,0:T(8,128)(2,1)} %pad_maximum_fusion), channel_id=1, source_target_pairs={{0,16},{16,0},{32,48},{48,32},{64,80},{80,64},{96,112},{112,96},{1... | collective-permute-start | bytes 1572872 | tf_op jit(solution)/shard_map/ppermute | solution.py:15
  42.6 2.5 %broadcast_in_dim.14 = bf16[2,8,2,64,1024]{4,3,2,1,0:T(8,128)(2,1)} broadcast(bf16[]{:T(256)} %constant.372.clone.1), dimensions={} | broadcast | bytes 4194306 | tf_op jit(solution)/shard_map/broadcast_in_dim | solution.py:68
  45.1 0.7 bitcast_dynamic-update-slice_fusion.3
  45.8 0.1 fusion.37
  45.9 5.8 %collective-permute-start.4 = (bf16[4,64,1024]{2,1,0:T(8,128)(2,1)}, bf16[4,64,1024]{2,1,0:T(8,128)(2,1)}, u32[]{:S(2)}, u32[]{:S(2)}) collective-permute-start(bf16[4,64,1024]{2,1,0:T(8,128)(2,1)} %pad_maximum_fusion), channel_id=1, source_target_pairs={{0,64},{16,80},{32,96},{48,112},{64,128},{80,144},{96,160},{112,17... | collective-permute-start | bytes 1572872 | tf_op jit(solution)/shard_map/ppermute | solution.py:11
  51.8 8.2 %collective-permute-start.6 = (bf16[4,64,1024]{2,1,0:T(8,128)(2,1)}, bf16[4,64,1024]{2,1,0:T(8,128)(2,1)}, u32[]{:S(2)}, u32[]{:S(2)}) collective-permute-start(bf16[4,64,1024]{2,1,0:T(8,128)(2,1)} %pad_maximum_fusion), channel_id=1, source_target_pairs={{0,32},{16,48},{32,64},{48,80},{64,96},{80,112},{96,128},{112,144}... | collective-permute-start | bytes 1572872 | tf_op jit(solution)/shard_map/ppermute | solution.py:11
  60.0 1.9 %collective-permute-start.8 = (bf16[4,64,1024]{2,1,0:T(8,128)(2,1)}, bf16[4,64,1024]{2,1,0:T(8,128)(2,1)S(1)}, u32[]{:S(2)}, u32[]{:S(2)}) collective-permute-start(bf16[4,64,1024]{2,1,0:T(8,128)(2,1)} %pad_maximum_fusion), channel_id=1, source_target_pairs={{0,480},{16,496},{32,0},{48,16},{64,32},{80,48},{96,64},{112,80},{... | collective-permute-start | bytes 1572872 | tf_op jit(solution)/shard_map/ppermute | solution.py:11
  61.9 0.1 copy.10
  62.0 1.8 %broadcast_in_dim.13 = bf16[8,2,512,128]{3,2,1,0:T(8,128)(2,1)} broadcast(bf16[2,512,128]{2,1,0:T(8,128)(2,1)S(1)} %pad_maximum_fusion.1), dimensions={1,2,3} | broadcast | bytes 2359296 | tf_op jit(solution)/shard_map/broadcast_in_dim | solution.py:53
  63.8 6.4 %all-to-all-start.1 = ((bf16[8,2,512,128]{3,2,1,0:T(8,128)(2,1)}), bf16[8,2,512,128]{3,2,1,0:T(8,128)(2,1)S(1)}, u32[]{:S(2)}, u32[]{:S(2)}) async-start(bf16[8,2,512,128]{3,2,1,0:T(8,128)(2,1)} %broadcast_in_dim.13), calls=%async_computation.1 | async-start | bytes 4194304 | tf_op jit(solution)/shard_map/all_to_all | solution.py:54
  70.1 3.4 %collective-permute-start.7 = (bf16[4,64,1024]{2,1,0:T(8,128)(2,1)S(1)}, bf16[4,64,1024]{2,1,0:T(8,128)(2,1)S(1)}, u32[]{:S(2)}, u32[]{:S(2)}) collective-permute-start(bf16[4,64,1024]{2,1,0:T(8,128)(2,1)S(1)} %collective-permute-done.3), channel_id=1, source_target_pairs={{0,32},{16,48},{32,64},{48,80},{64,96},{80,112},{96,128},{112,144}... | collective-permute-start | bytes 1572872 | tf_op jit(solution)/shard_map/ppermute | solution.py:11
  73.5 3.1 %collective-permute-start.9 = (bf16[4,64,1024]{2,1,0:T(8,128)(2,1)S(1)}, bf16[4,64,1024]{2,1,0:T(8,128)(2,1)S(1)}, u32[]{:S(2)}, u32[]{:S(2)}) collective-permute-start(bf16[4,64,1024]{2,1,0:T(8,128)(2,1)S(1)} %collective-permute-done.3), channel_id=1, source_target_pairs={{0,480},{16,496},{32,0},{48,16},{64,32},{80,48},{96,64},{112,80},{... | collective-permute-start | bytes 1572872 | tf_op jit(solution)/shard_map/ppermute | solution.py:11
  76.6 0.7 fusion.31
  77.3 0.7 bitcast_dynamic-update-slice_fusion.2
  78.0 0.7 fusion.30
  78.7 0.7 bitcast_dynamic-update-slice_fusion.1
  79.3 0.7 fusion.29
  80.0 1.9 %collective-permute-start.5 = (bf16[4,64,1024]{2,1,0:T(8,128)(2,1)}, bf16[4,64,1024]{2,1,0:T(8,128)(2,1)S(1)}, u32[]{:S(2)}, u32[]{:S(2)}) collective-permute-start(bf16[4,64,1024]{2,1,0:T(8,128)(2,1)} %collective-permute-done.4), channel_id=1, source_target_pairs={{0,16},{16,0},{32,48},{48,32},{64,80},{80,64},{96,112},{112,96},{1... | collective-permute-start | bytes 1572872 | tf_op jit(solution)/shard_map/ppermute | solution.py:15
  81.9 0.7 bitcast_dynamic-update-slice_fusion
  82.6 0.7 fusion.28
  83.2 1.6 %fusion.27 = bf16[2,8,2,64,1024]{4,3,2,1,0:T(8,128)(2,1)} fusion(bf16[2,8,2,64,1024]{4,3,2,1,0:T(8,128)(2,1)} %fusion.28, s32[]{:T(128)S(6)} %select_n.430, s32[]{:T(128)S(6)} %select_n.432, s32[]{:T(128)S(6)} %select_n.411, bf16[4,64,1024]{2,1,0:T(8,128)(2,1)} %collective-permute-done.4), kind=kLoop, calls=%fused_computation.60 | loop fusion | bytes 262156 | tf_op jit(solution)/shard_map/dynamic_update_slice | solution.py:25
  84.8 14.5 %collective-permute-done.5 = bf16[4,64,1024]{2,1,0:T(8,128)(2,1)S(1)} collective-permute-done((bf16[4,64,1024]{2,1,0:T(8,128)(2,1)}, bf16[4,64,1024]{2,1,0:T(8,128)(2,1)S(1)}, u32[]{:S(2)}, u32[]{:S(2)}) %collective-permute-start.5) | collective-permute-done | bytes 524320 | tf_op jit(solution)/shard_map/ppermute | solution.py:15
  99.3 0.6 fusion.26
  99.9 1.6 %fusion.25 = bf16[2,8,2,64,1024]{4,3,2,1,0:T(8,128)(2,1)} fusion(bf16[2,8,2,64,1024]{4,3,2,1,0:T(8,128)(2,1)} %fusion.26, s32[]{:T(128)S(6)} %select_n.435, s32[]{:T(128)S(6)} %select_n.437, s32[]{:T(128)S(6)} %select_n.411, bf16[4,64,1024]{2,1,0:T(8,128)(2,1)} %collective-permute-done.4), kind=kLoop, calls=%fused_computation.56 | loop fusion | bytes 262156 | tf_op jit(solution)/shard_map/dynamic_update_slice | solution.py:25
  101.5 0.7 fusion.24
  102.2 1.6 %fusion.23 = bf16[2,8,2,64,1024]{4,3,2,1,0:T(8,128)(2,1)} fusion(bf16[2,8,2,64,1024]{4,3,2,1,0:T(8,128)(2,1)} %fusion.24, s32[]{:T(128)S(6)} %select_n.440, s32[]{:T(128)S(6)} %select_n.442, s32[]{:T(128)S(6)} %select_n.411, bf16[4,64,1024]{2,1,0:T(8,128)(2,1)} %collective-permute-done.4), kind=kLoop, calls=%fused_computation.52 | loop fusion | bytes 262156 | tf_op jit(solution)/shard_map/dynamic_update_slice | solution.py:25
  103.7 0.7 fusion.22
  104.4 1.6 %fusion.21 = bf16[2,8,2,64,1024]{4,3,2,1,0:T(8,128)(2,1)} fusion(bf16[2,8,2,64,1024]{4,3,2,1,0:T(8,128)(2,1)} %fusion.22, s32[]{:T(128)S(6)} %select_n.445, s32[]{:T(128)S(6)} %select_n.447, s32[]{:T(128)S(6)} %select_n.411, bf16[4,64,1024]{2,1,0:T(8,128)(2,1)} %collective-permute-done.4), kind=kLoop, calls=%fused_computation.48 | loop fusion | bytes 262156 | tf_op jit(solution)/shard_map/dynamic_update_slice | solution.py:25
  106.0 0.7 fusion.20
  106.6 1.6 %fusion.19 = bf16[2,8,2,64,1024]{4,3,2,1,0:T(8,128)(2,1)} fusion(bf16[2,8,2,64,1024]{4,3,2,1,0:T(8,128)(2,1)} %fusion.20, s32[]{:T(128)S(6)} %select_n.450, s32[]{:T(128)S(6)} %select_n.452, s32[]{:T(128)S(6)} %select_n.411, bf16[4,64,1024]{2,1,0:T(8,128)(2,1)} %collective-permute-done.6), kind=kLoop, calls=%fused_computation.44 | loop fusion | bytes 262156 | tf_op jit(solution)/shard_map/dynamic_update_slice | solution.py:25
  108.2 0.7 fusion.18
  108.9 1.6 %fusion.17 = bf16[2,8,2,64,1024]{4,3,2,1,0:T(8,128)(2,1)} fusion(bf16[2,8,2,64,1024]{4,3,2,1,0:T(8,128)(2,1)} %fusion.18, s32[]{:T(128)S(6)} %select_n.455, s32[]{:T(128)S(6)} %select_n.457, s32[]{:T(128)S(6)} %select_n.411, bf16[4,64,1024]{2,1,0:T(8,128)(2,1)} %collective-permute-done.6), kind=kLoop, calls=%fused_computation.40 | loop fusion | bytes 262156 | tf_op jit(solution)/shard_map/dynamic_update_slice | solution.py:25
  110.4 0.7 fusion.16
  111.1 1.6 %fusion.15 = bf16[2,8,2,64,1024]{4,3,2,1,0:T(8,128)(2,1)} fusion(bf16[2,8,2,64,1024]{4,3,2,1,0:T(8,128)(2,1)} %fusion.16, s32[]{:T(128)S(6)} %select_n.460, s32[]{:T(128)S(6)} %select_n.462, s32[]{:T(128)S(6)} %select_n.411, bf16[4,64,1024]{2,1,0:T(8,128)(2,1)} %collective-permute-done.6), kind=kLoop, calls=%fused_computation.36 | loop fusion | bytes 262156 | tf_op jit(solution)/shard_map/dynamic_update_slice | solution.py:25
  112.7 0.6 fusion.14
  113.3 1.6 %fusion.13 = bf16[2,8,2,64,1024]{4,3,2,1,0:T(8,128)(2,1)} fusion(bf16[2,8,2,64,1024]{4,3,2,1,0:T(8,128)(2,1)} %fusion.14, s32[]{:T(128)S(6)} %select_n.465, s32[]{:T(128)S(6)} %select_n.467, s32[]{:T(128)S(6)} %select_n.411, bf16[4,64,1024]{2,1,0:T(8,128)(2,1)} %collective-permute-done.6), kind=kLoop, calls=%fused_computation.32 | loop fusion | bytes 262156 | tf_op jit(solution)/shard_map/dynamic_update_slice | solution.py:25
  114.9 0.7 fusion.12
  115.5 0.7 fusion.11
  116.2 0.7 fusion.10
  116.9 0.1 copy-done
  117.1 0.7 fusion.9
  117.7 0.1 copy.11
  117.9 8.1 %collective-permute-start.10 = (bf16[8,2,512,128]{3,2,0,1:T(8,128)(2,1)S(1)}, bf16[8,2,512,128]{3,2,0,1:T(8,128)(2,1)S(1)}, u32[]{:S(2)}, u32[]{:S(2)}) collective-permute-start(bf16[8,2,512,128]{3,2,0,1:T(8,128)(2,1)S(1)} %copy.11), channel_id=1, source_target_pairs={{0,1},{1,0},{2,3},{3,2},{4,5},{5,4},{6,7},{7,6},{8,9},{9,8},{10,11... | collective-permute-start | bytes 6291464 | tf_op jit(solution)/shard_map/ppermute | solution.py:19
  126.0 0.7 fusion.8
  126.7 0.7 fusion.7
  127.4 0.7 fusion.6
  128.0 0.7 fusion.5
  128.7 0.6 fusion.4
  129.3 2.7 %fusion.32 = (bf16[1,8,2,64,1024]{4,3,2,1,0:T(8,128)(2,1)S(1)}, bf16[1,8,2,64,1024]{4,3,2,1,0:T(8,128)(2,1)S(1)}) fusion(bf16[2,8,2,64,1024]{4,3,2,1,0:T(8,128)(2,1)} %fusion.4), kind=kLoop, calls=%fused_computation.76 | loop fusion | bytes 8388608 | tf_op jit(solution)/shard_map/slice | solution.py:81
  132.1 1.3 fusion.2
  133.4 1.3 fusion.3
  134.6 1.3 fusion.1
  135.9 2.3 %fusion = bf16[512,1024]{1,0:T(8,128)(2,1)} fusion(f32[512,1024,1]{1,0,2:T(8,128)S(1)} %fusion.1, f32[512,1024,1]{1,0,2:T(8,128)S(1)} %fusion.2, f32[512,1024,1]{1,0,2:T(8,128)S(1)} %fusion.3, bf16[8,128,1024]{2,1,0:T(8,128)(2,1)S(1)} %bitcast.171, bf16[8,2,512,128]{3,2,0,1:T(8,128)(2,1)S(1)} %collective-permute-done.10), kind=kOutput, calls=%fused_computation.1 | convolution fusion | flops 1075838976 | bytes 10485760 | tf_op jit(solution)/shard_map/dot_general | solution.py:29
  (17 shorter events, 0.1 us)
Async XLA Ops:
  0.0 45.1 %copy-start.2 = (bf16[64,1024]{1,0:T(8,128)(2,1)S(1)}, bf16[64,1024]{1,0:T(8,128)(2,1)}, u32[]{:S(2)}) copy-start(bf16[64,1024]{1,0:T(8,128)(2,1)} %param.4) | copy-start | bytes 393220
  0.0 35.4 %collective-permute-start = (bf16[64,1024]{1,0:T(8,128)(2,1)}, bf16[64,1024]{1,0:T(8,128)(2,1)S(1)}, u32[]{:S(2)}, u32[]{:S(2)}) collective-permute-start(bf16[64,1024]{1,0:T(8,128)(2,1)} %param.4), channel_id=1, source_target_pairs={{0,128},{16,144},{32,160},{48,176},{64,192},{80,208},{96,224},{112... | collective-permute-start | bytes 393224 | tf_op jit(solution)/shard_map/ppermute | solution.py:11
  9.8 25.6 %collective-permute-start.1 = (bf16[64,1024]{1,0:T(8,128)(2,1)}, bf16[64,1024]{1,0:T(8,128)(2,1)S(1)}, u32[]{:S(2)}, u32[]{:S(2)}) collective-permute-start(bf16[64,1024]{1,0:T(8,128)(2,1)} %param.4), channel_id=1, source_target_pairs={{0,384},{16,400},{32,416},{48,432},{64,448},{80,464},{96,480},{112... | collective-permute-start | bytes 393224 | tf_op jit(solution)/shard_map/ppermute | solution.py:11
  15.3 22.4 %collective-permute-start.2 = (bf16[64,1024]{1,0:T(8,128)(2,1)}, bf16[64,1024]{1,0:T(8,128)(2,1)S(1)}, u32[]{:S(2)}, u32[]{:S(2)}) collective-permute-start(bf16[64,1024]{1,0:T(8,128)(2,1)} %param.4), channel_id=1, source_target_pairs={{0,256},{16,272},{32,288},{48,304},{64,320},{80,336},{96,352},{112... | collective-permute-start | bytes 393224 | tf_op jit(solution)/shard_map/ppermute | solution.py:11
  28.2 33.7 %all-to-all-start = ((bf16[32,4,4,128]{3,1,2,0:T(4,128)(2,1)}), bf16[32,4,4,128]{3,1,2,0:T(4,128)(2,1)S(1)}, u32[]{:S(2)}, u32[]{:S(2)}) async-start(bf16[32,4,4,128]{3,1,2,0:T(4,128)(2,1)} %copy.9), calls=%async_computation | async-start | bytes 262144 | tf_op jit(solution)/shard_map/all_to_all | solution.py:49
  39.5 30.6 %collective-permute-start.3 = (bf16[4,64,1024]{2,1,0:T(8,128)(2,1)}, bf16[4,64,1024]{2,1,0:T(8,128)(2,1)S(1)}, u32[]{:S(2)}, u32[]{:S(2)}) collective-permute-start(bf16[4,64,1024]{2,1,0:T(8,128)(2,1)} %pad_maximum_fusion), channel_id=1, source_target_pairs={{0,16},{16,0},{32,48},{48,32},{64,80},{80,64},{96,112},{112,96},{1... | collective-permute-start | bytes 1572872 | tf_op jit(solution)/shard_map/ppermute | solution.py:15
  45.9 34.1 %collective-permute-start.4 = (bf16[4,64,1024]{2,1,0:T(8,128)(2,1)}, bf16[4,64,1024]{2,1,0:T(8,128)(2,1)}, u32[]{:S(2)}, u32[]{:S(2)}) collective-permute-start(bf16[4,64,1024]{2,1,0:T(8,128)(2,1)} %pad_maximum_fusion), channel_id=1, source_target_pairs={{0,64},{16,80},{32,96},{48,112},{64,128},{80,144},{96,160},{112,17... | collective-permute-start | bytes 1572872 | tf_op jit(solution)/shard_map/ppermute | solution.py:11
  51.8 54.9 %collective-permute-start.6 = (bf16[4,64,1024]{2,1,0:T(8,128)(2,1)}, bf16[4,64,1024]{2,1,0:T(8,128)(2,1)}, u32[]{:S(2)}, u32[]{:S(2)}) collective-permute-start(bf16[4,64,1024]{2,1,0:T(8,128)(2,1)} %pad_maximum_fusion), channel_id=1, source_target_pairs={{0,32},{16,48},{32,64},{48,80},{64,96},{80,112},{96,128},{112,144}... | collective-permute-start | bytes 1572872 | tf_op jit(solution)/shard_map/ppermute | solution.py:11
  60.0 55.6 %collective-permute-start.8 = (bf16[4,64,1024]{2,1,0:T(8,128)(2,1)}, bf16[4,64,1024]{2,1,0:T(8,128)(2,1)S(1)}, u32[]{:S(2)}, u32[]{:S(2)}) collective-permute-start(bf16[4,64,1024]{2,1,0:T(8,128)(2,1)} %pad_maximum_fusion), channel_id=1, source_target_pairs={{0,480},{16,496},{32,0},{48,16},{64,32},{80,48},{96,64},{112,80},{... | collective-permute-start | bytes 1572872 | tf_op jit(solution)/shard_map/ppermute | solution.py:11
  63.8 54.0 %all-to-all-start.1 = ((bf16[8,2,512,128]{3,2,1,0:T(8,128)(2,1)}), bf16[8,2,512,128]{3,2,1,0:T(8,128)(2,1)S(1)}, u32[]{:S(2)}, u32[]{:S(2)}) async-start(bf16[8,2,512,128]{3,2,1,0:T(8,128)(2,1)} %broadcast_in_dim.13), calls=%async_computation.1 | async-start | bytes 4194304 | tf_op jit(solution)/shard_map/all_to_all | solution.py:54
  70.1 38.1 %collective-permute-start.7 = (bf16[4,64,1024]{2,1,0:T(8,128)(2,1)S(1)}, bf16[4,64,1024]{2,1,0:T(8,128)(2,1)S(1)}, u32[]{:S(2)}, u32[]{:S(2)}) collective-permute-start(bf16[4,64,1024]{2,1,0:T(8,128)(2,1)S(1)} %collective-permute-done.3), channel_id=1, source_target_pairs={{0,32},{16,48},{32,64},{48,80},{64,96},{80,112},{96,128},{112,144}... | collective-permute-start | bytes 1572872 | tf_op jit(solution)/shard_map/ppermute | solution.py:11
  73.5 42.7 %collective-permute-start.9 = (bf16[4,64,1024]{2,1,0:T(8,128)(2,1)S(1)}, bf16[4,64,1024]{2,1,0:T(8,128)(2,1)S(1)}, u32[]{:S(2)}, u32[]{:S(2)}) collective-permute-start(bf16[4,64,1024]{2,1,0:T(8,128)(2,1)S(1)} %collective-permute-done.3), channel_id=1, source_target_pairs={{0,480},{16,496},{32,0},{48,16},{64,32},{80,48},{96,64},{112,80},{... | collective-permute-start | bytes 1572872 | tf_op jit(solution)/shard_map/ppermute | solution.py:11
  80.0 19.3 %collective-permute-start.5 = (bf16[4,64,1024]{2,1,0:T(8,128)(2,1)}, bf16[4,64,1024]{2,1,0:T(8,128)(2,1)S(1)}, u32[]{:S(2)}, u32[]{:S(2)}) collective-permute-start(bf16[4,64,1024]{2,1,0:T(8,128)(2,1)} %collective-permute-done.4), channel_id=1, source_target_pairs={{0,16},{16,0},{32,48},{48,32},{64,80},{80,64},{96,112},{112,96},{1... | collective-permute-start | bytes 1572872 | tf_op jit(solution)/shard_map/ppermute | solution.py:15
  116.2 0.8 copy-start
  117.7 8.3 %copy-start.1 = (bf16[4,64,1024]{2,1,0:T(8,128)(2,1)S(1)}, bf16[4,64,1024]{2,1,0:T(8,128)(2,1)}, u32[]{:S(2)}) copy-start(bf16[4,64,1024]{2,1,0:T(8,128)(2,1)} %copy-done) | copy-start | bytes 1572868
  117.9 16.8 %collective-permute-start.10 = (bf16[8,2,512,128]{3,2,0,1:T(8,128)(2,1)S(1)}, bf16[8,2,512,128]{3,2,0,1:T(8,128)(2,1)S(1)}, u32[]{:S(2)}, u32[]{:S(2)}) collective-permute-start(bf16[8,2,512,128]{3,2,0,1:T(8,128)(2,1)S(1)} %copy.11), channel_id=1, source_target_pairs={{0,1},{1,0},{2,3},{3,2},{4,5},{5,4},{6,7},{7,6},{8,9},{9,8},{10,11... | collective-permute-start | bytes 6291464 | tf_op jit(solution)/shard_map/ppermute | solution.py:19

commit v3 on v0

v3 whole, which is shorter than its diff:
```python
import jax
import jax.numpy as jnp
from jax import lax
from jax.experimental import pallas as pl
from jax.experimental.pallas import tpu as pltpu
from jax.sharding import PartitionSpec as P

OI = 4
CORE_GROUPS = [list(range(c, 16, 2)) for c in range(2)]
FAR_GROUPS = [[(4 * q + m) * 2 + x for q in range(4)] for m in range(4) for x in range(2)]
NTILE = 256


def z_shift(x, d):
    return lax.ppermute(x, "row", [(r, (r + 2 * d) % 32) for r in range(32)])


def x_swap(x):
    return lax.ppermute(x, "row", [(r, r ^ 1) for r in range(32)])


def core_swap(x):
    return lax.ppermute(x, "col", [(c, c ^ 1) for c in range(16)])


def spread(x, axis, groups):
    copies = jnp.broadcast_to(x[None], (len(groups[0]),) + x.shape)
    return lax.all_to_all(
        copies, axis, split_axis=0, concat_axis=0, tiled=True, axis_index_groups=groups
    )


def products(place, own, other, near, two, two_partner, up, down, out, ints, amps, sem):
    z, xl, core = place[0], place[1], place[2]
    copies = []
    for side, ref in enumerate((own, other)):
        for s in range(2):
            for g in range(8):
                copies.append((ref.at[g, s], amps.at[side, s, :, pl.ds(g * 128, 128)]))
    blocks = (
        (near.at[0], 0, xl),
        (near.at[1], 0, 1 - xl),
        (two, 2, xl),
        (two_partner, 2, 1 - xl),
        (up.at[0], 3, xl),
        (up.at[1], 3, 1 - xl),
        (down.at[0], 1, xl),
        (down.at[1], 1, 1 - xl),
    )
    for ref, shift, x_index in blocks:
        m = (z + shift) & 3
        copies.append((ref, ints.at[(m + core) & 1, :, m >> 1, x_index]))
    copies = [pltpu.make_async_copy(a, b, sem) for a, b in copies]
    for copy in copies:
        copy.start()
    for copy in copies:
        copy.wait()

    def tile(n, carry):
        cols = pl.ds(pl.multiple_of(n * NTILE, NTILE), NTILE)
        total = None
        for side in range(2):
            right = ints[side, :, :, :, :, cols].reshape(-1, NTILE)
            term = jnp.dot(
                amps[side, 0], right, preferred_element_type=jnp.float32
            ) - jnp.dot(amps[side, 1], right, preferred_element_type=jnp.float32)
            total = term if total is None else total + term
        out[:, cols] = total.astype(out.dtype)
        return carry

    lax.fori_loop(0, out.shape[1] // NTILE, tile, 0)


def on_device(amplitudes, integrals, tile_mask):
    row = lax.axis_index("row")
    place = jnp.stack([row // 2, row % 2, lax.axis_index("col") % 2]).astype(jnp.int32)
    rows, cols = integrals.shape
    depth, pairs = amplitudes.shape

    block = spread(integrals, "row", FAR_GROUPS)

    scale = jnp.repeat(tile_mask.astype(jnp.bfloat16).reshape(-1), pairs // OI)
    masked = (amplitudes * scale[None, :]).T
    sent = masked.reshape(OI, 32, OI, depth).transpose(1, 2, 0, 3)
    got = lax.all_to_all(sent, "row", split_axis=0, concat_axis=0, tiled=True)
    swapped = got.transpose(1, 0, 2, 3).reshape(pairs, depth)
    own = spread(jnp.stack([masked, swapped]), "col", CORE_GROUPS)
    other = core_swap(own)

    two = z_shift(block, 2)
    near = jnp.stack([block, x_swap(block)])
    up = z_shift(near, 1)
    down = z_shift(near, -1)
    two_partner = x_swap(two)

    anywhere = pl.BlockSpec(memory_space=pl.ANY)
    return pl.pallas_call(
        products,
        out_shape=jax.ShapeDtypeStruct((pairs, cols), jnp.bfloat16),
        in_specs=[pl.BlockSpec(memory_space=pltpu.SMEM)] + [anywhere] * 7,
        out_specs=pl.BlockSpec(memory_space=pltpu.VMEM),
        scratch_shapes=[
            pltpu.VMEM((2, 4, 2, 2, rows, cols), jnp.bfloat16),
            pltpu.VMEM((2, 2, pairs, 8 * depth), jnp.bfloat16),
            pltpu.SemaphoreType.DMA,
        ],
        compiler_params=pltpu.CompilerParams(vmem_limit_bytes=40 * 2**20),
        cost_estimate=pl.CostEstimate(
            flops=4 * pairs * 2048 * cols, bytes_accessed=9 * 2**20, transcendentals=0
        ),
    )(place, own, other, near, two, two_partner, up, down)


def solution(mesh):
    in_specs = (P("col", "row"), P("row", "col"), P("col", "row"))
    out_specs = P("row", "col")
    return jax.shard_map(
        on_device, mesh=mesh, in_specs=in_specs, out_specs=out_specs, check_vma=False
    )
```

time: 296 us -> 165 us (0.56)
  waiting for transfers between devices: 236 us -> 64.3 us
  starting transfers between devices: 0.08 us -> 54.6 us
  between operations: 13.1 us -> 0.14 us
  matrix products: 11.3 us -> 0 us
  Pallas kernels: 0 us -> 9.75 us
    all_gather x3 -> x0, waiting for transfers between devices: 235 us -> none  [the longest x1 123 us: on_device(): whole_ints = lax.all_gather(integrals, 'row', axis=0, tiled=True)]
    ppermute x0 -> x6, waiting for transfers between devices: none -> 38.7 us  [the longest x2 20.2 us: x_swap(): return lax.ppermute(x, 'row', [(r, r ^ 1) for r in range(32)])]
    ppermute x0 -> x6, starting transfers between devices: none -> 32.2 us  [the longest x2 16.6 us: x_swap(): return lax.ppermute(x, 'row', [(r, r ^ 1) for r in range(32)])]
    all_to_all x0 -> x2, waiting for transfers between devices: none -> 25.6 us  [the longest x1 13.9 us: on_device(): got = lax.all_to_all(sent, 'row', split_axis=0, concat_axis=0, tiled=True)]
    all_to_all x0 -> x2, starting transfers between devices: none -> 22.3 us  [the longest x1 17 us: on_device(): got = lax.all_to_all(sent, 'row', split_axis=0, concat_axis=0, tiled=True)]
    dot_general x2 -> x0, matrix products: 11.3 us -> none  [product(): lax.dot_general(left, right, (((0,), (0,)), ((), ())), preferred_element_...]
    pallas_call x0 -> x1, Pallas kernels: none -> 9.75 us  [on_device(): pl.pallas_call(products, out_shape=jax.ShapeDtypeStruct((pairs, cols), jn...]
  transfers between devices with their start and end apart: 3 -> 8, of which waited for: 3 -> 6; matrix products, arithmetic and copies ran while one was open for 2% -> 1% of each run, Pallas kernels for 0% -> 0%
where the time goes in v3:
time: 165 us
  waiting for transfers between devices  64.3 us (39%)
  starting transfers between devices  54.6 us (33%)
  blocking collectives  30.5 us (18%)
  Pallas kernels  9.75 us (6%)
  local copies, waits for them, and re-layouts  3.11 us (2%)
  other arithmetic  2.17 us (1%)
    all_to_all x1, blocking collectives, spread(): lax.all_to_all(copies, axis, split_axis=0, concat_axis=0, tiled=True, axi...  30.5 us
    ppermute x2, waiting for transfers between devices, x_swap(): return lax.ppermute(x, 'row', [(r, r ^ 1) for r in range(32)])  20.2 us
    ppermute x3, waiting for transfers between devices, z_shift(): return lax.ppermute(x, 'row', [(r, (r + 2 * d) % 32) for r in range(32)])  18.5 us
    all_to_all x1, starting transfers between devices, on_device(): got = lax.all_to_all(sent, 'row', split_axis=0, concat_axis=0, tiled=True)  17 us
    ppermute x2, starting transfers between devices, x_swap(): return lax.ppermute(x, 'row', [(r, r ^ 1) for r in range(32)])  16.6 us
    all_to_all x1, waiting for transfers between devices, on_device(): got = lax.all_to_all(sent, 'row', split_axis=0, concat_axis=0, tiled=True)  13.9 us
    all_to_all x1, waiting for transfers between devices, spread(): lax.all_to_all(copies, axis, split_axis=0, concat_axis=0, tiled=True, axi...  11.7 us
    pallas_call x1, Pallas kernels, on_device(): pl.pallas_call(products, out_shape=jax.ShapeDtypeStruct((pairs, cols), jn...  9.75 us
  transfers between devices with their start and end apart: 8, of which 6 were waited for; matrix products, arithmetic and copies ran while one was open for 1% of the time, Pallas kernels for 0%

profile of v3, /device:TPU:1, one launch (start us, length us, event | category | flops | bytes accessed | tf_op | source)
XLA Modules:
  0.0 164.6 jit_solution(3842341327134255918)
XLA Ops:
  0.0 0.7 convert_bitcast_fusion
  0.7 0.1 broadcast_bitcast_fusion
  0.7 1.0 copy.8
  1.8 0.1 broadcast_multiply_fusion
  1.9 0.7 copy.9
  2.6 17.0 %all-to-all-start = ((bf16[32,4,4,128]{3,1,2,0:T(4,128)(2,1)}), bf16[32,4,4,128]{3,1,2,0:T(4,128)(2,1)S(1)}, u32[]{:S(2)}, u32[]{:S(2)}) async-start(bf16[32,4,4,128]{3,1,2,0:T(4,128)(2,1)} %copy.9), calls=%async_computation | async-start | bytes 262144 | tf_op jit(solution)/shard_map/all_to_all | solution.py:85
  19.6 0.1 fusion
  19.7 13.9 %all-to-all-done = bf16[32,4,4,128]{3,1,2,0:T(4,128)(2,1)S(1)} async-done(((bf16[32,4,4,128]{3,1,2,0:T(4,128)(2,1)}), bf16[32,4,4,128]{3,1,2,0:T(4,128)(2,1)S(1)}, u32[]{:S(2)}, u32[]{:S(2)}) %all-to-all-start) | async-done | bytes 131104 | tf_op jit(solution)/shard_map/all_to_all | solution.py:85
  33.6 0.1 copy.10
  33.7 0.4 broadcast_in_dim.7
  34.1 0.0 copy-start
  34.1 30.5 %all_to_all.15.own = bf16[8,2,512,128]{3,2,1,0:T(8,128)(2,1)S(1)} all-to-all(bf16[8,2,512,128]{3,2,1,0:T(8,128)(2,1)S(1)} %broadcast_in_dim.7), channel_id=1, replica_groups={{0,2,4,6,8,10,12,14},{1,3,5,7,9,11,13,15},{16,18,20,22,24,26,28,30},{17..., dimensions={0} | all-to-all | bytes 4194304 | tf_op jit(solution)/shard_map/all_to_all | solution.py:28
  64.6 0.0 copy-done
  64.6 0.9 broadcast_in_dim.8
  65.5 5.4 %all-to-all-start.2 = ((bf16[4,64,1024]{2,1,0:T(8,128)(2,1)}), bf16[4,64,1024]{2,1,0:T(8,128)(2,1)}, u32[]{:S(2)}, u32[]{:S(2)}) async-start(bf16[4,64,1024]{2,1,0:T(8,128)(2,1)} %broadcast_in_dim.8), calls=%async_computation.2 | async-start | bytes 1048576 | tf_op jit(solution)/shard_map/all_to_all | solution.py:28
  70.8 5.9 %collective-permute-start = (bf16[8,2,512,128]{3,2,1,0:T(8,128)(2,1)S(1)}, bf16[8,2,512,128]{3,2,1,0:T(8,128)(2,1)}, u32[]{:S(2)}, u32[]{:S(2)}) collective-permute-start(bf16[8,2,512,128]{3,2,1,0:T(8,128)(2,1)S(1)} %all_to_all.15.own), channel_id=1, source_target_pairs={{0,1},{1,0},{2,3},{3,2},{4,5},{5,4},{6,7},{7,6},{8,9},{9,8},{10,11... | collective-permute-start | bytes 6291464 | tf_op jit(solution)/shard_map/ppermute | solution.py:23
  76.8 11.7 %all-to-all-done.2 = bf16[4,64,1024]{2,1,0:T(8,128)(2,1)} async-done(((bf16[4,64,1024]{2,1,0:T(8,128)(2,1)}), bf16[4,64,1024]{2,1,0:T(8,128)(2,1)}, u32[]{:S(2)}, u32[]{:S(2)}) %all-to-all-start.2) | async-done | bytes 524320 | tf_op jit(solution)/shard_map/all_to_all | solution.py:28
  88.5 14.0 %collective-permute-start.1 = (bf16[4,64,1024]{2,1,0:T(8,128)(2,1)}, bf16[4,64,1024]{2,1,0:T(8,128)(2,1)S(1)}, u32[]{:S(2)}, u32[]{:S(2)}) collective-permute-start(bf16[4,64,1024]{2,1,0:T(8,128)(2,1)} %all-to-all-done.2), channel_id=1, source_target_pairs={{0,16},{16,0},{32,48},{48,32},{64,80},{80,64},{96,112},{112,96},{1... | collective-permute-start | bytes 1572872 | tf_op jit(solution)/shard_map/ppermute | solution.py:19
  102.5 4.4 %collective-permute-start.2 = (bf16[4,64,1024]{2,1,0:T(8,128)(2,1)}, bf16[4,64,1024]{2,1,0:T(8,128)(2,1)}, u32[]{:S(2)}, u32[]{:S(2)}) collective-permute-start(bf16[4,64,1024]{2,1,0:T(8,128)(2,1)} %all-to-all-done.2), channel_id=1, source_target_pairs={{0,64},{16,80},{32,96},{48,112},{64,128},{80,144},{96,160},{112,17... | collective-permute-start | bytes 1572872 | tf_op jit(solution)/shard_map/ppermute | solution.py:15
  107.0 7.7 %collective-permute-done.1 = bf16[4,64,1024]{2,1,0:T(8,128)(2,1)S(1)} collective-permute-done((bf16[4,64,1024]{2,1,0:T(8,128)(2,1)}, bf16[4,64,1024]{2,1,0:T(8,128)(2,1)S(1)}, u32[]{:S(2)}, u32[]{:S(2)}) %collective-permute-start.1) | collective-permute-done | bytes 524320 | tf_op jit(solution)/shard_map/ppermute | solution.py:19
  114.7 1.1 pad_maximum_fusion.near
  115.8 2.1 %collective-permute-start.5 = (bf16[2,4,64,1024]{3,2,1,0:T(8,128)(2,1)S(1)}, bf16[2,4,64,1024]{3,2,1,0:T(8,128)(2,1)}, u32[]{:S(2)}, u32[]{:S(2)}) collective-permute-start(bf16[2,4,64,1024]{3,2,1,0:T(8,128)(2,1)S(1)} %pad_maximum_fusion.near), channel_id=1, source_target_pairs={{0,480},{16,496},{32,0},{48,16},{64,32},{80,48},{96,64},{112,80},{... | collective-permute-start | bytes 3145736 | tf_op jit(solution)/shard_map/ppermute | solution.py:15
  117.9 3.2 %collective-permute-start.4 = (bf16[2,4,64,1024]{3,2,1,0:T(8,128)(2,1)S(1)}, bf16[2,4,64,1024]{3,2,1,0:T(8,128)(2,1)}, u32[]{:S(2)}, u32[]{:S(2)}) collective-permute-start(bf16[2,4,64,1024]{3,2,1,0:T(8,128)(2,1)S(1)} %pad_maximum_fusion.near), channel_id=1, source_target_pairs={{0,32},{16,48},{32,64},{48,80},{64,96},{80,112},{96,128},{112,144}... | collective-permute-start | bytes 3145736 | tf_op jit(solution)/shard_map/ppermute | solution.py:15
  121.1 11.0 %collective-permute-done.2.two = bf16[4,64,1024]{2,1,0:T(8,128)(2,1)} collective-permute-done((bf16[4,64,1024]{2,1,0:T(8,128)(2,1)}, bf16[4,64,1024]{2,1,0:T(8,128)(2,1)}, u32[]{:S(2)}, u32[]{:S(2)}) %collective-permute-start.2) | collective-permute-done | bytes 524320 | tf_op jit(solution)/shard_map/ppermute | solution.py:15
  132.1 2.5 %collective-permute-start.3 = (bf16[4,64,1024]{2,1,0:T(8,128)(2,1)}, bf16[4,64,1024]{2,1,0:T(8,128)(2,1)}, u32[]{:S(2)}, u32[]{:S(2)}) collective-permute-start(bf16[4,64,1024]{2,1,0:T(8,128)(2,1)} %collective-permute-done.2.two), channel_id=1, source_target_pairs={{0,16},{16,0},{32,48},{48,32},{64,80},{80,64},{96,112},{112,96},{1... | collective-permute-start | bytes 1572872 | tf_op jit(solution)/shard_map/ppermute | solution.py:19
  134.7 0.1 pad_add_fusion.place
  134.8 12.5 %collective-permute-done.3.two_partner = bf16[4,64,1024]{2,1,0:T(8,128)(2,1)} collective-permute-done((bf16[4,64,1024]{2,1,0:T(8,128)(2,1)}, bf16[4,64,1024]{2,1,0:T(8,128)(2,1)}, u32[]{:S(2)}, u32[]{:S(2)}) %collective-permute-start.3) | collective-permute-done | bytes 524320 | tf_op jit(solution)/shard_map/ppermute | solution.py:19
  147.3 0.0 collective-permute-done.5.down
  147.3 7.5 %collective-permute-done.4.up = bf16[2,4,64,1024]{3,2,1,0:T(8,128)(2,1)} collective-permute-done((bf16[2,4,64,1024]{3,2,1,0:T(8,128)(2,1)S(1)}, bf16[2,4,64,1024]{3,2,1,0:T(8,128)(2,1)}, u32[]{:S(2)}, u32[]{:S(2)}) %collective-permute-start.4) | collective-permute-done | bytes 1048608 | tf_op jit(solution)/shard_map/ppermute | solution.py:15
  154.8 0.0 collective-permute-done.other
  154.8 9.8 %shard_map.37 = bf16[512,1024]{1,0:T(8,128)(2,1)} custom-call(s32[3]{0:T(128)S(1)} %pad_add_fusion.place, bf16[8,2,512,128]{3,2,1,0:T(8,128)(2,1)S(1)} %all_to_all.15.own, bf16[8,2,512,128]{3,2,1,0:T(8,128)(2,1)} %collective-permute-done.other, bf16[2,4,64,1024]{3,2,1,0:T(8,128)(2,1)S(1)} %pad_maximum_fusion.near, ...), custom_call_target="tpu_custom_call" | custom-call | flops 4294967296 | bytes 9437184 | tf_op jit(solution)/shard_map/pallas_call | solution.py:97
  (1 shorter events, 0.0 us)
Async XLA Ops:
  2.6 31.0 %all-to-all-start = ((bf16[32,4,4,128]{3,1,2,0:T(4,128)(2,1)}), bf16[32,4,4,128]{3,1,2,0:T(4,128)(2,1)S(1)}, u32[]{:S(2)}, u32[]{:S(2)}) async-start(bf16[32,4,4,128]{3,1,2,0:T(4,128)(2,1)} %copy.9), calls=%async_computation | async-start | bytes 262144 | tf_op jit(solution)/shard_map/all_to_all | solution.py:85
  34.1 30.5 %copy-start = (bf16[64,1024]{1,0:T(8,128)(2,1)S(1)}, bf16[64,1024]{1,0:T(8,128)(2,1)}, u32[]{:S(2)}) copy-start(bf16[64,1024]{1,0:T(8,128)(2,1)} %param.4) | copy-start | bytes 393220
  65.5 23.0 %all-to-all-start.2 = ((bf16[4,64,1024]{2,1,0:T(8,128)(2,1)}), bf16[4,64,1024]{2,1,0:T(8,128)(2,1)}, u32[]{:S(2)}, u32[]{:S(2)}) async-start(bf16[4,64,1024]{2,1,0:T(8,128)(2,1)} %broadcast_in_dim.8), calls=%async_computation.2 | async-start | bytes 1048576 | tf_op jit(solution)/shard_map/all_to_all | solution.py:28
  70.8 84.0 %collective-permute-start = (bf16[8,2,512,128]{3,2,1,0:T(8,128)(2,1)S(1)}, bf16[8,2,512,128]{3,2,1,0:T(8,128)(2,1)}, u32[]{:S(2)}, u32[]{:S(2)}) collective-permute-start(bf16[8,2,512,128]{3,2,1,0:T(8,128)(2,1)S(1)} %all_to_all.15.own), channel_id=1, source_target_pairs={{0,1},{1,0},{2,3},{3,2},{4,5},{5,4},{6,7},{7,6},{8,9},{9,8},{10,11... | collective-permute-start | bytes 6291464 | tf_op jit(solution)/shard_map/ppermute | solution.py:23
  88.5 26.2 %collective-permute-start.1 = (bf16[4,64,1024]{2,1,0:T(8,128)(2,1)}, bf16[4,64,1024]{2,1,0:T(8,128)(2,1)S(1)}, u32[]{:S(2)}, u32[]{:S(2)}) collective-permute-start(bf16[4,64,1024]{2,1,0:T(8,128)(2,1)} %all-to-all-done.2), channel_id=1, source_target_pairs={{0,16},{16,0},{32,48},{48,32},{64,80},{80,64},{96,112},{112,96},{1... | collective-permute-start | bytes 1572872 | tf_op jit(solution)/shard_map/ppermute | solution.py:19
  102.5 29.6 %collective-permute-start.2 = (bf16[4,64,1024]{2,1,0:T(8,128)(2,1)}, bf16[4,64,1024]{2,1,0:T(8,128)(2,1)}, u32[]{:S(2)}, u32[]{:S(2)}) collective-permute-start(bf16[4,64,1024]{2,1,0:T(8,128)(2,1)} %all-to-all-done.2), channel_id=1, source_target_pairs={{0,64},{16,80},{32,96},{48,112},{64,128},{80,144},{96,160},{112,17... | collective-permute-start | bytes 1572872 | tf_op jit(solution)/shard_map/ppermute | solution.py:15
  115.8 31.5 %collective-permute-start.5 = (bf16[2,4,64,1024]{3,2,1,0:T(8,128)(2,1)S(1)}, bf16[2,4,64,1024]{3,2,1,0:T(8,128)(2,1)}, u32[]{:S(2)}, u32[]{:S(2)}) collective-permute-start(bf16[2,4,64,1024]{3,2,1,0:T(8,128)(2,1)S(1)} %pad_maximum_fusion.near), channel_id=1, source_target_pairs={{0,480},{16,496},{32,0},{48,16},{64,32},{80,48},{96,64},{112,80},{... | collective-permute-start | bytes 3145736 | tf_op jit(solution)/shard_map/ppermute | solution.py:15
  117.9 36.9 %collective-permute-start.4 = (bf16[2,4,64,1024]{3,2,1,0:T(8,128)(2,1)S(1)}, bf16[2,4,64,1024]{3,2,1,0:T(8,128)(2,1)}, u32[]{:S(2)}, u32[]{:S(2)}) collective-permute-start(bf16[2,4,64,1024]{3,2,1,0:T(8,128)(2,1)S(1)} %pad_maximum_fusion.near), channel_id=1, source_target_pairs={{0,32},{16,48},{32,64},{48,80},{64,96},{80,112},{96,128},{112,144}... | collective-permute-start | bytes 3145736 | tf_op jit(solution)/shard_map/ppermute | solution.py:15
  132.1 15.1 %collective-permute-start.3 = (bf16[4,64,1024]{2,1,0:T(8,128)(2,1)}, bf16[4,64,1024]{2,1,0:T(8,128)(2,1)}, u32[]{:S(2)}, u32[]{:S(2)}) collective-permute-start(bf16[4,64,1024]{2,1,0:T(8,128)(2,1)} %collective-permute-done.2.two), channel_id=1, source_target_pairs={{0,16},{16,0},{32,48},{48,32},{64,80},{80,64},{96,112},{112,96},{1... | collective-permute-start | bytes 1572872 | tf_op jit(solution)/shard_map/ppermute | solution.py:19

commit v4 on v3

--- a/solution.py
+++ b/solution.py
@@ -7,7 +7,7 @@
 
 OI = 4
 CORE_GROUPS = [list(range(c, 16, 2)) for c in range(2)]
-FAR_GROUPS = [[(4 * q + m) * 2 + x for q in range(4)] for m in range(4) for x in range(2)]
+FAR = (0, -4, 4, 8)
 NTILE = 256
 
 
@@ -40,16 +40,17 @@
     blocks = (
         (near.at[0], 0, xl),
         (near.at[1], 0, 1 - xl),
-        (two, 2, xl),
-        (two_partner, 2, 1 - xl),
-        (up.at[0], 3, xl),
-        (up.at[1], 3, 1 - xl),
+        (two, -2, xl),
+        (two_partner, -2, 1 - xl),
+        (up.at[0], -1, xl),
+        (up.at[1], -1, 1 - xl),
         (down.at[0], 1, xl),
         (down.at[1], 1, 1 - xl),
     )
     for ref, shift, x_index in blocks:
-        m = (z + shift) & 3
-        copies.append((ref, ints.at[(m + core) & 1, :, m >> 1, x_index]))
+        for slot, offset in enumerate(FAR):
+            k = (z + shift + offset) & 15
+            copies.append((ref.at[slot], ints.at[(k + core) & 1, k >> 1, x_index]))
     copies = [pltpu.make_async_copy(a, b, sem) for a, b in copies]
     for copy in copies:
         copy.start()
@@ -60,7 +61,7 @@
         cols = pl.ds(pl.multiple_of(n * NTILE, NTILE), NTILE)
         total = None
         for side in range(2):
-            right = ints[side, :, :, :, :, cols].reshape(-1, NTILE)
+            right = ints[side, :, :, :, cols].reshape(-1, NTILE)
             term = jnp.dot(
                 amps[side, 0], right, preferred_element_type=jnp.float32
             ) - jnp.dot(amps[side, 1], right, preferred_element_type=jnp.float32)
@@ -77,7 +78,10 @@
     rows, cols = integrals.shape
     depth, pairs = amplitudes.shape
 
-    block = spread(integrals, "row", FAR_GROUPS)
+    far = z_shift(integrals, 8)
+    up4 = z_shift(integrals, 4)
+    down4 = z_shift(integrals, -4)
+    block = jnp.stack([integrals, up4, down4, far])
 
     scale = jnp.repeat(tile_mask.astype(jnp.bfloat16).reshape(-1), pairs // OI)
     masked = (amplitudes * scale[None, :]).T
@@ -100,7 +104,7 @@
         in_specs=[pl.BlockSpec(memory_space=pltpu.SMEM)] + [anywhere] * 7,
         out_specs=pl.BlockSpec(memory_space=pltpu.VMEM),
         scratch_shapes=[
-            pltpu.VMEM((2, 4, 2, 2, rows, cols), jnp.bfloat16),
+            pltpu.VMEM((2, 8, 2, rows, cols), jnp.bfloat16),
             pltpu.VMEM((2, 2, pairs, 8 * depth), jnp.bfloat16),
             pltpu.SemaphoreType.DMA,
         ],

time: 165 us -> 171 us (1.036)
  waiting for transfers between devices: 64.3 us -> 74.8 us
  starting transfers between devices: 54.6 us -> 50.8 us
    ppermute x3 -> x6, waiting for transfers between devices: 18.5 us -> 38.6 us  [z_shift(): return lax.ppermute(x, 'row', [(r, (r + 2 * d) % 32) for r in range(32)])]
    all_to_all x1 -> x0, waiting for transfers between devices: 11.7 us -> none  [spread(): lax.all_to_all(copies, axis, split_axis=0, concat_axis=0, tiled=True, axi...]
    ppermute x3 -> x6, starting transfers between devices: 9.72 us -> 21 us  [z_shift(): return lax.ppermute(x, 'row', [(r, (r + 2 * d) % 32) for r in range(32)])]
    ppermute x2, starting transfers between devices: 16.6 us -> 5.76 us  [x_swap(): return lax.ppermute(x, 'row', [(r, r ^ 1) for r in range(32)])]
    all_to_all x1 -> x0, starting transfers between devices: 5.37 us -> none  [spread(): lax.all_to_all(copies, axis, split_axis=0, concat_axis=0, tiled=True, axi...]
    ppermute x2, waiting for transfers between devices: 20.2 us -> 22.3 us  [x_swap(): return lax.ppermute(x, 'row', [(r, r ^ 1) for r in range(32)])]
  transfers between devices with their start and end apart: 8 -> 10, of which waited for: 6 -> 9; matrix products, arithmetic and copies ran while one was open for 1% -> 0% of each run, Pallas kernels for 0% -> 0%
where the time goes in v4:
time: 171 us; the launch traced here: 170 us
  waiting for transfers between devices  74.8 us (44%)
  starting transfers between devices  50.8 us (30%)
  blocking collectives  30.5 us (18%)
  Pallas kernels  10.4 us (6%)
  local copies, waits for them, and re-layouts  2.25 us (1%)
    ppermute x6, waiting for transfers between devices, z_shift(): return lax.ppermute(x, 'row', [(r, (r + 2 * d) % 32) for r in range(32)])  38.6 us
    all_to_all x1, blocking collectives, spread(): lax.all_to_all(copies, axis, split_axis=0, concat_axis=0, tiled=True, axi...  30.5 us
    ppermute x2, waiting for transfers between devices, x_swap(): return lax.ppermute(x, 'row', [(r, r ^ 1) for r in range(32)])  22.3 us
    ppermute x6, starting transfers between devices, z_shift(): return lax.ppermute(x, 'row', [(r, (r + 2 * d) % 32) for r in range(32)])  21 us
    all_to_all x1, starting transfers between devices, on_device(): got = lax.all_to_all(sent, 'row', split_axis=0, concat_axis=0, tiled=True)  17 us
    all_to_all x1, waiting for transfers between devices, on_device(): got = lax.all_to_all(sent, 'row', split_axis=0, concat_axis=0, tiled=True)  13.9 us
    pallas_call x1, Pallas kernels, on_device(): pl.pallas_call(products, out_shape=jax.ShapeDtypeStruct((pairs, cols), jn...  10.4 us
    ppermute x1, starting transfers between devices, core_swap(): return lax.ppermute(x, 'col', [(c, c ^ 1) for c in range(16)])  7.04 us
  transfers between devices with their start and end apart: 10, of which 9 were waited for; matrix products, arithmetic and copies ran while one was open for 0% of the time, Pallas kernels for 0%

profile of v4, /device:TPU:1, one launch (start us, length us, event | category | flops | bytes accessed | tf_op | source)
XLA Modules:
  0.0 170.1 jit_solution(14217431906589954174)
XLA Ops:
  0.0 0.7 convert_bitcast_fusion
  0.7 0.1 broadcast_bitcast_fusion
  0.7 1.0 copy.8
  1.8 0.1 broadcast_multiply_fusion
  1.9 0.7 copy.9
  2.6 17.0 %all-to-all-start = ((bf16[32,4,4,128]{3,1,2,0:T(4,128)(2,1)}), bf16[32,4,4,128]{3,1,2,0:T(4,128)(2,1)S(1)}, u32[]{:S(2)}, u32[]{:S(2)}) async-start(bf16[32,4,4,128]{3,1,2,0:T(4,128)(2,1)} %copy.9), calls=%async_computation | async-start | bytes 262144 | tf_op jit(solution)/shard_map/all_to_all | solution.py:89
  19.6 0.1 fusion.1
  19.7 13.9 %all-to-all-done = bf16[32,4,4,128]{3,1,2,0:T(4,128)(2,1)S(1)} async-done(((bf16[32,4,4,128]{3,1,2,0:T(4,128)(2,1)}), bf16[32,4,4,128]{3,1,2,0:T(4,128)(2,1)S(1)}, u32[]{:S(2)}, u32[]{:S(2)}) %all-to-all-start) | async-done | bytes 131104 | tf_op jit(solution)/shard_map/all_to_all | solution.py:89
  33.6 0.1 copy.10
  33.7 0.4 broadcast_in_dim.10
  34.1 0.0 copy-start
  34.1 30.5 %all_to_all.10.own = bf16[8,2,512,128]{3,2,1,0:T(8,128)(2,1)S(1)} all-to-all(bf16[8,2,512,128]{3,2,1,0:T(8,128)(2,1)S(1)} %broadcast_in_dim.10), channel_id=1, replica_groups={{0,2,4,6,8,10,12,14},{1,3,5,7,9,11,13,15},{16,18,20,22,24,26,28,30},{17..., dimensions={0} | all-to-all | bytes 4194304 | tf_op jit(solution)/shard_map/all_to_all | solution.py:28
  64.6 7.0 %collective-permute-start = (bf16[8,2,512,128]{3,2,1,0:T(8,128)(2,1)S(1)}, bf16[8,2,512,128]{3,2,1,0:T(8,128)(2,1)}, u32[]{:S(2)}, u32[]{:S(2)}) collective-permute-start(bf16[8,2,512,128]{3,2,1,0:T(8,128)(2,1)S(1)} %all_to_all.10.own), channel_id=1, source_target_pairs={{0,1},{1,0},{2,3},{3,2},{4,5},{5,4},{6,7},{7,6},{8,9},{9,8},{10,11... | collective-permute-start | bytes 6291464 | tf_op jit(solution)/shard_map/ppermute | solution.py:23
  71.6 0.0 copy-done
  71.7 3.4 %collective-permute-start.1 = (bf16[64,1024]{1,0:T(8,128)(2,1)S(1)}, bf16[64,1024]{1,0:T(8,128)(2,1)S(1)}, u32[]{:S(2)}, u32[]{:S(2)}) collective-permute-start(bf16[64,1024]{1,0:T(8,128)(2,1)S(1)} %copy-done), channel_id=1, source_target_pairs={{0,128},{16,144},{32,160},{48,176},{64,192},{80,208},{96,224},{112... | collective-permute-start | bytes 393224 | tf_op jit(solution)/shard_map/ppermute | solution.py:15
  75.0 8.0 %collective-permute-start.3 = (bf16[64,1024]{1,0:T(8,128)(2,1)S(1)}, bf16[64,1024]{1,0:T(8,128)(2,1)S(1)}, u32[]{:S(2)}, u32[]{:S(2)}) collective-permute-start(bf16[64,1024]{1,0:T(8,128)(2,1)S(1)} %copy-done), channel_id=1, source_target_pairs={{0,256},{16,272},{32,288},{48,304},{64,320},{80,336},{96,352},{112... | collective-permute-start | bytes 393224 | tf_op jit(solution)/shard_map/ppermute | solution.py:15
  83.0 2.5 %collective-permute-start.2 = (bf16[64,1024]{1,0:T(8,128)(2,1)S(1)}, bf16[64,1024]{1,0:T(8,128)(2,1)S(1)}, u32[]{:S(2)}, u32[]{:S(2)}) collective-permute-start(bf16[64,1024]{1,0:T(8,128)(2,1)S(1)} %copy-done), channel_id=1, source_target_pairs={{0,384},{16,400},{32,416},{48,432},{64,448},{80,464},{96,480},{112... | collective-permute-start | bytes 393224 | tf_op jit(solution)/shard_map/ppermute | solution.py:15
  85.5 4.7 %collective-permute-done.1 = bf16[64,1024]{1,0:T(8,128)(2,1)S(1)} collective-permute-done((bf16[64,1024]{1,0:T(8,128)(2,1)S(1)}, bf16[64,1024]{1,0:T(8,128)(2,1)S(1)}, u32[]{:S(2)}, u32[]{:S(2)}) %collective-permute-start.1) | collective-permute-done | bytes 131104 | tf_op jit(solution)/shard_map/ppermute | solution.py:15
  90.1 12.1 %collective-permute-done.3 = bf16[64,1024]{1,0:T(8,128)(2,1)S(1)} collective-permute-done((bf16[64,1024]{1,0:T(8,128)(2,1)S(1)}, bf16[64,1024]{1,0:T(8,128)(2,1)S(1)}, u32[]{:S(2)}, u32[]{:S(2)}) %collective-permute-start.3) | collective-permute-done | bytes 131104 | tf_op jit(solution)/shard_map/ppermute | solution.py:15
  102.2 7.9 %collective-permute-done.2 = bf16[64,1024]{1,0:T(8,128)(2,1)S(1)} collective-permute-done((bf16[64,1024]{1,0:T(8,128)(2,1)S(1)}, bf16[64,1024]{1,0:T(8,128)(2,1)S(1)}, u32[]{:S(2)}, u32[]{:S(2)}) %collective-permute-start.2) | collective-permute-done | bytes 131104 | tf_op jit(solution)/shard_map/ppermute | solution.py:15
  110.2 0.1 fusion
  110.2 2.4 %collective-permute-start.4 = (bf16[4,64,1024]{2,1,0:T(8,128)(2,1)S(1)}, bf16[4,64,1024]{2,1,0:T(8,128)(2,1)S(1)}, u32[]{:S(2)}, u32[]{:S(2)}) collective-permute-start(bf16[4,64,1024]{2,1,0:T(8,128)(2,1)S(1)} %get-tuple-element.6), channel_id=1, source_target_pairs={{0,16},{16,0},{32,48},{48,32},{64,80},{80,64},{96,112},{112,96},{1... | collective-permute-start | bytes 1572872 | tf_op jit(solution)/shard_map/ppermute | solution.py:19
  112.7 1.9 %collective-permute-start.5 = (bf16[4,64,1024]{2,1,0:T(8,128)(2,1)S(1)}, bf16[4,64,1024]{2,1,0:T(8,128)(2,1)}, u32[]{:S(2)}, u32[]{:S(2)}) collective-permute-start(bf16[4,64,1024]{2,1,0:T(8,128)(2,1)S(1)} %get-tuple-element.6), channel_id=1, source_target_pairs={{0,64},{16,80},{32,96},{48,112},{64,128},{80,144},{96,160},{112,17... | collective-permute-start | bytes 1572872 | tf_op jit(solution)/shard_map/ppermute | solution.py:15
  114.6 10.7 %collective-permute-done.4 = bf16[4,64,1024]{2,1,0:T(8,128)(2,1)S(1)} collective-permute-done((bf16[4,64,1024]{2,1,0:T(8,128)(2,1)S(1)}, bf16[4,64,1024]{2,1,0:T(8,128)(2,1)S(1)}, u32[]{:S(2)}, u32[]{:S(2)}) %collective-permute-start.4) | collective-permute-done | bytes 524320 | tf_op jit(solution)/shard_map/ppermute | solution.py:19
  125.2 0.1 pad_maximum_fusion.near
  125.3 1.9 %collective-permute-start.8 = (bf16[2,4,64,1024]{3,2,1,0:T(8,128)(2,1)S(1)}, bf16[2,4,64,1024]{3,2,1,0:T(8,128)(2,1)}, u32[]{:S(2)}, u32[]{:S(2)}) collective-permute-start(bf16[2,4,64,1024]{3,2,1,0:T(8,128)(2,1)S(1)} %pad_maximum_fusion.near), channel_id=1, source_target_pairs={{0,480},{16,496},{32,0},{48,16},{64,32},{80,48},{96,64},{112,80},{... | collective-permute-start | bytes 3145736 | tf_op jit(solution)/shard_map/ppermute | solution.py:15
  127.3 3.4 %collective-permute-start.7 = (bf16[2,4,64,1024]{3,2,1,0:T(8,128)(2,1)S(1)}, bf16[2,4,64,1024]{3,2,1,0:T(8,128)(2,1)}, u32[]{:S(2)}, u32[]{:S(2)}) collective-permute-start(bf16[2,4,64,1024]{3,2,1,0:T(8,128)(2,1)S(1)} %pad_maximum_fusion.near), channel_id=1, source_target_pairs={{0,32},{16,48},{32,64},{48,80},{64,96},{80,112},{96,128},{112,144}... | collective-permute-start | bytes 3145736 | tf_op jit(solution)/shard_map/ppermute | solution.py:15
  130.6 4.0 %collective-permute-done.5.two = bf16[4,64,1024]{2,1,0:T(8,128)(2,1)} collective-permute-done((bf16[4,64,1024]{2,1,0:T(8,128)(2,1)S(1)}, bf16[4,64,1024]{2,1,0:T(8,128)(2,1)}, u32[]{:S(2)}, u32[]{:S(2)}) %collective-permute-start.5) | collective-permute-done | bytes 524320 | tf_op jit(solution)/shard_map/ppermute | solution.py:15
  134.6 3.4 %collective-permute-start.6 = (bf16[4,64,1024]{2,1,0:T(8,128)(2,1)}, bf16[4,64,1024]{2,1,0:T(8,128)(2,1)}, u32[]{:S(2)}, u32[]{:S(2)}) collective-permute-start(bf16[4,64,1024]{2,1,0:T(8,128)(2,1)} %collective-permute-done.5.two), channel_id=1, source_target_pairs={{0,16},{16,0},{32,48},{48,32},{64,80},{80,64},{96,112},{112,96},{1... | collective-permute-start | bytes 1572872 | tf_op jit(solution)/shard_map/ppermute | solution.py:19
  138.0 0.1 pad_add_fusion.place
  138.1 11.6 %collective-permute-done.6.two_partner = bf16[4,64,1024]{2,1,0:T(8,128)(2,1)} collective-permute-done((bf16[4,64,1024]{2,1,0:T(8,128)(2,1)}, bf16[4,64,1024]{2,1,0:T(8,128)(2,1)}, u32[]{:S(2)}, u32[]{:S(2)}) %collective-permute-start.6) | collective-permute-done | bytes 524320 | tf_op jit(solution)/shard_map/ppermute | solution.py:19
  149.7 1.1 collective-permute-done.8.down
  150.8 8.9 %collective-permute-done.7.up = bf16[2,4,64,1024]{3,2,1,0:T(8,128)(2,1)} collective-permute-done((bf16[2,4,64,1024]{3,2,1,0:T(8,128)(2,1)S(1)}, bf16[2,4,64,1024]{3,2,1,0:T(8,128)(2,1)}, u32[]{:S(2)}, u32[]{:S(2)}) %collective-permute-start.7) | collective-permute-done | bytes 1048608 | tf_op jit(solution)/shard_map/ppermute | solution.py:15
  159.7 0.0 collective-permute-done.other
  159.7 10.4 %shard_map.37 = bf16[512,1024]{1,0:T(8,128)(2,1)} custom-call(s32[3]{0:T(128)S(1)} %pad_add_fusion.place, bf16[8,2,512,128]{3,2,1,0:T(8,128)(2,1)S(1)} %all_to_all.10.own, bf16[8,2,512,128]{3,2,1,0:T(8,128)(2,1)} %collective-permute-done.other, bf16[2,4,64,1024]{3,2,1,0:T(8,128)(2,1)S(1)} %pad_maximum_fusion.near, ...), custom_call_target="tpu_custom_call" | custom-call | flops 4294967296 | bytes 9437184 | tf_op jit(solution)/shard_map/pallas_call | solution.py:101
  (1 shorter events, 0.0 us)
Async XLA Ops:
  2.6 31.0 %all-to-all-start = ((bf16[32,4,4,128]{3,1,2,0:T(4,128)(2,1)}), bf16[32,4,4,128]{3,1,2,0:T(4,128)(2,1)S(1)}, u32[]{:S(2)}, u32[]{:S(2)}) async-start(bf16[32,4,4,128]{3,1,2,0:T(4,128)(2,1)} %copy.9), calls=%async_computation | async-start | bytes 262144 | tf_op jit(solution)/shard_map/all_to_all | solution.py:89
  34.1 37.5 %copy-start = (bf16[64,1024]{1,0:T(8,128)(2,1)S(1)}, bf16[64,1024]{1,0:T(8,128)(2,1)}, u32[]{:S(2)}) copy-start(bf16[64,1024]{1,0:T(8,128)(2,1)} %param.4) | copy-start | bytes 393220
  64.6 95.1 %collective-permute-start = (bf16[8,2,512,128]{3,2,1,0:T(8,128)(2,1)S(1)}, bf16[8,2,512,128]{3,2,1,0:T(8,128)(2,1)}, u32[]{:S(2)}, u32[]{:S(2)}) collective-permute-start(bf16[8,2,512,128]{3,2,1,0:T(8,128)(2,1)S(1)} %all_to_all.10.own), channel_id=1, source_target_pairs={{0,1},{1,0},{2,3},{3,2},{4,5},{5,4},{6,7},{7,6},{8,9},{9,8},{10,11... | collective-permute-start | bytes 6291464 | tf_op jit(solution)/shard_map/ppermute | solution.py:23
  71.7 18.5 %collective-permute-start.1 = (bf16[64,1024]{1,0:T(8,128)(2,1)S(1)}, bf16[64,1024]{1,0:T(8,128)(2,1)S(1)}, u32[]{:S(2)}, u32[]{:S(2)}) collective-permute-start(bf16[64,1024]{1,0:T(8,128)(2,1)S(1)} %copy-done), channel_id=1, source_target_pairs={{0,128},{16,144},{32,160},{48,176},{64,192},{80,208},{96,224},{112... | collective-permute-start | bytes 393224 | tf_op jit(solution)/shard_map/ppermute | solution.py:15
  75.0 27.2 %collective-permute-start.3 = (bf16[64,1024]{1,0:T(8,128)(2,1)S(1)}, bf16[64,1024]{1,0:T(8,128)(2,1)S(1)}, u32[]{:S(2)}, u32[]{:S(2)}) collective-permute-start(bf16[64,1024]{1,0:T(8,128)(2,1)S(1)} %copy-done), channel_id=1, source_target_pairs={{0,256},{16,272},{32,288},{48,304},{64,320},{80,336},{96,352},{112... | collective-permute-start | bytes 393224 | tf_op jit(solution)/shard_map/ppermute | solution.py:15
  83.0 27.1 %collective-permute-start.2 = (bf16[64,1024]{1,0:T(8,128)(2,1)S(1)}, bf16[64,1024]{1,0:T(8,128)(2,1)S(1)}, u32[]{:S(2)}, u32[]{:S(2)}) collective-permute-start(bf16[64,1024]{1,0:T(8,128)(2,1)S(1)} %copy-done), channel_id=1, source_target_pairs={{0,384},{16,400},{32,416},{48,432},{64,448},{80,464},{96,480},{112... | collective-permute-start | bytes 393224 | tf_op jit(solution)/shard_map/ppermute | solution.py:15
  110.2 15.0 %collective-permute-start.4 = (bf16[4,64,1024]{2,1,0:T(8,128)(2,1)S(1)}, bf16[4,64,1024]{2,1,0:T(8,128)(2,1)S(1)}, u32[]{:S(2)}, u32[]{:S(2)}) collective-permute-start(bf16[4,64,1024]{2,1,0:T(8,128)(2,1)S(1)} %get-tuple-element.6), channel_id=1, source_target_pairs={{0,16},{16,0},{32,48},{48,32},{64,80},{80,64},{96,112},{112,96},{1... | collective-permute-start | bytes 1572872 | tf_op jit(solution)/shard_map/ppermute | solution.py:19
  112.7 22.0 %collective-permute-start.5 = (bf16[4,64,1024]{2,1,0:T(8,128)(2,1)S(1)}, bf16[4,64,1024]{2,1,0:T(8,128)(2,1)}, u32[]{:S(2)}, u32[]{:S(2)}) collective-permute-start(bf16[4,64,1024]{2,1,0:T(8,128)(2,1)S(1)} %get-tuple-element.6), channel_id=1, source_target_pairs={{0,64},{16,80},{32,96},{48,112},{64,128},{80,144},{96,160},{112,17... | collective-permute-start | bytes 1572872 | tf_op jit(solution)/shard_map/ppermute | solution.py:15
  125.3 25.4 %collective-permute-start.8 = (bf16[2,4,64,1024]{3,2,1,0:T(8,128)(2,1)S(1)}, bf16[2,4,64,1024]{3,2,1,0:T(8,128)(2,1)}, u32[]{:S(2)}, u32[]{:S(2)}) collective-permute-start(bf16[2,4,64,1024]{3,2,1,0:T(8,128)(2,1)S(1)} %pad_maximum_fusion.near), channel_id=1, source_target_pairs={{0,480},{16,496},{32,0},{48,16},{64,32},{80,48},{96,64},{112,80},{... | collective-permute-start | bytes 3145736 | tf_op jit(solution)/shard_map/ppermute | solution.py:15
  127.3 32.4 %collective-permute-start.7 = (bf16[2,4,64,1024]{3,2,1,0:T(8,128)(2,1)S(1)}, bf16[2,4,64,1024]{3,2,1,0:T(8,128)(2,1)}, u32[]{:S(2)}, u32[]{:S(2)}) collective-permute-start(bf16[2,4,64,1024]{3,2,1,0:T(8,128)(2,1)S(1)} %pad_maximum_fusion.near), channel_id=1, source_target_pairs={{0,32},{16,48},{32,64},{48,80},{64,96},{80,112},{96,128},{112,144}... | collective-permute-start | bytes 3145736 | tf_op jit(solution)/shard_map/ppermute | solution.py:15
  134.6 15.1 %collective-permute-start.6 = (bf16[4,64,1024]{2,1,0:T(8,128)(2,1)}, bf16[4,64,1024]{2,1,0:T(8,128)(2,1)}, u32[]{:S(2)}, u32[]{:S(2)}) collective-permute-start(bf16[4,64,1024]{2,1,0:T(8,128)(2,1)} %collective-permute-done.5.two), channel_id=1, source_target_pairs={{0,16},{16,0},{32,48},{48,32},{64,80},{80,64},{96,112},{112,96},{1... | collective-permute-start | bytes 1572872 | tf_op jit(solution)/shard_map/ppermute | solution.py:19

commit v5 on v3

v5 whole, which is shorter than its diff:
```python
import jax
import jax.numpy as jnp
from jax import lax
from jax.experimental import pallas as pl
from jax.experimental.pallas import tpu as pltpu
from jax.sharding import PartitionSpec as P

OI = 4
Q = 4
FAR_GROUPS = [[(4 * q + m) * 2 + x for q in range(4)] for m in range(4) for x in range(2)]
NEAR_GROUPS = [list(range(8 * q, 8 * q + 8)) for q in range(4)]
CORE_PAIRS = [[2 * g, 2 * g + 1] for g in range(8)]
STEPS = (((0, 1), (0, 3)), ((0, 2), (1, 0)), ((1, 1), (1, 3)), ((1, 2), (1, 2)))
NTILE = 256


def z_shift(x, d):
    return lax.ppermute(x, "row", [(r, (r + 2 * d) % 32) for r in range(32)])


def x_swap(x):
    return lax.ppermute(x, "row", [(r, r ^ 1) for r in range(32)])


def core_swap(x):
    return lax.ppermute(x, "col", [(c, c ^ 1) for c in range(16)])


def chip_shift(x, step):
    pairs = []
    for xh in range(2):
        for y in range(4):
            for c in range(2):
                dx, dy = step[c]
                pairs.append(((xh * 4 + y) * 2 + c, ((xh ^ dx) * 4 + (y + dy) % 4) * 2 + c))
    return lax.ppermute(x, "col", pairs)


def gather_chips(x):
    chip = lax.all_gather(x, "col", axis=0, axis_index_groups=CORE_PAIRS)
    got = [chip_shift(chip, step) for step in STEPS[:3]]
    got.append(chip_shift(x, STEPS[3])[None])
    return chip, jnp.concatenate(got)


def products(place, *refs):
    z, xl, core, xh, y = (place[i] for i in range(5))
    amp_refs, blocks, (out, ints, amps, sem) = refs[:6], refs[6:12], refs[12:]
    near_own, near_swap, two, two_partner, up, down = blocks
    copies = []

    def amp_copy(ref, s, dx, dy, c):
        col = ((xh ^ dx) * 4 + ((y - dy) & 3)) * 2 + c
        lanes = pl.ds(pl.multiple_of(col * 128, 128), 128)
        copies.append((ref, amps.at[s, :, lanes]))

    for s in range(2):
        chip, mine, theirs = amp_refs[3 * s : 3 * s + 3]
        for c in range(2):
            amp_copy(chip.at[c], s, 0, 0, c)
        for ref, who in ((mine, core), (theirs, 1 - core)):
            for n, step in enumerate(STEPS):
                dx = jnp.where(who == 0, step[0][0], step[1][0])
                dy = jnp.where(who == 0, step[0][1], step[1][1])
                if n < 3:
                    for c in range(2):
                        amp_copy(ref.at[2 * n + c], s, dx, dy, c)
                else:
                    amp_copy(ref.at[6], s, dx, dy, who)
    for ref, shift, x_index in (
        (near_own, 0, xl),
        (near_swap, 0, 1 - xl),
        (two, 2, xl),
        (two_partner, 2, 1 - xl),
        (up.at[0], 3, xl),
        (up.at[1], 3, 1 - xl),
        (down.at[0], 1, xl),
        (down.at[1], 1, 1 - xl),
    ):
        copies.append((ref, ints.at[:, (z + shift) & 3, x_index]))
    copies = [pltpu.make_async_copy(a, b, sem) for a, b in copies]
    for copy in copies:
        copy.start()
    for copy in copies:
        copy.wait()

    def tile(n, carry):
        cols = pl.ds(pl.multiple_of(n * NTILE, NTILE), NTILE)
        right = ints[:, :, :, :, cols].reshape(-1, NTILE)
        total = jnp.dot(amps[0], right, preferred_element_type=jnp.float32) - jnp.dot(
            amps[1], right, preferred_element_type=jnp.float32
        )
        out[:, cols] = total.astype(out.dtype)
        return carry

    lax.fori_loop(0, out.shape[1] // NTILE, tile, 0)


def on_device(amplitudes, integrals, tile_mask):
    row, col = lax.axis_index("row"), lax.axis_index("col")
    place = jnp.stack([row // 2, row % 2, col % 2, col // 8, col // 2 % 4]).astype(jnp.int32)
    rows, cols = integrals.shape
    depth, pairs = amplitudes.shape

    scale = jnp.repeat(tile_mask.astype(jnp.bfloat16).reshape(-1), pairs // OI)
    masked = (amplitudes * scale[None, :]).T

    sent = masked.reshape(OI, Q, 8, OI, depth).transpose(1, 2, 3, 0, 4).reshape(Q, -1, cols)
    load = jnp.concatenate([jnp.broadcast_to(integrals[None], (Q, rows, cols)), sent], axis=1)
    far = lax.all_to_all(
        load, "row", split_axis=0, concat_axis=0, tiled=True, axis_index_groups=FAR_GROUPS
    )
    amps = gather_chips(masked)
    block = far[:, :rows]
    hop, amps = lax.optimization_barrier((far[:, rows:], amps))
    hop = hop.reshape(Q, 8, OI, OI, depth).transpose(1, 0, 2, 3, 4)
    got = lax.all_to_all(
        hop, "row", split_axis=0, concat_axis=0, tiled=True, axis_index_groups=NEAR_GROUPS
    )
    swapped = got.transpose(2, 1, 0, 3, 4).reshape(pairs, depth)

    two = z_shift(block, 2)
    partner = x_swap(block)
    partner, two = lax.optimization_barrier((partner, two))
    near = jnp.stack([block, partner])
    up = z_shift(near, 1)
    down = z_shift(near, -1)
    two_partner = x_swap(two)
    swap_amps = gather_chips(swapped)

    anywhere = pl.BlockSpec(memory_space=pl.ANY)
    return pl.pallas_call(
        products,
        out_shape=jax.ShapeDtypeStruct((pairs, cols), jnp.bfloat16),
        in_specs=[pl.BlockSpec(memory_space=pltpu.SMEM)] + [anywhere] * 12,
        out_specs=pl.BlockSpec(memory_space=pltpu.VMEM),
        scratch_shapes=[
            pltpu.VMEM((Q, 4, 2, rows, cols), jnp.bfloat16),
            pltpu.VMEM((2, pairs, 16 * depth), jnp.bfloat16),
            pltpu.SemaphoreType.DMA,
        ],
        compiler_params=pltpu.CompilerParams(vmem_limit_bytes=40 * 2**20),
        cost_estimate=pl.CostEstimate(
            flops=4 * pairs * 2048 * cols, bytes_accessed=9 * 2**20, transcendentals=0
        ),
    )(place, *amps, core_swap(amps[1]), *swap_amps, core_swap(swap_amps[1]), block, partner, two, two_partner, up, down)


def solution(mesh):
    in_specs = (P("col", "row"), P("row", "col"), P("col", "row"))
    out_specs = P("row", "col")
    return jax.shard_map(
        on_device, mesh=mesh, in_specs=in_specs, out_specs=out_specs, check_vma=False
    )
```

time: 165 us -> 146 us (0.88)
  waiting for transfers between devices: 64.3 us -> 35.5 us
  starting transfers between devices: 54.6 us -> 83.3 us
  blocking collectives: 30.5 us -> 10.4 us
    ppermute x0 -> x8, starting transfers between devices: none -> 32.7 us  [chip_shift(): return lax.ppermute(x, 'col', pairs)]
    all_to_all x1 -> x0, blocking collectives: 30.5 us -> none  [spread(): lax.all_to_all(copies, axis, split_axis=0, concat_axis=0, tiled=True, axi...]
    all_to_all x2, waiting for transfers between devices: 25.6 us -> 5.17 us  [the longest x1 5.17 us: on_device(): lax.all_to_all(load, 'row', split_axis=0, concat_axis=0, tiled=True, axis...]
    ppermute x3, waiting for transfers between devices: 18.5 us -> 7.38 us  [z_shift(): return lax.ppermute(x, 'row', [(r, (r + 2 * d) % 32) for r in range(32)])]
    ppermute x0 -> x8, waiting for transfers between devices: none -> 10.5 us  [chip_shift(): return lax.ppermute(x, 'col', pairs)]
    all_gather x0 -> x2, blocking collectives: none -> 10.4 us  [gather_chips(): chip = lax.all_gather(x, 'col', axis=0, axis_index_groups=CORE_PAIRS)]
    ppermute x2, starting transfers between devices: 16.6 us -> 7.01 us  [x_swap(): return lax.ppermute(x, 'row', [(r, r ^ 1) for r in range(32)])]
    ppermute x2, waiting for transfers between devices: 20.2 us -> 12.4 us  [x_swap(): return lax.ppermute(x, 'row', [(r, r ^ 1) for r in range(32)])]
  transfers between devices with their start and end apart: 8 -> 17, of which waited for: 6 -> 5; matrix products, arithmetic and copies ran while one was open for 1% -> 1% of each run, Pallas kernels for 0% -> 0%
where the time goes in v5:
time: 146 us; the launch traced here: 144 us
  starting transfers between devices  83.3 us (57%)
  waiting for transfers between devices  35.5 us (24%)
  blocking collectives  10.4 us (7%)
  Pallas kernels  9.48 us (6%)
  other arithmetic  3.13 us (2%)
  local copies, waits for them, and re-layouts  2.4 us (2%)
    ppermute x8, starting transfers between devices, chip_shift(): return lax.ppermute(x, 'col', pairs)  32.7 us
    all_to_all x1, starting transfers between devices, on_device(): lax.all_to_all(load, 'row', split_axis=0, concat_axis=0, tiled=True, axis...  15.6 us
    ppermute x3, starting transfers between devices, z_shift(): return lax.ppermute(x, 'row', [(r, (r + 2 * d) % 32) for r in range(32)])  13.7 us
    ppermute x2, waiting for transfers between devices, x_swap(): return lax.ppermute(x, 'row', [(r, r ^ 1) for r in range(32)])  12.4 us
    ppermute x8, waiting for transfers between devices, chip_shift(): return lax.ppermute(x, 'col', pairs)  10.5 us
    all_gather x2, blocking collectives, gather_chips(): chip = lax.all_gather(x, 'col', axis=0, axis_index_groups=CORE_PAIRS)  10.4 us
    pallas_call x1, Pallas kernels, on_device(): pl.pallas_call(products, out_shape=jax.ShapeDtypeStruct((pairs, cols), jn...  9.48 us
    ppermute x2, starting transfers between devices, core_swap(): return lax.ppermute(x, 'col', [(c, c ^ 1) for c in range(16)])  7.72 us
  transfers between devices with their start and end apart: 17, of which 5 were waited for; matrix products, arithmetic and copies ran while one was open for 1% of the time, Pallas kernels for 0%

profile of v5, /device:TPU:1, one launch (start us, length us, event | category | flops | bytes accessed | tf_op | source)
XLA Modules:
  0.0 144.5 jit_solution(6026262240355104337)
XLA Ops:
  0.0 0.0 copy-start
  0.0 1.1 copy.12
  1.1 0.7 convert_bitcast_fusion
  1.7 0.1 broadcast_bitcast_fusion
  1.8 0.1 broadcast_multiply_fusion
  1.9 0.1 copy.20
  2.1 0.1 reshape.19
  2.1 0.0 copy-done
  2.1 0.1 broadcast_in_dim.15
  2.2 0.9 pad_maximum_fusion.3
  3.1 15.6 %all-to-all-start = ((bf16[4,80,1024]{2,1,0:T(8,128)(2,1)}), bf16[4,80,1024]{2,1,0:T(8,128)(2,1)S(1)}, u32[]{:S(2)}, u32[]{:S(2)}) async-start(bf16[4,80,1024]{2,1,0:T(8,128)(2,1)} %pad_maximum_fusion.3), calls=%async_computation | async-start | bytes 1310720 | tf_op jit(solution)/shard_map/all_to_all | solution.py:110
  18.7 0.1 fusion
  18.9 2.6 %all-gather = bf16[1024,128]{1,0:T(8,128)(2,1)S(1)} all-gather(bf16[512,128]{1,0:T(8,128)(2,1)S(1)} %fusion), channel_id=2, replica_groups={{0,1},{2,3},{4,5},{6,7},{8,9},{10,11},{12,13},{14,15},{16,17},{18,19},{..., dimensions={0}, use_global_device_ids=true | all-gather | bytes 393216 | tf_op jit(solution)/shard_map/all_gather | solution.py:40
  21.4 4.6 %collective-permute-start = (bf16[2,512,128]{2,1,0:T(8,128)(2,1)S(1)}, bf16[2,512,128]{2,1,0:T(8,128)(2,1)S(1)}, u32[]{:S(2)}, u32[]{:S(2)}) collective-permute-start(bf16[2,512,128]{2,1,0:T(8,128)(2,1)S(1)} %bitcast.29), channel_id=1, source_target_pairs={{0,2},{1,7},{2,4},{3,1},{4,6},{5,3},{6,0},{7,5},{8,10},{9,15},{10,... | collective-permute-start | bytes 786440 | tf_op jit(solution)/shard_map/ppermute | solution.py:36
  26.1 4.7 %collective-permute-start.1 = (bf16[2,512,128]{2,1,0:T(8,128)(2,1)S(1)}, bf16[2,512,128]{2,1,0:T(8,128)(2,1)S(1)}, u32[]{:S(2)}, u32[]{:S(2)}) collective-permute-start(bf16[2,512,128]{2,1,0:T(8,128)(2,1)S(1)} %bitcast.30), channel_id=1, source_target_pairs={{0,4},{1,9},{2,6},{3,11},{4,0},{5,13},{6,2},{7,15},{8,12},{9,1},{1... | collective-permute-start | bytes 786440 | tf_op jit(solution)/shard_map/ppermute | solution.py:36
  30.7 2.3 %collective-permute-start.2 = (bf16[2,512,128]{2,1,0:T(8,128)(2,1)S(1)}, bf16[2,512,128]{2,1,0:T(8,128)(2,1)S(1)}, u32[]{:S(2)}, u32[]{:S(2)}) collective-permute-start(bf16[2,512,128]{2,1,0:T(8,128)(2,1)S(1)} %bitcast.31), channel_id=1, source_target_pairs={{0,10},{1,15},{2,12},{3,9},{4,14},{5,11},{6,8},{7,13},{8,2},{9,7},... | collective-permute-start | bytes 786440 | tf_op jit(solution)/shard_map/ppermute | solution.py:36
  33.1 4.4 %collective-permute-start.3 = (bf16[512,128]{1,0:T(8,128)(2,1)S(1)}, bf16[512,128]{1,0:T(8,128)(2,1)S(1)}, u32[]{:S(2)}, u32[]{:S(2)}) collective-permute-start(bf16[512,128]{1,0:T(8,128)(2,1)S(1)} %fusion), channel_id=1, source_target_pairs={{0,12},{1,13},{2,14},{3,15},{4,8},{5,9},{6,10},{7,11},{8,4},{9,5},... | collective-permute-start | bytes 393224 | tf_op jit(solution)/shard_map/ppermute | solution.py:36
  37.5 7.0 %collective-permute-done.3 = bf16[512,128]{1,0:T(8,128)(2,1)S(1)} collective-permute-done((bf16[512,128]{1,0:T(8,128)(2,1)S(1)}, bf16[512,128]{1,0:T(8,128)(2,1)S(1)}, u32[]{:S(2)}, u32[]{:S(2)}) %collective-permute-start.3) | collective-permute-done | bytes 131104 | tf_op jit(solution)/shard_map/ppermute | solution.py:36
  44.4 0.0 collective-permute-done
  44.5 0.0 collective-permute-done.1
  44.5 0.0 collective-permute-done.2
  44.5 0.1 pad_maximum_fusion.1.refs_1_
  44.6 5.2 %all-to-all-done = bf16[4,80,1024]{2,1,0:T(8,128)(2,1)S(1)} async-done(((bf16[4,80,1024]{2,1,0:T(8,128)(2,1)}), bf16[4,80,1024]{2,1,0:T(8,128)(2,1)S(1)}, u32[]{:S(2)}, u32[]{:S(2)}) %all-to-all-start) | async-done | bytes 655392 | tf_op jit(solution)/shard_map/all_to_all | solution.py:110
  49.8 0.1 reshape.20
  49.9 0.7 copy.19
  50.6 6.5 %all-to-all-start.1 = ((bf16[8,4,4,4,128]{4,3,2,1,0:T(4,128)(2,1)}), bf16[8,4,4,4,128]{4,3,2,1,0:T(4,128)(2,1)S(1)}, u32[]{:S(2)}, u32[]{:S(2)}) async-start(bf16[8,4,4,4,128]{4,3,2,1,0:T(4,128)(2,1)} %bitcast.26), calls=%async_computation.1 | async-start | bytes 262144 | tf_op jit(solution)/shard_map/all_to_all | solution.py:117
  57.1 0.1 slice_bitcast_fusion
  57.2 3.4 %collective-permute-start.10 = (bf16[4,64,1024]{2,1,0:T(8,128)(2,1)S(1)}, bf16[4,64,1024]{2,1,0:T(8,128)(2,1)S(1)}, u32[]{:S(2)}, u32[]{:S(2)}) collective-permute-start(bf16[4,64,1024]{2,1,0:T(8,128)(2,1)S(1)} %get-tuple-element.16.refs_6_), channel_id=1, source_target_pairs={{0,16},{16,0},{32,48},{48,32},{64,80},{80,64},{96,112},{112,96},{1... | collective-permute-start | bytes 1572872 | tf_op jit(solution)/shard_map/ppermute | solution.py:22
  60.6 4.0 %collective-permute-start.11 = (bf16[4,64,1024]{2,1,0:T(8,128)(2,1)S(1)}, bf16[4,64,1024]{2,1,0:T(8,128)(2,1)}, u32[]{:S(2)}, u32[]{:S(2)}) collective-permute-start(bf16[4,64,1024]{2,1,0:T(8,128)(2,1)S(1)} %get-tuple-element.16.refs_6_), channel_id=1, source_target_pairs={{0,64},{16,80},{32,96},{48,112},{64,128},{80,144},{96,160},{112,17... | collective-permute-start | bytes 1572872 | tf_op jit(solution)/shard_map/ppermute | solution.py:18
  64.6 0.0 all-to-all-done.1
  64.6 7.8 %all_gather.11.refs_3_ = bf16[2,512,128]{2,1,0:T(8,128)(2,1)S(1)} all-gather(bf16[1,512,128]{2,1,0:T(8,128)(2,1)S(1)} %bitcast.33), channel_id=1, replica_groups={{0,1},{2,3},{4,5},{6,7},{8,9},{10,11},{12,13},{14,15},{16,17},{18,19},{..., dimensions={0}, use_global_device_ids=true | all-gather | bytes 393216 | tf_op jit(solution)/shard_map/all_gather | solution.py:40
  72.5 4.6 %collective-permute-start.5 = (bf16[2,512,128]{2,1,0:T(8,128)(2,1)S(1)}, bf16[2,512,128]{2,1,0:T(8,128)(2,1)S(1)}, u32[]{:S(2)}, u32[]{:S(2)}) collective-permute-start(bf16[2,512,128]{2,1,0:T(8,128)(2,1)S(1)} %all_gather.11.refs_3_), channel_id=1, source_target_pairs={{0,2},{1,7},{2,4},{3,1},{4,6},{5,3},{6,0},{7,5},{8,10},{9,15},{10,... | collective-permute-start | bytes 786440 | tf_op jit(solution)/shard_map/ppermute | solution.py:36
  77.1 4.4 %collective-permute-start.6 = (bf16[2,512,128]{2,1,0:T(8,128)(2,1)S(1)}, bf16[2,512,128]{2,1,0:T(8,128)(2,1)S(1)}, u32[]{:S(2)}, u32[]{:S(2)}) collective-permute-start(bf16[2,512,128]{2,1,0:T(8,128)(2,1)S(1)} %all_gather.11.refs_3_), channel_id=1, source_target_pairs={{0,4},{1,9},{2,6},{3,11},{4,0},{5,13},{6,2},{7,15},{8,12},{9,1},{1... | collective-permute-start | bytes 786440 | tf_op jit(solution)/shard_map/ppermute | solution.py:36
  81.5 2.6 %collective-permute-start.7 = (bf16[2,512,128]{2,1,0:T(8,128)(2,1)S(1)}, bf16[2,512,128]{2,1,0:T(8,128)(2,1)S(1)}, u32[]{:S(2)}, u32[]{:S(2)}) collective-permute-start(bf16[2,512,128]{2,1,0:T(8,128)(2,1)S(1)} %all_gather.11.refs_3_), channel_id=1, source_target_pairs={{0,10},{1,15},{2,12},{3,9},{4,14},{5,11},{6,8},{7,13},{8,2},{9,7},... | collective-permute-start | bytes 786440 | tf_op jit(solution)/shard_map/ppermute | solution.py:36
  84.1 0.0 collective-permute-done.10.refs_7_
  84.1 2.6 %collective-permute-start.4 = (bf16[7,512,128]{2,1,0:T(8,128)(2,1)S(1)}, bf16[7,512,128]{2,1,0:T(8,128)(2,1)}, u32[]{:S(2)}, u32[]{:S(2)}) collective-permute-start(bf16[7,512,128]{2,1,0:T(8,128)(2,1)S(1)} %pad_maximum_fusion.1.refs_1_), channel_id=1, source_target_pairs={{0,1},{1,0},{2,3},{3,2},{4,5},{5,4},{6,7},{7,6},{8,9},{9,8},{10,11... | collective-permute-start | bytes 2752520 | tf_op jit(solution)/shard_map/ppermute | solution.py:26
  86.8 0.0 collective-permute-done.11.refs_8_
  86.8 5.1 %collective-permute-start.8 = (bf16[512,128]{1,0:T(8,128)(2,1)S(1)}, bf16[512,128]{1,0:T(8,128)(2,1)S(1)}, u32[]{:S(2)}, u32[]{:S(2)}) collective-permute-start(bf16[512,128]{1,0:T(8,128)(2,1)S(1)} %bitcast.34), channel_id=1, source_target_pairs={{0,12},{1,13},{2,14},{3,15},{4,8},{5,9},{6,10},{7,11},{8,4},{9,5},... | collective-permute-start | bytes 393224 | tf_op jit(solution)/shard_map/ppermute | solution.py:36
  91.9 1.1 pad_maximum_fusion
  92.9 3.5 %collective-permute-done.8 = bf16[512,128]{1,0:T(8,128)(2,1)S(1)} collective-permute-done((bf16[512,128]{1,0:T(8,128)(2,1)S(1)}, bf16[512,128]{1,0:T(8,128)(2,1)S(1)}, u32[]{:S(2)}, u32[]{:S(2)}) %collective-permute-start.8) | collective-permute-done | bytes 131104 | tf_op jit(solution)/shard_map/ppermute | solution.py:36
  96.4 7.8 %collective-permute-start.13 = (bf16[2,4,64,1024]{3,2,1,0:T(8,128)(2,1)}, bf16[2,4,64,1024]{3,2,1,0:T(8,128)(2,1)}, u32[]{:S(2)}, u32[]{:S(2)}) collective-permute-start(bf16[2,4,64,1024]{3,2,1,0:T(8,128)(2,1)} %pad_maximum_fusion), channel_id=1, source_target_pairs={{0,32},{16,48},{32,64},{48,80},{64,96},{80,112},{96,128},{112,144}... | collective-permute-start | bytes 3145736 | tf_op jit(solution)/shard_map/ppermute | solution.py:18
  104.2 0.0 collective-permute-done.5
  104.2 1.9 %collective-permute-start.14 = (bf16[2,4,64,1024]{3,2,1,0:T(8,128)(2,1)}, bf16[2,4,64,1024]{3,2,1,0:T(8,128)(2,1)}, u32[]{:S(2)}, u32[]{:S(2)}) collective-permute-start(bf16[2,4,64,1024]{3,2,1,0:T(8,128)(2,1)} %pad_maximum_fusion), channel_id=1, source_target_pairs={{0,480},{16,496},{32,0},{48,16},{64,32},{80,48},{96,64},{112,80},{... | collective-permute-start | bytes 3145736 | tf_op jit(solution)/shard_map/ppermute | solution.py:18
  106.2 0.0 collective-permute-done.6
  106.2 0.0 collective-permute-done.7
  106.2 0.1 pad_maximum_fusion.2.refs_4_
  106.3 5.1 %collective-permute-start.9 = (bf16[7,512,128]{2,1,0:T(8,128)(2,1)S(1)}, bf16[7,512,128]{2,1,0:T(8,128)(2,1)}, u32[]{:S(2)}, u32[]{:S(2)}) collective-permute-start(bf16[7,512,128]{2,1,0:T(8,128)(2,1)S(1)} %pad_maximum_fusion.2.refs_4_), channel_id=1, source_target_pairs={{0,1},{1,0},{2,3},{3,2},{4,5},{5,4},{6,7},{7,6},{8,9},{9,8},{10,11... | collective-permute-start | bytes 2752520 | tf_op jit(solution)/shard_map/ppermute | solution.py:26
  111.4 3.6 %collective-permute-start.12 = (bf16[4,64,1024]{2,1,0:T(8,128)(2,1)}, bf16[4,64,1024]{2,1,0:T(8,128)(2,1)}, u32[]{:S(2)}, u32[]{:S(2)}) collective-permute-start(bf16[4,64,1024]{2,1,0:T(8,128)(2,1)} %collective-permute-done.11.refs_8_), channel_id=1, source_target_pairs={{0,16},{16,0},{32,48},{48,32},{64,80},{80,64},{96,112},{112,96},{1... | collective-permute-start | bytes 1572872 | tf_op jit(solution)/shard_map/ppermute | solution.py:22
  115.1 0.1 stack.32.place
  115.2 0.0 collective-permute-done.4.refs_2_
  115.2 12.4 %collective-permute-done.12.refs_9_ = bf16[4,64,1024]{2,1,0:T(8,128)(2,1)} collective-permute-done((bf16[4,64,1024]{2,1,0:T(8,128)(2,1)}, bf16[4,64,1024]{2,1,0:T(8,128)(2,1)}, u32[]{:S(2)}, u32[]{:S(2)}) %collective-permute-start.12) | collective-permute-done | bytes 524320 | tf_op jit(solution)/shard_map/ppermute | solution.py:22
  127.6 0.0 collective-permute-done.13.refs_10_
  127.6 7.4 %collective-permute-done.14.refs_11_ = bf16[2,4,64,1024]{3,2,1,0:T(8,128)(2,1)} collective-permute-done((bf16[2,4,64,1024]{3,2,1,0:T(8,128)(2,1)}, bf16[2,4,64,1024]{3,2,1,0:T(8,128)(2,1)}, u32[]{:S(2)}, u32[]{:S(2)}) %collective-permute-start.14) | collective-permute-done | bytes 1048608 | tf_op jit(solution)/shard_map/ppermute | solution.py:18
  135.0 0.0 collective-permute-done.9.refs_5_
  135.0 9.5 %shard_map.37 = bf16[512,1024]{1,0:T(8,128)(2,1)} custom-call(s32[5]{0:T(128)S(1)} %stack.32.place, bf16[2,512,128]{2,1,0:T(8,128)(2,1)S(1)} %bitcast.32, bf16[7,512,128]{2,1,0:T(8,128)(2,1)S(1)} %pad_maximum_fusion.1.refs_1_, bf16[7,512,128]{2,1,0:T(8,128)(2,1)} %collective-permute-done.4.refs_2_, bf16[2,512,128]{2,1,0:T(8,128)(2,1)S(1)} %all_gather.11.refs_3_, ...), custom_call_target="tpu_custom_call" | custom-call | flops 4294967296 | bytes 9437184 | tf_op jit(solution)/shard_map/pallas_call | solution.py:132
  (2 shorter events, 0.1 us)
Async XLA Ops:
  0.0 2.1 %copy-start = (bf16[64,1024]{1,0:T(8,128)(2,1)S(1)}, bf16[64,1024]{1,0:T(8,128)(2,1)}, u32[]{:S(2)}) copy-start(bf16[64,1024]{1,0:T(8,128)(2,1)} %param.4) | copy-start | bytes 393220
  3.1 46.7 %all-to-all-start = ((bf16[4,80,1024]{2,1,0:T(8,128)(2,1)}), bf16[4,80,1024]{2,1,0:T(8,128)(2,1)S(1)}, u32[]{:S(2)}, u32[]{:S(2)}) async-start(bf16[4,80,1024]{2,1,0:T(8,128)(2,1)} %pad_maximum_fusion.3), calls=%async_computation | async-start | bytes 1310720 | tf_op jit(solution)/shard_map/all_to_all | solution.py:110
  21.4 23.0 %collective-permute-start = (bf16[2,512,128]{2,1,0:T(8,128)(2,1)S(1)}, bf16[2,512,128]{2,1,0:T(8,128)(2,1)S(1)}, u32[]{:S(2)}, u32[]{:S(2)}) collective-permute-start(bf16[2,512,128]{2,1,0:T(8,128)(2,1)S(1)} %bitcast.29), channel_id=1, source_target_pairs={{0,2},{1,7},{2,4},{3,1},{4,6},{5,3},{6,0},{7,5},{8,10},{9,15},{10,... | collective-permute-start | bytes 786440 | tf_op jit(solution)/shard_map/ppermute | solution.py:36
  26.1 18.4 %collective-permute-start.1 = (bf16[2,512,128]{2,1,0:T(8,128)(2,1)S(1)}, bf16[2,512,128]{2,1,0:T(8,128)(2,1)S(1)}, u32[]{:S(2)}, u32[]{:S(2)}) collective-permute-start(bf16[2,512,128]{2,1,0:T(8,128)(2,1)S(1)} %bitcast.30), channel_id=1, source_target_pairs={{0,4},{1,9},{2,6},{3,11},{4,0},{5,13},{6,2},{7,15},{8,12},{9,1},{1... | collective-permute-start | bytes 786440 | tf_op jit(solution)/shard_map/ppermute | solution.py:36
  30.7 13.7 %collective-permute-start.2 = (bf16[2,512,128]{2,1,0:T(8,128)(2,1)S(1)}, bf16[2,512,128]{2,1,0:T(8,128)(2,1)S(1)}, u32[]{:S(2)}, u32[]{:S(2)}) collective-permute-start(bf16[2,512,128]{2,1,0:T(8,128)(2,1)S(1)} %bitcast.31), channel_id=1, source_target_pairs={{0,10},{1,15},{2,12},{3,9},{4,14},{5,11},{6,8},{7,13},{8,2},{9,7},... | collective-permute-start | bytes 786440 | tf_op jit(solution)/shard_map/ppermute | solution.py:36
  33.1 11.4 %collective-permute-start.3 = (bf16[512,128]{1,0:T(8,128)(2,1)S(1)}, bf16[512,128]{1,0:T(8,128)(2,1)S(1)}, u32[]{:S(2)}, u32[]{:S(2)}) collective-permute-start(bf16[512,128]{1,0:T(8,128)(2,1)S(1)} %fusion), channel_id=1, source_target_pairs={{0,12},{1,13},{2,14},{3,15},{4,8},{5,9},{6,10},{7,11},{8,4},{9,5},... | collective-permute-start | bytes 393224 | tf_op jit(solution)/shard_map/ppermute | solution.py:36
  50.6 14.0 %all-to-all-start.1 = ((bf16[8,4,4,4,128]{4,3,2,1,0:T(4,128)(2,1)}), bf16[8,4,4,4,128]{4,3,2,1,0:T(4,128)(2,1)S(1)}, u32[]{:S(2)}, u32[]{:S(2)}) async-start(bf16[8,4,4,4,128]{4,3,2,1,0:T(4,128)(2,1)} %bitcast.26), calls=%async_computation.1 | async-start | bytes 262144 | tf_op jit(solution)/shard_map/all_to_all | solution.py:117
  57.2 26.9 %collective-permute-start.10 = (bf16[4,64,1024]{2,1,0:T(8,128)(2,1)S(1)}, bf16[4,64,1024]{2,1,0:T(8,128)(2,1)S(1)}, u32[]{:S(2)}, u32[]{:S(2)}) collective-permute-start(bf16[4,64,1024]{2,1,0:T(8,128)(2,1)S(1)} %get-tuple-element.16.refs_6_), channel_id=1, source_target_pairs={{0,16},{16,0},{32,48},{48,32},{64,80},{80,64},{96,112},{112,96},{1... | collective-permute-start | bytes 1572872 | tf_op jit(solution)/shard_map/ppermute | solution.py:22
  60.6 26.2 %collective-permute-start.11 = (bf16[4,64,1024]{2,1,0:T(8,128)(2,1)S(1)}, bf16[4,64,1024]{2,1,0:T(8,128)(2,1)}, u32[]{:S(2)}, u32[]{:S(2)}) collective-permute-start(bf16[4,64,1024]{2,1,0:T(8,128)(2,1)S(1)} %get-tuple-element.16.refs_6_), channel_id=1, source_target_pairs={{0,64},{16,80},{32,96},{48,112},{64,128},{80,144},{96,160},{112,17... | collective-permute-start | bytes 1572872 | tf_op jit(solution)/shard_map/ppermute | solution.py:18
  72.5 31.7 %collective-permute-start.5 = (bf16[2,512,128]{2,1,0:T(8,128)(2,1)S(1)}, bf16[2,512,128]{2,1,0:T(8,128)(2,1)S(1)}, u32[]{:S(2)}, u32[]{:S(2)}) collective-permute-start(bf16[2,512,128]{2,1,0:T(8,128)(2,1)S(1)} %all_gather.11.refs_3_), channel_id=1, source_target_pairs={{0,2},{1,7},{2,4},{3,1},{4,6},{5,3},{6,0},{7,5},{8,10},{9,15},{10,... | collective-permute-start | bytes 786440 | tf_op jit(solution)/shard_map/ppermute | solution.py:36
  77.1 29.0 %collective-permute-start.6 = (bf16[2,512,128]{2,1,0:T(8,128)(2,1)S(1)}, bf16[2,512,128]{2,1,0:T(8,128)(2,1)S(1)}, u32[]{:S(2)}, u32[]{:S(2)}) collective-permute-start(bf16[2,512,128]{2,1,0:T(8,128)(2,1)S(1)} %all_gather.11.refs_3_), channel_id=1, source_target_pairs={{0,4},{1,9},{2,6},{3,11},{4,0},{5,13},{6,2},{7,15},{8,12},{9,1},{1... | collective-permute-start | bytes 786440 | tf_op jit(solution)/shard_map/ppermute | solution.py:36
  81.5 24.7 %collective-permute-start.7 = (bf16[2,512,128]{2,1,0:T(8,128)(2,1)S(1)}, bf16[2,512,128]{2,1,0:T(8,128)(2,1)S(1)}, u32[]{:S(2)}, u32[]{:S(2)}) collective-permute-start(bf16[2,512,128]{2,1,0:T(8,128)(2,1)S(1)} %all_gather.11.refs_3_), channel_id=1, source_target_pairs={{0,10},{1,15},{2,12},{3,9},{4,14},{5,11},{6,8},{7,13},{8,2},{9,7},... | collective-permute-start | bytes 786440 | tf_op jit(solution)/shard_map/ppermute | solution.py:36
  84.1 31.1 %collective-permute-start.4 = (bf16[7,512,128]{2,1,0:T(8,128)(2,1)S(1)}, bf16[7,512,128]{2,1,0:T(8,128)(2,1)}, u32[]{:S(2)}, u32[]{:S(2)}) collective-permute-start(bf16[7,512,128]{2,1,0:T(8,128)(2,1)S(1)} %pad_maximum_fusion.1.refs_1_), channel_id=1, source_target_pairs={{0,1},{1,0},{2,3},{3,2},{4,5},{5,4},{6,7},{7,6},{8,9},{9,8},{10,11... | collective-permute-start | bytes 2752520 | tf_op jit(solution)/shard_map/ppermute | solution.py:26
  86.8 9.6 %collective-permute-start.8 = (bf16[512,128]{1,0:T(8,128)(2,1)S(1)}, bf16[512,128]{1,0:T(8,128)(2,1)S(1)}, u32[]{:S(2)}, u32[]{:S(2)}) collective-permute-start(bf16[512,128]{1,0:T(8,128)(2,1)S(1)} %bitcast.34), channel_id=1, source_target_pairs={{0,12},{1,13},{2,14},{3,15},{4,8},{5,9},{6,10},{7,11},{8,4},{9,5},... | collective-permute-start | bytes 393224 | tf_op jit(solution)/shard_map/ppermute | solution.py:36
  96.4 31.2 %collective-permute-start.13 = (bf16[2,4,64,1024]{3,2,1,0:T(8,128)(2,1)}, bf16[2,4,64,1024]{3,2,1,0:T(8,128)(2,1)}, u32[]{:S(2)}, u32[]{:S(2)}) collective-permute-start(bf16[2,4,64,1024]{3,2,1,0:T(8,128)(2,1)} %pad_maximum_fusion), channel_id=1, source_target_pairs={{0,32},{16,48},{32,64},{48,80},{64,96},{80,112},{96,128},{112,144}... | collective-permute-start | bytes 3145736 | tf_op jit(solution)/shard_map/ppermute | solution.py:18
  104.2 30.8 %collective-permute-start.14 = (bf16[2,4,64,1024]{3,2,1,0:T(8,128)(2,1)}, bf16[2,4,64,1024]{3,2,1,0:T(8,128)(2,1)}, u32[]{:S(2)}, u32[]{:S(2)}) collective-permute-start(bf16[2,4,64,1024]{3,2,1,0:T(8,128)(2,1)} %pad_maximum_fusion), channel_id=1, source_target_pairs={{0,480},{16,496},{32,0},{48,16},{64,32},{80,48},{96,64},{112,80},{... | collective-permute-start | bytes 3145736 | tf_op jit(solution)/shard_map/ppermute | solution.py:18
  106.3 28.7 %collective-permute-start.9 = (bf16[7,512,128]{2,1,0:T(8,128)(2,1)S(1)}, bf16[7,512,128]{2,1,0:T(8,128)(2,1)}, u32[]{:S(2)}, u32[]{:S(2)}) collective-permute-start(bf16[7,512,128]{2,1,0:T(8,128)(2,1)S(1)} %pad_maximum_fusion.2.refs_4_), channel_id=1, source_target_pairs={{0,1},{1,0},{2,3},{3,2},{4,5},{5,4},{6,7},{7,6},{8,9},{9,8},{10,11... | collective-permute-start | bytes 2752520 | tf_op jit(solution)/shard_map/ppermute | solution.py:26
  111.4 16.2 %collective-permute-start.12 = (bf16[4,64,1024]{2,1,0:T(8,128)(2,1)}, bf16[4,64,1024]{2,1,0:T(8,128)(2,1)}, u32[]{:S(2)}, u32[]{:S(2)}) collective-permute-start(bf16[4,64,1024]{2,1,0:T(8,128)(2,1)} %collective-permute-done.11.refs_8_), channel_id=1, source_target_pairs={{0,16},{16,0},{32,48},{48,32},{64,80},{80,64},{96,112},{112,96},{1... | collective-permute-start | bytes 1572872 | tf_op jit(solution)/shard_map/ppermute | solution.py:22

commit v6 on v5

--- a/solution.py
+++ b/solution.py
@@ -8,7 +8,10 @@
 OI = 4
 Q = 4
 FAR_GROUPS = [[(4 * q + m) * 2 + x for q in range(4)] for m in range(4) for x in range(2)]
-NEAR_GROUPS = [list(range(8 * q, 8 * q + 8)) for q in range(4)]
+TWO = [
+    (r * 16 + c, (r + (4 if c % 2 == 0 else 28)) % 32 * 16 + c) for r in range(32) for c in range(16)
+]
+CORE_GROUPS = [list(range(c, 16, 2)) for c in range(2)]
 CORE_PAIRS = [[2 * g, 2 * g + 1] for g in range(8)]
 STEPS = (((0, 1), (0, 3)), ((0, 2), (1, 0)), ((1, 1), (1, 3)), ((1, 2), (1, 2)))
 NTILE = 256
@@ -45,7 +48,7 @@
 
 def products(place, *refs):
     z, xl, core, xh, y = (place[i] for i in range(5))
-    amp_refs, blocks, (out, ints, amps, sem) = refs[:6], refs[6:12], refs[12:]
+    amp_refs, blocks, (out, ints, amps, sem) = refs[:5], refs[5:11], refs[11:]
     near_own, near_swap, two, two_partner, up, down = blocks
     copies = []
 
@@ -54,19 +57,22 @@
         lanes = pl.ds(pl.multiple_of(col * 128, 128), 128)
         copies.append((ref, amps.at[s, :, lanes]))
 
-    for s in range(2):
-        chip, mine, theirs = amp_refs[3 * s : 3 * s + 3]
-        for c in range(2):
-            amp_copy(chip.at[c], s, 0, 0, c)
-        for ref, who in ((mine, core), (theirs, 1 - core)):
-            for n, step in enumerate(STEPS):
-                dx = jnp.where(who == 0, step[0][0], step[1][0])
-                dy = jnp.where(who == 0, step[0][1], step[1][1])
-                if n < 3:
-                    for c in range(2):
-                        amp_copy(ref.at[2 * n + c], s, dx, dy, c)
-                else:
-                    amp_copy(ref.at[6], s, dx, dy, who)
+    chip, mine, theirs, swap_mine, swap_theirs = amp_refs
+    for c in range(2):
+        amp_copy(chip.at[c], 0, 0, 0, c)
+    for ref, who in ((mine, core), (theirs, 1 - core)):
+        for n, step in enumerate(STEPS):
+            dx = jnp.where(who == 0, step[0][0], step[1][0])
+            dy = jnp.where(who == 0, step[0][1], step[1][1])
+            if n < 3:
+                for c in range(2):
+                    amp_copy(ref.at[2 * n + c], 0, dx, dy, c)
+            else:
+                amp_copy(ref.at[6], 0, dx, dy, who)
+    for ref, who in ((swap_mine, core), (swap_theirs, 1 - core)):
+        for g in range(8):
+            lanes = pl.ds(pl.multiple_of((2 * g + who) * 128, 128), 128)
+            copies.append((ref.at[g], amps.at[1, :, lanes]))
     for ref, shift, x_index in (
         (near_own, 0, xl),
         (near_swap, 0, 1 - xl),
@@ -102,37 +108,36 @@
     rows, cols = integrals.shape
     depth, pairs = amplitudes.shape
 
+    copies = jnp.broadcast_to(integrals[None], (Q, rows, cols))
+    block = lax.all_to_all(
+        copies, "row", split_axis=0, concat_axis=0, tiled=True, axis_index_groups=FAR_GROUPS
+    )
+
     scale = jnp.repeat(tile_mask.astype(jnp.bfloat16).reshape(-1), pairs // OI)
     masked = (amplitudes * scale[None, :]).T
+    amps = gather_chips(masked)
+    sent = masked.reshape(OI, 32, OI, depth).transpose(1, 2, 0, 3)
+    sent, amps = lax.optimization_barrier((sent, amps))
+    got = lax.all_to_all(sent, "row", split_axis=0, concat_axis=0, tiled=True)
+    swapped = got.transpose(1, 0, 2, 3).reshape(pairs, depth)
 
-    sent = masked.reshape(OI, Q, 8, OI, depth).transpose(1, 2, 3, 0, 4).reshape(Q, -1, cols)
-    load = jnp.concatenate([jnp.broadcast_to(integrals[None], (Q, rows, cols)), sent], axis=1)
-    far = lax.all_to_all(
-        load, "row", split_axis=0, concat_axis=0, tiled=True, axis_index_groups=FAR_GROUPS
-    )
-    amps = gather_chips(masked)
-    block = far[:, :rows]
-    hop, amps = lax.optimization_barrier((far[:, rows:], amps))
-    hop = hop.reshape(Q, 8, OI, OI, depth).transpose(1, 0, 2, 3, 4)
-    got = lax.all_to_all(
-        hop, "row", split_axis=0, concat_axis=0, tiled=True, axis_index_groups=NEAR_GROUPS
-    )
-    swapped = got.transpose(2, 1, 0, 3, 4).reshape(pairs, depth)
-
-    two = z_shift(block, 2)
+    two = lax.ppermute(block, ("row", "col"), TWO)
     partner = x_swap(block)
-    partner, two = lax.optimization_barrier((partner, two))
     near = jnp.stack([block, partner])
     up = z_shift(near, 1)
     down = z_shift(near, -1)
     two_partner = x_swap(two)
-    swap_amps = gather_chips(swapped)
+    swapped, partner, two = lax.optimization_barrier((swapped, partner, two))
+    spread = jnp.broadcast_to(swapped[None], (8, pairs, depth))
+    own = lax.all_to_all(
+        spread, "col", split_axis=0, concat_axis=0, tiled=True, axis_index_groups=CORE_GROUPS
+    )
 
     anywhere = pl.BlockSpec(memory_space=pl.ANY)
     return pl.pallas_call(
         products,
         out_shape=jax.ShapeDtypeStruct((pairs, cols), jnp.bfloat16),
-        in_specs=[pl.BlockSpec(memory_space=pltpu.SMEM)] + [anywhere] * 12,
+        in_specs=[pl.BlockSpec(memory_space=pltpu.SMEM)] + [anywhere] * 11,
         out_specs=pl.BlockSpec(memory_space=pltpu.VMEM),
         scratch_shapes=[
             pltpu.VMEM((Q, 4, 2, rows, cols), jnp.bfloat16),
@@ -143,7 +148,7 @@
         cost_estimate=pl.CostEstimate(
             flops=4 * pairs * 2048 * cols, bytes_accessed=9 * 2**20, transcendentals=0
         ),
-    )(place, *amps, core_swap(amps[1]), *swap_amps, core_swap(swap_amps[1]), block, partner, two, two_partner, up, down)
+    )(place, *amps, core_swap(amps[1]), own, core_swap(own), block, partner, two, two_partner, up, down)
 
 
 def solution(mesh):

time: 146 us -> 132 us (0.904)
  starting transfers between devices: 83.3 us -> 65 us
  blocking collectives: 10.4 us -> 23.5 us
  waiting for transfers between devices: 35.5 us -> 25.7 us
  local copies, waits for them, and re-layouts: 2.4 us -> 5.53 us
    all_to_all x0 -> x1, blocking collectives: none -> 20.9 us  [on_device(): got = lax.all_to_all(sent, 'row', split_axis=0, concat_axis=0, tiled=True)]
    ppermute x8 -> x4, starting transfers between devices: 32.7 us -> 16 us  [chip_shift(): return lax.ppermute(x, 'col', pairs)]
    ppermute x8 -> x4, waiting for transfers between devices: 10.5 us -> 0.01 us  [chip_shift(): return lax.ppermute(x, 'col', pairs)]
    ppermute x3 -> x2, starting transfers between devices: 13.7 us -> 5.27 us  [z_shift(): return lax.ppermute(x, 'row', [(r, (r + 2 * d) % 32) for r in range(32)])]
    ppermute x0 -> x1, starting transfers between devices: none -> 8.42 us  [on_device(): two = lax.ppermute(block, ('row', 'col'), TWO)]
    all_to_all x2, waiting for transfers between devices: 5.17 us -> 13.1 us  [the longest x1 6.93 us: on_device(): lax.all_to_all(spread, 'col', split_axis=0, concat_axis=0, tiled=True, ax...]
    all_gather x2 -> x1, blocking collectives: 10.4 us -> 2.59 us  [gather_chips(): chip = lax.all_gather(x, 'col', axis=0, axis_index_groups=CORE_PAIRS)]
    ppermute x3 -> x2, waiting for transfers between devices: 7.38 us -> 0.01 us  [z_shift(): return lax.ppermute(x, 'row', [(r, (r + 2 * d) % 32) for r in range(32)])]
  transfers between devices with their start and end apart: 17 -> 13, of which waited for: 5 -> 3; matrix products, arithmetic and copies ran while one was open for 1% -> 2% of each run, Pallas kernels for 0% -> 0%
where the time goes in v6:
time: 132 us
  starting transfers between devices  65 us (49%)
  waiting for transfers between devices  25.7 us (19%)
  blocking collectives  23.5 us (18%)
  Pallas kernels  9.37 us (7%)
  local copies, waits for them, and re-layouts  5.53 us (4%)
  other arithmetic  2.43 us (2%)
    all_to_all x1, blocking collectives, on_device(): got = lax.all_to_all(sent, 'row', split_axis=0, concat_axis=0, tiled=True)  20.9 us
    ppermute x4, starting transfers between devices, chip_shift(): return lax.ppermute(x, 'col', pairs)  16 us
    all_to_all x1, starting transfers between devices, on_device(): lax.all_to_all(copies, 'row', split_axis=0, concat_axis=0, tiled=True, ax...  15.8 us
    ppermute x2, waiting for transfers between devices, x_swap(): return lax.ppermute(x, 'row', [(r, r ^ 1) for r in range(32)])  12.6 us
    pallas_call x1, Pallas kernels, on_device(): pl.pallas_call(products, out_shape=jax.ShapeDtypeStruct((pairs, cols), jn...  9.37 us
    ppermute x1, starting transfers between devices, on_device(): two = lax.ppermute(block, ('row', 'col'), TWO)  8.42 us
    ppermute x2, starting transfers between devices, core_swap(): return lax.ppermute(x, 'col', [(c, c ^ 1) for c in range(16)])  7.31 us
    all_to_all x1, waiting for transfers between devices, on_device(): lax.all_to_all(spread, 'col', split_axis=0, concat_axis=0, tiled=True, ax...  6.93 us
  transfers between devices with their start and end apart: 13, of which 3 were waited for; matrix products, arithmetic and copies ran while one was open for 2% of the time, Pallas kernels for 0%

profile of v6, /device:TPU:1, one launch (start us, length us, event | category | flops | bytes accessed | tf_op | source)
XLA Modules:
  0.0 131.7 jit_solution(13895653507360295249)
XLA Ops:
  0.0 1.8 %broadcast_in_dim.20 = bf16[4,64,1024]{2,1,0:T(8,128)(2,1)} broadcast(bf16[64,1024]{1,0:T(8,128)(2,1)} %param.4), dimensions={1,2} | broadcast | bytes 655360 | tf_op jit(solution)/shard_map/broadcast_in_dim | solution.py:111
  1.8 0.0 copy-start.3
  1.8 15.8 %all-to-all-start.1 = ((bf16[4,64,1024]{2,1,0:T(8,128)(2,1)}), bf16[4,64,1024]{2,1,0:T(8,128)(2,1)S(1)}, u32[]{:S(2)}, u32[]{:S(2)}) async-start(bf16[4,64,1024]{2,1,0:T(8,128)(2,1)} %broadcast_in_dim.20), calls=%async_computation.1 | async-start | bytes 1048576 | tf_op jit(solution)/shard_map/all_to_all | solution.py:112
  17.5 0.0 copy-done.3
  17.5 0.0 copy-start.4
  17.5 0.1 copy.8
  17.7 0.5 copy-done.4
  18.2 0.1 broadcast_bitcast_fusion
  18.3 0.1 fusion
  18.4 2.6 %all-gather = bf16[1024,128]{1,0:T(8,128)(2,1)S(1)} all-gather(bf16[512,128]{1,0:T(8,128)(2,1)S(1)} %fusion), channel_id=2, replica_groups={{0,1},{2,3},{4,5},{6,7},{8,9},{10,11},{12,13},{14,15},{16,17},{18,19},{..., dimensions={0}, use_global_device_ids=true | all-gather | bytes 393216 | tf_op jit(solution)/shard_map/all_gather | solution.py:43
  21.0 7.1 %collective-permute-start.2 = (bf16[2,512,128]{2,1,0:T(8,128)(2,1)S(1)}, bf16[2,512,128]{2,1,0:T(8,128)(2,1)S(1)}, u32[]{:S(2)}, u32[]{:S(2)}) collective-permute-start(bf16[2,512,128]{2,1,0:T(8,128)(2,1)S(1)} %bitcast.24), channel_id=1, source_target_pairs={{0,10},{1,15},{2,12},{3,9},{4,14},{5,11},{6,8},{7,13},{8,2},{9,7},... | collective-permute-start | bytes 786440 | tf_op jit(solution)/shard_map/ppermute | solution.py:39
  28.1 2.1 %collective-permute-start.1 = (bf16[2,512,128]{2,1,0:T(8,128)(2,1)S(1)}, bf16[2,512,128]{2,1,0:T(8,128)(2,1)S(1)}, u32[]{:S(2)}, u32[]{:S(2)}) collective-permute-start(bf16[2,512,128]{2,1,0:T(8,128)(2,1)S(1)} %bitcast.25), channel_id=1, source_target_pairs={{0,4},{1,9},{2,6},{3,11},{4,0},{5,13},{6,2},{7,15},{8,12},{9,1},{1... | collective-permute-start | bytes 786440 | tf_op jit(solution)/shard_map/ppermute | solution.py:39
  30.2 2.4 %collective-permute-start = (bf16[2,512,128]{2,1,0:T(8,128)(2,1)S(1)}, bf16[2,512,128]{2,1,0:T(8,128)(2,1)S(1)}, u32[]{:S(2)}, u32[]{:S(2)}) collective-permute-start(bf16[2,512,128]{2,1,0:T(8,128)(2,1)S(1)} %bitcast.26), channel_id=1, source_target_pairs={{0,2},{1,7},{2,4},{3,1},{4,6},{5,3},{6,0},{7,5},{8,10},{9,15},{10,... | collective-permute-start | bytes 786440 | tf_op jit(solution)/shard_map/ppermute | solution.py:39
  32.6 4.4 %collective-permute-start.3 = (bf16[512,128]{1,0:T(8,128)(2,1)S(1)}, bf16[512,128]{1,0:T(8,128)(2,1)S(1)}, u32[]{:S(2)}, u32[]{:S(2)}) collective-permute-start(bf16[512,128]{1,0:T(8,128)(2,1)S(1)} %fusion), channel_id=1, source_target_pairs={{0,12},{1,13},{2,14},{3,15},{4,8},{5,9},{6,10},{7,11},{8,4},{9,5},... | collective-permute-start | bytes 393224 | tf_op jit(solution)/shard_map/ppermute | solution.py:39
  37.0 0.1 broadcast_multiply_fusion
  37.2 6.2 %all-to-all-done.1.refs_5_ = bf16[4,64,1024]{2,1,0:T(8,128)(2,1)S(1)} async-done(((bf16[4,64,1024]{2,1,0:T(8,128)(2,1)}), bf16[4,64,1024]{2,1,0:T(8,128)(2,1)S(1)}, u32[]{:S(2)}, u32[]{:S(2)}) %all-to-all-start.1) | async-done | bytes 524320 | tf_op jit(solution)/shard_map/all_to_all | solution.py:112
  43.4 8.4 %collective-permute-start.6 = (bf16[4,64,1024]{2,1,0:T(8,128)(2,1)S(1)}, bf16[4,64,1024]{2,1,0:T(8,128)(2,1)S(1)}, u32[]{:S(2)}, u32[]{:S(2)}) collective-permute-start(bf16[4,64,1024]{2,1,0:T(8,128)(2,1)S(1)} %all-to-all-done.1.refs_5_), channel_id=1, source_target_pairs={{0,64},{1,449},{2,66},{3,451},{4,68},{5,453},{6,70},{7,455},{8,72}... | collective-permute-start | bytes 1572872 | tf_op jit(solution)/shard_map/ppermute | solution.py:124
  51.8 0.0 collective-permute-done.3
  51.8 3.1 %collective-permute-start.5 = (bf16[4,64,1024]{2,1,0:T(8,128)(2,1)S(1)}, bf16[4,64,1024]{2,1,0:T(8,128)(2,1)S(1)}, u32[]{:S(2)}, u32[]{:S(2)}) collective-permute-start(bf16[4,64,1024]{2,1,0:T(8,128)(2,1)S(1)} %all-to-all-done.1.refs_5_), channel_id=1, source_target_pairs={{0,16},{16,0},{32,48},{48,32},{64,80},{80,64},{96,112},{112,96},{1... | collective-permute-start | bytes 1572872 | tf_op jit(solution)/shard_map/ppermute | solution.py:25
  55.0 0.0 collective-permute-done.2
  55.0 0.0 collective-permute-done.1
  55.0 0.0 collective-permute-done
  55.0 0.0 copy-start.2
  55.0 0.7 copy-done.2
  55.7 1.1 pad_maximum_fusion.1.refs_1_
  56.8 20.9 %all_to_all.15 = bf16[32,4,4,128]{3,1,2,0:T(4,128)(2,1)S(1)} all-to-all(bf16[32,4,4,128]{3,1,2,0:T(4,128)(2,1)S(1)} %bitcast.29), channel_id=1, replica_groups=mesh['row'=32,'col'=16] {'row'}, dimensions={0} | all-to-all | bytes 262144 | tf_op jit(solution)/shard_map/all_to_all | solution.py:121
  77.6 0.1 copy.10
  77.7 0.0 collective-permute-done.6.refs_7_
  77.7 0.0 copy-start
  77.7 0.0 collective-permute-done.5.refs_6_
  77.7 1.1 broadcast_in_dim.21
  78.9 0.0 copy-done
  78.9 6.6 %all-to-all-start.2 = ((bf16[8,512,128]{2,1,0:T(8,128)(2,1)}), bf16[8,512,128]{2,1,0:T(8,128)(2,1)S(1)}, u32[]{:S(2)}, u32[]{:S(2)}) async-start(bf16[8,512,128]{2,1,0:T(8,128)(2,1)} %broadcast_in_dim.21), calls=%async_computation.2 | async-start | bytes 2097152 | tf_op jit(solution)/shard_map/all_to_all | solution.py:132
  85.5 1.1 pad_maximum_fusion
  86.6 2.1 %collective-permute-start.10 = (bf16[2,4,64,1024]{3,2,1,0:T(8,128)(2,1)}, bf16[2,4,64,1024]{3,2,1,0:T(8,128)(2,1)}, u32[]{:S(2)}, u32[]{:S(2)}) collective-permute-start(bf16[2,4,64,1024]{3,2,1,0:T(8,128)(2,1)} %pad_maximum_fusion), channel_id=1, source_target_pairs={{0,480},{16,496},{32,0},{48,16},{64,32},{80,48},{96,64},{112,80},{... | collective-permute-start | bytes 3145736 | tf_op jit(solution)/shard_map/ppermute | solution.py:21
  88.7 3.2 %collective-permute-start.9 = (bf16[2,4,64,1024]{3,2,1,0:T(8,128)(2,1)}, bf16[2,4,64,1024]{3,2,1,0:T(8,128)(2,1)}, u32[]{:S(2)}, u32[]{:S(2)}) collective-permute-start(bf16[2,4,64,1024]{3,2,1,0:T(8,128)(2,1)} %pad_maximum_fusion), channel_id=1, source_target_pairs={{0,32},{16,48},{32,64},{48,80},{64,96},{80,112},{96,128},{112,144}... | collective-permute-start | bytes 3145736 | tf_op jit(solution)/shard_map/ppermute | solution.py:21
  91.9 6.9 %all-to-all-done.2.refs_3_ = bf16[8,512,128]{2,1,0:T(8,128)(2,1)S(1)} async-done(((bf16[8,512,128]{2,1,0:T(8,128)(2,1)}), bf16[8,512,128]{2,1,0:T(8,128)(2,1)S(1)}, u32[]{:S(2)}, u32[]{:S(2)}) %all-to-all-start.2) | async-done | bytes 1048608 | tf_op jit(solution)/shard_map/all_to_all | solution.py:132
  98.8 5.4 %collective-permute-start.7 = (bf16[8,512,128]{2,1,0:T(8,128)(2,1)S(1)}, bf16[8,512,128]{2,1,0:T(8,128)(2,1)}, u32[]{:S(2)}, u32[]{:S(2)}) collective-permute-start(bf16[8,512,128]{2,1,0:T(8,128)(2,1)S(1)} %all-to-all-done.2.refs_3_), channel_id=1, source_target_pairs={{0,1},{1,0},{2,3},{3,2},{4,5},{5,4},{6,7},{7,6},{8,9},{9,8},{10,11... | collective-permute-start | bytes 3145736 | tf_op jit(solution)/shard_map/ppermute | solution.py:29
  104.2 1.9 %collective-permute-start.4 = (bf16[7,512,128]{2,1,0:T(8,128)(2,1)S(1)}, bf16[7,512,128]{2,1,0:T(8,128)(2,1)}, u32[]{:S(2)}, u32[]{:S(2)}) collective-permute-start(bf16[7,512,128]{2,1,0:T(8,128)(2,1)S(1)} %pad_maximum_fusion.1.refs_1_), channel_id=1, source_target_pairs={{0,1},{1,0},{2,3},{3,2},{4,5},{5,4},{6,7},{7,6},{8,9},{9,8},{10,11... | collective-permute-start | bytes 2752520 | tf_op jit(solution)/shard_map/ppermute | solution.py:29
  106.1 2.4 %collective-permute-start.8 = (bf16[4,64,1024]{2,1,0:T(8,128)(2,1)}, bf16[4,64,1024]{2,1,0:T(8,128)(2,1)}, u32[]{:S(2)}, u32[]{:S(2)}) collective-permute-start(bf16[4,64,1024]{2,1,0:T(8,128)(2,1)} %copy-done), channel_id=1, source_target_pairs={{0,16},{16,0},{32,48},{48,32},{64,80},{80,64},{96,112},{112,96},{1... | collective-permute-start | bytes 1572872 | tf_op jit(solution)/shard_map/ppermute | solution.py:25
  108.6 0.1 stack.32.place
  108.7 0.0 collective-permute-done.4.refs_2_
  108.7 12.6 %collective-permute-done.8.refs_8_ = bf16[4,64,1024]{2,1,0:T(8,128)(2,1)} collective-permute-done((bf16[4,64,1024]{2,1,0:T(8,128)(2,1)}, bf16[4,64,1024]{2,1,0:T(8,128)(2,1)}, u32[]{:S(2)}, u32[]{:S(2)}) %collective-permute-start.8) | collective-permute-done | bytes 524320 | tf_op jit(solution)/shard_map/ppermute | solution.py:25
  121.3 0.0 collective-permute-done.10.refs_10_
  121.3 0.0 collective-permute-done.9.refs_9_
  121.3 0.0 collective-permute-done.7.refs_4_
  121.3 0.0 copy-start.1
  121.3 1.0 copy-done.1
  122.4 9.4 %shard_map.37 = bf16[512,1024]{1,0:T(8,128)(2,1)} custom-call(s32[5]{0:T(128)S(1)} %stack.32.place, bf16[2,512,128]{2,1,0:T(8,128)(2,1)S(1)} %bitcast.27, bf16[7,512,128]{2,1,0:T(8,128)(2,1)S(1)} %pad_maximum_fusion.1.refs_1_, bf16[7,512,128]{2,1,0:T(8,128)(2,1)} %collective-permute-done.4.refs_2_, bf16[8,512,128]{2,1,0:T(8,128)(2,1)S(1)} %all-to-all-done.2.refs_3_, ...), custom_call_target="tpu_custom_call" | custom-call | flops 4294967296 | bytes 9437184 | tf_op jit(solution)/shard_map/pallas_call | solution.py:137
  (2 shorter events, 0.1 us)
Async XLA Ops:
  1.8 15.8 %copy-start.3 = (bf16[128,512]{1,0:T(8,128)(2,1)S(1)}, bf16[128,512]{1,0:T(8,128)(2,1)}, u32[]{:S(2)}) copy-start(bf16[128,512]{1,0:T(8,128)(2,1)} %param.3) | copy-start | bytes 393220
  1.8 41.6 %all-to-all-start.1 = ((bf16[4,64,1024]{2,1,0:T(8,128)(2,1)}), bf16[4,64,1024]{2,1,0:T(8,128)(2,1)S(1)}, u32[]{:S(2)}, u32[]{:S(2)}) async-start(bf16[4,64,1024]{2,1,0:T(8,128)(2,1)} %broadcast_in_dim.20), calls=%async_computation.1 | async-start | bytes 1048576 | tf_op jit(solution)/shard_map/all_to_all | solution.py:112
  17.5 0.7 copy-start.4
  21.0 34.0 %collective-permute-start.2 = (bf16[2,512,128]{2,1,0:T(8,128)(2,1)S(1)}, bf16[2,512,128]{2,1,0:T(8,128)(2,1)S(1)}, u32[]{:S(2)}, u32[]{:S(2)}) collective-permute-start(bf16[2,512,128]{2,1,0:T(8,128)(2,1)S(1)} %bitcast.24), channel_id=1, source_target_pairs={{0,10},{1,15},{2,12},{3,9},{4,14},{5,11},{6,8},{7,13},{8,2},{9,7},... | collective-permute-start | bytes 786440 | tf_op jit(solution)/shard_map/ppermute | solution.py:39
  28.1 26.9 %collective-permute-start.1 = (bf16[2,512,128]{2,1,0:T(8,128)(2,1)S(1)}, bf16[2,512,128]{2,1,0:T(8,128)(2,1)S(1)}, u32[]{:S(2)}, u32[]{:S(2)}) collective-permute-start(bf16[2,512,128]{2,1,0:T(8,128)(2,1)S(1)} %bitcast.25), channel_id=1, source_target_pairs={{0,4},{1,9},{2,6},{3,11},{4,0},{5,13},{6,2},{7,15},{8,12},{9,1},{1... | collective-permute-start | bytes 786440 | tf_op jit(solution)/shard_map/ppermute | solution.py:39
  30.2 24.8 %collective-permute-start = (bf16[2,512,128]{2,1,0:T(8,128)(2,1)S(1)}, bf16[2,512,128]{2,1,0:T(8,128)(2,1)S(1)}, u32[]{:S(2)}, u32[]{:S(2)}) collective-permute-start(bf16[2,512,128]{2,1,0:T(8,128)(2,1)S(1)} %bitcast.26), channel_id=1, source_target_pairs={{0,2},{1,7},{2,4},{3,1},{4,6},{5,3},{6,0},{7,5},{8,10},{9,15},{10,... | collective-permute-start | bytes 786440 | tf_op jit(solution)/shard_map/ppermute | solution.py:39
  32.6 19.2 %collective-permute-start.3 = (bf16[512,128]{1,0:T(8,128)(2,1)S(1)}, bf16[512,128]{1,0:T(8,128)(2,1)S(1)}, u32[]{:S(2)}, u32[]{:S(2)}) collective-permute-start(bf16[512,128]{1,0:T(8,128)(2,1)S(1)} %fusion), channel_id=1, source_target_pairs={{0,12},{1,13},{2,14},{3,15},{4,8},{5,9},{6,10},{7,11},{8,4},{9,5},... | collective-permute-start | bytes 393224 | tf_op jit(solution)/shard_map/ppermute | solution.py:39
  43.4 34.3 %collective-permute-start.6 = (bf16[4,64,1024]{2,1,0:T(8,128)(2,1)S(1)}, bf16[4,64,1024]{2,1,0:T(8,128)(2,1)S(1)}, u32[]{:S(2)}, u32[]{:S(2)}) collective-permute-start(bf16[4,64,1024]{2,1,0:T(8,128)(2,1)S(1)} %all-to-all-done.1.refs_5_), channel_id=1, source_target_pairs={{0,64},{1,449},{2,66},{3,451},{4,68},{5,453},{6,70},{7,455},{8,72}... | collective-permute-start | bytes 1572872 | tf_op jit(solution)/shard_map/ppermute | solution.py:124
  51.8 25.9 %collective-permute-start.5 = (bf16[4,64,1024]{2,1,0:T(8,128)(2,1)S(1)}, bf16[4,64,1024]{2,1,0:T(8,128)(2,1)S(1)}, u32[]{:S(2)}, u32[]{:S(2)}) collective-permute-start(bf16[4,64,1024]{2,1,0:T(8,128)(2,1)S(1)} %all-to-all-done.1.refs_5_), channel_id=1, source_target_pairs={{0,16},{16,0},{32,48},{48,32},{64,80},{80,64},{96,112},{112,96},{1... | collective-permute-start | bytes 1572872 | tf_op jit(solution)/shard_map/ppermute | solution.py:25
  55.0 0.7 copy-start.2
  77.7 1.1 copy-start
  78.9 19.9 %all-to-all-start.2 = ((bf16[8,512,128]{2,1,0:T(8,128)(2,1)}), bf16[8,512,128]{2,1,0:T(8,128)(2,1)S(1)}, u32[]{:S(2)}, u32[]{:S(2)}) async-start(bf16[8,512,128]{2,1,0:T(8,128)(2,1)} %broadcast_in_dim.21), calls=%async_computation.2 | async-start | bytes 2097152 | tf_op jit(solution)/shard_map/all_to_all | solution.py:132
  86.6 34.8 %collective-permute-start.10 = (bf16[2,4,64,1024]{3,2,1,0:T(8,128)(2,1)}, bf16[2,4,64,1024]{3,2,1,0:T(8,128)(2,1)}, u32[]{:S(2)}, u32[]{:S(2)}) collective-permute-start(bf16[2,4,64,1024]{3,2,1,0:T(8,128)(2,1)} %pad_maximum_fusion), channel_id=1, source_target_pairs={{0,480},{16,496},{32,0},{48,16},{64,32},{80,48},{96,64},{112,80},{... | collective-permute-start | bytes 3145736 | tf_op jit(solution)/shard_map/ppermute | solution.py:21
  88.7 32.7 %collective-permute-start.9 = (bf16[2,4,64,1024]{3,2,1,0:T(8,128)(2,1)}, bf16[2,4,64,1024]{3,2,1,0:T(8,128)(2,1)}, u32[]{:S(2)}, u32[]{:S(2)}) collective-permute-start(bf16[2,4,64,1024]{3,2,1,0:T(8,128)(2,1)} %pad_maximum_fusion), channel_id=1, source_target_pairs={{0,32},{16,48},{32,64},{48,80},{64,96},{80,112},{96,128},{112,144}... | collective-permute-start | bytes 3145736 | tf_op jit(solution)/shard_map/ppermute | solution.py:21
  98.8 22.5 %collective-permute-start.7 = (bf16[8,512,128]{2,1,0:T(8,128)(2,1)S(1)}, bf16[8,512,128]{2,1,0:T(8,128)(2,1)}, u32[]{:S(2)}, u32[]{:S(2)}) collective-permute-start(bf16[8,512,128]{2,1,0:T(8,128)(2,1)S(1)} %all-to-all-done.2.refs_3_), channel_id=1, source_target_pairs={{0,1},{1,0},{2,3},{3,2},{4,5},{5,4},{6,7},{7,6},{8,9},{9,8},{10,11... | collective-permute-start | bytes 3145736 | tf_op jit(solution)/shard_map/ppermute | solution.py:29
  104.2 4.5 %collective-permute-start.4 = (bf16[7,512,128]{2,1,0:T(8,128)(2,1)S(1)}, bf16[7,512,128]{2,1,0:T(8,128)(2,1)}, u32[]{:S(2)}, u32[]{:S(2)}) collective-permute-start(bf16[7,512,128]{2,1,0:T(8,128)(2,1)S(1)} %pad_maximum_fusion.1.refs_1_), channel_id=1, source_target_pairs={{0,1},{1,0},{2,3},{3,2},{4,5},{5,4},{6,7},{7,6},{8,9},{9,8},{10,11... | collective-permute-start | bytes 2752520 | tf_op jit(solution)/shard_map/ppermute | solution.py:29
  106.1 15.2 %collective-permute-start.8 = (bf16[4,64,1024]{2,1,0:T(8,128)(2,1)}, bf16[4,64,1024]{2,1,0:T(8,128)(2,1)}, u32[]{:S(2)}, u32[]{:S(2)}) collective-permute-start(bf16[4,64,1024]{2,1,0:T(8,128)(2,1)} %copy-done), channel_id=1, source_target_pairs={{0,16},{16,0},{32,48},{48,32},{64,80},{80,64},{96,112},{112,96},{1... | collective-permute-start | bytes 1572872 | tf_op jit(solution)/shard_map/ppermute | solution.py:25
  121.3 1.0 copy-start.1

commit v7 on v6

v7 whole, which is shorter than its diff:
```python
import jax
import jax.numpy as jnp
from jax import lax
from jax.experimental import pallas as pl
from jax.experimental.pallas import tpu as pltpu
from jax.sharding import PartitionSpec as P

OI = 4
Q = 4
FAR_GROUPS = [[(4 * q + m) * 2 + x for q in range(4)] for m in range(4) for x in range(2)]
TWO = [
    (r * 16 + c, (r + (4 if c % 2 == 0 else 28)) % 32 * 16 + c) for r in range(32) for c in range(16)
]
CORE_PAIRS = [[2 * g, 2 * g + 1] for g in range(8)]
STEPS = (((0, 1), (0, 3)), ((0, 2), (1, 0)), ((1, 1), (1, 3)), ((1, 2), (1, 2)))
NTILE = 256


def z_shift(x, d):
    return lax.ppermute(x, "row", [(r, (r + 2 * d) % 32) for r in range(32)])


def x_swap(x):
    return lax.ppermute(x, "row", [(r, r ^ 1) for r in range(32)])


def core_swap(x):
    return lax.ppermute(x, "col", [(c, c ^ 1) for c in range(16)])


def chip_shift(x, step):
    pairs = []
    for xh in range(2):
        for y in range(4):
            for c in range(2):
                dx, dy = step[c]
                pairs.append(((xh * 4 + y) * 2 + c, ((xh ^ dx) * 4 + (y + dy) % 4) * 2 + c))
    return lax.ppermute(x, "col", pairs)


def products(place, *refs):
    z, xl, core, xh, y = (place[i] for i in range(5))
    chip, mine, theirs, *blocks = refs[:11]
    out, ints, amps, total, early, late = refs[11:]
    first, second = [], []

    def amp_copy(ref, col):
        half = (col + z) & 1
        lanes = pl.ds(pl.multiple_of((col >> 1) * 128, 128), 128)
        for s in range(2):
            first.append((ref.at[s], amps.at[s, half, :, lanes]))

    for c in range(2):
        amp_copy(chip.at[c], (xh * 4 + y) * 2 + c)
    for ref, who in ((mine, core), (theirs, 1 - core)):
        for n, step in enumerate(STEPS):
            dx = jnp.where(who == 0, step[0][0], step[1][0])
            dy = jnp.where(who == 0, step[0][1], step[1][1])
            place_of = ((xh ^ dx) * 4 + ((y - dy) & 3)) * 2
            if n < 3:
                for c in range(2):
                    amp_copy(ref.at[2 * n + c], place_of + c)
            else:
                amp_copy(ref.at[6], place_of + who)
    for ref, shift, x_index in zip(
        blocks, (0, 0, 2, 2, 3, 3, 1, 1), (xl, 1 - xl, xl, 1 - xl, xl, 1 - xl, xl, 1 - xl)
    ):
        m = (z + shift) & 3
        pair = (ref, ints.at[shift & 1, :, m >> 1, x_index])
        (second if shift & 1 else first).append(pair)
    first = [pltpu.make_async_copy(a, b, early) for a, b in first]
    second = [pltpu.make_async_copy(a, b, late) for a, b in second]
    for copy in first + second:
        copy.start()

    def tile(half, n):
        cols = pl.ds(pl.multiple_of(n * NTILE, NTILE), NTILE)
        right = ints[half, :, :, :, :, cols].reshape(-1, NTILE)
        return cols, jnp.dot(
            amps[0, half], right, preferred_element_type=jnp.float32
        ) - jnp.dot(amps[1, half], right, preferred_element_type=jnp.float32)

    def begin(n, carry):
        cols, part = tile(0, n)
        total[:, cols] = part
        return carry

    def finish(n, carry):
        cols, part = tile(1, n)
        out[:, cols] = (total[:, cols] + part).astype(out.dtype)
        return carry

    for copy in first:
        copy.wait()
    lax.fori_loop(0, out.shape[1] // NTILE, begin, 0)
    for copy in second:
        copy.wait()
    lax.fori_loop(0, out.shape[1] // NTILE, finish, 0)


def on_device(amplitudes, integrals, tile_mask):
    row, col = lax.axis_index("row"), lax.axis_index("col")
    place = jnp.stack([row // 2, row % 2, col % 2, col // 8, col // 2 % 4]).astype(jnp.int32)
    rows, cols = integrals.shape
    depth, pairs = amplitudes.shape

    scale = jnp.repeat(tile_mask.astype(jnp.bfloat16).reshape(-1), pairs // OI)
    masked = (amplitudes * scale[None, :]).T

    sent = masked.reshape(OI, 32, OI, depth).transpose(1, 2, 0, 3)
    got = lax.all_to_all(sent, "row", split_axis=0, concat_axis=0, tiled=True)
    got, integrals = lax.optimization_barrier((got, integrals))
    swapped = got.transpose(1, 0, 2, 3).reshape(pairs, depth)

    copies = jnp.broadcast_to(integrals[None], (Q, rows, cols))
    block = lax.all_to_all(
        copies, "row", split_axis=0, concat_axis=0, tiled=True, axis_index_groups=FAR_GROUPS
    )

    both = jnp.stack([masked, swapped])
    chip = lax.all_gather(both, "col", axis=0, axis_index_groups=CORE_PAIRS)
    mine = [chip_shift(chip, step) for step in STEPS[:3]]
    mine.append(chip_shift(both, STEPS[3])[None])
    block, mine[:2] = lax.optimization_barrier((block, mine[:2]))
    mine = jnp.concatenate(mine)

    partner = x_swap(block)
    up = z_shift(block, 1)
    down = z_shift(block, -1)
    two = lax.ppermute(block, ("row", "col"), TWO)
    up_partner = z_shift(partner, 1)
    down_partner = z_shift(partner, -1)
    two_partner = x_swap(two)

    anywhere = pl.BlockSpec(memory_space=pl.ANY)
    return pl.pallas_call(
        products,
        out_shape=jax.ShapeDtypeStruct((pairs, cols), jnp.bfloat16),
        in_specs=[pl.BlockSpec(memory_space=pltpu.SMEM)] + [anywhere] * 11,
        out_specs=pl.BlockSpec(memory_space=pltpu.VMEM),
        scratch_shapes=[
            pltpu.VMEM((2, Q, 2, 2, rows, cols), jnp.bfloat16),
            pltpu.VMEM((2, 2, pairs, 8 * depth), jnp.bfloat16),
            pltpu.VMEM((pairs, cols), jnp.float32),
            pltpu.SemaphoreType.DMA,
            pltpu.SemaphoreType.DMA,
        ],
        compiler_params=pltpu.CompilerParams(vmem_limit_bytes=40 * 2**20),
        cost_estimate=pl.CostEstimate(
            flops=4 * pairs * 2048 * cols, bytes_accessed=9 * 2**20, transcendentals=0
        ),
    )(
        place,
        chip,
        mine,
        core_swap(mine),
        block,
        partner,
        two,
        two_partner,
        up,
        up_partner,
        down,
        down_partner,
    )


def solution(mesh):
    in_specs = (P("col", "row"), P("row", "col"), P("col", "row"))
    out_specs = P("row", "col")
    return jax.shard_map(
        on_device, mesh=mesh, in_specs=in_specs, out_specs=out_specs, check_vma=False
    )
```

time: 132 us -> 139 us (1.053)
  starting transfers between devices: 65 us -> 51 us
  blocking collectives: 23.5 us -> 35.4 us
  waiting for transfers between devices: 25.7 us -> 33 us
    ppermute x2 -> x4, waiting for transfers between devices: 0.01 us -> 14.1 us  [z_shift(): return lax.ppermute(x, 'row', [(r, (r + 2 * d) % 32) for r in range(32)])]
    ppermute x4, waiting for transfers between devices: 0.01 us -> 13.7 us  [chip_shift(): return lax.ppermute(x, 'col', pairs)]
    ppermute x2, waiting for transfers between devices: 12.6 us -> 0.01 us  [x_swap(): return lax.ppermute(x, 'row', [(r, r ^ 1) for r in range(32)])]
    all_to_all x1, starting transfers between devices: 15.8 us -> 3.95 us  [on_device(): lax.all_to_all(copies, 'row', split_axis=0, concat_axis=0, tiled=True, ax...]
    all_to_all x1, blocking collectives: 20.9 us -> 30.8 us  [on_device(): got = lax.all_to_all(sent, 'row', split_axis=0, concat_axis=0, tiled=True)]
    ppermute x2 -> x4, starting transfers between devices: 5.27 us -> 14.6 us  [z_shift(): return lax.ppermute(x, 'row', [(r, (r + 2 * d) % 32) for r in range(32)])]
    all_to_all x1 -> x0, waiting for transfers between devices: 6.93 us -> none  [on_device(): lax.all_to_all(spread, 'col', split_axis=0, concat_axis=0, tiled=True, ax...]
    all_to_all x1 -> x0, starting transfers between devices: 6.63 us -> none  [on_device(): lax.all_to_all(spread, 'col', split_axis=0, concat_axis=0, tiled=True, ax...]
  transfers between devices with their start and end apart: 13 -> 13, of which waited for: 3 -> 6; matrix products, arithmetic and copies ran while one was open for 2% -> 0% of each run, Pallas kernels for 0% -> 0%
where the time goes in v7:
time: 139 us; the launch traced here: 138 us
  starting transfers between devices  51 us (37%)
  blocking collectives  35.4 us (25%)
  waiting for transfers between devices  33 us (24%)
  Pallas kernels  9.88 us (7%)
  local copies, waits for them, and re-layouts  6.41 us (5%)
  other arithmetic  2.48 us (2%)
    all_to_all x1, blocking collectives, on_device(): got = lax.all_to_all(sent, 'row', split_axis=0, concat_axis=0, tiled=True)  30.8 us
    ppermute x4, starting transfers between devices, chip_shift(): return lax.ppermute(x, 'col', pairs)  15.7 us
    ppermute x4, starting transfers between devices, z_shift(): return lax.ppermute(x, 'row', [(r, (r + 2 * d) % 32) for r in range(32)])  14.6 us
    ppermute x4, waiting for transfers between devices, z_shift(): return lax.ppermute(x, 'row', [(r, (r + 2 * d) % 32) for r in range(32)])  14.1 us
    ppermute x4, waiting for transfers between devices, chip_shift(): return lax.ppermute(x, 'col', pairs)  13.7 us
    pallas_call x1, Pallas kernels, on_device(): pl.pallas_call(products, out_shape=jax.ShapeDtypeStruct((pairs, cols), jn...  9.88 us
    ppermute x1, starting transfers between devices, on_device(): two = lax.ppermute(block, ('row', 'col'), TWO)  6.6 us
    ppermute x2, starting transfers between devices, x_swap(): return lax.ppermute(x, 'row', [(r, r ^ 1) for r in range(32)])  5.28 us
  transfers between devices with their start and end apart: 13, of which 6 were waited for; matrix products, arithmetic and copies ran while one was open for 0% of the time, Pallas kernels for 0%

profile of v7, /device:TPU:1, one launch (start us, length us, event | category | flops | bytes accessed | tf_op | source)
XLA Modules:
  0.0 138.4 jit_solution(9007529218234224631)
XLA Ops:
  0.0 0.7 convert_bitcast_fusion
  0.7 0.1 broadcast_bitcast_fusion
  0.7 1.0 copy.6
  1.8 0.1 broadcast_multiply_fusion
  1.9 0.1 copy.10
  2.0 30.8 %all_to_all.10 = bf16[32,4,4,128]{3,2,1,0:T(4,128)(2,1)S(1)} all-to-all(bf16[32,4,4,128]{3,2,1,0:T(4,128)(2,1)S(1)} %bitcast.27), channel_id=1, replica_groups=mesh['row'=32,'col'=16] {'row'}, dimensions={0} | all-to-all | bytes 262144 | tf_op jit(solution)/shard_map/all_to_all | solution.py:111
  32.8 1.8 %broadcast_in_dim.13 = bf16[4,64,1024]{2,1,0:T(8,128)(2,1)} broadcast(bf16[64,1024]{1,0:T(8,128)(2,1)} %param.4), dimensions={1,2} | broadcast | bytes 655360 | tf_op jit(solution)/shard_map/broadcast_in_dim | solution.py:115
  34.6 4.0 %all-to-all-start.1 = ((bf16[4,64,1024]{2,1,0:T(8,128)(2,1)}), bf16[4,64,1024]{2,1,0:T(8,128)(2,1)S(1)}, u32[]{:S(2)}, u32[]{:S(2)}) async-start(bf16[4,64,1024]{2,1,0:T(8,128)(2,1)} %broadcast_in_dim.13), calls=%async_computation.1 | async-start | bytes 1048576 | tf_op jit(solution)/shard_map/all_to_all | solution.py:116
  38.5 0.1 fusion
  38.8 4.6 %all-gather = bf16[4,512,128]{2,1,0:T(8,128)(2,1)S(1)} all-gather(bf16[2,512,128]{2,1,0:T(8,128)(2,1)S(1)} %pad_maximum_fusion.1), channel_id=2, replica_groups={{0,1},{2,3},{4,5},{6,7},{8,9},{10,11},{12,13},{14,15},{16,17},{18,19},{..., dimensions={0}, use_global_device_ids=true | all-gather | bytes 786432 | tf_op jit(solution)/shard_map/all_gather | solution.py:121
  43.3 4.3 %collective-permute-start.1 = (bf16[2,2,512,128]{3,2,1,0:T(8,128)(2,1)S(1)}, bf16[2,2,512,128]{3,2,1,0:T(8,128)(2,1)S(1)}, u32[]{:S(2)}, u32[]{:S(2)}) collective-permute-start(bf16[2,2,512,128]{3,2,1,0:T(8,128)(2,1)S(1)} %bitcast.22), channel_id=1, source_target_pairs={{0,4},{1,9},{2,6},{3,11},{4,0},{5,13},{6,2},{7,15},{8,12},{9,1},{1... | collective-permute-start | bytes 1572872 | tf_op jit(solution)/shard_map/ppermute | solution.py:38
  47.7 4.6 %collective-permute-start = (bf16[2,2,512,128]{3,2,1,0:T(8,128)(2,1)S(1)}, bf16[2,2,512,128]{3,2,1,0:T(8,128)(2,1)S(1)}, u32[]{:S(2)}, u32[]{:S(2)}) collective-permute-start(bf16[2,2,512,128]{3,2,1,0:T(8,128)(2,1)S(1)} %bitcast.23), channel_id=1, source_target_pairs={{0,2},{1,7},{2,4},{3,1},{4,6},{5,3},{6,0},{7,5},{8,10},{9,15},{10,... | collective-permute-start | bytes 1572872 | tf_op jit(solution)/shard_map/ppermute | solution.py:38
  52.4 2.6 %collective-permute-start.2 = (bf16[2,2,512,128]{3,2,1,0:T(8,128)(2,1)S(1)}, bf16[2,2,512,128]{3,2,1,0:T(8,128)(2,1)S(1)}, u32[]{:S(2)}, u32[]{:S(2)}) collective-permute-start(bf16[2,2,512,128]{3,2,1,0:T(8,128)(2,1)S(1)} %bitcast.24), channel_id=1, source_target_pairs={{0,10},{1,15},{2,12},{3,9},{4,14},{5,11},{6,8},{7,13},{8,2},{9,7},... | collective-permute-start | bytes 1572872 | tf_op jit(solution)/shard_map/ppermute | solution.py:38
  55.0 4.1 %collective-permute-start.3 = (bf16[2,512,128]{2,1,0:T(8,128)(2,1)S(1)}, bf16[2,512,128]{2,1,0:T(8,128)(2,1)S(1)}, u32[]{:S(2)}, u32[]{:S(2)}) collective-permute-start(bf16[2,512,128]{2,1,0:T(8,128)(2,1)S(1)} %pad_maximum_fusion.1), channel_id=1, source_target_pairs={{0,12},{1,13},{2,14},{3,15},{4,8},{5,9},{6,10},{7,11},{8,4},{9,5},... | collective-permute-start | bytes 786440 | tf_op jit(solution)/shard_map/ppermute | solution.py:38
  59.1 0.0 collective-permute-done.1
  59.1 6.2 %collective-permute-done = bf16[2,2,512,128]{3,2,1,0:T(8,128)(2,1)S(1)} collective-permute-done((bf16[2,2,512,128]{3,2,1,0:T(8,128)(2,1)S(1)}, bf16[2,2,512,128]{3,2,1,0:T(8,128)(2,1)S(1)}, u32[]{:S(2)}, u32[]{:S(2)}) %collective-permute-start) | collective-permute-done | bytes 524320 | tf_op jit(solution)/shard_map/ppermute | solution.py:38
  65.4 0.0 copy-start.2
  65.4 0.0 all-to-all-done.1.refs_3_
  65.4 7.4 %collective-permute-done.3 = bf16[2,512,128]{2,1,0:T(8,128)(2,1)S(1)} collective-permute-done((bf16[2,512,128]{2,1,0:T(8,128)(2,1)S(1)}, bf16[2,512,128]{2,1,0:T(8,128)(2,1)S(1)}, u32[]{:S(2)}, u32[]{:S(2)}) %collective-permute-start.3) | collective-permute-done | bytes 262176 | tf_op jit(solution)/shard_map/ppermute | solution.py:38
  72.8 0.0 copy-start.4
  72.8 0.0 collective-permute-done.2
  72.8 0.0 copy-done.2
  72.8 0.7 copy-done.4
  73.5 0.0 copy-start.3
  73.5 0.8 copy-done.3
  74.3 1.5 %pad_maximum_fusion.refs_1_ = bf16[7,2,512,128]{3,2,1,0:T(8,128)(2,1)S(1)} fusion(bf16[1,2,512,128]{3,2,1,0:T(8,128)(2,1)} %bitcast.30, bf16[2,2,512,128]{3,2,1,0:T(8,128)(2,1)} %copy-done.3, bf16[2,2,512,128]{3,2,1,0:T(8,128)(2,1)S(1)} %collective-permute-done.1, bf16[2,2,512,128]{3,2,1,0:T(8,128)(2,1)} %copy-done.2), kind=kLoop, calls=%fused_computation | loop fusion | flops 2752512 | bytes 3670016 | tf_op jit(solution)/shard_map/concatenate | solution.py:125
  75.8 4.9 %collective-permute-start.4 = (bf16[7,2,512,128]{3,2,1,0:T(8,128)(2,1)S(1)}, bf16[7,2,512,128]{3,2,1,0:T(8,128)(2,1)}, u32[]{:S(2)}, u32[]{:S(2)}) collective-permute-start(bf16[7,2,512,128]{3,2,1,0:T(8,128)(2,1)S(1)} %pad_maximum_fusion.refs_1_), channel_id=1, source_target_pairs={{0,1},{1,0},{2,3},{3,2},{4,5},{5,4},{6,7},{7,6},{8,9},{9,8},{10,11... | collective-permute-start | bytes 5505032 | tf_op jit(solution)/shard_map/ppermute | solution.py:28
  80.7 6.6 %collective-permute-start.6 = (bf16[4,64,1024]{2,1,0:T(8,128)(2,1)S(1)}, bf16[4,64,1024]{2,1,0:T(8,128)(2,1)S(1)}, u32[]{:S(2)}, u32[]{:S(2)}) collective-permute-start(bf16[4,64,1024]{2,1,0:T(8,128)(2,1)S(1)} %all-to-all-done.1.refs_3_), channel_id=1, source_target_pairs={{0,64},{1,449},{2,66},{3,451},{4,68},{5,453},{6,70},{7,455},{8,72}... | collective-permute-start | bytes 1572872 | tf_op jit(solution)/shard_map/ppermute | solution.py:130
  87.3 2.2 %collective-permute-start.5 = (bf16[4,64,1024]{2,1,0:T(8,128)(2,1)S(1)}, bf16[4,64,1024]{2,1,0:T(8,128)(2,1)}, u32[]{:S(2)}, u32[]{:S(2)}) collective-permute-start(bf16[4,64,1024]{2,1,0:T(8,128)(2,1)S(1)} %all-to-all-done.1.refs_3_), channel_id=1, source_target_pairs={{0,16},{16,0},{32,48},{48,32},{64,80},{80,64},{96,112},{112,96},{1... | collective-permute-start | bytes 1572872 | tf_op jit(solution)/shard_map/ppermute | solution.py:24
  89.5 2.8 %collective-permute-start.10 = (bf16[4,64,1024]{2,1,0:T(8,128)(2,1)S(1)}, bf16[4,64,1024]{2,1,0:T(8,128)(2,1)S(1)}, u32[]{:S(2)}, u32[]{:S(2)}) collective-permute-start(bf16[4,64,1024]{2,1,0:T(8,128)(2,1)S(1)} %all-to-all-done.1.refs_3_), channel_id=1, source_target_pairs={{0,480},{16,496},{32,0},{48,16},{64,32},{80,48},{96,64},{112,80},{... | collective-permute-start | bytes 1572872 | tf_op jit(solution)/shard_map/ppermute | solution.py:20
  92.3 2.5 %collective-permute-start.8 = (bf16[4,64,1024]{2,1,0:T(8,128)(2,1)S(1)}, bf16[4,64,1024]{2,1,0:T(8,128)(2,1)}, u32[]{:S(2)}, u32[]{:S(2)}) collective-permute-start(bf16[4,64,1024]{2,1,0:T(8,128)(2,1)S(1)} %all-to-all-done.1.refs_3_), channel_id=1, source_target_pairs={{0,32},{16,48},{32,64},{48,80},{64,96},{80,112},{96,128},{112,144}... | collective-permute-start | bytes 1572872 | tf_op jit(solution)/shard_map/ppermute | solution.py:20
  94.8 5.2 %collective-permute-done.6.refs_5_ = bf16[4,64,1024]{2,1,0:T(8,128)(2,1)S(1)} collective-permute-done((bf16[4,64,1024]{2,1,0:T(8,128)(2,1)S(1)}, bf16[4,64,1024]{2,1,0:T(8,128)(2,1)S(1)}, u32[]{:S(2)}, u32[]{:S(2)}) %collective-permute-start.6) | collective-permute-done | bytes 524320 | tf_op jit(solution)/shard_map/ppermute | solution.py:130
  100.0 3.1 %collective-permute-start.7 = (bf16[4,64,1024]{2,1,0:T(8,128)(2,1)S(1)}, bf16[4,64,1024]{2,1,0:T(8,128)(2,1)}, u32[]{:S(2)}, u32[]{:S(2)}) collective-permute-start(bf16[4,64,1024]{2,1,0:T(8,128)(2,1)S(1)} %collective-permute-done.6.refs_5_), channel_id=1, source_target_pairs={{0,16},{16,0},{32,48},{48,32},{64,80},{80,64},{96,112},{112,96},{1... | collective-permute-start | bytes 1572872 | tf_op jit(solution)/shard_map/ppermute | solution.py:24
  103.1 0.0 collective-permute-done.5.refs_4_
  103.1 7.4 %collective-permute-start.11 = (bf16[4,64,1024]{2,1,0:T(8,128)(2,1)}, bf16[4,64,1024]{2,1,0:T(8,128)(2,1)}, u32[]{:S(2)}, u32[]{:S(2)}) collective-permute-start(bf16[4,64,1024]{2,1,0:T(8,128)(2,1)} %collective-permute-done.5.refs_4_), channel_id=1, source_target_pairs={{0,480},{16,496},{32,0},{48,16},{64,32},{80,48},{96,64},{112,80},{... | collective-permute-start | bytes 1572872 | tf_op jit(solution)/shard_map/ppermute | solution.py:20
  110.5 4.7 %collective-permute-done.10.refs_9_ = bf16[4,64,1024]{2,1,0:T(8,128)(2,1)S(1)} collective-permute-done((bf16[4,64,1024]{2,1,0:T(8,128)(2,1)S(1)}, bf16[4,64,1024]{2,1,0:T(8,128)(2,1)S(1)}, u32[]{:S(2)}, u32[]{:S(2)}) %collective-permute-start.10) | collective-permute-done | bytes 524320 | tf_op jit(solution)/shard_map/ppermute | solution.py:20
  115.2 0.0 copy-start
  115.2 0.8 copy-done
  116.0 1.9 %collective-permute-start.9 = (bf16[4,64,1024]{2,1,0:T(8,128)(2,1)}, bf16[4,64,1024]{2,1,0:T(8,128)(2,1)}, u32[]{:S(2)}, u32[]{:S(2)}) collective-permute-start(bf16[4,64,1024]{2,1,0:T(8,128)(2,1)} %collective-permute-done.5.refs_4_), channel_id=1, source_target_pairs={{0,32},{16,48},{32,64},{48,80},{64,96},{80,112},{96,128},{112,144}... | collective-permute-start | bytes 1572872 | tf_op jit(solution)/shard_map/ppermute | solution.py:20
  118.0 0.1 stack.29.place
  118.1 0.0 collective-permute-done.8.refs_7_
  118.1 0.0 collective-permute-done.7.refs_6_
  118.1 4.9 %collective-permute-done.11.refs_10_ = bf16[4,64,1024]{2,1,0:T(8,128)(2,1)} collective-permute-done((bf16[4,64,1024]{2,1,0:T(8,128)(2,1)}, bf16[4,64,1024]{2,1,0:T(8,128)(2,1)}, u32[]{:S(2)}, u32[]{:S(2)}) %collective-permute-start.11) | collective-permute-done | bytes 524320 | tf_op jit(solution)/shard_map/ppermute | solution.py:20
  123.0 4.5 %collective-permute-done.9.refs_8_ = bf16[4,64,1024]{2,1,0:T(8,128)(2,1)} collective-permute-done((bf16[4,64,1024]{2,1,0:T(8,128)(2,1)}, bf16[4,64,1024]{2,1,0:T(8,128)(2,1)}, u32[]{:S(2)}, u32[]{:S(2)}) %collective-permute-start.9) | collective-permute-done | bytes 524320 | tf_op jit(solution)/shard_map/ppermute | solution.py:20
  127.5 0.0 collective-permute-done.4.refs_2_
  127.5 0.0 copy-start.1
  127.5 1.0 copy-done.1
  128.5 9.9 %shard_map.37 = bf16[512,1024]{1,0:T(8,128)(2,1)} custom-call(s32[5]{0:T(128)S(1)} %stack.29.place, bf16[2,2,512,128]{3,2,1,0:T(8,128)(2,1)S(1)} %bitcast.25, bf16[7,2,512,128]{3,2,1,0:T(8,128)(2,1)S(1)} %pad_maximum_fusion.refs_1_, bf16[7,2,512,128]{3,2,1,0:T(8,128)(2,1)} %collective-permute-done.4.refs_2_, ...), custom_call_target="tpu_custom_call" | custom-call | flops 4294967296 | bytes 9437184 | tf_op jit(solution)/shard_map/pallas_call | solution.py:136
  (2 shorter events, 0.1 us)
Async XLA Ops:
  34.6 30.8 %all-to-all-start.1 = ((bf16[4,64,1024]{2,1,0:T(8,128)(2,1)}), bf16[4,64,1024]{2,1,0:T(8,128)(2,1)S(1)}, u32[]{:S(2)}, u32[]{:S(2)}) async-start(bf16[4,64,1024]{2,1,0:T(8,128)(2,1)} %broadcast_in_dim.13), calls=%async_computation.1 | async-start | bytes 1048576 | tf_op jit(solution)/shard_map/all_to_all | solution.py:116
  43.3 15.8 %collective-permute-start.1 = (bf16[2,2,512,128]{3,2,1,0:T(8,128)(2,1)S(1)}, bf16[2,2,512,128]{3,2,1,0:T(8,128)(2,1)S(1)}, u32[]{:S(2)}, u32[]{:S(2)}) collective-permute-start(bf16[2,2,512,128]{3,2,1,0:T(8,128)(2,1)S(1)} %bitcast.22), channel_id=1, source_target_pairs={{0,4},{1,9},{2,6},{3,11},{4,0},{5,13},{6,2},{7,15},{8,12},{9,1},{1... | collective-permute-start | bytes 1572872 | tf_op jit(solution)/shard_map/ppermute | solution.py:38
  47.7 17.7 %collective-permute-start = (bf16[2,2,512,128]{3,2,1,0:T(8,128)(2,1)S(1)}, bf16[2,2,512,128]{3,2,1,0:T(8,128)(2,1)S(1)}, u32[]{:S(2)}, u32[]{:S(2)}) collective-permute-start(bf16[2,2,512,128]{3,2,1,0:T(8,128)(2,1)S(1)} %bitcast.23), channel_id=1, source_target_pairs={{0,2},{1,7},{2,4},{3,1},{4,6},{5,3},{6,0},{7,5},{8,10},{9,15},{10,... | collective-permute-start | bytes 1572872 | tf_op jit(solution)/shard_map/ppermute | solution.py:38
  52.4 20.5 %collective-permute-start.2 = (bf16[2,2,512,128]{3,2,1,0:T(8,128)(2,1)S(1)}, bf16[2,2,512,128]{3,2,1,0:T(8,128)(2,1)S(1)}, u32[]{:S(2)}, u32[]{:S(2)}) collective-permute-start(bf16[2,2,512,128]{3,2,1,0:T(8,128)(2,1)S(1)} %bitcast.24), channel_id=1, source_target_pairs={{0,10},{1,15},{2,12},{3,9},{4,14},{5,11},{6,8},{7,13},{8,2},{9,7},... | collective-permute-start | bytes 1572872 | tf_op jit(solution)/shard_map/ppermute | solution.py:38
  55.0 17.8 %collective-permute-start.3 = (bf16[2,512,128]{2,1,0:T(8,128)(2,1)S(1)}, bf16[2,512,128]{2,1,0:T(8,128)(2,1)S(1)}, u32[]{:S(2)}, u32[]{:S(2)}) collective-permute-start(bf16[2,512,128]{2,1,0:T(8,128)(2,1)S(1)} %pad_maximum_fusion.1), channel_id=1, source_target_pairs={{0,12},{1,13},{2,14},{3,15},{4,8},{5,9},{6,10},{7,11},{8,4},{9,5},... | collective-permute-start | bytes 786440 | tf_op jit(solution)/shard_map/ppermute | solution.py:38
  65.4 7.5 %copy-start.2 = (bf16[2,2,512,128]{3,2,1,0:T(8,128)(2,1)}, bf16[2,2,512,128]{3,2,1,0:T(8,128)(2,1)S(1)}, u32[]{:S(2)}) copy-start(bf16[2,2,512,128]{3,2,1,0:T(8,128)(2,1)S(1)} %collective-permute-done) | copy-start | bytes 1572868
  72.8 0.7 copy-start.4
  73.5 0.8 copy-start.3
  75.8 51.6 %collective-permute-start.4 = (bf16[7,2,512,128]{3,2,1,0:T(8,128)(2,1)S(1)}, bf16[7,2,512,128]{3,2,1,0:T(8,128)(2,1)}, u32[]{:S(2)}, u32[]{:S(2)}) collective-permute-start(bf16[7,2,512,128]{3,2,1,0:T(8,128)(2,1)S(1)} %pad_maximum_fusion.refs_1_), channel_id=1, source_target_pairs={{0,1},{1,0},{2,3},{3,2},{4,5},{5,4},{6,7},{7,6},{8,9},{9,8},{10,11... | collective-permute-start | bytes 5505032 | tf_op jit(solution)/shard_map/ppermute | solution.py:28
  80.7 19.3 %collective-permute-start.6 = (bf16[4,64,1024]{2,1,0:T(8,128)(2,1)S(1)}, bf16[4,64,1024]{2,1,0:T(8,128)(2,1)S(1)}, u32[]{:S(2)}, u32[]{:S(2)}) collective-permute-start(bf16[4,64,1024]{2,1,0:T(8,128)(2,1)S(1)} %all-to-all-done.1.refs_3_), channel_id=1, source_target_pairs={{0,64},{1,449},{2,66},{3,451},{4,68},{5,453},{6,70},{7,455},{8,72}... | collective-permute-start | bytes 1572872 | tf_op jit(solution)/shard_map/ppermute | solution.py:130
  87.3 15.8 %collective-permute-start.5 = (bf16[4,64,1024]{2,1,0:T(8,128)(2,1)S(1)}, bf16[4,64,1024]{2,1,0:T(8,128)(2,1)}, u32[]{:S(2)}, u32[]{:S(2)}) collective-permute-start(bf16[4,64,1024]{2,1,0:T(8,128)(2,1)S(1)} %all-to-all-done.1.refs_3_), channel_id=1, source_target_pairs={{0,16},{16,0},{32,48},{48,32},{64,80},{80,64},{96,112},{112,96},{1... | collective-permute-start | bytes 1572872 | tf_op jit(solution)/shard_map/ppermute | solution.py:24
  89.5 25.7 %collective-permute-start.10 = (bf16[4,64,1024]{2,1,0:T(8,128)(2,1)S(1)}, bf16[4,64,1024]{2,1,0:T(8,128)(2,1)S(1)}, u32[]{:S(2)}, u32[]{:S(2)}) collective-permute-start(bf16[4,64,1024]{2,1,0:T(8,128)(2,1)S(1)} %all-to-all-done.1.refs_3_), channel_id=1, source_target_pairs={{0,480},{16,496},{32,0},{48,16},{64,32},{80,48},{96,64},{112,80},{... | collective-permute-start | bytes 1572872 | tf_op jit(solution)/shard_map/ppermute | solution.py:20
  92.3 25.8 %collective-permute-start.8 = (bf16[4,64,1024]{2,1,0:T(8,128)(2,1)S(1)}, bf16[4,64,1024]{2,1,0:T(8,128)(2,1)}, u32[]{:S(2)}, u32[]{:S(2)}) collective-permute-start(bf16[4,64,1024]{2,1,0:T(8,128)(2,1)S(1)} %all-to-all-done.1.refs_3_), channel_id=1, source_target_pairs={{0,32},{16,48},{32,64},{48,80},{64,96},{80,112},{96,128},{112,144}... | collective-permute-start | bytes 1572872 | tf_op jit(solution)/shard_map/ppermute | solution.py:20
  100.0 18.1 %collective-permute-start.7 = (bf16[4,64,1024]{2,1,0:T(8,128)(2,1)S(1)}, bf16[4,64,1024]{2,1,0:T(8,128)(2,1)}, u32[]{:S(2)}, u32[]{:S(2)}) collective-permute-start(bf16[4,64,1024]{2,1,0:T(8,128)(2,1)S(1)} %collective-permute-done.6.refs_5_), channel_id=1, source_target_pairs={{0,16},{16,0},{32,48},{48,32},{64,80},{80,64},{96,112},{112,96},{1... | collective-permute-start | bytes 1572872 | tf_op jit(solution)/shard_map/ppermute | solution.py:24
  103.1 19.9 %collective-permute-start.11 = (bf16[4,64,1024]{2,1,0:T(8,128)(2,1)}, bf16[4,64,1024]{2,1,0:T(8,128)(2,1)}, u32[]{:S(2)}, u32[]{:S(2)}) collective-permute-start(bf16[4,64,1024]{2,1,0:T(8,128)(2,1)} %collective-permute-done.5.refs_4_), channel_id=1, source_target_pairs={{0,480},{16,496},{32,0},{48,16},{64,32},{80,48},{96,64},{112,80},{... | collective-permute-start | bytes 1572872 | tf_op jit(solution)/shard_map/ppermute | solution.py:20
  115.2 0.8 copy-start
  116.0 11.4 %collective-permute-start.9 = (bf16[4,64,1024]{2,1,0:T(8,128)(2,1)}, bf16[4,64,1024]{2,1,0:T(8,128)(2,1)}, u32[]{:S(2)}, u32[]{:S(2)}) collective-permute-start(bf16[4,64,1024]{2,1,0:T(8,128)(2,1)} %collective-permute-done.5.refs_4_), channel_id=1, source_target_pairs={{0,32},{16,48},{32,64},{48,80},{64,96},{80,112},{96,128},{112,144}... | collective-permute-start | bytes 1572872 | tf_op jit(solution)/shard_map/ppermute | solution.py:20
  127.5 1.0 copy-start.1

commit v8 on v7

v8 whole, which is shorter than its diff:
```python
import jax
import jax.numpy as jnp
from jax import lax
from jax.experimental import pallas as pl
from jax.experimental.pallas import tpu as pltpu
from jax.sharding import PartitionSpec as P

OI = 4
Q = 4
FAR_GROUPS = [[(4 * q + m) * 2 + x for q in range(4)] for m in range(4) for x in range(2)]
TWO = [
    (r * 16 + c, (r + (4 if c % 2 == 0 else 28)) % 32 * 16 + c) for r in range(32) for c in range(16)
]
CORE_PAIRS = [[2 * g, 2 * g + 1] for g in range(8)]
STEPS = (((0, 1), (0, 3)), ((0, 2), (1, 0)), ((1, 1), (1, 3)), ((1, 2), (1, 2)))
NTILE = 256


def z_shift(x, d):
    return lax.ppermute(x, "row", [(r, (r + 2 * d) % 32) for r in range(32)])


def x_swap(x):
    return lax.ppermute(x, "row", [(r, r ^ 1) for r in range(32)])


def core_swap(x):
    return lax.ppermute(x, "col", [(c, c ^ 1) for c in range(16)])


def chip_shift(x, step):
    pairs = []
    for xh in range(2):
        for y in range(4):
            for c in range(2):
                dx, dy = step[c]
                pairs.append(((xh * 4 + y) * 2 + c, ((xh ^ dx) * 4 + (y + dy) % 4) * 2 + c))
    return lax.ppermute(x, "col", pairs)


def multiply(amps, ints, cols):
    right = ints[:, :, :, :, cols].reshape(-1, NTILE)
    return jnp.dot(amps[0], right, preferred_element_type=jnp.float32) - jnp.dot(
        amps[1], right, preferred_element_type=jnp.float32
    )


def columns(n):
    return pl.ds(pl.multiple_of(n * NTILE, NTILE), NTILE)


def block_copies(place, refs, shifts, ints):
    z, xl = place[0], place[1]
    copies = []
    for ref, partner, shift in zip(refs[::2], refs[1::2], shifts):
        m = (z + shift) & 3
        copies.append((ref, ints.at[:, m >> 1, xl]))
        copies.append((partner, ints.at[:, m >> 1, 1 - xl]))
    return copies


def run_copies(copies, sem):
    copies = [pltpu.make_async_copy(a, b, sem) for a, b in copies]
    for copy in copies:
        copy.start()
    for copy in copies:
        copy.wait()


def first_half(place, whole, chip, mine, theirs, *refs):
    z, core, xh, y = place[0], place[2], place[3], place[4]
    blocks, (total, kept, ints, sem) = refs[:4], refs[4:]
    copies = block_copies(place, blocks, (0, 2), ints)
    for k in range(8):
        lanes = pl.ds(k * 128, 128)
        for half in range(2):
            copies.append((whole.at[2 * k + ((z + half) & 1)], kept.at[half, 0, :, lanes]))
    swaps = []
    for c in range(2):
        swaps.append((chip.at[c], (xh * 4 + y) * 2 + c))
    for ref, who in ((mine, core), (theirs, 1 - core)):
        for n, step in enumerate(STEPS):
            dx = jnp.where(who == 0, step[0][0], step[1][0])
            dy = jnp.where(who == 0, step[0][1], step[1][1])
            place_of = ((xh ^ dx) * 4 + ((y - dy) & 3)) * 2
            if n < 3:
                for c in range(2):
                    swaps.append((ref.at[2 * n + c], place_of + c))
            else:
                swaps.append((ref.at[6], place_of + who))
    for ref, col in swaps:
        lanes = pl.ds(pl.multiple_of((col >> 1) * 128, 128), 128)
        copies.append((ref, kept.at[(col + z) & 1, 1, :, lanes]))
    run_copies(copies, sem)

    def tile(n, carry):
        cols = columns(n)
        total[:, cols] = multiply(kept.at[0], ints, cols)
        return carry

    lax.fori_loop(0, total.shape[1] // NTILE, tile, 0)


def second_half(place, total, kept, *refs):
    blocks, (out, ints, sem) = refs[:4], refs[4:]
    run_copies(block_copies(place, blocks, (1, 3), ints), sem)

    def tile(n, carry):
        cols = columns(n)
        out[:, cols] = (total[:, cols] + multiply(kept.at[1], ints, cols)).astype(out.dtype)
        return carry

    lax.fori_loop(0, out.shape[1] // NTILE, tile, 0)


def on_device(amplitudes, integrals, tile_mask):
    row, col = lax.axis_index("row"), lax.axis_index("col")
    place = jnp.stack([row // 2, row % 2, col % 2, col // 8, col // 2 % 4]).astype(jnp.int32)
    rows, cols = integrals.shape
    depth, pairs = amplitudes.shape

    scale = jnp.repeat(tile_mask.astype(jnp.bfloat16).reshape(-1), pairs // OI)
    masked = (amplitudes * scale[None, :]).T

    sent = masked.reshape(OI, 32, OI, depth).transpose(1, 2, 0, 3)
    got = lax.all_to_all(sent, "row", split_axis=0, concat_axis=0, tiled=True)
    got, integrals = lax.optimization_barrier((got, integrals))
    swapped = got.transpose(1, 0, 2, 3).reshape(pairs, depth)

    copies = jnp.broadcast_to(integrals[None], (Q, rows, cols))
    block = lax.all_to_all(
        copies, "row", split_axis=0, concat_axis=0, tiled=True, axis_index_groups=FAR_GROUPS
    )

    whole = lax.all_gather(masked, "col", axis=0)
    chip = lax.all_gather(swapped, "col", axis=0, axis_index_groups=CORE_PAIRS)
    mine = [chip_shift(chip, step) for step in STEPS[:3]]
    mine.append(chip_shift(swapped, STEPS[3])[None])
    mine = jnp.concatenate(mine)
    block, mine = lax.optimization_barrier((block, mine))

    partner = x_swap(block)
    two = lax.ppermute(block, ("row", "col"), TWO)
    up = z_shift(block, 1)
    down = z_shift(block, -1)
    up_partner = z_shift(partner, 1)
    down_partner = z_shift(partner, -1)
    two_partner = x_swap(two)

    anywhere = pl.BlockSpec(memory_space=pl.ANY)
    scalars = pl.BlockSpec(memory_space=pltpu.SMEM)
    vector = pl.BlockSpec(memory_space=pltpu.VMEM)
    ints = pltpu.VMEM((Q, 2, 2, rows, cols), jnp.bfloat16)
    params = pltpu.CompilerParams(vmem_limit_bytes=32 * 2**20)
    cost = pl.CostEstimate(
        flops=2 * pairs * 2048 * cols, bytes_accessed=10 * 2**20, transcendentals=0
    )
    total, kept = pl.pallas_call(
        first_half,
        out_shape=(
            jax.ShapeDtypeStruct((pairs, cols), jnp.float32),
            jax.ShapeDtypeStruct((2, 2, pairs, 8 * depth), jnp.bfloat16),
        ),
        in_specs=[scalars] + [anywhere] * 8,
        out_specs=(vector, vector),
        scratch_shapes=[ints, pltpu.SemaphoreType.DMA],
        compiler_params=params,
        cost_estimate=cost,
    )(place, whole, chip, mine, core_swap(mine), block, partner, two, two_partner)
    return pl.pallas_call(
        second_half,
        out_shape=jax.ShapeDtypeStruct((pairs, cols), jnp.bfloat16),
        in_specs=[scalars, vector, vector] + [anywhere] * 4,
        out_specs=vector,
        scratch_shapes=[ints, pltpu.SemaphoreType.DMA],
        compiler_params=params,
        cost_estimate=cost,
    )(place, total, kept, down, down_partner, up, up_partner)


def solution(mesh):
    in_specs = (P("col", "row"), P("row", "col"), P("col", "row"))
    out_specs = P("row", "col")
    return jax.shard_map(
        on_device, mesh=mesh, in_specs=in_specs, out_specs=out_specs, check_vma=False
    )
```

time: 139 us -> 145 us (1.043)
  between operations: 0.23 us -> 13.7 us
  waiting for transfers between devices: 33 us -> 24.4 us
  local copies, waits for them, and re-layouts: 6.41 us -> 8.36 us
    ppermute x4, waiting for transfers between devices: 14.1 us -> 6.16 us  [z_shift(): return lax.ppermute(x, 'row', [(r, (r + 2 * d) % 32) for r in range(32)])]
    ppermute x4, waiting for transfers between devices: 13.7 us -> 10.5 us  [chip_shift(): return lax.ppermute(x, 'col', pairs)]
    ppermute x1, waiting for transfers between devices: 5.2 us -> 7.76 us  [on_device(): two = lax.ppermute(block, ('row', 'col'), TWO)]
    unnamed x11, local copies, waits for them, and re-layouts: 4.34 us -> 6.34 us
    pallas_call x1 -> x2, Pallas kernels: 9.88 us -> 9.39 us  [the longest x1 4.85 us: on_device(): pl.pallas_call(first_half, out_shape=(jax.ShapeDtypeStruct((pairs, cols),...]
  transfers between devices with their start and end apart: 13 -> 14, of which waited for: 6 -> 5; matrix products, arithmetic and copies ran while one was open for 0% -> 2% of each run, Pallas kernels for 0% -> 3%
where the time goes in v8:
time: 145 us; the launch traced here: 144 us
  starting transfers between devices  51.2 us (35%)
  blocking collectives  35.2 us (24%)
  waiting for transfers between devices  24.4 us (17%)
  between operations  13.7 us (9%)
  Pallas kernels  9.39 us (6%)
  local copies, waits for them, and re-layouts  8.36 us (6%)
  other arithmetic  1.7 us (1%)
    all_to_all x1, blocking collectives, on_device(): got = lax.all_to_all(sent, 'row', split_axis=0, concat_axis=0, tiled=True)  30.8 us
    ppermute x4, starting transfers between devices, chip_shift(): return lax.ppermute(x, 'col', pairs)  15.7 us
    ppermute x4, starting transfers between devices, z_shift(): return lax.ppermute(x, 'row', [(r, (r + 2 * d) % 32) for r in range(32)])  15.4 us
    ppermute x4, waiting for transfers between devices, chip_shift(): return lax.ppermute(x, 'col', pairs)  10.5 us
    ppermute x1, waiting for transfers between devices, on_device(): two = lax.ppermute(block, ('row', 'col'), TWO)  7.76 us
    ppermute x1, starting transfers between devices, on_device(): two = lax.ppermute(block, ('row', 'col'), TWO)  6.6 us
    unnamed x11, local copies, waits for them, and re-layouts  6.34 us
    ppermute x4, waiting for transfers between devices, z_shift(): return lax.ppermute(x, 'row', [(r, (r + 2 * d) % 32) for r in range(32)])  6.16 us
  transfers between devices with their start and end apart: 14, of which 5 were waited for; matrix products, arithmetic and copies ran while one was open for 2% of the time, Pallas kernels for 3%

profile of v8, /device:TPU:1, one launch (start us, length us, event | category | flops | bytes accessed | tf_op | source)
XLA Modules:
  0.0 144.0 jit_solution(12509956063372654156)
XLA Ops:
  6.5 0.0 all-gather.3.cloned.1.call-start
  6.5 1.0 copy.12
  7.6 0.7 convert_bitcast_fusion
  8.2 0.1 broadcast_bitcast_fusion
  8.3 0.8 fusion
  9.1 0.0 all-gather.3.cloned.1.call-update
  9.1 0.1 broadcast_multiply_fusion
  9.3 30.8 %all_to_all.10 = bf16[32,4,4,128]{3,1,2,0:T(4,128)(2,1)S(1)} all-to-all(bf16[32,4,4,128]{3,1,2,0:T(4,128)(2,1)S(1)} %copy.13), channel_id=1, replica_groups=mesh['row'=32,'col'=16] {'row'}, dimensions={0} | all-to-all | bytes 262144 | tf_op jit(solution)/shard_map/all_to_all | solution.py:126
  40.1 1.8 %broadcast_in_dim.13 = bf16[4,64,1024]{2,1,0:T(8,128)(2,1)} broadcast(bf16[64,1024]{1,0:T(8,128)(2,1)} %param.4), dimensions={1,2} | broadcast | bytes 655360 | tf_op jit(solution)/shard_map/broadcast_in_dim | solution.py:130
  41.9 4.0 %all-to-all-start.1 = ((bf16[4,64,1024]{2,1,0:T(8,128)(2,1)}), bf16[4,64,1024]{2,1,0:T(8,128)(2,1)S(1)}, u32[]{:S(2)}, u32[]{:S(2)}) async-start(bf16[4,64,1024]{2,1,0:T(8,128)(2,1)} %broadcast_in_dim.13), calls=%async_computation.1 | async-start | bytes 1048576 | tf_op jit(solution)/shard_map/all_to_all | solution.py:131
  45.8 0.1 copy.14
  45.9 4.4 %all_gather.11.chip = bf16[2,512,128]{2,1,0:T(8,128)(2,1)S(1)} all-gather(bf16[1,512,128]{2,1,0:T(8,128)(2,1)S(1)} %bitcast.21), channel_id=1, replica_groups={{0,1},{2,3},{4,5},{6,7},{8,9},{10,11},{12,13},{14,15},{16,17},{18,19},{..., dimensions={0}, use_global_device_ids=true | all-gather | bytes 393216 | tf_op jit(solution)/shard_map/all_gather | solution.py:136
  50.3 4.6 %collective-permute-start = (bf16[2,512,128]{2,1,0:T(8,128)(2,1)S(1)}, bf16[2,512,128]{2,1,0:T(8,128)(2,1)S(1)}, u32[]{:S(2)}, u32[]{:S(2)}) collective-permute-start(bf16[2,512,128]{2,1,0:T(8,128)(2,1)S(1)} %all_gather.11.chip), channel_id=1, source_target_pairs={{0,2},{1,7},{2,4},{3,1},{4,6},{5,3},{6,0},{7,5},{8,10},{9,15},{10,... | collective-permute-start | bytes 786440 | tf_op jit(solution)/shard_map/ppermute | solution.py:38
  54.9 4.4 %collective-permute-start.1 = (bf16[2,512,128]{2,1,0:T(8,128)(2,1)S(1)}, bf16[2,512,128]{2,1,0:T(8,128)(2,1)S(1)}, u32[]{:S(2)}, u32[]{:S(2)}) collective-permute-start(bf16[2,512,128]{2,1,0:T(8,128)(2,1)S(1)} %all_gather.11.chip), channel_id=1, source_target_pairs={{0,4},{1,9},{2,6},{3,11},{4,0},{5,13},{6,2},{7,15},{8,12},{9,1},{1... | collective-permute-start | bytes 786440 | tf_op jit(solution)/shard_map/ppermute | solution.py:38
  59.3 2.6 %collective-permute-start.2 = (bf16[2,512,128]{2,1,0:T(8,128)(2,1)S(1)}, bf16[2,512,128]{2,1,0:T(8,128)(2,1)S(1)}, u32[]{:S(2)}, u32[]{:S(2)}) collective-permute-start(bf16[2,512,128]{2,1,0:T(8,128)(2,1)S(1)} %all_gather.11.chip), channel_id=1, source_target_pairs={{0,10},{1,15},{2,12},{3,9},{4,14},{5,11},{6,8},{7,13},{8,2},{9,7},... | collective-permute-start | bytes 786440 | tf_op jit(solution)/shard_map/ppermute | solution.py:38
  61.9 0.0 copy-start
  61.9 0.7 copy-done
  62.6 4.1 %collective-permute-start.3 = (bf16[512,128]{1,0:T(8,128)(2,1)S(1)}, bf16[512,128]{1,0:T(8,128)(2,1)S(1)}, u32[]{:S(2)}, u32[]{:S(2)}) collective-permute-start(bf16[512,128]{1,0:T(8,128)(2,1)S(1)} %bitcast.22), channel_id=1, source_target_pairs={{0,12},{1,13},{2,14},{3,15},{4,8},{5,9},{6,10},{7,11},{8,4},{9,5},... | collective-permute-start | bytes 393224 | tf_op jit(solution)/shard_map/ppermute | solution.py:38
  66.7 10.0 %collective-permute-done.3 = bf16[512,128]{1,0:T(8,128)(2,1)S(1)} collective-permute-done((bf16[512,128]{1,0:T(8,128)(2,1)S(1)}, bf16[512,128]{1,0:T(8,128)(2,1)S(1)}, u32[]{:S(2)}, u32[]{:S(2)}) %collective-permute-start.3) | collective-permute-done | bytes 131104 | tf_op jit(solution)/shard_map/ppermute | solution.py:38
  76.7 0.0 collective-permute-done
  76.7 0.0 collective-permute-done.1
  76.7 0.5 collective-permute-done.2
  77.2 0.1 pad_maximum_fusion.mine
  77.3 0.0 all-to-all-done.1.refs_0_
  77.3 4.6 %collective-permute-start.4 = (bf16[7,512,128]{2,1,0:T(8,128)(2,1)S(1)}, bf16[7,512,128]{2,1,0:T(8,128)(2,1)S(1)}, u32[]{:S(2)}, u32[]{:S(2)}) collective-permute-start(bf16[7,512,128]{2,1,0:T(8,128)(2,1)S(1)} %pad_maximum_fusion.mine), channel_id=1, source_target_pairs={{0,1},{1,0},{2,3},{3,2},{4,5},{5,4},{6,7},{7,6},{8,9},{9,8},{10,11... | collective-permute-start | bytes 2752520 | tf_op jit(solution)/shard_map/ppermute | solution.py:28
  82.0 6.6 %collective-permute-start.6 = (bf16[4,64,1024]{2,1,0:T(8,128)(2,1)S(1)}, bf16[4,64,1024]{2,1,0:T(8,128)(2,1)}, u32[]{:S(2)}, u32[]{:S(2)}) collective-permute-start(bf16[4,64,1024]{2,1,0:T(8,128)(2,1)S(1)} %all-to-all-done.1.refs_0_), channel_id=1, source_target_pairs={{0,64},{1,449},{2,66},{3,451},{4,68},{5,453},{6,70},{7,455},{8,72}... | collective-permute-start | bytes 1572872 | tf_op jit(solution)/shard_map/ppermute | solution.py:143
  88.6 2.2 %collective-permute-start.5 = (bf16[4,64,1024]{2,1,0:T(8,128)(2,1)S(1)}, bf16[4,64,1024]{2,1,0:T(8,128)(2,1)}, u32[]{:S(2)}, u32[]{:S(2)}) collective-permute-start(bf16[4,64,1024]{2,1,0:T(8,128)(2,1)S(1)} %all-to-all-done.1.refs_0_), channel_id=1, source_target_pairs={{0,16},{16,0},{32,48},{48,32},{64,80},{80,64},{96,112},{112,96},{1... | collective-permute-start | bytes 1572872 | tf_op jit(solution)/shard_map/ppermute | solution.py:24
  90.8 7.8 %collective-permute-done.6.refs_2_ = bf16[4,64,1024]{2,1,0:T(8,128)(2,1)} collective-permute-done((bf16[4,64,1024]{2,1,0:T(8,128)(2,1)S(1)}, bf16[4,64,1024]{2,1,0:T(8,128)(2,1)}, u32[]{:S(2)}, u32[]{:S(2)}) %collective-permute-start.6) | collective-permute-done | bytes 524320 | tf_op jit(solution)/shard_map/ppermute | solution.py:143
  98.5 2.7 %collective-permute-start.7 = (bf16[4,64,1024]{2,1,0:T(8,128)(2,1)}, bf16[4,64,1024]{2,1,0:T(8,128)(2,1)}, u32[]{:S(2)}, u32[]{:S(2)}) collective-permute-start(bf16[4,64,1024]{2,1,0:T(8,128)(2,1)} %collective-permute-done.6.refs_2_), channel_id=1, source_target_pairs={{0,16},{16,0},{32,48},{48,32},{64,80},{80,64},{96,112},{112,96},{1... | collective-permute-start | bytes 1572872 | tf_op jit(solution)/shard_map/ppermute | solution.py:24
  101.2 4.1 %collective-permute-start.10 = (bf16[4,64,1024]{2,1,0:T(8,128)(2,1)S(1)}, bf16[4,64,1024]{2,1,0:T(8,128)(2,1)S(1)}, u32[]{:S(2)}, u32[]{:S(2)}) collective-permute-start(bf16[4,64,1024]{2,1,0:T(8,128)(2,1)S(1)} %all-to-all-done.1.refs_0_), channel_id=1, source_target_pairs={{0,32},{16,48},{32,64},{48,80},{64,96},{80,112},{96,128},{112,144}... | collective-permute-start | bytes 1572872 | tf_op jit(solution)/shard_map/ppermute | solution.py:20
  105.3 4.9 %collective-permute-start.8 = (bf16[4,64,1024]{2,1,0:T(8,128)(2,1)S(1)}, bf16[4,64,1024]{2,1,0:T(8,128)(2,1)S(1)}, u32[]{:S(2)}, u32[]{:S(2)}) collective-permute-start(bf16[4,64,1024]{2,1,0:T(8,128)(2,1)S(1)} %all-to-all-done.1.refs_0_), channel_id=1, source_target_pairs={{0,480},{16,496},{32,0},{48,16},{64,32},{80,48},{96,64},{112,80},{... | collective-permute-start | bytes 1572872 | tf_op jit(solution)/shard_map/ppermute | solution.py:20
  110.2 0.0 collective-permute-done.5.refs_1_
  110.2 1.9 %collective-permute-start.11 = (bf16[4,64,1024]{2,1,0:T(8,128)(2,1)}, bf16[4,64,1024]{2,1,0:T(8,128)(2,1)S(1)}, u32[]{:S(2)}, u32[]{:S(2)}) collective-permute-start(bf16[4,64,1024]{2,1,0:T(8,128)(2,1)} %collective-permute-done.5.refs_1_), channel_id=1, source_target_pairs={{0,32},{16,48},{32,64},{48,80},{64,96},{80,112},{96,128},{112,144}... | collective-permute-start | bytes 1572872 | tf_op jit(solution)/shard_map/ppermute | solution.py:20
  112.1 0.0 collective-permute-done.4.theirs
  112.2 0.0 copy-start.3
  112.2 0.9 copy-done.3
  113.1 4.6 %collective-permute-start.9 = (bf16[4,64,1024]{2,1,0:T(8,128)(2,1)}, bf16[4,64,1024]{2,1,0:T(8,128)(2,1)S(1)}, u32[]{:S(2)}, u32[]{:S(2)}) collective-permute-start(bf16[4,64,1024]{2,1,0:T(8,128)(2,1)} %collective-permute-done.5.refs_1_), channel_id=1, source_target_pairs={{0,480},{16,496},{32,0},{48,16},{64,32},{80,48},{96,64},{112,80},{... | collective-permute-start | bytes 1572872 | tf_op jit(solution)/shard_map/ppermute | solution.py:20
  117.7 0.1 stack.23.place
  117.8 0.0 collective-permute-done.7.refs_3_
  117.8 0.0 all-gather.3.cloned.1.call-done
  117.8 0.0 copy-start.1
  117.8 1.0 copy-done.1
  118.7 0.0 copy-start.2
  118.8 1.6 %copy-done.2 = bf16[8192,128]{1,0:T(8,128)(2,1)S(1)} copy-done((bf16[8192,128]{1,0:T(8,128)(2,1)S(1)}, bf16[8192,128]{1,0:T(8,128)(2,1)}, u32[]{:S(2)}) %copy-start.2) | copy-done | bytes 2097176
  120.3 0.0 copy-start.4
  120.3 1.2 copy-done.4
  121.5 4.8 %shard_map.37 = (f32[512,1024]{1,0:T(8,128)S(1)}, bf16[2,2,512,1024]{3,2,1,0:T(8,128)(2,1)S(1)}) custom-call(s32[5]{0:T(128)S(1)} %stack.23.place, bf16[16,512,128]{2,1,0:T(8,128)(2,1)S(1)} %bitcast.20, bf16[2,512,128]{2,1,0:T(8,128)(2,1)S(1)} %copy-done.1, bf16[7,512,128]{2,1,0:T(8,128)(2,1)S(1)} %pad_maximum_fusion.mine, ...), custom_call_target="tpu_custom_call" | custom-call | flops 2147483648 | bytes 10485760 | tf_op jit(solution)/shard_map/pallas_call | solution.py:158
  126.4 0.0 collective-permute-done.10.refs_2_
  126.4 0.0 collective-permute-done.8.refs_0_
  126.4 5.2 %collective-permute-done.11.refs_3_ = bf16[4,64,1024]{2,1,0:T(8,128)(2,1)S(1)} collective-permute-done((bf16[4,64,1024]{2,1,0:T(8,128)(2,1)}, bf16[4,64,1024]{2,1,0:T(8,128)(2,1)S(1)}, u32[]{:S(2)}, u32[]{:S(2)}) %collective-permute-start.11) | collective-permute-done | bytes 524320 | tf_op jit(solution)/shard_map/ppermute | solution.py:20
  131.6 1.0 collective-permute-done.9.refs_1_
  132.6 4.5 %shard_map.38 = bf16[512,1024]{1,0:T(8,128)(2,1)} custom-call(s32[5]{0:T(128)S(1)} %stack.23.place, f32[512,1024]{1,0:T(8,128)S(1)} %get-tuple-element.15.total, bf16[2,2,512,1024]{3,2,1,0:T(8,128)(2,1)S(1)} %get-tuple-element.16.kept, bf16[4,64,1024]{2,1,0:T(8,128)(2,1)S(1)} %collective-permute-done.8.refs_0_, ...), custom_call_target="tpu_custom_call" | custom-call | flops 2147483648 | bytes 10485760 | tf_op jit(solution)/shard_map/pallas_call | solution.py:170
  (1 shorter events, 0.0 us)
Async XLA Ops:
  6.5 111.3 %all-gather.3.cloned.1.call-start = ((), (), s32[]{:S(2)}) async-start(), calls=%async_computation.2 | async-start | bytes 2228224 | tf_op jit(solution)/shard_map/all_gather | solution.py:135
  41.9 35.5 %all-to-all-start.1 = ((bf16[4,64,1024]{2,1,0:T(8,128)(2,1)}), bf16[4,64,1024]{2,1,0:T(8,128)(2,1)S(1)}, u32[]{:S(2)}, u32[]{:S(2)}) async-start(bf16[4,64,1024]{2,1,0:T(8,128)(2,1)} %broadcast_in_dim.13), calls=%async_computation.1 | async-start | bytes 1048576 | tf_op jit(solution)/shard_map/all_to_all | solution.py:131
  50.3 26.4 %collective-permute-start = (bf16[2,512,128]{2,1,0:T(8,128)(2,1)S(1)}, bf16[2,512,128]{2,1,0:T(8,128)(2,1)S(1)}, u32[]{:S(2)}, u32[]{:S(2)}) collective-permute-start(bf16[2,512,128]{2,1,0:T(8,128)(2,1)S(1)} %all_gather.11.chip), channel_id=1, source_target_pairs={{0,2},{1,7},{2,4},{3,1},{4,6},{5,3},{6,0},{7,5},{8,10},{9,15},{10,... | collective-permute-start | bytes 786440 | tf_op jit(solution)/shard_map/ppermute | solution.py:38
  54.9 21.8 %collective-permute-start.1 = (bf16[2,512,128]{2,1,0:T(8,128)(2,1)S(1)}, bf16[2,512,128]{2,1,0:T(8,128)(2,1)S(1)}, u32[]{:S(2)}, u32[]{:S(2)}) collective-permute-start(bf16[2,512,128]{2,1,0:T(8,128)(2,1)S(1)} %all_gather.11.chip), channel_id=1, source_target_pairs={{0,4},{1,9},{2,6},{3,11},{4,0},{5,13},{6,2},{7,15},{8,12},{9,1},{1... | collective-permute-start | bytes 786440 | tf_op jit(solution)/shard_map/ppermute | solution.py:38
  59.3 17.9 %collective-permute-start.2 = (bf16[2,512,128]{2,1,0:T(8,128)(2,1)S(1)}, bf16[2,512,128]{2,1,0:T(8,128)(2,1)S(1)}, u32[]{:S(2)}, u32[]{:S(2)}) collective-permute-start(bf16[2,512,128]{2,1,0:T(8,128)(2,1)S(1)} %all_gather.11.chip), channel_id=1, source_target_pairs={{0,10},{1,15},{2,12},{3,9},{4,14},{5,11},{6,8},{7,13},{8,2},{9,7},... | collective-permute-start | bytes 786440 | tf_op jit(solution)/shard_map/ppermute | solution.py:38
  61.9 0.7 copy-start
  62.6 14.1 %collective-permute-start.3 = (bf16[512,128]{1,0:T(8,128)(2,1)S(1)}, bf16[512,128]{1,0:T(8,128)(2,1)S(1)}, u32[]{:S(2)}, u32[]{:S(2)}) collective-permute-start(bf16[512,128]{1,0:T(8,128)(2,1)S(1)} %bitcast.22), channel_id=1, source_target_pairs={{0,12},{1,13},{2,14},{3,15},{4,8},{5,9},{6,10},{7,11},{8,4},{9,5},... | collective-permute-start | bytes 393224 | tf_op jit(solution)/shard_map/ppermute | solution.py:38
  77.3 34.8 %collective-permute-start.4 = (bf16[7,512,128]{2,1,0:T(8,128)(2,1)S(1)}, bf16[7,512,128]{2,1,0:T(8,128)(2,1)S(1)}, u32[]{:S(2)}, u32[]{:S(2)}) collective-permute-start(bf16[7,512,128]{2,1,0:T(8,128)(2,1)S(1)} %pad_maximum_fusion.mine), channel_id=1, source_target_pairs={{0,1},{1,0},{2,3},{3,2},{4,5},{5,4},{6,7},{7,6},{8,9},{9,8},{10,11... | collective-permute-start | bytes 2752520 | tf_op jit(solution)/shard_map/ppermute | solution.py:28
  82.0 16.6 %collective-permute-start.6 = (bf16[4,64,1024]{2,1,0:T(8,128)(2,1)S(1)}, bf16[4,64,1024]{2,1,0:T(8,128)(2,1)}, u32[]{:S(2)}, u32[]{:S(2)}) collective-permute-start(bf16[4,64,1024]{2,1,0:T(8,128)(2,1)S(1)} %all-to-all-done.1.refs_0_), channel_id=1, source_target_pairs={{0,64},{1,449},{2,66},{3,451},{4,68},{5,453},{6,70},{7,455},{8,72}... | collective-permute-start | bytes 1572872 | tf_op jit(solution)/shard_map/ppermute | solution.py:143
  88.6 21.6 %collective-permute-start.5 = (bf16[4,64,1024]{2,1,0:T(8,128)(2,1)S(1)}, bf16[4,64,1024]{2,1,0:T(8,128)(2,1)}, u32[]{:S(2)}, u32[]{:S(2)}) collective-permute-start(bf16[4,64,1024]{2,1,0:T(8,128)(2,1)S(1)} %all-to-all-done.1.refs_0_), channel_id=1, source_target_pairs={{0,16},{16,0},{32,48},{48,32},{64,80},{80,64},{96,112},{112,96},{1... | collective-permute-start | bytes 1572872 | tf_op jit(solution)/shard_map/ppermute | solution.py:24
  98.5 19.3 %collective-permute-start.7 = (bf16[4,64,1024]{2,1,0:T(8,128)(2,1)}, bf16[4,64,1024]{2,1,0:T(8,128)(2,1)}, u32[]{:S(2)}, u32[]{:S(2)}) collective-permute-start(bf16[4,64,1024]{2,1,0:T(8,128)(2,1)} %collective-permute-done.6.refs_2_), channel_id=1, source_target_pairs={{0,16},{16,0},{32,48},{48,32},{64,80},{80,64},{96,112},{112,96},{1... | collective-permute-start | bytes 1572872 | tf_op jit(solution)/shard_map/ppermute | solution.py:24
  101.2 25.1 %collective-permute-start.10 = (bf16[4,64,1024]{2,1,0:T(8,128)(2,1)S(1)}, bf16[4,64,1024]{2,1,0:T(8,128)(2,1)S(1)}, u32[]{:S(2)}, u32[]{:S(2)}) collective-permute-start(bf16[4,64,1024]{2,1,0:T(8,128)(2,1)S(1)} %all-to-all-done.1.refs_0_), channel_id=1, source_target_pairs={{0,32},{16,48},{32,64},{48,80},{64,96},{80,112},{96,128},{112,144}... | collective-permute-start | bytes 1572872 | tf_op jit(solution)/shard_map/ppermute | solution.py:20
  105.3 21.0 %collective-permute-start.8 = (bf16[4,64,1024]{2,1,0:T(8,128)(2,1)S(1)}, bf16[4,64,1024]{2,1,0:T(8,128)(2,1)S(1)}, u32[]{:S(2)}, u32[]{:S(2)}) collective-permute-start(bf16[4,64,1024]{2,1,0:T(8,128)(2,1)S(1)} %all-to-all-done.1.refs_0_), channel_id=1, source_target_pairs={{0,480},{16,496},{32,0},{48,16},{64,32},{80,48},{96,64},{112,80},{... | collective-permute-start | bytes 1572872 | tf_op jit(solution)/shard_map/ppermute | solution.py:20
  110.2 21.4 %collective-permute-start.11 = (bf16[4,64,1024]{2,1,0:T(8,128)(2,1)}, bf16[4,64,1024]{2,1,0:T(8,128)(2,1)S(1)}, u32[]{:S(2)}, u32[]{:S(2)}) collective-permute-start(bf16[4,64,1024]{2,1,0:T(8,128)(2,1)} %collective-permute-done.5.refs_1_), channel_id=1, source_target_pairs={{0,32},{16,48},{32,64},{48,80},{64,96},{80,112},{96,128},{112,144}... | collective-permute-start | bytes 1572872 | tf_op jit(solution)/shard_map/ppermute | solution.py:20
  112.2 0.9 copy-start.3
  113.1 19.5 %collective-permute-start.9 = (bf16[4,64,1024]{2,1,0:T(8,128)(2,1)}, bf16[4,64,1024]{2,1,0:T(8,128)(2,1)S(1)}, u32[]{:S(2)}, u32[]{:S(2)}) collective-permute-start(bf16[4,64,1024]{2,1,0:T(8,128)(2,1)} %collective-permute-done.5.refs_1_), channel_id=1, source_target_pairs={{0,480},{16,496},{32,0},{48,16},{64,32},{80,48},{96,64},{112,80},{... | collective-permute-start | bytes 1572872 | tf_op jit(solution)/shard_map/ppermute | solution.py:20
  117.8 1.0 copy-start.1
  118.7 1.6 %copy-start.2 = (bf16[8192,128]{1,0:T(8,128)(2,1)S(1)}, bf16[8192,128]{1,0:T(8,128)(2,1)}, u32[]{:S(2)}) copy-start(bf16[8192,128]{1,0:T(8,128)(2,1)} %all-gather.3.cloned.1.call-done) | copy-start | bytes 6291460
  120.3 1.2 copy-start.4
Sparse Core Ops, SparseCore 0:
  10.7 73.7 all-gather.2

commit v9 on v8

v9 whole, which is shorter than its diff:
```python
import jax
import jax.numpy as jnp
from jax import lax
from jax.experimental import pallas as pl
from jax.experimental.pallas import tpu as pltpu
from jax.sharding import PartitionSpec as P

OI = 4
FAR = (0, -4, 4, 8)
TWO = [
    (r * 16 + c, (r + (4 if c % 2 == 0 else 28)) % 32 * 16 + c) for r in range(32) for c in range(16)
]
CORE_PAIRS = [[2 * g, 2 * g + 1] for g in range(8)]
STEPS = (((0, 1), (0, 3)), ((0, 2), (1, 0)), ((1, 1), (1, 3)), ((1, 2), (1, 2)))
NTILE = 256


def z_shift(x, d):
    return lax.ppermute(x, "row", [(r, (r + 2 * d) % 32) for r in range(32)])


def x_swap(x):
    return lax.ppermute(x, "row", [(r, r ^ 1) for r in range(32)])


def core_swap(x):
    return lax.ppermute(x, "col", [(c, c ^ 1) for c in range(16)])


def chip_shift(x, step):
    pairs = []
    for xh in range(2):
        for y in range(4):
            for c in range(2):
                dx, dy = step[c]
                pairs.append(((xh * 4 + y) * 2 + c, ((xh ^ dx) * 4 + (y + dy) % 4) * 2 + c))
    return lax.ppermute(x, "col", pairs)


def multiply(amps, ints, cols):
    right = ints[:, :, :, cols].reshape(-1, NTILE)
    return jnp.dot(amps[0], right, preferred_element_type=jnp.float32) - jnp.dot(
        amps[1], right, preferred_element_type=jnp.float32
    )


def columns(n):
    return pl.ds(pl.multiple_of(n * NTILE, NTILE), NTILE)


def block_copies(place, refs, shifts, ints):
    z, xl = place[0], place[1]
    copies = []
    for ref, partner, shift in zip(refs[::2], refs[1::2], shifts):
        for slot, offset in enumerate(FAR):
            k = (z + shift + offset) & 15
            copies.append((ref.at[slot], ints.at[k >> 1, xl]))
            copies.append((partner.at[slot], ints.at[k >> 1, 1 - xl]))
    return copies


def run_copies(copies, sem):
    copies = [pltpu.make_async_copy(a, b, sem) for a, b in copies]
    for copy in copies:
        copy.start()
    for copy in copies:
        copy.wait()


def first_half(place, chip, *refs):
    z, core, xh, y = place[0], place[2], place[3], place[4]
    mine, theirs, blocks = refs[:4], refs[4:8], refs[8:12]
    total, kept, ints, sem = refs[12:]
    copies = block_copies(place, blocks, (0, 4 * core - 2), ints)
    shards = [(chip.at[c], (xh * 4 + y) * 2 + c) for c in range(2)]
    for refs, who in ((mine, core), (theirs, 1 - core)):
        for n, step in enumerate(STEPS):
            dx = jnp.where(who == 0, step[0][0], step[1][0])
            dy = jnp.where(who == 0, step[0][1], step[1][1])
            place_of = ((xh ^ dx) * 4 + ((y - dy) & 3)) * 2
            if n < 3:
                for c in range(2):
                    shards.append((refs[n].at[c], place_of + c))
            else:
                shards.append((refs[n].at[0], place_of + who))
    for ref, col in shards:
        lanes = pl.ds(pl.multiple_of((col >> 1) * 128, 128), 128)
        for s in range(2):
            copies.append((ref.at[s], kept.at[(col + z) & 1, s, :, lanes]))
    run_copies(copies, sem)

    def tile(n, carry):
        cols = columns(n)
        total[:, cols] = multiply(kept.at[0], ints, cols)
        return carry

    lax.fori_loop(0, total.shape[1] // NTILE, tile, 0)


def second_half(place, total, kept, *refs):
    blocks = [refs[i].at[x] for i in range(2) for x in range(2)]
    out, ints, sem = refs[2:]
    run_copies(block_copies(place, blocks, (1, -1), ints), sem)

    def tile(n, carry):
        cols = columns(n)
        out[:, cols] = (total[:, cols] + multiply(kept.at[1], ints, cols)).astype(out.dtype)
        return carry

    lax.fori_loop(0, out.shape[1] // NTILE, tile, 0)


def on_device(amplitudes, integrals, tile_mask):
    row, col = lax.axis_index("row"), lax.axis_index("col")
    place = jnp.stack([row // 2, row % 2, col % 2, col // 8, col // 2 % 4]).astype(jnp.int32)
    rows, cols = integrals.shape
    depth, pairs = amplitudes.shape

    far = z_shift(integrals, 8)
    block = jnp.stack([integrals, z_shift(integrals, 4), z_shift(integrals, -4), far])

    scale = jnp.repeat(tile_mask.astype(jnp.bfloat16).reshape(-1), pairs // OI)
    masked = (amplitudes * scale[None, :]).T

    sent = masked.reshape(OI, 32, OI, depth).transpose(1, 2, 0, 3)
    got = lax.all_to_all(sent, "row", split_axis=0, concat_axis=0, tiled=True)
    swapped = got.transpose(1, 0, 2, 3).reshape(pairs, depth)
    swapped, block = lax.optimization_barrier((swapped, block))

    both = jnp.stack([masked, swapped])
    chip = lax.all_gather(both, "col", axis=0, axis_index_groups=CORE_PAIRS)
    mine = [chip_shift(chip, step) for step in STEPS[:3]]

    partner = x_swap(block)
    two = lax.ppermute(block, ("row", "col"), TWO)
    both, partner, two = lax.optimization_barrier((both, partner, two))
    mine.append(chip_shift(both, STEPS[3])[None])
    theirs = [core_swap(m) for m in mine]
    near = jnp.stack([block, partner])
    up = z_shift(near, 1)
    down = z_shift(near, -1)
    two_partner = x_swap(two)

    anywhere = pl.BlockSpec(memory_space=pl.ANY)
    scalars = pl.BlockSpec(memory_space=pltpu.SMEM)
    vector = pl.BlockSpec(memory_space=pltpu.VMEM)
    ints = pltpu.VMEM((8, 2, rows, cols), jnp.bfloat16)
    params = pltpu.CompilerParams(vmem_limit_bytes=32 * 2**20)
    cost = pl.CostEstimate(
        flops=2 * pairs * 2048 * cols, bytes_accessed=10 * 2**20, transcendentals=0
    )
    total, kept = pl.pallas_call(
        first_half,
        out_shape=(
            jax.ShapeDtypeStruct((pairs, cols), jnp.float32),
            jax.ShapeDtypeStruct((2, 2, pairs, 8 * depth), jnp.bfloat16),
        ),
        in_specs=[scalars] + [anywhere] * 13,
        out_specs=(vector, vector),
        scratch_shapes=[ints, pltpu.SemaphoreType.DMA],
        compiler_params=params,
        cost_estimate=cost,
    )(place, chip, *mine, *theirs, block, partner, two, two_partner)
    return pl.pallas_call(
        second_half,
        out_shape=jax.ShapeDtypeStruct((pairs, cols), jnp.bfloat16),
        in_specs=[scalars, vector, vector] + [anywhere] * 2,
        out_specs=vector,
        scratch_shapes=[ints, pltpu.SemaphoreType.DMA],
        compiler_params=params,
        cost_estimate=cost,
    )(place, total, kept, down, up)


def solution(mesh):
    in_specs = (P("col", "row"), P("row", "col"), P("col", "row"))
    out_specs = P("row", "col")
    return jax.shard_map(
        on_device, mesh=mesh, in_specs=in_specs, out_specs=out_specs, check_vma=False
    )
```

time: 145 us -> 139 us (0.959)
  blocking collectives: 35.2 us -> 3.44 us
  starting transfers between devices: 51.2 us -> 78.9 us
  between operations: 13.7 us -> 0.36 us
  Pallas kernels: 9.39 us -> 15.7 us
  waiting for transfers between devices: 24.4 us -> 28.5 us
    all_to_all x1 -> x0, blocking collectives: 30.8 us -> none  [on_device(): got = lax.all_to_all(sent, 'row', split_axis=0, concat_axis=0, tiled=True)]
    all_to_all x1, starting transfers between devices: 3.95 us -> 17 us  [on_device(): got = lax.all_to_all(sent, 'row', split_axis=0, concat_axis=0, tiled=True)]
    ppermute x4 -> x5, starting transfers between devices: 15.4 us -> 28.4 us  [z_shift(): return lax.ppermute(x, 'row', [(r, (r + 2 * d) % 32) for r in range(32)])]
    ppermute x4 -> x5, waiting for transfers between devices: 6.16 us -> 17.6 us  [z_shift(): return lax.ppermute(x, 'row', [(r, (r + 2 * d) % 32) for r in range(32)])]
    ppermute x1, waiting for transfers between devices: 7.76 us -> 0.01 us  [on_device(): two = lax.ppermute(block, ('row', 'col'), TWO)]
    ppermute x1, starting transfers between devices: 6.6 us -> 1.92 us  [on_device(): two = lax.ppermute(block, ('row', 'col'), TWO)]
    ppermute x1 -> x4, starting transfers between devices: 4.61 us -> 8.62 us  [core_swap(): return lax.ppermute(x, 'col', [(c, c ^ 1) for c in range(16)])]
    pallas_call x1, Pallas kernels: 4.85 us -> 8.55 us  [on_device(): pl.pallas_call(first_half, out_shape=(jax.ShapeDtypeStruct((pairs, cols),...]
  transfers between devices with their start and end apart: 14 -> 17, of which waited for: 5 -> 5; matrix products, arithmetic and copies ran while one was open for 2% -> 2% of each run, Pallas kernels for 3% -> 6%
where the time goes in v9:
time: 139 us; the launch traced here: 137 us
  starting transfers between devices  78.9 us (57%)
  waiting for transfers between devices  28.5 us (21%)
  Pallas kernels  15.7 us (11%)
  local copies, waits for them, and re-layouts  7.56 us (5%)
  blocking collectives  3.44 us (2%)
  other arithmetic  2.99 us (2%)
    ppermute x5, starting transfers between devices, z_shift(): return lax.ppermute(x, 'row', [(r, (r + 2 * d) % 32) for r in range(32)])  28.4 us
    ppermute x4, starting transfers between devices, chip_shift(): return lax.ppermute(x, 'col', pairs)  18.4 us
    ppermute x5, waiting for transfers between devices, z_shift(): return lax.ppermute(x, 'row', [(r, (r + 2 * d) % 32) for r in range(32)])  17.6 us
    all_to_all x1, starting transfers between devices, on_device(): got = lax.all_to_all(sent, 'row', split_axis=0, concat_axis=0, tiled=True)  17 us
    ppermute x4, waiting for transfers between devices, chip_shift(): return lax.ppermute(x, 'col', pairs)  9.16 us
    ppermute x4, starting transfers between devices, core_swap(): return lax.ppermute(x, 'col', [(c, c ^ 1) for c in range(16)])  8.62 us
    pallas_call x1, Pallas kernels, on_device(): pl.pallas_call(first_half, out_shape=(jax.ShapeDtypeStruct((pairs, cols),...  8.55 us
    pallas_call x1, Pallas kernels, on_device(): pl.pallas_call(second_half, out_shape=jax.ShapeDtypeStruct((pairs, cols),...  7.12 us
  transfers between devices with their start and end apart: 17, of which 5 were waited for; matrix products, arithmetic and copies ran while one was open for 2% of the time, Pallas kernels for 6%

profile of v9, /device:TPU:1, one launch (start us, length us, event | category | flops | bytes accessed | tf_op | source)
XLA Modules:
  0.0 137.5 jit_solution(13164518700677931478)
XLA Ops:
  0.0 1.0 copy.6
  1.0 0.7 convert_bitcast_fusion
  1.7 0.1 broadcast_bitcast_fusion
  1.8 0.1 broadcast_multiply_fusion
  1.9 0.8 copy.10
  2.7 17.0 %all-to-all-start = ((bf16[32,4,4,128]{3,2,1,0:T(4,128)(2,1)}), bf16[32,4,4,128]{3,2,1,0:T(4,128)(2,1)S(1)}, u32[]{:S(2)}, u32[]{:S(2)}) async-start(bf16[32,4,4,128]{3,2,1,0:T(4,128)(2,1)} %bitcast.28), calls=%async_computation | async-start | bytes 262144 | tf_op jit(solution)/shard_map/all_to_all | solution.py:126
  19.6 7.1 %collective-permute-start = (bf16[64,1024]{1,0:T(8,128)(2,1)}, bf16[64,1024]{1,0:T(8,128)(2,1)S(1)}, u32[]{:S(2)}, u32[]{:S(2)}) collective-permute-start(bf16[64,1024]{1,0:T(8,128)(2,1)} %param.4), channel_id=1, source_target_pairs={{0,128},{16,144},{32,160},{48,176},{64,192},{80,208},{96,224},{112... | collective-permute-start | bytes 393224 | tf_op jit(solution)/shard_map/ppermute | solution.py:19
  26.7 2.1 %collective-permute-start.1 = (bf16[64,1024]{1,0:T(8,128)(2,1)}, bf16[64,1024]{1,0:T(8,128)(2,1)S(1)}, u32[]{:S(2)}, u32[]{:S(2)}) collective-permute-start(bf16[64,1024]{1,0:T(8,128)(2,1)} %param.4), channel_id=1, source_target_pairs={{0,384},{16,400},{32,416},{48,432},{64,448},{80,464},{96,480},{112... | collective-permute-start | bytes 393224 | tf_op jit(solution)/shard_map/ppermute | solution.py:19
  28.8 11.9 %collective-permute-start.2 = (bf16[64,1024]{1,0:T(8,128)(2,1)}, bf16[64,1024]{1,0:T(8,128)(2,1)S(1)}, u32[]{:S(2)}, u32[]{:S(2)}) collective-permute-start(bf16[64,1024]{1,0:T(8,128)(2,1)} %param.4), channel_id=1, source_target_pairs={{0,256},{16,272},{32,288},{48,304},{64,320},{80,336},{96,352},{112... | collective-permute-start | bytes 393224 | tf_op jit(solution)/shard_map/ppermute | solution.py:19
  40.7 0.1 fusion
  40.9 0.0 collective-permute-done
  40.9 4.9 %collective-permute-done.1 = bf16[64,1024]{1,0:T(8,128)(2,1)S(1)} collective-permute-done((bf16[64,1024]{1,0:T(8,128)(2,1)}, bf16[64,1024]{1,0:T(8,128)(2,1)S(1)}, u32[]{:S(2)}, u32[]{:S(2)}) %collective-permute-start.1) | collective-permute-done | bytes 131104 | tf_op jit(solution)/shard_map/ppermute | solution.py:19
  45.8 12.7 %collective-permute-done.2 = bf16[64,1024]{1,0:T(8,128)(2,1)S(1)} collective-permute-done((bf16[64,1024]{1,0:T(8,128)(2,1)}, bf16[64,1024]{1,0:T(8,128)(2,1)S(1)}, u32[]{:S(2)}, u32[]{:S(2)}) %collective-permute-start.2) | collective-permute-done | bytes 131104 | tf_op jit(solution)/shard_map/ppermute | solution.py:19
  58.5 1.0 pad_maximum_fusion.1.refs_8_
  59.5 0.0 all-to-all-done
  59.5 2.6 %collective-permute-start.6 = (bf16[4,64,1024]{2,1,0:T(8,128)(2,1)S(1)}, bf16[4,64,1024]{2,1,0:T(8,128)(2,1)S(1)}, u32[]{:S(2)}, u32[]{:S(2)}) collective-permute-start(bf16[4,64,1024]{2,1,0:T(8,128)(2,1)S(1)} %pad_maximum_fusion.1.refs_8_), channel_id=1, source_target_pairs={{0,16},{16,0},{32,48},{48,32},{64,80},{80,64},{96,112},{112,96},{1... | collective-permute-start | bytes 1572872 | tf_op jit(solution)/shard_map/ppermute | solution.py:23
  62.2 1.9 %collective-permute-start.7 = (bf16[4,64,1024]{2,1,0:T(8,128)(2,1)S(1)}, bf16[4,64,1024]{2,1,0:T(8,128)(2,1)S(1)}, u32[]{:S(2)}, u32[]{:S(2)}) collective-permute-start(bf16[4,64,1024]{2,1,0:T(8,128)(2,1)S(1)} %pad_maximum_fusion.1.refs_8_), channel_id=1, source_target_pairs={{0,64},{1,449},{2,66},{3,451},{4,68},{5,453},{6,70},{7,455},{8,72}... | collective-permute-start | bytes 1572872 | tf_op jit(solution)/shard_map/ppermute | solution.py:135
  64.2 3.4 %all-gather = bf16[4,512,128]{2,1,0:T(8,128)(2,1)S(1)} all-gather(bf16[2,512,128]{2,1,0:T(8,128)(2,1)S(1)} %pad_maximum_fusion.2), channel_id=2, replica_groups={{0,1},{2,3},{4,5},{6,7},{8,9},{10,11},{12,13},{14,15},{16,17},{18,19},{..., dimensions={0}, use_global_device_ids=true | all-gather | bytes 786432 | tf_op jit(solution)/shard_map/all_gather | solution.py:131
  67.6 4.3 %collective-permute-start.4 = (bf16[2,2,512,128]{3,2,1,0:T(8,128)(2,1)S(1)}, bf16[2,2,512,128]{3,2,1,0:T(8,128)(2,1)}, u32[]{:S(2)}, u32[]{:S(2)}) collective-permute-start(bf16[2,2,512,128]{3,2,1,0:T(8,128)(2,1)S(1)} %bitcast.30), channel_id=1, source_target_pairs={{0,4},{1,9},{2,6},{3,11},{4,0},{5,13},{6,2},{7,15},{8,12},{9,1},{1... | collective-permute-start | bytes 1572872 | tf_op jit(solution)/shard_map/ppermute | solution.py:37
  72.0 4.9 %collective-permute-start.5 = (bf16[2,2,512,128]{3,2,1,0:T(8,128)(2,1)S(1)}, bf16[2,2,512,128]{3,2,1,0:T(8,128)(2,1)}, u32[]{:S(2)}, u32[]{:S(2)}) collective-permute-start(bf16[2,2,512,128]{3,2,1,0:T(8,128)(2,1)S(1)} %bitcast.31), channel_id=1, source_target_pairs={{0,10},{1,15},{2,12},{3,9},{4,14},{5,11},{6,8},{7,13},{8,2},{9,7},... | collective-permute-start | bytes 1572872 | tf_op jit(solution)/shard_map/ppermute | solution.py:37
  76.8 2.4 %collective-permute-start.3 = (bf16[2,2,512,128]{3,2,1,0:T(8,128)(2,1)S(1)}, bf16[2,2,512,128]{3,2,1,0:T(8,128)(2,1)}, u32[]{:S(2)}, u32[]{:S(2)}) collective-permute-start(bf16[2,2,512,128]{3,2,1,0:T(8,128)(2,1)S(1)} %bitcast.32), channel_id=1, source_target_pairs={{0,2},{1,7},{2,4},{3,1},{4,6},{5,3},{6,0},{7,5},{8,10},{9,15},{10,... | collective-permute-start | bytes 1572872 | tf_op jit(solution)/shard_map/ppermute | solution.py:37
  79.2 0.0 collective-permute-done.6.refs_9_
  79.2 0.0 copy-start
  79.2 0.0 collective-permute-done.7.refs_10_
  79.3 0.0 copy-start.2
  79.3 6.8 %collective-permute-start.8 = (bf16[2,512,128]{2,1,0:T(8,128)(2,1)S(1)}, bf16[2,512,128]{2,1,0:T(8,128)(2,1)S(1)}, u32[]{:S(2)}, u32[]{:S(2)}) collective-permute-start(bf16[2,512,128]{2,1,0:T(8,128)(2,1)S(1)} %pad_maximum_fusion.2), channel_id=1, source_target_pairs={{0,12},{1,13},{2,14},{3,15},{4,8},{5,9},{6,10},{7,11},{8,4},{9,5},... | collective-permute-start | bytes 786440 | tf_op jit(solution)/shard_map/ppermute | solution.py:37
  86.1 2.0 %collective-permute-start.13 = (bf16[4,64,1024]{2,1,0:T(8,128)(2,1)S(1)}, bf16[4,64,1024]{2,1,0:T(8,128)(2,1)S(1)}, u32[]{:S(2)}, u32[]{:S(2)}) collective-permute-start(bf16[4,64,1024]{2,1,0:T(8,128)(2,1)S(1)} %collective-permute-done.7.refs_10_), channel_id=1, source_target_pairs={{0,16},{16,0},{32,48},{48,32},{64,80},{80,64},{96,112},{112,96},{1... | collective-permute-start | bytes 1572872 | tf_op jit(solution)/shard_map/ppermute | solution.py:23
  88.1 1.1 pad_maximum_fusion
  89.2 0.0 copy-done
  89.2 0.0 collective-permute-done.4.refs_1_
  89.2 5.4 %collective-permute-start.14 = (bf16[2,4,64,1024]{3,2,1,0:T(8,128)(2,1)}, bf16[2,4,64,1024]{3,2,1,0:T(8,128)(2,1)S(1)}, u32[]{:S(2)}, u32[]{:S(2)}) collective-permute-start(bf16[2,4,64,1024]{3,2,1,0:T(8,128)(2,1)} %pad_maximum_fusion), channel_id=1, source_target_pairs={{0,480},{16,496},{32,0},{48,16},{64,32},{80,48},{96,64},{112,80},{... | collective-permute-start | bytes 3145736 | tf_op jit(solution)/shard_map/ppermute | solution.py:19
  94.6 3.4 %collective-permute-done.5.refs_2_ = bf16[2,2,512,128]{3,2,1,0:T(8,128)(2,1)} collective-permute-done((bf16[2,2,512,128]{3,2,1,0:T(8,128)(2,1)S(1)}, bf16[2,2,512,128]{3,2,1,0:T(8,128)(2,1)}, u32[]{:S(2)}, u32[]{:S(2)}) %collective-permute-start.5) | collective-permute-done | bytes 524320 | tf_op jit(solution)/shard_map/ppermute | solution.py:37
  97.9 1.9 %collective-permute-start.15 = (bf16[2,4,64,1024]{3,2,1,0:T(8,128)(2,1)}, bf16[2,4,64,1024]{3,2,1,0:T(8,128)(2,1)S(1)}, u32[]{:S(2)}, u32[]{:S(2)}) collective-permute-start(bf16[2,4,64,1024]{3,2,1,0:T(8,128)(2,1)} %pad_maximum_fusion), channel_id=1, source_target_pairs={{0,32},{16,48},{32,64},{48,80},{64,96},{80,112},{96,128},{112,144}... | collective-permute-start | bytes 3145736 | tf_op jit(solution)/shard_map/ppermute | solution.py:19
  99.9 5.8 %collective-permute-done.8 = bf16[2,512,128]{2,1,0:T(8,128)(2,1)S(1)} collective-permute-done((bf16[2,512,128]{2,1,0:T(8,128)(2,1)S(1)}, bf16[2,512,128]{2,1,0:T(8,128)(2,1)S(1)}, u32[]{:S(2)}, u32[]{:S(2)}) %collective-permute-start.8) | collective-permute-done | bytes 262176 | tf_op jit(solution)/shard_map/ppermute | solution.py:37
  105.6 1.9 %collective-permute-start.12 = (bf16[1,2,512,128]{3,2,1,0:T(8,128)(2,1)S(1)}, bf16[1,2,512,128]{3,2,1,0:T(8,128)(2,1)S(1)}, u32[]{:S(2)}, u32[]{:S(2)}) collective-permute-start(bf16[1,2,512,128]{3,2,1,0:T(8,128)(2,1)S(1)} %bitcast.35), channel_id=1, source_target_pairs={{0,1},{1,0},{2,3},{3,2},{4,5},{5,4},{6,7},{7,6},{8,9},{9,8},{10,11... | collective-permute-start | bytes 786440 | tf_op jit(solution)/shard_map/ppermute | solution.py:27
  107.6 0.0 collective-permute-done.3.refs_0_
  107.6 0.0 copy-done.2
  107.6 2.4 %collective-permute-start.10 = (bf16[2,2,512,128]{3,2,1,0:T(8,128)(2,1)}, bf16[2,2,512,128]{3,2,1,0:T(8,128)(2,1)}, u32[]{:S(2)}, u32[]{:S(2)}) collective-permute-start(bf16[2,2,512,128]{3,2,1,0:T(8,128)(2,1)} %collective-permute-done.4.refs_1_), channel_id=1, source_target_pairs={{0,1},{1,0},{2,3},{3,2},{4,5},{5,4},{6,7},{7,6},{8,9},{9,8},{10,11... | collective-permute-start | bytes 1572872 | tf_op jit(solution)/shard_map/ppermute | solution.py:27
  110.0 0.0 collective-permute-done.12.refs_7_
  110.0 0.0 copy-start.6
  110.0 0.7 copy-done.6
  110.7 1.9 %collective-permute-start.11 = (bf16[2,2,512,128]{3,2,1,0:T(8,128)(2,1)}, bf16[2,2,512,128]{3,2,1,0:T(8,128)(2,1)}, u32[]{:S(2)}, u32[]{:S(2)}) collective-permute-start(bf16[2,2,512,128]{3,2,1,0:T(8,128)(2,1)} %collective-permute-done.5.refs_2_), channel_id=1, source_target_pairs={{0,1},{1,0},{2,3},{3,2},{4,5},{5,4},{6,7},{7,6},{8,9},{9,8},{10,11... | collective-permute-start | bytes 1572872 | tf_op jit(solution)/shard_map/ppermute | solution.py:27
  112.6 0.0 collective-permute-done.13.refs_11_
  112.6 0.0 copy-start.4
  112.7 0.8 copy-done.4
  113.5 2.4 %collective-permute-start.9 = (bf16[2,2,512,128]{3,2,1,0:T(8,128)(2,1)}, bf16[2,2,512,128]{3,2,1,0:T(8,128)(2,1)}, u32[]{:S(2)}, u32[]{:S(2)}) collective-permute-start(bf16[2,2,512,128]{3,2,1,0:T(8,128)(2,1)} %collective-permute-done.3.refs_0_), channel_id=1, source_target_pairs={{0,1},{1,0},{2,3},{3,2},{4,5},{5,4},{6,7},{7,6},{8,9},{9,8},{10,11... | collective-permute-start | bytes 1572872 | tf_op jit(solution)/shard_map/ppermute | solution.py:27
  115.9 0.1 stack.56.place
  116.0 0.0 collective-permute-done.10.refs_5_
  116.0 0.0 collective-permute-done.11.refs_6_
  116.0 1.7 %collective-permute-done.9.refs_4_ = bf16[2,2,512,128]{3,2,1,0:T(8,128)(2,1)} collective-permute-done((bf16[2,2,512,128]{3,2,1,0:T(8,128)(2,1)}, bf16[2,2,512,128]{3,2,1,0:T(8,128)(2,1)}, u32[]{:S(2)}, u32[]{:S(2)}) %collective-permute-start.9) | collective-permute-done | bytes 524320 | tf_op jit(solution)/shard_map/ppermute | solution.py:27
  117.7 0.0 copy-start.1
  117.7 1.0 copy-done.1
  118.8 0.0 copy-start.3
  118.8 1.0 copy-done.3
  119.8 0.0 copy-start.5
  119.8 1.0 copy-done.5
  120.8 0.0 copy-start.7
  120.8 0.9 copy-done.7
  121.8 8.5 %shard_map.37 = (f32[512,1024]{1,0:T(8,128)S(1)}, bf16[2,2,512,1024]{3,2,1,0:T(8,128)(2,1)S(1)}) custom-call(s32[5]{0:T(128)S(1)} %stack.56.place, bf16[2,2,512,128]{3,2,1,0:T(8,128)(2,1)S(1)} %bitcast.33, bf16[2,2,512,128]{3,2,1,0:T(8,128)(2,1)} %collective-permute-done.3.refs_0_, bf16[2,2,512,128]{3,2,1,0:T(8,128)(2,1)} %collective-permute-done.4.refs_1_, ...), custom_call_target="tpu_custom_call" | custom-call | flops 2147483648 | bytes 10485760 | tf_op jit(solution)/shard_map/pallas_call | solution.py:152
  130.3 0.0 collective-permute-done.14.refs_0_
  130.4 0.0 collective-permute-done.15.refs_1_
  130.4 7.1 %shard_map.38 = bf16[512,1024]{1,0:T(8,128)(2,1)} custom-call(s32[5]{0:T(128)S(1)} %stack.56.place, f32[512,1024]{1,0:T(8,128)S(1)} %get-tuple-element.17.total, bf16[2,2,512,1024]{3,2,1,0:T(8,128)(2,1)S(1)} %get-tuple-element.18.kept, bf16[2,4,64,1024]{3,2,1,0:T(8,128)(2,1)S(1)} %collective-permute-done.14.refs_0_, ...), custom_call_target="tpu_custom_call" | custom-call | flops 2147483648 | bytes 10485760 | tf_op jit(solution)/shard_map/pallas_call | solution.py:164
  (2 shorter events, 0.1 us)
Async XLA Ops:
  2.7 56.8 %all-to-all-start = ((bf16[32,4,4,128]{3,2,1,0:T(4,128)(2,1)}), bf16[32,4,4,128]{3,2,1,0:T(4,128)(2,1)S(1)}, u32[]{:S(2)}, u32[]{:S(2)}) async-start(bf16[32,4,4,128]{3,2,1,0:T(4,128)(2,1)} %bitcast.28), calls=%async_computation | async-start | bytes 262144 | tf_op jit(solution)/shard_map/all_to_all | solution.py:126
  19.6 21.2 %collective-permute-start = (bf16[64,1024]{1,0:T(8,128)(2,1)}, bf16[64,1024]{1,0:T(8,128)(2,1)S(1)}, u32[]{:S(2)}, u32[]{:S(2)}) collective-permute-start(bf16[64,1024]{1,0:T(8,128)(2,1)} %param.4), channel_id=1, source_target_pairs={{0,128},{16,144},{32,160},{48,176},{64,192},{80,208},{96,224},{112... | collective-permute-start | bytes 393224 | tf_op jit(solution)/shard_map/ppermute | solution.py:19
  26.7 19.1 %collective-permute-start.1 = (bf16[64,1024]{1,0:T(8,128)(2,1)}, bf16[64,1024]{1,0:T(8,128)(2,1)S(1)}, u32[]{:S(2)}, u32[]{:S(2)}) collective-permute-start(bf16[64,1024]{1,0:T(8,128)(2,1)} %param.4), channel_id=1, source_target_pairs={{0,384},{16,400},{32,416},{48,432},{64,448},{80,464},{96,480},{112... | collective-permute-start | bytes 393224 | tf_op jit(solution)/shard_map/ppermute | solution.py:19
  28.8 29.7 %collective-permute-start.2 = (bf16[64,1024]{1,0:T(8,128)(2,1)}, bf16[64,1024]{1,0:T(8,128)(2,1)S(1)}, u32[]{:S(2)}, u32[]{:S(2)}) collective-permute-start(bf16[64,1024]{1,0:T(8,128)(2,1)} %param.4), channel_id=1, source_target_pairs={{0,256},{16,272},{32,288},{48,304},{64,320},{80,336},{96,352},{112... | collective-permute-start | bytes 393224 | tf_op jit(solution)/shard_map/ppermute | solution.py:19
  59.5 19.7 %collective-permute-start.6 = (bf16[4,64,1024]{2,1,0:T(8,128)(2,1)S(1)}, bf16[4,64,1024]{2,1,0:T(8,128)(2,1)S(1)}, u32[]{:S(2)}, u32[]{:S(2)}) collective-permute-start(bf16[4,64,1024]{2,1,0:T(8,128)(2,1)S(1)} %pad_maximum_fusion.1.refs_8_), channel_id=1, source_target_pairs={{0,16},{16,0},{32,48},{48,32},{64,80},{80,64},{96,112},{112,96},{1... | collective-permute-start | bytes 1572872 | tf_op jit(solution)/shard_map/ppermute | solution.py:23
  62.2 17.0 %collective-permute-start.7 = (bf16[4,64,1024]{2,1,0:T(8,128)(2,1)S(1)}, bf16[4,64,1024]{2,1,0:T(8,128)(2,1)S(1)}, u32[]{:S(2)}, u32[]{:S(2)}) collective-permute-start(bf16[4,64,1024]{2,1,0:T(8,128)(2,1)S(1)} %pad_maximum_fusion.1.refs_8_), channel_id=1, source_target_pairs={{0,64},{1,449},{2,66},{3,451},{4,68},{5,453},{6,70},{7,455},{8,72}... | collective-permute-start | bytes 1572872 | tf_op jit(solution)/shard_map/ppermute | solution.py:135
  67.6 21.6 %collective-permute-start.4 = (bf16[2,2,512,128]{3,2,1,0:T(8,128)(2,1)S(1)}, bf16[2,2,512,128]{3,2,1,0:T(8,128)(2,1)}, u32[]{:S(2)}, u32[]{:S(2)}) collective-permute-start(bf16[2,2,512,128]{3,2,1,0:T(8,128)(2,1)S(1)} %bitcast.30), channel_id=1, source_target_pairs={{0,4},{1,9},{2,6},{3,11},{4,0},{5,13},{6,2},{7,15},{8,12},{9,1},{1... | collective-permute-start | bytes 1572872 | tf_op jit(solution)/shard_map/ppermute | solution.py:37
  72.0 26.0 %collective-permute-start.5 = (bf16[2,2,512,128]{3,2,1,0:T(8,128)(2,1)S(1)}, bf16[2,2,512,128]{3,2,1,0:T(8,128)(2,1)}, u32[]{:S(2)}, u32[]{:S(2)}) collective-permute-start(bf16[2,2,512,128]{3,2,1,0:T(8,128)(2,1)S(1)} %bitcast.31), channel_id=1, source_target_pairs={{0,10},{1,15},{2,12},{3,9},{4,14},{5,11},{6,8},{7,13},{8,2},{9,7},... | collective-permute-start | bytes 1572872 | tf_op jit(solution)/shard_map/ppermute | solution.py:37
  76.8 30.7 %collective-permute-start.3 = (bf16[2,2,512,128]{3,2,1,0:T(8,128)(2,1)S(1)}, bf16[2,2,512,128]{3,2,1,0:T(8,128)(2,1)}, u32[]{:S(2)}, u32[]{:S(2)}) collective-permute-start(bf16[2,2,512,128]{3,2,1,0:T(8,128)(2,1)S(1)} %bitcast.32), channel_id=1, source_target_pairs={{0,2},{1,7},{2,4},{3,1},{4,6},{5,3},{6,0},{7,5},{8,10},{9,15},{10,... | collective-permute-start | bytes 1572872 | tf_op jit(solution)/shard_map/ppermute | solution.py:37
  79.2 9.9 %copy-start = (bf16[4,64,1024]{2,1,0:T(8,128)(2,1)}, bf16[4,64,1024]{2,1,0:T(8,128)(2,1)S(1)}, u32[]{:S(2)}) copy-start(bf16[4,64,1024]{2,1,0:T(8,128)(2,1)S(1)} %collective-permute-done.6.refs_9_) | copy-start | bytes 1572868
  79.3 28.3 %copy-start.2 = (bf16[4,64,1024]{2,1,0:T(8,128)(2,1)}, bf16[4,64,1024]{2,1,0:T(8,128)(2,1)S(1)}, u32[]{:S(2)}) copy-start(bf16[4,64,1024]{2,1,0:T(8,128)(2,1)S(1)} %collective-permute-done.7.refs_10_) | copy-start | bytes 1572868
  79.3 26.4 %collective-permute-start.8 = (bf16[2,512,128]{2,1,0:T(8,128)(2,1)S(1)}, bf16[2,512,128]{2,1,0:T(8,128)(2,1)S(1)}, u32[]{:S(2)}, u32[]{:S(2)}) collective-permute-start(bf16[2,512,128]{2,1,0:T(8,128)(2,1)S(1)} %pad_maximum_fusion.2), channel_id=1, source_target_pairs={{0,12},{1,13},{2,14},{3,15},{4,8},{5,9},{6,10},{7,11},{8,4},{9,5},... | collective-permute-start | bytes 786440 | tf_op jit(solution)/shard_map/ppermute | solution.py:37
  86.1 26.6 %collective-permute-start.13 = (bf16[4,64,1024]{2,1,0:T(8,128)(2,1)S(1)}, bf16[4,64,1024]{2,1,0:T(8,128)(2,1)S(1)}, u32[]{:S(2)}, u32[]{:S(2)}) collective-permute-start(bf16[4,64,1024]{2,1,0:T(8,128)(2,1)S(1)} %collective-permute-done.7.refs_10_), channel_id=1, source_target_pairs={{0,16},{16,0},{32,48},{48,32},{64,80},{80,64},{96,112},{112,96},{1... | collective-permute-start | bytes 1572872 | tf_op jit(solution)/shard_map/ppermute | solution.py:23
  89.2 41.2 %collective-permute-start.14 = (bf16[2,4,64,1024]{3,2,1,0:T(8,128)(2,1)}, bf16[2,4,64,1024]{3,2,1,0:T(8,128)(2,1)S(1)}, u32[]{:S(2)}, u32[]{:S(2)}) collective-permute-start(bf16[2,4,64,1024]{3,2,1,0:T(8,128)(2,1)} %pad_maximum_fusion), channel_id=1, source_target_pairs={{0,480},{16,496},{32,0},{48,16},{64,32},{80,48},{96,64},{112,80},{... | collective-permute-start | bytes 3145736 | tf_op jit(solution)/shard_map/ppermute | solution.py:19
  97.9 32.4 %collective-permute-start.15 = (bf16[2,4,64,1024]{3,2,1,0:T(8,128)(2,1)}, bf16[2,4,64,1024]{3,2,1,0:T(8,128)(2,1)S(1)}, u32[]{:S(2)}, u32[]{:S(2)}) collective-permute-start(bf16[2,4,64,1024]{3,2,1,0:T(8,128)(2,1)} %pad_maximum_fusion), channel_id=1, source_target_pairs={{0,32},{16,48},{32,64},{48,80},{64,96},{80,112},{96,128},{112,144}... | collective-permute-start | bytes 3145736 | tf_op jit(solution)/shard_map/ppermute | solution.py:19
  105.6 4.4 %collective-permute-start.12 = (bf16[1,2,512,128]{3,2,1,0:T(8,128)(2,1)S(1)}, bf16[1,2,512,128]{3,2,1,0:T(8,128)(2,1)S(1)}, u32[]{:S(2)}, u32[]{:S(2)}) collective-permute-start(bf16[1,2,512,128]{3,2,1,0:T(8,128)(2,1)S(1)} %bitcast.35), channel_id=1, source_target_pairs={{0,1},{1,0},{2,3},{3,2},{4,5},{5,4},{6,7},{7,6},{8,9},{9,8},{10,11... | collective-permute-start | bytes 786440 | tf_op jit(solution)/shard_map/ppermute | solution.py:27
  107.6 8.4 %collective-permute-start.10 = (bf16[2,2,512,128]{3,2,1,0:T(8,128)(2,1)}, bf16[2,2,512,128]{3,2,1,0:T(8,128)(2,1)}, u32[]{:S(2)}, u32[]{:S(2)}) collective-permute-start(bf16[2,2,512,128]{3,2,1,0:T(8,128)(2,1)} %collective-permute-done.4.refs_1_), channel_id=1, source_target_pairs={{0,1},{1,0},{2,3},{3,2},{4,5},{5,4},{6,7},{7,6},{8,9},{9,8},{10,11... | collective-permute-start | bytes 1572872 | tf_op jit(solution)/shard_map/ppermute | solution.py:27
  110.0 0.7 copy-start.6
  110.7 5.3 %collective-permute-start.11 = (bf16[2,2,512,128]{3,2,1,0:T(8,128)(2,1)}, bf16[2,2,512,128]{3,2,1,0:T(8,128)(2,1)}, u32[]{:S(2)}, u32[]{:S(2)}) collective-permute-start(bf16[2,2,512,128]{3,2,1,0:T(8,128)(2,1)} %collective-permute-done.5.refs_2_), channel_id=1, source_target_pairs={{0,1},{1,0},{2,3},{3,2},{4,5},{5,4},{6,7},{7,6},{8,9},{9,8},{10,11... | collective-permute-start | bytes 1572872 | tf_op jit(solution)/shard_map/ppermute | solution.py:27
  112.6 0.8 copy-start.4
  113.5 4.3 %collective-permute-start.9 = (bf16[2,2,512,128]{3,2,1,0:T(8,128)(2,1)}, bf16[2,2,512,128]{3,2,1,0:T(8,128)(2,1)}, u32[]{:S(2)}, u32[]{:S(2)}) collective-permute-start(bf16[2,2,512,128]{3,2,1,0:T(8,128)(2,1)} %collective-permute-done.3.refs_0_), channel_id=1, source_target_pairs={{0,1},{1,0},{2,3},{3,2},{4,5},{5,4},{6,7},{7,6},{8,9},{9,8},{10,11... | collective-permute-start | bytes 1572872 | tf_op jit(solution)/shard_map/ppermute | solution.py:27
  117.7 1.0 copy-start.1
  118.8 1.0 copy-start.3
  119.8 1.0 copy-start.5
  120.8 0.9 copy-start.7

commit v10 on v9

v10 whole, which is shorter than its diff:
```python
import jax
import jax.numpy as jnp
from jax import lax
from jax.experimental import pallas as pl
from jax.experimental.pallas import tpu as pltpu
from jax.sharding import PartitionSpec as P

OI = 4
NTILE = 256


def z_shift(x, d):
    return lax.ppermute(x, "row", [(r, (r + 2 * d) % 32) for r in range(32)])


def split_shift(d):
    step = (2 * d, 32 - 2 * d)
    return [(r * 16 + c, (r + step[c % 2]) % 32 * 16 + c) for r in range(32) for c in range(16)]


def x_swap(x):
    return lax.ppermute(x, "row", [(r, r ^ 1) for r in range(32)])


def core_swap(x):
    return lax.ppermute(x, "col", [(c, c ^ 1) for c in range(16)])


def chip_shift(x, step):
    dx, dy = step
    return lax.ppermute(
        x, "col", [(c, (c // 8 ^ dx) * 8 + (c // 2 % 4 + dy) % 4 * 2 + c % 2) for c in range(16)]
    )


def multiply(amps, ints, cols):
    right = ints[:, :, :, :, cols].reshape(-1, NTILE)
    return jnp.dot(amps[0], right, preferred_element_type=jnp.float32) - jnp.dot(
        amps[1], right, preferred_element_type=jnp.float32
    )


def columns(n):
    return pl.ds(pl.multiple_of(n * NTILE, NTILE), NTILE)


def block_copies(place, refs, shifts, ints):
    z, xl = place[0], place[1]
    copies = []
    for ref, partner, shift in zip(refs[::2], refs[1::2], shifts):
        m = (z + shift) & 3
        copies.append((ref, ints.at[:, m >> 1, xl]))
        copies.append((partner, ints.at[:, m >> 1, 1 - xl]))
    return copies


def run_copies(copies, sem):
    copies = [pltpu.make_async_copy(a, b, sem) for a, b in copies]
    for copy in copies:
        copy.start()
    for copy in copies:
        copy.wait()


def four(place, here, below, above, far, out):
    q = place[0] >> 2
    for step, shard in enumerate((here, above, far, below)):
        out[(q + step) & 3] = shard[...]


def gather_four(place, *shards):
    return pl.pallas_call(
        four,
        out_shape=jax.ShapeDtypeStruct((4,) + shards[0].shape, shards[0].dtype),
        in_specs=[pl.BlockSpec(memory_space=pltpu.SMEM)]
        + [pl.BlockSpec(memory_space=pltpu.VMEM)] * 4,
        out_specs=pl.BlockSpec(memory_space=pltpu.VMEM),
    )(place, *shards)


def first_half(place, *refs):
    z, core, xh, y = place[0], place[2], place[3], place[4]
    mine, theirs, blocks = refs[:4], refs[4:8], refs[8:12]
    total, kept, ints, sem = refs[12:]
    copies = block_copies(place, blocks, (0, 2), ints)
    shards = []
    for refs, who in ((mine, core), (theirs, 1 - core)):
        for ref, dy in zip(refs, (0, 1, 3, 2)):
            for dx in range(2):
                shards.append((ref.at[dx], ((xh ^ dx) * 4 + ((y - dy) & 3)) * 2 + who))
    for ref, col in shards:
        lanes = pl.ds(pl.multiple_of((col >> 1) * 128, 128), 128)
        for s in range(2):
            copies.append((ref.at[s], kept.at[(col + z) & 1, s, :, lanes]))
    run_copies(copies, sem)

    def tile(n, carry):
        cols = columns(n)
        total[:, cols] = multiply(kept.at[0], ints, cols)
        return carry

    lax.fori_loop(0, total.shape[1] // NTILE, tile, 0)


def second_half(place, total, kept, *refs):
    blocks = [refs[i].at[x] for i in range(2) for x in range(2)]
    out, ints, sem = refs[2:]
    run_copies(block_copies(place, blocks, (1, -1), ints), sem)

    def tile(n, carry):
        cols = columns(n)
        out[:, cols] = (total[:, cols] + multiply(kept.at[1], ints, cols)).astype(out.dtype)
        return carry

    lax.fori_loop(0, out.shape[1] // NTILE, tile, 0)


def on_device(amplitudes, integrals, tile_mask):
    row, col = lax.axis_index("row"), lax.axis_index("col")
    core = col % 2
    place = jnp.stack([row // 2, row % 2, core, col // 8, col // 2 % 4]).astype(jnp.int32)
    rows, cols = integrals.shape
    depth, pairs = amplitudes.shape

    up4 = z_shift(integrals, 4)
    down4 = z_shift(integrals, -4)
    far = lax.ppermute(jnp.where(core == 0, up4, down4), ("row", "col"), split_shift(4))

    scale = jnp.repeat(tile_mask.astype(jnp.bfloat16).reshape(-1), pairs // OI)
    masked = (amplitudes * scale[None, :]).T

    masked, up4, down4 = lax.optimization_barrier((masked, up4, down4))
    sent = masked.reshape(OI, 32, OI, depth).transpose(1, 2, 0, 3)
    got = lax.all_to_all(sent, "row", split_axis=0, concat_axis=0, tiled=True)
    swapped = got.transpose(1, 0, 2, 3).reshape(pairs, depth)
    block = gather_four(place, integrals, up4, down4, far)
    swapped, block = lax.optimization_barrier((swapped, block))

    both = jnp.stack([masked, swapped])
    pair = jnp.stack([both, chip_shift(both, (1, 0))])
    mine = [pair] + [chip_shift(pair, (0, dy)) for dy in (1, 3)]

    partner = x_swap(block)
    two = lax.ppermute(block, ("row", "col"), split_shift(2))
    pair, partner, two = lax.optimization_barrier((pair, partner, two))
    mine.append(chip_shift(pair, (0, 2)))
    theirs = [core_swap(m) for m in mine]
    near = jnp.stack([block, partner])
    up = z_shift(near, 1)
    down = z_shift(near, -1)
    two_partner = x_swap(two)

    anywhere = pl.BlockSpec(memory_space=pl.ANY)
    scalars = pl.BlockSpec(memory_space=pltpu.SMEM)
    vector = pl.BlockSpec(memory_space=pltpu.VMEM)
    ints = pltpu.VMEM((4, 2, 2, rows, cols), jnp.bfloat16)
    params = pltpu.CompilerParams(vmem_limit_bytes=32 * 2**20)
    cost = pl.CostEstimate(
        flops=2 * pairs * 2048 * cols, bytes_accessed=10 * 2**20, transcendentals=0
    )
    total, kept = pl.pallas_call(
        first_half,
        out_shape=(
            jax.ShapeDtypeStruct((pairs, cols), jnp.float32),
            jax.ShapeDtypeStruct((2, 2, pairs, 8 * depth), jnp.bfloat16),
        ),
        in_specs=[scalars] + [anywhere] * 12,
        out_specs=(vector, vector),
        scratch_shapes=[ints, pltpu.SemaphoreType.DMA],
        compiler_params=params,
        cost_estimate=cost,
    )(place, *mine, *theirs, block, partner, two, two_partner)
    return pl.pallas_call(
        second_half,
        out_shape=jax.ShapeDtypeStruct((pairs, cols), jnp.bfloat16),
        in_specs=[scalars, vector, vector] + [anywhere] * 2,
        out_specs=vector,
        scratch_shapes=[ints, pltpu.SemaphoreType.DMA],
        compiler_params=params,
        cost_estimate=cost,
    )(place, total, kept, down, up)


def solution(mesh):
    in_specs = (P("col", "row"), P("row", "col"), P("col", "row"))
    out_specs = P("row", "col")
    return jax.shard_map(
        on_device, mesh=mesh, in_specs=in_specs, out_specs=out_specs, check_vma=False
    )
```

time: 139 us -> 130 us (0.935)
  the two profiles are of different devices: /device:TPU:1 before, /device:TPU:186 now
where the time goes in v10:
time: 130 us; the launch traced here: 129 us
  starting transfers between devices  66.6 us (51%)
  waiting for transfers between devices  45.8 us (35%)
  Pallas kernels  11.3 us (9%)
  local copies, waits for them, and re-layouts  3.23 us (2%)
  other arithmetic  2.04 us (2%)
    ppermute x4, waiting for transfers between devices, z_shift(): return lax.ppermute(x, 'row', [(r, (r + 2 * d) % 32) for r in range(32)])  25.1 us
    ppermute x4, starting transfers between devices, z_shift(): return lax.ppermute(x, 'row', [(r, (r + 2 * d) % 32) for r in range(32)])  15 us
    ppermute x4, starting transfers between devices, chip_shift(): lax.ppermute(x, 'col', [(c, (c // 8 ^ dx) * 8 + (c // 2 % 4 + dy) % 4 * 2...  13.1 us
    all_to_all x1, starting transfers between devices, on_device(): got = lax.all_to_all(sent, 'row', split_axis=0, concat_axis=0, tiled=True)  12.4 us
    ppermute x4, starting transfers between devices, core_swap(): return lax.ppermute(x, 'col', [(c, c ^ 1) for c in range(16)])  8.17 us
    ppermute x1, waiting for transfers between devices, on_device(): lax.ppermute(jnp.where(core == 0, up4, down4), ('row', 'col'), split_shif...  7.79 us
    ppermute x4, waiting for transfers between devices, chip_shift(): lax.ppermute(x, 'col', [(c, (c // 8 ^ dx) * 8 + (c // 2 % 4 + dy) % 4 * 2...  7.65 us
    ppermute x2, starting transfers between devices, x_swap(): return lax.ppermute(x, 'row', [(r, r ^ 1) for r in range(32)])  7.09 us
  transfers between devices with their start and end apart: 17, of which 10 were waited for; matrix products, arithmetic and copies ran while one was open for 3% of the time, Pallas kernels for 5%

profile of v10, /device:TPU:186, one launch (start us, length us, event | category | flops | bytes accessed | tf_op | source)
XLA Modules:
  0.0 129.4 jit_solution(11698261925740716850)
XLA Ops:
  0.0 8.2 %collective-permute-start = (bf16[64,1024]{1,0:T(8,128)(2,1)}, bf16[64,1024]{1,0:T(8,128)(2,1)S(1)}, u32[]{:S(2)}, u32[]{:S(2)}) collective-permute-start(bf16[64,1024]{1,0:T(8,128)(2,1)} %here.1), channel_id=1, source_target_pairs={{0,128},{16,144},{32,160},{48,176},{64,192},{80,208},{96,224},{112... | collective-permute-start | bytes 393224 | tf_op jit(solution)/shard_map/ppermute | solution.py:13
  8.2 1.9 %collective-permute-start.1 = (bf16[64,1024]{1,0:T(8,128)(2,1)}, bf16[64,1024]{1,0:T(8,128)(2,1)S(1)}, u32[]{:S(2)}, u32[]{:S(2)}) collective-permute-start(bf16[64,1024]{1,0:T(8,128)(2,1)} %here.1), channel_id=1, source_target_pairs={{0,384},{16,400},{32,416},{48,432},{64,448},{80,464},{96,480},{112... | collective-permute-start | bytes 393224 | tf_op jit(solution)/shard_map/ppermute | solution.py:13
  10.1 1.0 copy.6
  11.2 0.7 convert_bitcast_fusion
  11.8 0.1 broadcast_bitcast_fusion
  11.9 0.1 multiply_bitcast_fusion
  12.0 2.9 %collective-permute-done.below = bf16[64,1024]{1,0:T(8,128)(2,1)S(1)} collective-permute-done((bf16[64,1024]{1,0:T(8,128)(2,1)}, bf16[64,1024]{1,0:T(8,128)(2,1)S(1)}, u32[]{:S(2)}, u32[]{:S(2)}) %collective-permute-start) | collective-permute-done | bytes 131104 | tf_op jit(solution)/shard_map/ppermute | solution.py:13
  14.9 0.0 copy-start.2
  14.9 10.9 %collective-permute-done.1.above = bf16[64,1024]{1,0:T(8,128)(2,1)S(1)} collective-permute-done((bf16[64,1024]{1,0:T(8,128)(2,1)}, bf16[64,1024]{1,0:T(8,128)(2,1)S(1)}, u32[]{:S(2)}, u32[]{:S(2)}) %collective-permute-start.1) | collective-permute-done | bytes 131104 | tf_op jit(solution)/shard_map/ppermute | solution.py:13
  25.8 0.0 copy-start.3
  25.8 0.7 copy.10
  26.5 12.4 %all-to-all-start = ((bf16[32,4,4,128]{3,2,1,0:T(4,128)(2,1)}), bf16[32,4,4,128]{3,2,1,0:T(4,128)(2,1)S(1)}, u32[]{:S(2)}, u32[]{:S(2)}) async-start(bf16[32,4,4,128]{3,2,1,0:T(4,128)(2,1)} %bitcast.23), calls=%async_computation | async-start | bytes 262144 | tf_op jit(solution)/shard_map/all_to_all | solution.py:134
  39.0 6.4 %collective-permute-start.2 = (bf16[64,1024]{1,0:T(8,128)(2,1)S(1)}, bf16[64,1024]{1,0:T(8,128)(2,1)S(1)}, u32[]{:S(2)}, u32[]{:S(2)}) collective-permute-start(bf16[64,1024]{1,0:T(8,128)(2,1)S(1)} %broadcast_select_fusion), channel_id=1, source_target_pairs={{0,128},{1,385},{2,130},{3,387},{4,132},{5,389},{6,134},{7,391},{8... | collective-permute-start | bytes 393224 | tf_op jit(solution)/shard_map/ppermute | solution.py:127
  45.4 0.7 stack.50.place
  46.1 0.0 copy-start.1
  46.1 7.8 %collective-permute-done.2.far = bf16[64,1024]{1,0:T(8,128)(2,1)S(1)} collective-permute-done((bf16[64,1024]{1,0:T(8,128)(2,1)S(1)}, bf16[64,1024]{1,0:T(8,128)(2,1)S(1)}, u32[]{:S(2)}, u32[]{:S(2)}) %collective-permute-start.2) | collective-permute-done | bytes 131104 | tf_op jit(solution)/shard_map/ppermute | solution.py:127
  53.9 0.0 copy-done.2
  53.9 0.0 copy-done.3
  53.9 0.0 copy-start.4
  53.9 0.7 copy-done.4
  54.5 1.9 %shard_map.37.refs_8_ = bf16[4,64,1024]{2,1,0:T(8,128)(2,1)} custom-call(s32[5]{0:T(128)} %stack.50.place, bf16[64,1024]{1,0:T(8,128)(2,1)} %here.1, bf16[64,1024]{1,0:T(8,128)(2,1)} %copy-done.2, bf16[64,1024]{1,0:T(8,128)(2,1)} %copy-done.3, bf16[64,1024]{1,0:T(8,128)(2,1)} %copy-done.4), custom_call_target="tpu_custom_call" | custom-call | tf_op jit(solution)/shard_map/pallas_call | solution.py:72
  56.5 0.0 copy-start
  56.5 0.0 all-to-all-done
  56.6 4.2 %collective-permute-start.3 = (bf16[2,512,128]{2,1,0:T(8,128)(2,1)S(1)}, bf16[2,512,128]{2,1,0:T(8,128)(2,1)S(1)}, u32[]{:S(2)}, u32[]{:S(2)}) collective-permute-start(bf16[2,512,128]{2,1,0:T(8,128)(2,1)S(1)} %get-tuple-element.26), channel_id=1, source_target_pairs={{0,8},{1,9},{2,10},{3,11},{4,12},{5,13},{6,14},{7,15},{8,0},{9,1},... | collective-permute-start | bytes 786440 | tf_op jit(solution)/shard_map/ppermute | solution.py:31
  60.7 2.9 %collective-permute-start.6 = (bf16[4,64,1024]{2,1,0:T(8,128)(2,1)}, bf16[4,64,1024]{2,1,0:T(8,128)(2,1)S(1)}, u32[]{:S(2)}, u32[]{:S(2)}) collective-permute-start(bf16[4,64,1024]{2,1,0:T(8,128)(2,1)} %shard_map.37.refs_8_), channel_id=1, source_target_pairs={{0,16},{16,0},{32,48},{48,32},{64,80},{80,64},{96,112},{112,96},{1... | collective-permute-start | bytes 1572872 | tf_op jit(solution)/shard_map/ppermute | solution.py:22
  63.7 4.5 %collective-permute-start.7 = (bf16[4,64,1024]{2,1,0:T(8,128)(2,1)}, bf16[4,64,1024]{2,1,0:T(8,128)(2,1)S(1)}, u32[]{:S(2)}, u32[]{:S(2)}) collective-permute-start(bf16[4,64,1024]{2,1,0:T(8,128)(2,1)} %shard_map.37.refs_8_), channel_id=1, source_target_pairs={{0,64},{1,449},{2,66},{3,451},{4,68},{5,453},{6,70},{7,455},{8,72}... | collective-permute-start | bytes 1572872 | tf_op jit(solution)/shard_map/ppermute | solution.py:144
  68.2 1.1 collective-permute-done.3
  69.3 0.1 pad_maximum_fusion.1.refs_0_
  69.3 2.1 %collective-permute-start.4 = (bf16[2,2,512,128]{3,2,1,0:T(8,128)(2,1)S(1)}, bf16[2,2,512,128]{3,2,1,0:T(8,128)(2,1)S(1)}, u32[]{:S(2)}, u32[]{:S(2)}) collective-permute-start(bf16[2,2,512,128]{3,2,1,0:T(8,128)(2,1)S(1)} %pad_maximum_fusion.1.refs_0_), channel_id=1, source_target_pairs={{0,2},{1,3},{2,4},{3,5},{4,6},{5,7},{6,0},{7,1},{8,10},{9,11},{10,... | collective-permute-start | bytes 1572872 | tf_op jit(solution)/shard_map/ppermute | solution.py:31
  71.5 3.7 %collective-permute-start.5 = (bf16[2,2,512,128]{3,2,1,0:T(8,128)(2,1)S(1)}, bf16[2,2,512,128]{3,2,1,0:T(8,128)(2,1)S(1)}, u32[]{:S(2)}, u32[]{:S(2)}) collective-permute-start(bf16[2,2,512,128]{3,2,1,0:T(8,128)(2,1)S(1)} %pad_maximum_fusion.1.refs_0_), channel_id=1, source_target_pairs={{0,6},{1,7},{2,0},{3,1},{4,2},{5,3},{6,4},{7,5},{8,14},{9,15},{10,... | collective-permute-start | bytes 1572872 | tf_op jit(solution)/shard_map/ppermute | solution.py:31
  75.2 1.9 %collective-permute-start.9 = (bf16[2,2,512,128]{3,2,1,0:T(8,128)(2,1)S(1)}, bf16[2,2,512,128]{3,2,1,0:T(8,128)(2,1)S(1)}, u32[]{:S(2)}, u32[]{:S(2)}) collective-permute-start(bf16[2,2,512,128]{3,2,1,0:T(8,128)(2,1)S(1)} %pad_maximum_fusion.1.refs_0_), channel_id=1, source_target_pairs={{0,1},{1,0},{2,3},{3,2},{4,5},{5,4},{6,7},{7,6},{8,9},{9,8},{10,11... | collective-permute-start | bytes 1572872 | tf_op jit(solution)/shard_map/ppermute | solution.py:26
  77.1 2.2 %collective-permute-done.6.refs_9_ = bf16[4,64,1024]{2,1,0:T(8,128)(2,1)S(1)} collective-permute-done((bf16[4,64,1024]{2,1,0:T(8,128)(2,1)}, bf16[4,64,1024]{2,1,0:T(8,128)(2,1)S(1)}, u32[]{:S(2)}, u32[]{:S(2)}) %collective-permute-start.6) | collective-permute-done | bytes 524320 | tf_op jit(solution)/shard_map/ppermute | solution.py:22
  79.3 1.2 collective-permute-done.7.refs_10_
  80.5 3.1 %collective-permute-start.8 = (bf16[2,2,512,128]{3,2,1,0:T(8,128)(2,1)S(1)}, bf16[2,2,512,128]{3,2,1,0:T(8,128)(2,1)S(1)}, u32[]{:S(2)}, u32[]{:S(2)}) collective-permute-start(bf16[2,2,512,128]{3,2,1,0:T(8,128)(2,1)S(1)} %pad_maximum_fusion.1.refs_0_), channel_id=1, source_target_pairs={{0,4},{1,5},{2,6},{3,7},{4,0},{5,1},{6,2},{7,3},{8,12},{9,13},{10,... | collective-permute-start | bytes 1572872 | tf_op jit(solution)/shard_map/ppermute | solution.py:31
  83.6 4.1 %collective-permute-start.13 = (bf16[4,64,1024]{2,1,0:T(8,128)(2,1)S(1)}, bf16[4,64,1024]{2,1,0:T(8,128)(2,1)S(1)}, u32[]{:S(2)}, u32[]{:S(2)}) collective-permute-start(bf16[4,64,1024]{2,1,0:T(8,128)(2,1)S(1)} %collective-permute-done.7.refs_10_), channel_id=1, source_target_pairs={{0,16},{16,0},{32,48},{48,32},{64,80},{80,64},{96,112},{112,96},{1... | collective-permute-start | bytes 1572872 | tf_op jit(solution)/shard_map/ppermute | solution.py:22
  87.8 1.1 pad_maximum_fusion
  88.9 0.0 collective-permute-done.4.refs_1_
  88.9 2.3 %collective-permute-start.14 = (bf16[2,4,64,1024]{3,2,1,0:T(8,128)(2,1)S(1)}, bf16[2,4,64,1024]{3,2,1,0:T(8,128)(2,1)S(1)}, u32[]{:S(2)}, u32[]{:S(2)}) collective-permute-start(bf16[2,4,64,1024]{3,2,1,0:T(8,128)(2,1)S(1)} %pad_maximum_fusion), channel_id=1, source_target_pairs={{0,480},{16,496},{32,0},{48,16},{64,32},{80,48},{96,64},{112,80},{... | collective-permute-start | bytes 3145736 | tf_op jit(solution)/shard_map/ppermute | solution.py:13
  91.2 6.6 %collective-permute-done.5.refs_2_ = bf16[2,2,512,128]{3,2,1,0:T(8,128)(2,1)S(1)} collective-permute-done((bf16[2,2,512,128]{3,2,1,0:T(8,128)(2,1)S(1)}, bf16[2,2,512,128]{3,2,1,0:T(8,128)(2,1)S(1)}, u32[]{:S(2)}, u32[]{:S(2)}) %collective-permute-start.5) | collective-permute-done | bytes 524320 | tf_op jit(solution)/shard_map/ppermute | solution.py:31
  97.8 2.6 %collective-permute-start.15 = (bf16[2,4,64,1024]{3,2,1,0:T(8,128)(2,1)S(1)}, bf16[2,4,64,1024]{3,2,1,0:T(8,128)(2,1)S(1)}, u32[]{:S(2)}, u32[]{:S(2)}) collective-permute-start(bf16[2,4,64,1024]{3,2,1,0:T(8,128)(2,1)S(1)} %pad_maximum_fusion), channel_id=1, source_target_pairs={{0,32},{16,48},{32,64},{48,80},{64,96},{80,112},{96,128},{112,144}... | collective-permute-start | bytes 3145736 | tf_op jit(solution)/shard_map/ppermute | solution.py:13
  100.4 0.0 collective-permute-done.9.refs_4_
  100.4 1.9 %collective-permute-start.10 = (bf16[2,2,512,128]{3,2,1,0:T(8,128)(2,1)S(1)}, bf16[2,2,512,128]{3,2,1,0:T(8,128)(2,1)S(1)}, u32[]{:S(2)}, u32[]{:S(2)}) collective-permute-start(bf16[2,2,512,128]{3,2,1,0:T(8,128)(2,1)S(1)} %collective-permute-done.4.refs_1_), channel_id=1, source_target_pairs={{0,1},{1,0},{2,3},{3,2},{4,5},{5,4},{6,7},{7,6},{8,9},{9,8},{10,11... | collective-permute-start | bytes 1572872 | tf_op jit(solution)/shard_map/ppermute | solution.py:26
  102.3 0.0 collective-permute-done.8.refs_3_
  102.3 2.4 %collective-permute-start.11 = (bf16[2,2,512,128]{3,2,1,0:T(8,128)(2,1)S(1)}, bf16[2,2,512,128]{3,2,1,0:T(8,128)(2,1)S(1)}, u32[]{:S(2)}, u32[]{:S(2)}) collective-permute-start(bf16[2,2,512,128]{3,2,1,0:T(8,128)(2,1)S(1)} %collective-permute-done.5.refs_2_), channel_id=1, source_target_pairs={{0,1},{1,0},{2,3},{3,2},{4,5},{5,4},{6,7},{7,6},{8,9},{9,8},{10,11... | collective-permute-start | bytes 1572872 | tf_op jit(solution)/shard_map/ppermute | solution.py:26
  104.7 0.0 collective-permute-done.13.refs_11_
  104.8 1.9 %collective-permute-start.12 = (bf16[2,2,512,128]{3,2,1,0:T(8,128)(2,1)S(1)}, bf16[2,2,512,128]{3,2,1,0:T(8,128)(2,1)S(1)}, u32[]{:S(2)}, u32[]{:S(2)}) collective-permute-start(bf16[2,2,512,128]{3,2,1,0:T(8,128)(2,1)S(1)} %collective-permute-done.8.refs_3_), channel_id=1, source_target_pairs={{0,1},{1,0},{2,3},{3,2},{4,5},{5,4},{6,7},{7,6},{8,9},{9,8},{10,11... | collective-permute-start | bytes 1572872 | tf_op jit(solution)/shard_map/ppermute | solution.py:26
  106.7 0.0 collective-permute-done.10.refs_5_
  106.7 0.0 collective-permute-done.11.refs_6_
  106.7 1.9 %collective-permute-done.12.refs_7_ = bf16[2,2,512,128]{3,2,1,0:T(8,128)(2,1)S(1)} collective-permute-done((bf16[2,2,512,128]{3,2,1,0:T(8,128)(2,1)S(1)}, bf16[2,2,512,128]{3,2,1,0:T(8,128)(2,1)S(1)}, u32[]{:S(2)}, u32[]{:S(2)}) %collective-permute-start.12) | collective-permute-done | bytes 524320 | tf_op jit(solution)/shard_map/ppermute | solution.py:26
  108.6 0.0 copy-done.1
  108.6 0.0 copy-done
  108.6 4.8 %shard_map.38 = (f32[512,1024]{1,0:T(8,128)S(1)}, bf16[2,2,512,1024]{3,2,1,0:T(8,128)(2,1)S(1)}) custom-call(s32[5]{0:T(128)S(1)} %copy-done.1, bf16[2,2,512,128]{3,2,1,0:T(8,128)(2,1)S(1)} %pad_maximum_fusion.1.refs_0_, bf16[2,2,512,128]{3,2,1,0:T(8,128)(2,1)S(1)} %collective-permute-done.4.refs_1_, ...), custom_call_target="tpu_custom_call" | custom-call | flops 2147483648 | bytes 10485760 | tf_op jit(solution)/shard_map/pallas_call | solution.py:161
  113.4 0.4 collective-permute-done.14.refs_0_
  113.8 11.1 %collective-permute-done.15.refs_1_ = bf16[2,4,64,1024]{3,2,1,0:T(8,128)(2,1)S(1)} collective-permute-done((bf16[2,4,64,1024]{3,2,1,0:T(8,128)(2,1)S(1)}, bf16[2,4,64,1024]{3,2,1,0:T(8,128)(2,1)S(1)}, u32[]{:S(2)}, u32[]{:S(2)}) %collective-permute-start.15) | collective-permute-done | bytes 1048608 | tf_op jit(solution)/shard_map/ppermute | solution.py:13
  124.8 4.5 %shard_map.39 = bf16[512,1024]{1,0:T(8,128)(2,1)} custom-call(s32[5]{0:T(128)S(1)} %copy-done.1, f32[512,1024]{1,0:T(8,128)S(1)} %get-tuple-element.23.total, bf16[2,2,512,1024]{3,2,1,0:T(8,128)(2,1)S(1)} %get-tuple-element.24.kept, bf16[2,4,64,1024]{3,2,1,0:T(8,128)(2,1)S(1)} %collective-permute-done.14.refs_0_, ...), custom_call_target="tpu_custom_call" | custom-call | flops 2147483648 | bytes 10485760 | tf_op jit(solution)/shard_map/pallas_call | solution.py:173
  (3 shorter events, 0.1 us)
Async XLA Ops:
  0.0 14.9 %collective-permute-start = (bf16[64,1024]{1,0:T(8,128)(2,1)}, bf16[64,1024]{1,0:T(8,128)(2,1)S(1)}, u32[]{:S(2)}, u32[]{:S(2)}) collective-permute-start(bf16[64,1024]{1,0:T(8,128)(2,1)} %here.1), channel_id=1, source_target_pairs={{0,128},{16,144},{32,160},{48,176},{64,192},{80,208},{96,224},{112... | collective-permute-start | bytes 393224 | tf_op jit(solution)/shard_map/ppermute | solution.py:13
  8.2 17.6 %collective-permute-start.1 = (bf16[64,1024]{1,0:T(8,128)(2,1)}, bf16[64,1024]{1,0:T(8,128)(2,1)S(1)}, u32[]{:S(2)}, u32[]{:S(2)}) collective-permute-start(bf16[64,1024]{1,0:T(8,128)(2,1)} %here.1), channel_id=1, source_target_pairs={{0,384},{16,400},{32,416},{48,432},{64,448},{80,464},{96,480},{112... | collective-permute-start | bytes 393224 | tf_op jit(solution)/shard_map/ppermute | solution.py:13
  14.9 39.0 %copy-start.2 = (bf16[64,1024]{1,0:T(8,128)(2,1)}, bf16[64,1024]{1,0:T(8,128)(2,1)S(1)}, u32[]{:S(2)}) copy-start(bf16[64,1024]{1,0:T(8,128)(2,1)S(1)} %collective-permute-done.below) | copy-start | bytes 393220
  25.8 28.1 %copy-start.3 = (bf16[64,1024]{1,0:T(8,128)(2,1)}, bf16[64,1024]{1,0:T(8,128)(2,1)S(1)}, u32[]{:S(2)}) copy-start(bf16[64,1024]{1,0:T(8,128)(2,1)S(1)} %collective-permute-done.1.above) | copy-start | bytes 393220
  26.5 29.9 %all-to-all-start = ((bf16[32,4,4,128]{3,2,1,0:T(4,128)(2,1)}), bf16[32,4,4,128]{3,2,1,0:T(4,128)(2,1)S(1)}, u32[]{:S(2)}, u32[]{:S(2)}) async-start(bf16[32,4,4,128]{3,2,1,0:T(4,128)(2,1)} %bitcast.23), calls=%async_computation | async-start | bytes 262144 | tf_op jit(solution)/shard_map/all_to_all | solution.py:134
  39.0 14.9 %collective-permute-start.2 = (bf16[64,1024]{1,0:T(8,128)(2,1)S(1)}, bf16[64,1024]{1,0:T(8,128)(2,1)S(1)}, u32[]{:S(2)}, u32[]{:S(2)}) collective-permute-start(bf16[64,1024]{1,0:T(8,128)(2,1)S(1)} %broadcast_select_fusion), channel_id=1, source_target_pairs={{0,128},{1,385},{2,130},{3,387},{4,132},{5,389},{6,134},{7,391},{8... | collective-permute-start | bytes 393224 | tf_op jit(solution)/shard_map/ppermute | solution.py:127
  46.1 62.5 %copy-start.1 = (s32[5]{0:T(128)S(1)}, s32[5]{0:T(128)}, u32[]{:S(2)}) copy-start(s32[5]{0:T(128)} %stack.50.place) | copy-start | bytes 64
  53.9 0.7 copy-start.4
  56.5 52.1 %copy-start = (bf16[4,64,1024]{2,1,0:T(8,128)(2,1)S(1)}, bf16[4,64,1024]{2,1,0:T(8,128)(2,1)}, u32[]{:S(2)}) copy-start(bf16[4,64,1024]{2,1,0:T(8,128)(2,1)} %shard_map.37.refs_8_) | copy-start | bytes 1572868
  56.6 12.7 %collective-permute-start.3 = (bf16[2,512,128]{2,1,0:T(8,128)(2,1)S(1)}, bf16[2,512,128]{2,1,0:T(8,128)(2,1)S(1)}, u32[]{:S(2)}, u32[]{:S(2)}) collective-permute-start(bf16[2,512,128]{2,1,0:T(8,128)(2,1)S(1)} %get-tuple-element.26), channel_id=1, source_target_pairs={{0,8},{1,9},{2,10},{3,11},{4,12},{5,13},{6,14},{7,15},{8,0},{9,1},... | collective-permute-start | bytes 786440 | tf_op jit(solution)/shard_map/ppermute | solution.py:31
  60.7 18.5 %collective-permute-start.6 = (bf16[4,64,1024]{2,1,0:T(8,128)(2,1)}, bf16[4,64,1024]{2,1,0:T(8,128)(2,1)S(1)}, u32[]{:S(2)}, u32[]{:S(2)}) collective-permute-start(bf16[4,64,1024]{2,1,0:T(8,128)(2,1)} %shard_map.37.refs_8_), channel_id=1, source_target_pairs={{0,16},{16,0},{32,48},{48,32},{64,80},{80,64},{96,112},{112,96},{1... | collective-permute-start | bytes 1572872 | tf_op jit(solution)/shard_map/ppermute | solution.py:22
  63.7 16.8 %collective-permute-start.7 = (bf16[4,64,1024]{2,1,0:T(8,128)(2,1)}, bf16[4,64,1024]{2,1,0:T(8,128)(2,1)S(1)}, u32[]{:S(2)}, u32[]{:S(2)}) collective-permute-start(bf16[4,64,1024]{2,1,0:T(8,128)(2,1)} %shard_map.37.refs_8_), channel_id=1, source_target_pairs={{0,64},{1,449},{2,66},{3,451},{4,68},{5,453},{6,70},{7,455},{8,72}... | collective-permute-start | bytes 1572872 | tf_op jit(solution)/shard_map/ppermute | solution.py:144
  69.3 19.6 %collective-permute-start.4 = (bf16[2,2,512,128]{3,2,1,0:T(8,128)(2,1)S(1)}, bf16[2,2,512,128]{3,2,1,0:T(8,128)(2,1)S(1)}, u32[]{:S(2)}, u32[]{:S(2)}) collective-permute-start(bf16[2,2,512,128]{3,2,1,0:T(8,128)(2,1)S(1)} %pad_maximum_fusion.1.refs_0_), channel_id=1, source_target_pairs={{0,2},{1,3},{2,4},{3,5},{4,6},{5,7},{6,0},{7,1},{8,10},{9,11},{10,... | collective-permute-start | bytes 1572872 | tf_op jit(solution)/shard_map/ppermute | solution.py:31
  71.5 26.3 %collective-permute-start.5 = (bf16[2,2,512,128]{3,2,1,0:T(8,128)(2,1)S(1)}, bf16[2,2,512,128]{3,2,1,0:T(8,128)(2,1)S(1)}, u32[]{:S(2)}, u32[]{:S(2)}) collective-permute-start(bf16[2,2,512,128]{3,2,1,0:T(8,128)(2,1)S(1)} %pad_maximum_fusion.1.refs_0_), channel_id=1, source_target_pairs={{0,6},{1,7},{2,0},{3,1},{4,2},{5,3},{6,4},{7,5},{8,14},{9,15},{10,... | collective-permute-start | bytes 1572872 | tf_op jit(solution)/shard_map/ppermute | solution.py:31
  75.2 25.2 %collective-permute-start.9 = (bf16[2,2,512,128]{3,2,1,0:T(8,128)(2,1)S(1)}, bf16[2,2,512,128]{3,2,1,0:T(8,128)(2,1)S(1)}, u32[]{:S(2)}, u32[]{:S(2)}) collective-permute-start(bf16[2,2,512,128]{3,2,1,0:T(8,128)(2,1)S(1)} %pad_maximum_fusion.1.refs_0_), channel_id=1, source_target_pairs={{0,1},{1,0},{2,3},{3,2},{4,5},{5,4},{6,7},{7,6},{8,9},{9,8},{10,11... | collective-permute-start | bytes 1572872 | tf_op jit(solution)/shard_map/ppermute | solution.py:26
  80.5 21.8 %collective-permute-start.8 = (bf16[2,2,512,128]{3,2,1,0:T(8,128)(2,1)S(1)}, bf16[2,2,512,128]{3,2,1,0:T(8,128)(2,1)S(1)}, u32[]{:S(2)}, u32[]{:S(2)}) collective-permute-start(bf16[2,2,512,128]{3,2,1,0:T(8,128)(2,1)S(1)} %pad_maximum_fusion.1.refs_0_), channel_id=1, source_target_pairs={{0,4},{1,5},{2,6},{3,7},{4,0},{5,1},{6,2},{7,3},{8,12},{9,13},{10,... | collective-permute-start | bytes 1572872 | tf_op jit(solution)/shard_map/ppermute | solution.py:31
  83.6 21.1 %collective-permute-start.13 = (bf16[4,64,1024]{2,1,0:T(8,128)(2,1)S(1)}, bf16[4,64,1024]{2,1,0:T(8,128)(2,1)S(1)}, u32[]{:S(2)}, u32[]{:S(2)}) collective-permute-start(bf16[4,64,1024]{2,1,0:T(8,128)(2,1)S(1)} %collective-permute-done.7.refs_10_), channel_id=1, source_target_pairs={{0,16},{16,0},{32,48},{48,32},{64,80},{80,64},{96,112},{112,96},{1... | collective-permute-start | bytes 1572872 | tf_op jit(solution)/shard_map/ppermute | solution.py:22
  88.9 24.8 %collective-permute-start.14 = (bf16[2,4,64,1024]{3,2,1,0:T(8,128)(2,1)S(1)}, bf16[2,4,64,1024]{3,2,1,0:T(8,128)(2,1)S(1)}, u32[]{:S(2)}, u32[]{:S(2)}) collective-permute-start(bf16[2,4,64,1024]{3,2,1,0:T(8,128)(2,1)S(1)} %pad_maximum_fusion), channel_id=1, source_target_pairs={{0,480},{16,496},{32,0},{48,16},{64,32},{80,48},{96,64},{112,80},{... | collective-permute-start | bytes 3145736 | tf_op jit(solution)/shard_map/ppermute | solution.py:13
  97.8 27.0 %collective-permute-start.15 = (bf16[2,4,64,1024]{3,2,1,0:T(8,128)(2,1)S(1)}, bf16[2,4,64,1024]{3,2,1,0:T(8,128)(2,1)S(1)}, u32[]{:S(2)}, u32[]{:S(2)}) collective-permute-start(bf16[2,4,64,1024]{3,2,1,0:T(8,128)(2,1)S(1)} %pad_maximum_fusion), channel_id=1, source_target_pairs={{0,32},{16,48},{32,64},{48,80},{64,96},{80,112},{96,128},{112,144}... | collective-permute-start | bytes 3145736 | tf_op jit(solution)/shard_map/ppermute | solution.py:13
  100.4 6.3 %collective-permute-start.10 = (bf16[2,2,512,128]{3,2,1,0:T(8,128)(2,1)S(1)}, bf16[2,2,512,128]{3,2,1,0:T(8,128)(2,1)S(1)}, u32[]{:S(2)}, u32[]{:S(2)}) collective-permute-start(bf16[2,2,512,128]{3,2,1,0:T(8,128)(2,1)S(1)} %collective-permute-done.4.refs_1_), channel_id=1, source_target_pairs={{0,1},{1,0},{2,3},{3,2},{4,5},{5,4},{6,7},{7,6},{8,9},{9,8},{10,11... | collective-permute-start | bytes 1572872 | tf_op jit(solution)/shard_map/ppermute | solution.py:26
  102.3 4.4 %collective-permute-start.11 = (bf16[2,2,512,128]{3,2,1,0:T(8,128)(2,1)S(1)}, bf16[2,2,512,128]{3,2,1,0:T(8,128)(2,1)S(1)}, u32[]{:S(2)}, u32[]{:S(2)}) collective-permute-start(bf16[2,2,512,128]{3,2,1,0:T(8,128)(2,1)S(1)} %collective-permute-done.5.refs_2_), channel_id=1, source_target_pairs={{0,1},{1,0},{2,3},{3,2},{4,5},{5,4},{6,7},{7,6},{8,9},{9,8},{10,11... | collective-permute-start | bytes 1572872 | tf_op jit(solution)/shard_map/ppermute | solution.py:26
  104.8 3.8 %collective-permute-start.12 = (bf16[2,2,512,128]{3,2,1,0:T(8,128)(2,1)S(1)}, bf16[2,2,512,128]{3,2,1,0:T(8,128)(2,1)S(1)}, u32[]{:S(2)}, u32[]{:S(2)}) collective-permute-start(bf16[2,2,512,128]{3,2,1,0:T(8,128)(2,1)S(1)} %collective-permute-done.8.refs_3_), channel_id=1, source_target_pairs={{0,1},{1,0},{2,3},{3,2},{4,5},{5,4},{6,7},{7,6},{8,9},{9,8},{10,11... | collective-permute-start | bytes 1572872 | tf_op jit(solution)/shard_map/ppermute | solution.py:26

commit v11 on v10

--- a/solution.py
+++ b/solution.py
@@ -129,12 +129,11 @@
     scale = jnp.repeat(tile_mask.astype(jnp.bfloat16).reshape(-1), pairs // OI)
     masked = (amplitudes * scale[None, :]).T
 
-    masked, up4, down4 = lax.optimization_barrier((masked, up4, down4))
     sent = masked.reshape(OI, 32, OI, depth).transpose(1, 2, 0, 3)
     got = lax.all_to_all(sent, "row", split_axis=0, concat_axis=0, tiled=True)
     swapped = got.transpose(1, 0, 2, 3).reshape(pairs, depth)
+    swapped, up4, down4 = lax.optimization_barrier((swapped, up4, down4))
     block = gather_four(place, integrals, up4, down4, far)
-    swapped, block = lax.optimization_barrier((swapped, block))
 
     both = jnp.stack([masked, swapped])
     pair = jnp.stack([both, chip_shift(both, (1, 0))])
@@ -142,7 +141,6 @@
 
     partner = x_swap(block)
     two = lax.ppermute(block, ("row", "col"), split_shift(2))
-    pair, partner, two = lax.optimization_barrier((pair, partner, two))
     mine.append(chip_shift(pair, (0, 2)))
     theirs = [core_swap(m) for m in mine]
     near = jnp.stack([block, partner])

time: 130 us -> 123 us (0.946)
  the two profiles are of different devices: /device:TPU:186 before, /device:TPU:2 now
where the time goes in v11:
time: 123 us
  starting transfers between devices  70.7 us (57%)
  waiting for transfers between devices  33.8 us (27%)
  Pallas kernels  11.3 us (9%)
  local copies, waits for them, and re-layouts  4.18 us (3%)
  other arithmetic  2.17 us (2%)
    all_to_all x1, starting transfers between devices, on_device(): got = lax.all_to_all(sent, 'row', split_axis=0, concat_axis=0, tiled=True)  16.7 us
    ppermute x4, waiting for transfers between devices, z_shift(): return lax.ppermute(x, 'row', [(r, (r + 2 * d) % 32) for r in range(32)])  15.8 us
    ppermute x4, starting transfers between devices, z_shift(): return lax.ppermute(x, 'row', [(r, (r + 2 * d) % 32) for r in range(32)])  15.7 us
    ppermute x4, starting transfers between devices, chip_shift(): lax.ppermute(x, 'col', [(c, (c // 8 ^ dx) * 8 + (c // 2 % 4 + dy) % 4 * 2...  15 us
    all_to_all x1, waiting for transfers between devices, on_device(): got = lax.all_to_all(sent, 'row', split_axis=0, concat_axis=0, tiled=True)  8.6 us
    ppermute x4, starting transfers between devices, core_swap(): return lax.ppermute(x, 'col', [(c, c ^ 1) for c in range(16)])  8.14 us
    ppermute x1, starting transfers between devices, on_device(): lax.ppermute(jnp.where(core == 0, up4, down4), ('row', 'col'), split_shif...  6.99 us
    ppermute x2, starting transfers between devices, x_swap(): return lax.ppermute(x, 'row', [(r, r ^ 1) for r in range(32)])  6.26 us
  transfers between devices with their start and end apart: 17, of which 9 were waited for; matrix products, arithmetic and copies ran while one was open for 2% of the time, Pallas kernels for 6%

profile of v11, /device:TPU:2, one launch (start us, length us, event | category | flops | bytes accessed | tf_op | source)
XLA Modules:
  0.0 122.6 jit_solution(10984750037113222709)
XLA Ops:
  0.0 1.0 copy.6
  1.0 0.7 convert_bitcast_fusion
  1.7 0.1 broadcast_bitcast_fusion
  1.8 0.1 broadcast_multiply_fusion
  1.9 0.8 copy.10
  2.7 16.7 %all-to-all-start = ((bf16[32,4,4,128]{3,2,1,0:T(4,128)(2,1)}), bf16[32,4,4,128]{3,2,1,0:T(4,128)(2,1)S(1)}, u32[]{:S(2)}, u32[]{:S(2)}) async-start(bf16[32,4,4,128]{3,2,1,0:T(4,128)(2,1)} %bitcast.25), calls=%async_computation | async-start | bytes 262144 | tf_op jit(solution)/shard_map/all_to_all | solution.py:133
  19.4 7.3 %collective-permute-start = (bf16[64,1024]{1,0:T(8,128)(2,1)}, bf16[64,1024]{1,0:T(8,128)(2,1)S(1)}, u32[]{:S(2)}, u32[]{:S(2)}) collective-permute-start(bf16[64,1024]{1,0:T(8,128)(2,1)} %here.1), channel_id=1, source_target_pairs={{0,128},{16,144},{32,160},{48,176},{64,192},{80,208},{96,224},{112... | collective-permute-start | bytes 393224 | tf_op jit(solution)/shard_map/ppermute | solution.py:13
  26.7 2.5 %collective-permute-start.1 = (bf16[64,1024]{1,0:T(8,128)(2,1)}, bf16[64,1024]{1,0:T(8,128)(2,1)S(1)}, u32[]{:S(2)}, u32[]{:S(2)}) collective-permute-start(bf16[64,1024]{1,0:T(8,128)(2,1)} %here.1), channel_id=1, source_target_pairs={{0,384},{16,400},{32,416},{48,432},{64,448},{80,464},{96,480},{112... | collective-permute-start | bytes 393224 | tf_op jit(solution)/shard_map/ppermute | solution.py:13
  29.2 0.1 fusion.1
  29.3 8.6 %all-to-all-done = bf16[32,4,4,128]{3,2,1,0:T(4,128)(2,1)S(1)} async-done(((bf16[32,4,4,128]{3,2,1,0:T(4,128)(2,1)}), bf16[32,4,4,128]{3,2,1,0:T(4,128)(2,1)S(1)}, u32[]{:S(2)}, u32[]{:S(2)}) %all-to-all-start) | async-done | bytes 131104 | tf_op jit(solution)/shard_map/all_to_all | solution.py:133
  38.0 1.5 %collective-permute-done.below = bf16[64,1024]{1,0:T(8,128)(2,1)S(1)} collective-permute-done((bf16[64,1024]{1,0:T(8,128)(2,1)}, bf16[64,1024]{1,0:T(8,128)(2,1)S(1)}, u32[]{:S(2)}, u32[]{:S(2)}) %collective-permute-start) | collective-permute-done | bytes 131104 | tf_op jit(solution)/shard_map/ppermute | solution.py:13
  39.5 0.0 copy-start.2
  39.5 6.3 %collective-permute-done.1.above = bf16[64,1024]{1,0:T(8,128)(2,1)S(1)} collective-permute-done((bf16[64,1024]{1,0:T(8,128)(2,1)}, bf16[64,1024]{1,0:T(8,128)(2,1)S(1)}, u32[]{:S(2)}, u32[]{:S(2)}) %collective-permute-start.1) | collective-permute-done | bytes 131104 | tf_op jit(solution)/shard_map/ppermute | solution.py:13
  45.8 0.0 copy-start.3
  45.8 4.0 %collective-permute-start.2 = (bf16[2,512,128]{2,1,0:T(8,128)(2,1)S(1)}, bf16[2,512,128]{2,1,0:T(8,128)(2,1)S(1)}, u32[]{:S(2)}, u32[]{:S(2)}) collective-permute-start(bf16[2,512,128]{2,1,0:T(8,128)(2,1)S(1)} %get-tuple-element.16), channel_id=1, source_target_pairs={{0,8},{1,9},{2,10},{3,11},{4,12},{5,13},{6,14},{7,15},{8,0},{9,1},... | collective-permute-start | bytes 786440 | tf_op jit(solution)/shard_map/ppermute | solution.py:31
  49.9 7.0 %collective-permute-start.10 = (bf16[64,1024]{1,0:T(8,128)(2,1)S(1)}, bf16[64,1024]{1,0:T(8,128)(2,1)S(1)}, u32[]{:S(2)}, u32[]{:S(2)}) collective-permute-start(bf16[64,1024]{1,0:T(8,128)(2,1)S(1)} %broadcast_select_fusion), channel_id=1, source_target_pairs={{0,128},{1,385},{2,130},{3,387},{4,132},{5,389},{6,134},{7,391},{8... | collective-permute-start | bytes 393224 | tf_op jit(solution)/shard_map/ppermute | solution.py:127
  57.0 0.6 stack.50.place
  57.5 0.0 copy-start.1
  57.5 3.8 %collective-permute-done.10.far = bf16[64,1024]{1,0:T(8,128)(2,1)S(1)} collective-permute-done((bf16[64,1024]{1,0:T(8,128)(2,1)S(1)}, bf16[64,1024]{1,0:T(8,128)(2,1)S(1)}, u32[]{:S(2)}, u32[]{:S(2)}) %collective-permute-start.10) | collective-permute-done | bytes 131104 | tf_op jit(solution)/shard_map/ppermute | solution.py:127
  61.3 0.0 copy-done.2
  61.3 0.0 copy-done.3
  61.3 0.0 copy-start.4
  61.3 0.7 copy-done.4
  61.9 1.9 %shard_map.37.refs_8_ = bf16[4,64,1024]{2,1,0:T(8,128)(2,1)} custom-call(s32[5]{0:T(128)} %stack.50.place, bf16[64,1024]{1,0:T(8,128)(2,1)} %here.1, bf16[64,1024]{1,0:T(8,128)(2,1)} %copy-done.2, bf16[64,1024]{1,0:T(8,128)(2,1)} %copy-done.3, bf16[64,1024]{1,0:T(8,128)(2,1)} %copy-done.4), custom_call_target="tpu_custom_call" | custom-call | tf_op jit(solution)/shard_map/pallas_call | solution.py:72
  63.9 1.9 %collective-permute-start.12 = (bf16[4,64,1024]{2,1,0:T(8,128)(2,1)}, bf16[4,64,1024]{2,1,0:T(8,128)(2,1)S(1)}, u32[]{:S(2)}, u32[]{:S(2)}) collective-permute-start(bf16[4,64,1024]{2,1,0:T(8,128)(2,1)} %shard_map.37.refs_8_), channel_id=1, source_target_pairs={{0,64},{1,449},{2,66},{3,451},{4,68},{5,453},{6,70},{7,455},{8,72}... | collective-permute-start | bytes 1572872 | tf_op jit(solution)/shard_map/ppermute | solution.py:143
  65.8 3.1 %collective-permute-start.11 = (bf16[4,64,1024]{2,1,0:T(8,128)(2,1)}, bf16[4,64,1024]{2,1,0:T(8,128)(2,1)S(1)}, u32[]{:S(2)}, u32[]{:S(2)}) collective-permute-start(bf16[4,64,1024]{2,1,0:T(8,128)(2,1)} %shard_map.37.refs_8_), channel_id=1, source_target_pairs={{0,16},{16,0},{32,48},{48,32},{64,80},{80,64},{96,112},{112,96},{1... | collective-permute-start | bytes 1572872 | tf_op jit(solution)/shard_map/ppermute | solution.py:22
  68.9 0.0 collective-permute-done.2
  68.9 0.1 pad_maximum_fusion.1.refs_0_
  69.0 3.5 %collective-permute-start.3 = (bf16[2,2,512,128]{3,2,1,0:T(8,128)(2,1)S(1)}, bf16[2,2,512,128]{3,2,1,0:T(8,128)(2,1)S(1)}, u32[]{:S(2)}, u32[]{:S(2)}) collective-permute-start(bf16[2,2,512,128]{3,2,1,0:T(8,128)(2,1)S(1)} %pad_maximum_fusion.1.refs_0_), channel_id=1, source_target_pairs={{0,2},{1,3},{2,4},{3,5},{4,6},{5,7},{6,0},{7,1},{8,10},{9,11},{10,... | collective-permute-start | bytes 1572872 | tf_op jit(solution)/shard_map/ppermute | solution.py:31
  72.5 3.6 %collective-permute-start.4 = (bf16[2,2,512,128]{3,2,1,0:T(8,128)(2,1)S(1)}, bf16[2,2,512,128]{3,2,1,0:T(8,128)(2,1)S(1)}, u32[]{:S(2)}, u32[]{:S(2)}) collective-permute-start(bf16[2,2,512,128]{3,2,1,0:T(8,128)(2,1)S(1)} %pad_maximum_fusion.1.refs_0_), channel_id=1, source_target_pairs={{0,6},{1,7},{2,0},{3,1},{4,2},{5,3},{6,4},{7,5},{8,14},{9,15},{10,... | collective-permute-start | bytes 1572872 | tf_op jit(solution)/shard_map/ppermute | solution.py:31
  76.1 3.9 %collective-permute-start.5 = (bf16[2,2,512,128]{3,2,1,0:T(8,128)(2,1)S(1)}, bf16[2,2,512,128]{3,2,1,0:T(8,128)(2,1)S(1)}, u32[]{:S(2)}, u32[]{:S(2)}) collective-permute-start(bf16[2,2,512,128]{3,2,1,0:T(8,128)(2,1)S(1)} %pad_maximum_fusion.1.refs_0_), channel_id=1, source_target_pairs={{0,4},{1,5},{2,6},{3,7},{4,0},{5,1},{6,2},{7,3},{8,12},{9,13},{10,... | collective-permute-start | bytes 1572872 | tf_op jit(solution)/shard_map/ppermute | solution.py:31
  80.0 0.5 collective-permute-done.12.refs_10_
  80.4 1.9 %collective-permute-start.6 = (bf16[2,2,512,128]{3,2,1,0:T(8,128)(2,1)S(1)}, bf16[2,2,512,128]{3,2,1,0:T(8,128)(2,1)S(1)}, u32[]{:S(2)}, u32[]{:S(2)}) collective-permute-start(bf16[2,2,512,128]{3,2,1,0:T(8,128)(2,1)S(1)} %pad_maximum_fusion.1.refs_0_), channel_id=1, source_target_pairs={{0,1},{1,0},{2,3},{3,2},{4,5},{5,4},{6,7},{7,6},{8,9},{9,8},{10,11... | collective-permute-start | bytes 1572872 | tf_op jit(solution)/shard_map/ppermute | solution.py:26
  82.4 0.0 collective-permute-done.11.refs_9_
  82.4 3.1 %collective-permute-start.13 = (bf16[4,64,1024]{2,1,0:T(8,128)(2,1)S(1)}, bf16[4,64,1024]{2,1,0:T(8,128)(2,1)S(1)}, u32[]{:S(2)}, u32[]{:S(2)}) collective-permute-start(bf16[4,64,1024]{2,1,0:T(8,128)(2,1)S(1)} %collective-permute-done.12.refs_10_), channel_id=1, source_target_pairs={{0,16},{16,0},{32,48},{48,32},{64,80},{80,64},{96,112},{112,96},{1... | collective-permute-start | bytes 1572872 | tf_op jit(solution)/shard_map/ppermute | solution.py:22
  85.5 1.1 pad_maximum_fusion
  86.6 0.0 collective-permute-done.3.refs_1_
  86.7 3.3 %collective-permute-start.14 = (bf16[2,4,64,1024]{3,2,1,0:T(8,128)(2,1)S(1)}, bf16[2,4,64,1024]{3,2,1,0:T(8,128)(2,1)S(1)}, u32[]{:S(2)}, u32[]{:S(2)}) collective-permute-start(bf16[2,4,64,1024]{3,2,1,0:T(8,128)(2,1)S(1)} %pad_maximum_fusion), channel_id=1, source_target_pairs={{0,480},{16,496},{32,0},{48,16},{64,32},{80,48},{96,64},{112,80},{... | collective-permute-start | bytes 3145736 | tf_op jit(solution)/shard_map/ppermute | solution.py:13
  89.9 0.0 collective-permute-done.4.refs_2_
  89.9 2.7 %collective-permute-start.15 = (bf16[2,4,64,1024]{3,2,1,0:T(8,128)(2,1)S(1)}, bf16[2,4,64,1024]{3,2,1,0:T(8,128)(2,1)S(1)}, u32[]{:S(2)}, u32[]{:S(2)}) collective-permute-start(bf16[2,4,64,1024]{3,2,1,0:T(8,128)(2,1)S(1)} %pad_maximum_fusion), channel_id=1, source_target_pairs={{0,32},{16,48},{32,64},{48,80},{64,96},{80,112},{96,128},{112,144}... | collective-permute-start | bytes 3145736 | tf_op jit(solution)/shard_map/ppermute | solution.py:13
  92.7 3.3 %collective-permute-done.5.refs_3_ = bf16[2,2,512,128]{3,2,1,0:T(8,128)(2,1)S(1)} collective-permute-done((bf16[2,2,512,128]{3,2,1,0:T(8,128)(2,1)S(1)}, bf16[2,2,512,128]{3,2,1,0:T(8,128)(2,1)S(1)}, u32[]{:S(2)}, u32[]{:S(2)}) %collective-permute-start.5) | collective-permute-done | bytes 524320 | tf_op jit(solution)/shard_map/ppermute | solution.py:31
  96.0 1.9 %collective-permute-start.7 = (bf16[2,2,512,128]{3,2,1,0:T(8,128)(2,1)S(1)}, bf16[2,2,512,128]{3,2,1,0:T(8,128)(2,1)S(1)}, u32[]{:S(2)}, u32[]{:S(2)}) collective-permute-start(bf16[2,2,512,128]{3,2,1,0:T(8,128)(2,1)S(1)} %collective-permute-done.3.refs_1_), channel_id=1, source_target_pairs={{0,1},{1,0},{2,3},{3,2},{4,5},{5,4},{6,7},{7,6},{8,9},{9,8},{10,11... | collective-permute-start | bytes 1572872 | tf_op jit(solution)/shard_map/ppermute | solution.py:26
  97.9 0.0 collective-permute-done.6.refs_4_
  97.9 2.4 %collective-permute-start.8 = (bf16[2,2,512,128]{3,2,1,0:T(8,128)(2,1)S(1)}, bf16[2,2,512,128]{3,2,1,0:T(8,128)(2,1)S(1)}, u32[]{:S(2)}, u32[]{:S(2)}) collective-permute-start(bf16[2,2,512,128]{3,2,1,0:T(8,128)(2,1)S(1)} %collective-permute-done.4.refs_2_), channel_id=1, source_target_pairs={{0,1},{1,0},{2,3},{3,2},{4,5},{5,4},{6,7},{7,6},{8,9},{9,8},{10,11... | collective-permute-start | bytes 1572872 | tf_op jit(solution)/shard_map/ppermute | solution.py:26
  100.3 0.0 collective-permute-done.13.refs_11_
  100.3 1.9 %collective-permute-start.9 = (bf16[2,2,512,128]{3,2,1,0:T(8,128)(2,1)S(1)}, bf16[2,2,512,128]{3,2,1,0:T(8,128)(2,1)S(1)}, u32[]{:S(2)}, u32[]{:S(2)}) collective-permute-start(bf16[2,2,512,128]{3,2,1,0:T(8,128)(2,1)S(1)} %collective-permute-done.5.refs_3_), channel_id=1, source_target_pairs={{0,1},{1,0},{2,3},{3,2},{4,5},{5,4},{6,7},{7,6},{8,9},{9,8},{10,11... | collective-permute-start | bytes 1572872 | tf_op jit(solution)/shard_map/ppermute | solution.py:26
  102.2 0.0 collective-permute-done.7.refs_5_
  102.3 0.0 collective-permute-done.8.refs_6_
  102.3 1.9 %collective-permute-done.9.refs_7_ = bf16[2,2,512,128]{3,2,1,0:T(8,128)(2,1)S(1)} collective-permute-done((bf16[2,2,512,128]{3,2,1,0:T(8,128)(2,1)S(1)}, bf16[2,2,512,128]{3,2,1,0:T(8,128)(2,1)S(1)}, u32[]{:S(2)}, u32[]{:S(2)}) %collective-permute-start.9) | collective-permute-done | bytes 524320 | tf_op jit(solution)/shard_map/ppermute | solution.py:26
  104.1 0.0 copy-done.1
  104.1 0.0 copy-start
  104.1 1.0 copy-done
  105.2 4.8 %shard_map.38 = (f32[512,1024]{1,0:T(8,128)S(1)}, bf16[2,2,512,1024]{3,2,1,0:T(8,128)(2,1)S(1)}) custom-call(s32[5]{0:T(128)S(1)} %copy-done.1, bf16[2,2,512,128]{3,2,1,0:T(8,128)(2,1)S(1)} %pad_maximum_fusion.1.refs_0_, bf16[2,2,512,128]{3,2,1,0:T(8,128)(2,1)S(1)} %collective-permute-done.3.refs_1_, ...), custom_call_target="tpu_custom_call" | custom-call | flops 2147483648 | bytes 10485760 | tf_op jit(solution)/shard_map/pallas_call | solution.py:159
  110.0 4.0 %collective-permute-done.14.refs_0_ = bf16[2,4,64,1024]{3,2,1,0:T(8,128)(2,1)S(1)} collective-permute-done((bf16[2,4,64,1024]{3,2,1,0:T(8,128)(2,1)S(1)}, bf16[2,4,64,1024]{3,2,1,0:T(8,128)(2,1)S(1)}, u32[]{:S(2)}, u32[]{:S(2)}) %collective-permute-start.14) | collective-permute-done | bytes 1048608 | tf_op jit(solution)/shard_map/ppermute | solution.py:13
  114.0 4.0 %collective-permute-done.15.refs_1_ = bf16[2,4,64,1024]{3,2,1,0:T(8,128)(2,1)S(1)} collective-permute-done((bf16[2,4,64,1024]{3,2,1,0:T(8,128)(2,1)S(1)}, bf16[2,4,64,1024]{3,2,1,0:T(8,128)(2,1)S(1)}, u32[]{:S(2)}, u32[]{:S(2)}) %collective-permute-start.15) | collective-permute-done | bytes 1048608 | tf_op jit(solution)/shard_map/ppermute | solution.py:13
  118.0 4.5 %shard_map.39 = bf16[512,1024]{1,0:T(8,128)(2,1)} custom-call(s32[5]{0:T(128)S(1)} %copy-done.1, f32[512,1024]{1,0:T(8,128)S(1)} %get-tuple-element.13.total, bf16[2,2,512,1024]{3,2,1,0:T(8,128)(2,1)S(1)} %get-tuple-element.14.kept, bf16[2,4,64,1024]{3,2,1,0:T(8,128)(2,1)S(1)} %collective-permute-done.14.refs_0_, ...), custom_call_target="tpu_custom_call" | custom-call | flops 2147483648 | bytes 10485760 | tf_op jit(solution)/shard_map/pallas_call | solution.py:171
  (3 shorter events, 0.1 us)
Async XLA Ops:
  2.7 35.2 %all-to-all-start = ((bf16[32,4,4,128]{3,2,1,0:T(4,128)(2,1)}), bf16[32,4,4,128]{3,2,1,0:T(4,128)(2,1)S(1)}, u32[]{:S(2)}, u32[]{:S(2)}) async-start(bf16[32,4,4,128]{3,2,1,0:T(4,128)(2,1)} %bitcast.25), calls=%async_computation | async-start | bytes 262144 | tf_op jit(solution)/shard_map/all_to_all | solution.py:133
  19.4 20.1 %collective-permute-start = (bf16[64,1024]{1,0:T(8,128)(2,1)}, bf16[64,1024]{1,0:T(8,128)(2,1)S(1)}, u32[]{:S(2)}, u32[]{:S(2)}) collective-permute-start(bf16[64,1024]{1,0:T(8,128)(2,1)} %here.1), channel_id=1, source_target_pairs={{0,128},{16,144},{32,160},{48,176},{64,192},{80,208},{96,224},{112... | collective-permute-start | bytes 393224 | tf_op jit(solution)/shard_map/ppermute | solution.py:13
  26.7 19.1 %collective-permute-start.1 = (bf16[64,1024]{1,0:T(8,128)(2,1)}, bf16[64,1024]{1,0:T(8,128)(2,1)S(1)}, u32[]{:S(2)}, u32[]{:S(2)}) collective-permute-start(bf16[64,1024]{1,0:T(8,128)(2,1)} %here.1), channel_id=1, source_target_pairs={{0,384},{16,400},{32,416},{48,432},{64,448},{80,464},{96,480},{112... | collective-permute-start | bytes 393224 | tf_op jit(solution)/shard_map/ppermute | solution.py:13
  39.5 21.8 %copy-start.2 = (bf16[64,1024]{1,0:T(8,128)(2,1)}, bf16[64,1024]{1,0:T(8,128)(2,1)S(1)}, u32[]{:S(2)}) copy-start(bf16[64,1024]{1,0:T(8,128)(2,1)S(1)} %collective-permute-done.below) | copy-start | bytes 393220
  45.8 15.5 %copy-start.3 = (bf16[64,1024]{1,0:T(8,128)(2,1)}, bf16[64,1024]{1,0:T(8,128)(2,1)S(1)}, u32[]{:S(2)}) copy-start(bf16[64,1024]{1,0:T(8,128)(2,1)S(1)} %collective-permute-done.1.above) | copy-start | bytes 393220
  45.8 23.1 %collective-permute-start.2 = (bf16[2,512,128]{2,1,0:T(8,128)(2,1)S(1)}, bf16[2,512,128]{2,1,0:T(8,128)(2,1)S(1)}, u32[]{:S(2)}, u32[]{:S(2)}) collective-permute-start(bf16[2,512,128]{2,1,0:T(8,128)(2,1)S(1)} %get-tuple-element.16), channel_id=1, source_target_pairs={{0,8},{1,9},{2,10},{3,11},{4,12},{5,13},{6,14},{7,15},{8,0},{9,1},... | collective-permute-start | bytes 786440 | tf_op jit(solution)/shard_map/ppermute | solution.py:31
  49.9 11.4 %collective-permute-start.10 = (bf16[64,1024]{1,0:T(8,128)(2,1)S(1)}, bf16[64,1024]{1,0:T(8,128)(2,1)S(1)}, u32[]{:S(2)}, u32[]{:S(2)}) collective-permute-start(bf16[64,1024]{1,0:T(8,128)(2,1)S(1)} %broadcast_select_fusion), channel_id=1, source_target_pairs={{0,128},{1,385},{2,130},{3,387},{4,132},{5,389},{6,134},{7,391},{8... | collective-permute-start | bytes 393224 | tf_op jit(solution)/shard_map/ppermute | solution.py:127
  57.5 46.6 %copy-start.1 = (s32[5]{0:T(128)S(1)}, s32[5]{0:T(128)}, u32[]{:S(2)}) copy-start(s32[5]{0:T(128)} %stack.50.place) | copy-start | bytes 64
  61.3 0.7 copy-start.4
  63.9 16.6 %collective-permute-start.12 = (bf16[4,64,1024]{2,1,0:T(8,128)(2,1)}, bf16[4,64,1024]{2,1,0:T(8,128)(2,1)S(1)}, u32[]{:S(2)}, u32[]{:S(2)}) collective-permute-start(bf16[4,64,1024]{2,1,0:T(8,128)(2,1)} %shard_map.37.refs_8_), channel_id=1, source_target_pairs={{0,64},{1,449},{2,66},{3,451},{4,68},{5,453},{6,70},{7,455},{8,72}... | collective-permute-start | bytes 1572872 | tf_op jit(solution)/shard_map/ppermute | solution.py:143
  65.8 16.6 %collective-permute-start.11 = (bf16[4,64,1024]{2,1,0:T(8,128)(2,1)}, bf16[4,64,1024]{2,1,0:T(8,128)(2,1)S(1)}, u32[]{:S(2)}, u32[]{:S(2)}) collective-permute-start(bf16[4,64,1024]{2,1,0:T(8,128)(2,1)} %shard_map.37.refs_8_), channel_id=1, source_target_pairs={{0,16},{16,0},{32,48},{48,32},{64,80},{80,64},{96,112},{112,96},{1... | collective-permute-start | bytes 1572872 | tf_op jit(solution)/shard_map/ppermute | solution.py:22
  69.0 17.6 %collective-permute-start.3 = (bf16[2,2,512,128]{3,2,1,0:T(8,128)(2,1)S(1)}, bf16[2,2,512,128]{3,2,1,0:T(8,128)(2,1)S(1)}, u32[]{:S(2)}, u32[]{:S(2)}) collective-permute-start(bf16[2,2,512,128]{3,2,1,0:T(8,128)(2,1)S(1)} %pad_maximum_fusion.1.refs_0_), channel_id=1, source_target_pairs={{0,2},{1,3},{2,4},{3,5},{4,6},{5,7},{6,0},{7,1},{8,10},{9,11},{10,... | collective-permute-start | bytes 1572872 | tf_op jit(solution)/shard_map/ppermute | solution.py:31
  72.5 17.4 %collective-permute-start.4 = (bf16[2,2,512,128]{3,2,1,0:T(8,128)(2,1)S(1)}, bf16[2,2,512,128]{3,2,1,0:T(8,128)(2,1)S(1)}, u32[]{:S(2)}, u32[]{:S(2)}) collective-permute-start(bf16[2,2,512,128]{3,2,1,0:T(8,128)(2,1)S(1)} %pad_maximum_fusion.1.refs_0_), channel_id=1, source_target_pairs={{0,6},{1,7},{2,0},{3,1},{4,2},{5,3},{6,4},{7,5},{8,14},{9,15},{10,... | collective-permute-start | bytes 1572872 | tf_op jit(solution)/shard_map/ppermute | solution.py:31
  76.1 19.9 %collective-permute-start.5 = (bf16[2,2,512,128]{3,2,1,0:T(8,128)(2,1)S(1)}, bf16[2,2,512,128]{3,2,1,0:T(8,128)(2,1)S(1)}, u32[]{:S(2)}, u32[]{:S(2)}) collective-permute-start(bf16[2,2,512,128]{3,2,1,0:T(8,128)(2,1)S(1)} %pad_maximum_fusion.1.refs_0_), channel_id=1, source_target_pairs={{0,4},{1,5},{2,6},{3,7},{4,0},{5,1},{6,2},{7,3},{8,12},{9,13},{10,... | collective-permute-start | bytes 1572872 | tf_op jit(solution)/shard_map/ppermute | solution.py:31
  80.4 17.4 %collective-permute-start.6 = (bf16[2,2,512,128]{3,2,1,0:T(8,128)(2,1)S(1)}, bf16[2,2,512,128]{3,2,1,0:T(8,128)(2,1)S(1)}, u32[]{:S(2)}, u32[]{:S(2)}) collective-permute-start(bf16[2,2,512,128]{3,2,1,0:T(8,128)(2,1)S(1)} %pad_maximum_fusion.1.refs_0_), channel_id=1, source_target_pairs={{0,1},{1,0},{2,3},{3,2},{4,5},{5,4},{6,7},{7,6},{8,9},{9,8},{10,11... | collective-permute-start | bytes 1572872 | tf_op jit(solution)/shard_map/ppermute | solution.py:26
  82.4 17.9 %collective-permute-start.13 = (bf16[4,64,1024]{2,1,0:T(8,128)(2,1)S(1)}, bf16[4,64,1024]{2,1,0:T(8,128)(2,1)S(1)}, u32[]{:S(2)}, u32[]{:S(2)}) collective-permute-start(bf16[4,64,1024]{2,1,0:T(8,128)(2,1)S(1)} %collective-permute-done.12.refs_10_), channel_id=1, source_target_pairs={{0,16},{16,0},{32,48},{48,32},{64,80},{80,64},{96,112},{112,96},{1... | collective-permute-start | bytes 1572872 | tf_op jit(solution)/shard_map/ppermute | solution.py:22
  86.7 27.3 %collective-permute-start.14 = (bf16[2,4,64,1024]{3,2,1,0:T(8,128)(2,1)S(1)}, bf16[2,4,64,1024]{3,2,1,0:T(8,128)(2,1)S(1)}, u32[]{:S(2)}, u32[]{:S(2)}) collective-permute-start(bf16[2,4,64,1024]{3,2,1,0:T(8,128)(2,1)S(1)} %pad_maximum_fusion), channel_id=1, source_target_pairs={{0,480},{16,496},{32,0},{48,16},{64,32},{80,48},{96,64},{112,80},{... | collective-permute-start | bytes 3145736 | tf_op jit(solution)/shard_map/ppermute | solution.py:13
  89.9 28.1 %collective-permute-start.15 = (bf16[2,4,64,1024]{3,2,1,0:T(8,128)(2,1)S(1)}, bf16[2,4,64,1024]{3,2,1,0:T(8,128)(2,1)S(1)}, u32[]{:S(2)}, u32[]{:S(2)}) collective-permute-start(bf16[2,4,64,1024]{3,2,1,0:T(8,128)(2,1)S(1)} %pad_maximum_fusion), channel_id=1, source_target_pairs={{0,32},{16,48},{32,64},{48,80},{64,96},{80,112},{96,128},{112,144}... | collective-permute-start | bytes 3145736 | tf_op jit(solution)/shard_map/ppermute | solution.py:13
  96.0 6.3 %collective-permute-start.7 = (bf16[2,2,512,128]{3,2,1,0:T(8,128)(2,1)S(1)}, bf16[2,2,512,128]{3,2,1,0:T(8,128)(2,1)S(1)}, u32[]{:S(2)}, u32[]{:S(2)}) collective-permute-start(bf16[2,2,512,128]{3,2,1,0:T(8,128)(2,1)S(1)} %collective-permute-done.3.refs_1_), channel_id=1, source_target_pairs={{0,1},{1,0},{2,3},{3,2},{4,5},{5,4},{6,7},{7,6},{8,9},{9,8},{10,11... | collective-permute-start | bytes 1572872 | tf_op jit(solution)/shard_map/ppermute | solution.py:26
  97.9 4.4 %collective-permute-start.8 = (bf16[2,2,512,128]{3,2,1,0:T(8,128)(2,1)S(1)}, bf16[2,2,512,128]{3,2,1,0:T(8,128)(2,1)S(1)}, u32[]{:S(2)}, u32[]{:S(2)}) collective-permute-start(bf16[2,2,512,128]{3,2,1,0:T(8,128)(2,1)S(1)} %collective-permute-done.4.refs_2_), channel_id=1, source_target_pairs={{0,1},{1,0},{2,3},{3,2},{4,5},{5,4},{6,7},{7,6},{8,9},{9,8},{10,11... | collective-permute-start | bytes 1572872 | tf_op jit(solution)/shard_map/ppermute | solution.py:26
  100.3 3.8 %collective-permute-start.9 = (bf16[2,2,512,128]{3,2,1,0:T(8,128)(2,1)S(1)}, bf16[2,2,512,128]{3,2,1,0:T(8,128)(2,1)S(1)}, u32[]{:S(2)}, u32[]{:S(2)}) collective-permute-start(bf16[2,2,512,128]{3,2,1,0:T(8,128)(2,1)S(1)} %collective-permute-done.5.refs_3_), channel_id=1, source_target_pairs={{0,1},{1,0},{2,3},{3,2},{4,5},{5,4},{6,7},{7,6},{8,9},{9,8},{10,11... | collective-permute-start | bytes 1572872 | tf_op jit(solution)/shard_map/ppermute | solution.py:26
  104.1 1.0 copy-start

commit v12 on v11

--- a/solution.py
+++ b/solution.py
@@ -1,3 +1,5 @@
+import functools
+
 import jax
 import jax.numpy as jnp
 from jax import lax
@@ -49,8 +51,8 @@
     copies = []
     for ref, partner, shift in zip(refs[::2], refs[1::2], shifts):
         m = (z + shift) & 3
-        copies.append((ref, ints.at[:, m >> 1, xl]))
-        copies.append((partner, ints.at[:, m >> 1, 1 - xl]))
+        copies.append((ref, ints.at[m >> 1, :, xl]))
+        copies.append((partner, ints.at[m >> 1, :, 1 - xl]))
     return copies
 
 
@@ -89,7 +91,8 @@
             for dx in range(2):
                 shards.append((ref.at[dx], ((xh ^ dx) * 4 + ((y - dy) & 3)) * 2 + who))
     for ref, col in shards:
-        lanes = pl.ds(pl.multiple_of((col >> 1) * 128, 128), 128)
+        slot = ((col >> 1) & 1) * 4 + (col >> 2)
+        lanes = pl.ds(pl.multiple_of(slot * 128, 128), 128)
         for s in range(2):
             copies.append((ref.at[s], kept.at[(col + z) & 1, s, :, lanes]))
     run_copies(copies, sem)
@@ -102,14 +105,16 @@
     lax.fori_loop(0, total.shape[1] // NTILE, tile, 0)
 
 
-def second_half(place, total, kept, *refs):
-    blocks = [refs[i].at[x] for i in range(2) for x in range(2)]
-    out, ints, sem = refs[2:]
-    run_copies(block_copies(place, blocks, (1, -1), ints), sem)
+def add_neighbour(shift, place, total, kept, block, out, ints, sem):
+    z, xl = place[0], place[1]
+    run_copies([(block.at[0], ints.at[0, :, xl]), (block.at[1], ints.at[0, :, 1 - xl])], sem)
+    depth = kept.shape[3] // 2
+    lanes = pl.ds(pl.multiple_of((((z + shift) & 3) >> 1) * depth, depth), depth)
 
     def tile(n, carry):
         cols = columns(n)
-        out[:, cols] = (total[:, cols] + multiply(kept.at[1], ints, cols)).astype(out.dtype)
+        amps = [kept[1, s, :, lanes] for s in range(2)]
+        out[:, cols] = (total[:, cols] + multiply(amps, ints, cols)).astype(out.dtype)
         return carry
 
     lax.fori_loop(0, out.shape[1] // NTILE, tile, 0)
@@ -132,7 +137,7 @@
     sent = masked.reshape(OI, 32, OI, depth).transpose(1, 2, 0, 3)
     got = lax.all_to_all(sent, "row", split_axis=0, concat_axis=0, tiled=True)
     swapped = got.transpose(1, 0, 2, 3).reshape(pairs, depth)
-    swapped, up4, down4 = lax.optimization_barrier((swapped, up4, down4))
+    swapped, up4 = lax.optimization_barrier((swapped, up4))
     block = gather_four(place, integrals, up4, down4, far)
 
     both = jnp.stack([masked, swapped])
@@ -151,7 +156,7 @@
     anywhere = pl.BlockSpec(memory_space=pl.ANY)
     scalars = pl.BlockSpec(memory_space=pltpu.SMEM)
     vector = pl.BlockSpec(memory_space=pltpu.VMEM)
-    ints = pltpu.VMEM((4, 2, 2, rows, cols), jnp.bfloat16)
+    ints = pltpu.VMEM((2, 4, 2, rows, cols), jnp.bfloat16)
     params = pltpu.CompilerParams(vmem_limit_bytes=32 * 2**20)
     cost = pl.CostEstimate(
         flops=2 * pairs * 2048 * cols, bytes_accessed=10 * 2**20, transcendentals=0
@@ -168,15 +173,20 @@
         compiler_params=params,
         cost_estimate=cost,
     )(place, *mine, *theirs, block, partner, two, two_partner)
-    return pl.pallas_call(
-        second_half,
-        out_shape=jax.ShapeDtypeStruct((pairs, cols), jnp.bfloat16),
-        in_specs=[scalars, vector, vector] + [anywhere] * 2,
-        out_specs=vector,
-        scratch_shapes=[ints, pltpu.SemaphoreType.DMA],
-        compiler_params=params,
-        cost_estimate=cost,
-    )(place, total, kept, down, up)
+    for shift, block, kind in ((1, down, jnp.float32), (-1, up, jnp.bfloat16)):
+        total = pl.pallas_call(
+            functools.partial(add_neighbour, shift),
+            out_shape=jax.ShapeDtypeStruct((pairs, cols), kind),
+            in_specs=[scalars, vector, vector, anywhere],
+            out_specs=vector,
+            scratch_shapes=[
+                pltpu.VMEM((1, 4, 2, rows, cols), jnp.bfloat16),
+                pltpu.SemaphoreType.DMA,
+            ],
+            compiler_params=params,
+            cost_estimate=cost,
+        )(place, total, kept, block)
+    return total
 
 
 def solution(mesh):

time: 123 us -> 127 us (1.033)
  the two profiles are of different devices: /device:TPU:2 before, /device:TPU:60 now
where the time goes in v12:
time: 127 us; the launch traced here: 126 us
  starting transfers between devices  69.8 us (55%)
  waiting for transfers between devices  38 us (30%)
  Pallas kernels  12.6 us (10%)
  local copies, waits for them, and re-layouts  3.14 us (2%)
  other arithmetic  2.17 us (2%)
    ppermute x4, starting transfers between devices, z_shift(): return lax.ppermute(x, 'row', [(r, (r + 2 * d) % 32) for r in range(32)])  17.1 us
    ppermute x4, waiting for transfers between devices, z_shift(): return lax.ppermute(x, 'row', [(r, (r + 2 * d) % 32) for r in range(32)])  16.6 us
    all_to_all x1, starting transfers between devices, on_device(): got = lax.all_to_all(sent, 'row', split_axis=0, concat_axis=0, tiled=True)  16 us
    ppermute x4, starting transfers between devices, chip_shift(): lax.ppermute(x, 'col', [(c, (c // 8 ^ dx) * 8 + (c // 2 % 4 + dy) % 4 * 2...  11.7 us
    ppermute x4, starting transfers between devices, core_swap(): return lax.ppermute(x, 'col', [(c, c ^ 1) for c in range(16)])  9.01 us
    ppermute x4, waiting for transfers between devices, chip_shift(): lax.ppermute(x, 'col', [(c, (c // 8 ^ dx) * 8 + (c // 2 % 4 + dy) % 4 * 2...  8.14 us
    ppermute x2, starting transfers between devices, x_swap(): return lax.ppermute(x, 'row', [(r, r ^ 1) for r in range(32)])  7.62 us
    ppermute x1, starting transfers between devices, on_device(): lax.ppermute(jnp.where(core == 0, up4, down4), ('row', 'col'), split_shif...  6.3 us
  transfers between devices with their start and end apart: 17, of which 8 were waited for; matrix products, arithmetic and copies ran while one was open for 2% of the time, Pallas kernels for 7%

profile of v12, /device:TPU:60, one launch (start us, length us, event | category | flops | bytes accessed | tf_op | source)
XLA Modules:
  0.0 126.1 jit_solution(16576158897825889264)
XLA Ops:
  0.0 1.0 copy.6
  1.0 0.7 convert_bitcast_fusion
  1.7 0.1 broadcast_bitcast_fusion
  1.8 0.1 broadcast_multiply_fusion
  1.9 0.8 copy.10
  2.7 16.0 %all-to-all-start = ((bf16[32,4,4,128]{3,2,1,0:T(4,128)(2,1)}), bf16[32,4,4,128]{3,2,1,0:T(4,128)(2,1)S(1)}, u32[]{:S(2)}, u32[]{:S(2)}) async-start(bf16[32,4,4,128]{3,2,1,0:T(4,128)(2,1)} %bitcast.25), calls=%async_computation | async-start | bytes 262144 | tf_op jit(solution)/shard_map/all_to_all | solution.py:138
  18.7 7.3 %collective-permute-start = (bf16[64,1024]{1,0:T(8,128)(2,1)}, bf16[64,1024]{1,0:T(8,128)(2,1)S(1)}, u32[]{:S(2)}, u32[]{:S(2)}) collective-permute-start(bf16[64,1024]{1,0:T(8,128)(2,1)} %here.1), channel_id=1, source_target_pairs={{0,128},{16,144},{32,160},{48,176},{64,192},{80,208},{96,224},{112... | collective-permute-start | bytes 393224 | tf_op jit(solution)/shard_map/ppermute | solution.py:15
  26.0 2.5 %collective-permute-start.9 = (bf16[64,1024]{1,0:T(8,128)(2,1)}, bf16[64,1024]{1,0:T(8,128)(2,1)S(1)}, u32[]{:S(2)}, u32[]{:S(2)}) collective-permute-start(bf16[64,1024]{1,0:T(8,128)(2,1)} %here.1), channel_id=1, source_target_pairs={{0,384},{16,400},{32,416},{48,432},{64,448},{80,464},{96,480},{112... | collective-permute-start | bytes 393224 | tf_op jit(solution)/shard_map/ppermute | solution.py:15
  28.4 0.1 fusion.1
  28.6 5.2 %all-to-all-done = bf16[32,4,4,128]{3,2,1,0:T(4,128)(2,1)S(1)} async-done(((bf16[32,4,4,128]{3,2,1,0:T(4,128)(2,1)}), bf16[32,4,4,128]{3,2,1,0:T(4,128)(2,1)S(1)}, u32[]{:S(2)}, u32[]{:S(2)}) %all-to-all-start) | async-done | bytes 131104 | tf_op jit(solution)/shard_map/all_to_all | solution.py:138
  33.8 4.1 %collective-permute-done.below = bf16[64,1024]{1,0:T(8,128)(2,1)S(1)} collective-permute-done((bf16[64,1024]{1,0:T(8,128)(2,1)}, bf16[64,1024]{1,0:T(8,128)(2,1)S(1)}, u32[]{:S(2)}, u32[]{:S(2)}) %collective-permute-start) | collective-permute-done | bytes 131104 | tf_op jit(solution)/shard_map/ppermute | solution.py:15
  38.0 0.0 copy-start.2
  38.0 2.7 %collective-permute-start.1 = (bf16[2,512,128]{2,1,0:T(8,128)(2,1)S(1)}, bf16[2,512,128]{2,1,0:T(8,128)(2,1)S(1)}, u32[]{:S(2)}, u32[]{:S(2)}) collective-permute-start(bf16[2,512,128]{2,1,0:T(8,128)(2,1)S(1)} %get-tuple-element.14), channel_id=1, source_target_pairs={{0,8},{1,9},{2,10},{3,11},{4,12},{5,13},{6,14},{7,15},{8,0},{9,1},... | collective-permute-start | bytes 786440 | tf_op jit(solution)/shard_map/ppermute | solution.py:33
  40.7 2.9 %collective-permute-done.9.above = bf16[64,1024]{1,0:T(8,128)(2,1)S(1)} collective-permute-done((bf16[64,1024]{1,0:T(8,128)(2,1)}, bf16[64,1024]{1,0:T(8,128)(2,1)S(1)}, u32[]{:S(2)}, u32[]{:S(2)}) %collective-permute-start.9) | collective-permute-done | bytes 131104 | tf_op jit(solution)/shard_map/ppermute | solution.py:15
  43.6 0.0 copy-start.3
  43.6 6.3 %collective-permute-start.10 = (bf16[64,1024]{1,0:T(8,128)(2,1)S(1)}, bf16[64,1024]{1,0:T(8,128)(2,1)S(1)}, u32[]{:S(2)}, u32[]{:S(2)}) collective-permute-start(bf16[64,1024]{1,0:T(8,128)(2,1)S(1)} %broadcast_select_fusion), channel_id=1, source_target_pairs={{0,128},{1,385},{2,130},{3,387},{4,132},{5,389},{6,134},{7,391},{8... | collective-permute-start | bytes 393224 | tf_op jit(solution)/shard_map/ppermute | solution.py:132
  50.0 0.6 stack.50.place
  50.6 0.0 copy-start.1
  50.6 5.5 %collective-permute-done.10.far = bf16[64,1024]{1,0:T(8,128)(2,1)S(1)} collective-permute-done((bf16[64,1024]{1,0:T(8,128)(2,1)S(1)}, bf16[64,1024]{1,0:T(8,128)(2,1)S(1)}, u32[]{:S(2)}, u32[]{:S(2)}) %collective-permute-start.10) | collective-permute-done | bytes 131104 | tf_op jit(solution)/shard_map/ppermute | solution.py:132
  56.1 0.0 copy-done.2
  56.1 0.0 copy-done.3
  56.1 0.0 copy-start.4
  56.1 0.7 copy-done.4
  56.7 1.9 %shard_map.37.refs_8_ = bf16[4,64,1024]{2,1,0:T(8,128)(2,1)} custom-call(s32[5]{0:T(128)} %stack.50.place, bf16[64,1024]{1,0:T(8,128)(2,1)} %here.1, bf16[64,1024]{1,0:T(8,128)(2,1)} %copy-done.2, bf16[64,1024]{1,0:T(8,128)(2,1)} %copy-done.3, bf16[64,1024]{1,0:T(8,128)(2,1)} %copy-done.4), custom_call_target="tpu_custom_call" | custom-call | tf_op jit(solution)/shard_map/pallas_call | solution.py:74
  58.7 0.0 copy-start
  58.7 2.0 %collective-permute-start.12 = (bf16[4,64,1024]{2,1,0:T(8,128)(2,1)}, bf16[4,64,1024]{2,1,0:T(8,128)(2,1)S(1)}, u32[]{:S(2)}, u32[]{:S(2)}) collective-permute-start(bf16[4,64,1024]{2,1,0:T(8,128)(2,1)} %shard_map.37.refs_8_), channel_id=1, source_target_pairs={{0,64},{1,449},{2,66},{3,451},{4,68},{5,453},{6,70},{7,455},{8,72}... | collective-permute-start | bytes 1572872 | tf_op jit(solution)/shard_map/ppermute | solution.py:148
  60.7 3.7 %collective-permute-start.11 = (bf16[4,64,1024]{2,1,0:T(8,128)(2,1)}, bf16[4,64,1024]{2,1,0:T(8,128)(2,1)S(1)}, u32[]{:S(2)}, u32[]{:S(2)}) collective-permute-start(bf16[4,64,1024]{2,1,0:T(8,128)(2,1)} %shard_map.37.refs_8_), channel_id=1, source_target_pairs={{0,16},{16,0},{32,48},{48,32},{64,80},{80,64},{96,112},{112,96},{1... | collective-permute-start | bytes 1572872 | tf_op jit(solution)/shard_map/ppermute | solution.py:24
  64.4 0.0 collective-permute-done.1
  64.4 0.1 pad_maximum_fusion.1.refs_0_
  64.5 2.1 %collective-permute-start.2 = (bf16[2,2,512,128]{3,2,1,0:T(8,128)(2,1)S(1)}, bf16[2,2,512,128]{3,2,1,0:T(8,128)(2,1)S(1)}, u32[]{:S(2)}, u32[]{:S(2)}) collective-permute-start(bf16[2,2,512,128]{3,2,1,0:T(8,128)(2,1)S(1)} %pad_maximum_fusion.1.refs_0_), channel_id=1, source_target_pairs={{0,2},{1,3},{2,4},{3,5},{4,6},{5,7},{6,0},{7,1},{8,10},{9,11},{10,... | collective-permute-start | bytes 1572872 | tf_op jit(solution)/shard_map/ppermute | solution.py:33
  66.6 3.7 %collective-permute-start.3 = (bf16[2,2,512,128]{3,2,1,0:T(8,128)(2,1)S(1)}, bf16[2,2,512,128]{3,2,1,0:T(8,128)(2,1)S(1)}, u32[]{:S(2)}, u32[]{:S(2)}) collective-permute-start(bf16[2,2,512,128]{3,2,1,0:T(8,128)(2,1)S(1)} %pad_maximum_fusion.1.refs_0_), channel_id=1, source_target_pairs={{0,6},{1,7},{2,0},{3,1},{4,2},{5,3},{6,4},{7,5},{8,14},{9,15},{10,... | collective-permute-start | bytes 1572872 | tf_op jit(solution)/shard_map/ppermute | solution.py:33
  70.3 3.1 %collective-permute-start.4 = (bf16[2,2,512,128]{3,2,1,0:T(8,128)(2,1)S(1)}, bf16[2,2,512,128]{3,2,1,0:T(8,128)(2,1)S(1)}, u32[]{:S(2)}, u32[]{:S(2)}) collective-permute-start(bf16[2,2,512,128]{3,2,1,0:T(8,128)(2,1)S(1)} %pad_maximum_fusion.1.refs_0_), channel_id=1, source_target_pairs={{0,4},{1,5},{2,6},{3,7},{4,0},{5,1},{6,2},{7,3},{8,12},{9,13},{10,... | collective-permute-start | bytes 1572872 | tf_op jit(solution)/shard_map/ppermute | solution.py:33
  73.5 0.0 collective-permute-done.12.refs_10_
  73.5 2.7 %collective-permute-start.5 = (bf16[2,2,512,128]{3,2,1,0:T(8,128)(2,1)S(1)}, bf16[2,2,512,128]{3,2,1,0:T(8,128)(2,1)S(1)}, u32[]{:S(2)}, u32[]{:S(2)}) collective-permute-start(bf16[2,2,512,128]{3,2,1,0:T(8,128)(2,1)S(1)} %pad_maximum_fusion.1.refs_0_), channel_id=1, source_target_pairs={{0,1},{1,0},{2,3},{3,2},{4,5},{5,4},{6,7},{7,6},{8,9},{9,8},{10,11... | collective-permute-start | bytes 1572872 | tf_op jit(solution)/shard_map/ppermute | solution.py:28
  76.2 0.8 collective-permute-done.11.refs_9_
  77.0 3.9 %collective-permute-start.13 = (bf16[4,64,1024]{2,1,0:T(8,128)(2,1)S(1)}, bf16[4,64,1024]{2,1,0:T(8,128)(2,1)S(1)}, u32[]{:S(2)}, u32[]{:S(2)}) collective-permute-start(bf16[4,64,1024]{2,1,0:T(8,128)(2,1)S(1)} %collective-permute-done.12.refs_10_), channel_id=1, source_target_pairs={{0,16},{16,0},{32,48},{48,32},{64,80},{80,64},{96,112},{112,96},{1... | collective-permute-start | bytes 1572872 | tf_op jit(solution)/shard_map/ppermute | solution.py:24
  80.9 1.1 pad_maximum_fusion
  82.1 0.0 collective-permute-done.2.refs_1_
  82.1 5.5 %collective-permute-start.14 = (bf16[2,4,64,1024]{3,2,1,0:T(8,128)(2,1)S(1)}, bf16[2,4,64,1024]{3,2,1,0:T(8,128)(2,1)S(1)}, u32[]{:S(2)}, u32[]{:S(2)}) collective-permute-start(bf16[2,4,64,1024]{3,2,1,0:T(8,128)(2,1)S(1)} %pad_maximum_fusion), channel_id=1, source_target_pairs={{0,480},{16,496},{32,0},{48,16},{64,32},{80,48},{96,64},{112,80},{... | collective-permute-start | bytes 3145736 | tf_op jit(solution)/shard_map/ppermute | solution.py:15
  87.6 8.1 %collective-permute-done.3.refs_2_ = bf16[2,2,512,128]{3,2,1,0:T(8,128)(2,1)S(1)} collective-permute-done((bf16[2,2,512,128]{3,2,1,0:T(8,128)(2,1)S(1)}, bf16[2,2,512,128]{3,2,1,0:T(8,128)(2,1)S(1)}, u32[]{:S(2)}, u32[]{:S(2)}) %collective-permute-start.3) | collective-permute-done | bytes 524320 | tf_op jit(solution)/shard_map/ppermute | solution.py:33
  95.7 1.9 %collective-permute-start.15 = (bf16[2,4,64,1024]{3,2,1,0:T(8,128)(2,1)S(1)}, bf16[2,4,64,1024]{3,2,1,0:T(8,128)(2,1)S(1)}, u32[]{:S(2)}, u32[]{:S(2)}) collective-permute-start(bf16[2,4,64,1024]{3,2,1,0:T(8,128)(2,1)S(1)} %pad_maximum_fusion), channel_id=1, source_target_pairs={{0,32},{16,48},{32,64},{48,80},{64,96},{80,112},{96,128},{112,144}... | collective-permute-start | bytes 3145736 | tf_op jit(solution)/shard_map/ppermute | solution.py:15
  97.6 0.0 collective-permute-done.4.refs_3_
  97.6 2.0 %collective-permute-start.6 = (bf16[2,2,512,128]{3,2,1,0:T(8,128)(2,1)S(1)}, bf16[2,2,512,128]{3,2,1,0:T(8,128)(2,1)S(1)}, u32[]{:S(2)}, u32[]{:S(2)}) collective-permute-start(bf16[2,2,512,128]{3,2,1,0:T(8,128)(2,1)S(1)} %collective-permute-done.2.refs_1_), channel_id=1, source_target_pairs={{0,1},{1,0},{2,3},{3,2},{4,5},{5,4},{6,7},{7,6},{8,9},{9,8},{10,11... | collective-permute-start | bytes 1572872 | tf_op jit(solution)/shard_map/ppermute | solution.py:28
  99.6 0.0 collective-permute-done.5.refs_4_
  99.6 2.4 %collective-permute-start.7 = (bf16[2,2,512,128]{3,2,1,0:T(8,128)(2,1)S(1)}, bf16[2,2,512,128]{3,2,1,0:T(8,128)(2,1)S(1)}, u32[]{:S(2)}, u32[]{:S(2)}) collective-permute-start(bf16[2,2,512,128]{3,2,1,0:T(8,128)(2,1)S(1)} %collective-permute-done.3.refs_2_), channel_id=1, source_target_pairs={{0,1},{1,0},{2,3},{3,2},{4,5},{5,4},{6,7},{7,6},{8,9},{9,8},{10,11... | collective-permute-start | bytes 1572872 | tf_op jit(solution)/shard_map/ppermute | solution.py:28
  102.0 0.0 collective-permute-done.13.refs_11_
  102.0 2.0 %collective-permute-start.8 = (bf16[2,2,512,128]{3,2,1,0:T(8,128)(2,1)S(1)}, bf16[2,2,512,128]{3,2,1,0:T(8,128)(2,1)S(1)}, u32[]{:S(2)}, u32[]{:S(2)}) collective-permute-start(bf16[2,2,512,128]{3,2,1,0:T(8,128)(2,1)S(1)} %collective-permute-done.4.refs_3_), channel_id=1, source_target_pairs={{0,1},{1,0},{2,3},{3,2},{4,5},{5,4},{6,7},{7,6},{8,9},{9,8},{10,11... | collective-permute-start | bytes 1572872 | tf_op jit(solution)/shard_map/ppermute | solution.py:28
  103.9 0.0 collective-permute-done.6.refs_5_
  104.0 0.0 collective-permute-done.7.refs_6_
  104.0 1.8 %collective-permute-done.8.refs_7_ = bf16[2,2,512,128]{3,2,1,0:T(8,128)(2,1)S(1)} collective-permute-done((bf16[2,2,512,128]{3,2,1,0:T(8,128)(2,1)S(1)}, bf16[2,2,512,128]{3,2,1,0:T(8,128)(2,1)S(1)}, u32[]{:S(2)}, u32[]{:S(2)}) %collective-permute-start.8) | collective-permute-done | bytes 524320 | tf_op jit(solution)/shard_map/ppermute | solution.py:28
  105.8 0.0 copy-done.1
  105.8 0.0 copy-done
  105.8 4.9 %shard_map.38 = (f32[512,1024]{1,0:T(8,128)S(1)}, bf16[2,2,512,1024]{3,2,1,0:T(8,128)(2,1)S(1)}) custom-call(s32[5]{0:T(128)S(1)} %copy-done.1, bf16[2,2,512,128]{3,2,1,0:T(8,128)(2,1)S(1)} %pad_maximum_fusion.1.refs_0_, bf16[2,2,512,128]{3,2,1,0:T(8,128)(2,1)S(1)} %collective-permute-done.2.refs_1_, ...), custom_call_target="tpu_custom_call" | custom-call | flops 2147483648 | bytes 10485760 | tf_op jit(solution)/shard_map/pallas_call | solution.py:164
  110.7 0.0 collective-permute-done.14.block
  110.7 2.4 %shard_map.39.total = f32[512,1024]{1,0:T(8,128)S(1)} custom-call(s32[5]{0:T(128)S(1)} %copy-done.1, f32[512,1024]{1,0:T(8,128)S(1)} %get-tuple-element.11.total, bf16[2,2,512,1024]{3,2,1,0:T(8,128)(2,1)S(1)} %get-tuple-element.12.kept, bf16[2,4,64,1024]{3,2,1,0:T(8,128)(2,1)S(1)} %collective-permute-done.14.block), custom_call_target="tpu_custom_call" | custom-call | flops 2147483648 | bytes 10485760 | tf_op jit(solution)/shard_map/pallas_call | solution.py:177
  113.1 9.6 %collective-permute-done.15.block = bf16[2,4,64,1024]{3,2,1,0:T(8,128)(2,1)S(1)} collective-permute-done((bf16[2,4,64,1024]{3,2,1,0:T(8,128)(2,1)S(1)}, bf16[2,4,64,1024]{3,2,1,0:T(8,128)(2,1)S(1)}, u32[]{:S(2)}, u32[]{:S(2)}) %collective-permute-start.15) | collective-permute-done | bytes 1048608 | tf_op jit(solution)/shard_map/ppermute | solution.py:15
  122.7 3.4 %shard_map.40 = bf16[512,1024]{1,0:T(8,128)(2,1)} custom-call(s32[5]{0:T(128)S(1)} %copy-done.1, f32[512,1024]{1,0:T(8,128)S(1)} %shard_map.39.total, bf16[2,2,512,1024]{3,2,1,0:T(8,128)(2,1)S(1)} %get-tuple-element.12.kept, bf16[2,4,64,1024]{3,2,1,0:T(8,128)(2,1)S(1)} %collective-permute-done.15.block), custom_call_target="tpu_custom_call" | custom-call | flops 2147483648 | bytes 10485760 | tf_op jit(solution)/shard_map/pallas_call | solution.py:177
  (3 shorter events, 0.1 us)
Async XLA Ops:
  2.7 31.1 %all-to-all-start = ((bf16[32,4,4,128]{3,2,1,0:T(4,128)(2,1)}), bf16[32,4,4,128]{3,2,1,0:T(4,128)(2,1)S(1)}, u32[]{:S(2)}, u32[]{:S(2)}) async-start(bf16[32,4,4,128]{3,2,1,0:T(4,128)(2,1)} %bitcast.25), calls=%async_computation | async-start | bytes 262144 | tf_op jit(solution)/shard_map/all_to_all | solution.py:138
  18.7 19.3 %collective-permute-start = (bf16[64,1024]{1,0:T(8,128)(2,1)}, bf16[64,1024]{1,0:T(8,128)(2,1)S(1)}, u32[]{:S(2)}, u32[]{:S(2)}) collective-permute-start(bf16[64,1024]{1,0:T(8,128)(2,1)} %here.1), channel_id=1, source_target_pairs={{0,128},{16,144},{32,160},{48,176},{64,192},{80,208},{96,224},{112... | collective-permute-start | bytes 393224 | tf_op jit(solution)/shard_map/ppermute | solution.py:15
  26.0 17.6 %collective-permute-start.9 = (bf16[64,1024]{1,0:T(8,128)(2,1)}, bf16[64,1024]{1,0:T(8,128)(2,1)S(1)}, u32[]{:S(2)}, u32[]{:S(2)}) collective-permute-start(bf16[64,1024]{1,0:T(8,128)(2,1)} %here.1), channel_id=1, source_target_pairs={{0,384},{16,400},{32,416},{48,432},{64,448},{80,464},{96,480},{112... | collective-permute-start | bytes 393224 | tf_op jit(solution)/shard_map/ppermute | solution.py:15
  38.0 18.1 %copy-start.2 = (bf16[64,1024]{1,0:T(8,128)(2,1)}, bf16[64,1024]{1,0:T(8,128)(2,1)S(1)}, u32[]{:S(2)}) copy-start(bf16[64,1024]{1,0:T(8,128)(2,1)S(1)} %collective-permute-done.below) | copy-start | bytes 393220
  38.0 26.4 %collective-permute-start.1 = (bf16[2,512,128]{2,1,0:T(8,128)(2,1)S(1)}, bf16[2,512,128]{2,1,0:T(8,128)(2,1)S(1)}, u32[]{:S(2)}, u32[]{:S(2)}) collective-permute-start(bf16[2,512,128]{2,1,0:T(8,128)(2,1)S(1)} %get-tuple-element.14), channel_id=1, source_target_pairs={{0,8},{1,9},{2,10},{3,11},{4,12},{5,13},{6,14},{7,15},{8,0},{9,1},... | collective-permute-start | bytes 786440 | tf_op jit(solution)/shard_map/ppermute | solution.py:33
  43.6 12.5 %copy-start.3 = (bf16[64,1024]{1,0:T(8,128)(2,1)}, bf16[64,1024]{1,0:T(8,128)(2,1)S(1)}, u32[]{:S(2)}) copy-start(bf16[64,1024]{1,0:T(8,128)(2,1)S(1)} %collective-permute-done.9.above) | copy-start | bytes 393220
  43.6 12.5 %collective-permute-start.10 = (bf16[64,1024]{1,0:T(8,128)(2,1)S(1)}, bf16[64,1024]{1,0:T(8,128)(2,1)S(1)}, u32[]{:S(2)}, u32[]{:S(2)}) collective-permute-start(bf16[64,1024]{1,0:T(8,128)(2,1)S(1)} %broadcast_select_fusion), channel_id=1, source_target_pairs={{0,128},{1,385},{2,130},{3,387},{4,132},{5,389},{6,134},{7,391},{8... | collective-permute-start | bytes 393224 | tf_op jit(solution)/shard_map/ppermute | solution.py:132
  50.6 55.2 %copy-start.1 = (s32[5]{0:T(128)S(1)}, s32[5]{0:T(128)}, u32[]{:S(2)}) copy-start(s32[5]{0:T(128)} %stack.50.place) | copy-start | bytes 64
  56.1 0.7 copy-start.4
  58.7 47.1 %copy-start = (bf16[4,64,1024]{2,1,0:T(8,128)(2,1)S(1)}, bf16[4,64,1024]{2,1,0:T(8,128)(2,1)}, u32[]{:S(2)}) copy-start(bf16[4,64,1024]{2,1,0:T(8,128)(2,1)} %shard_map.37.refs_8_) | copy-start | bytes 1572868
  58.7 14.8 %collective-permute-start.12 = (bf16[4,64,1024]{2,1,0:T(8,128)(2,1)}, bf16[4,64,1024]{2,1,0:T(8,128)(2,1)S(1)}, u32[]{:S(2)}, u32[]{:S(2)}) collective-permute-start(bf16[4,64,1024]{2,1,0:T(8,128)(2,1)} %shard_map.37.refs_8_), channel_id=1, source_target_pairs={{0,64},{1,449},{2,66},{3,451},{4,68},{5,453},{6,70},{7,455},{8,72}... | collective-permute-start | bytes 1572872 | tf_op jit(solution)/shard_map/ppermute | solution.py:148
  60.7 16.3 %collective-permute-start.11 = (bf16[4,64,1024]{2,1,0:T(8,128)(2,1)}, bf16[4,64,1024]{2,1,0:T(8,128)(2,1)S(1)}, u32[]{:S(2)}, u32[]{:S(2)}) collective-permute-start(bf16[4,64,1024]{2,1,0:T(8,128)(2,1)} %shard_map.37.refs_8_), channel_id=1, source_target_pairs={{0,16},{16,0},{32,48},{48,32},{64,80},{80,64},{96,112},{112,96},{1... | collective-permute-start | bytes 1572872 | tf_op jit(solution)/shard_map/ppermute | solution.py:24
  64.5 17.6 %collective-permute-start.2 = (bf16[2,2,512,128]{3,2,1,0:T(8,128)(2,1)S(1)}, bf16[2,2,512,128]{3,2,1,0:T(8,128)(2,1)S(1)}, u32[]{:S(2)}, u32[]{:S(2)}) collective-permute-start(bf16[2,2,512,128]{3,2,1,0:T(8,128)(2,1)S(1)} %pad_maximum_fusion.1.refs_0_), channel_id=1, source_target_pairs={{0,2},{1,3},{2,4},{3,5},{4,6},{5,7},{6,0},{7,1},{8,10},{9,11},{10,... | collective-permute-start | bytes 1572872 | tf_op jit(solution)/shard_map/ppermute | solution.py:33
  66.6 29.1 %collective-permute-start.3 = (bf16[2,2,512,128]{3,2,1,0:T(8,128)(2,1)S(1)}, bf16[2,2,512,128]{3,2,1,0:T(8,128)(2,1)S(1)}, u32[]{:S(2)}, u32[]{:S(2)}) collective-permute-start(bf16[2,2,512,128]{3,2,1,0:T(8,128)(2,1)S(1)} %pad_maximum_fusion.1.refs_0_), channel_id=1, source_target_pairs={{0,6},{1,7},{2,0},{3,1},{4,2},{5,3},{6,4},{7,5},{8,14},{9,15},{10,... | collective-permute-start | bytes 1572872 | tf_op jit(solution)/shard_map/ppermute | solution.py:33
  70.3 27.3 %collective-permute-start.4 = (bf16[2,2,512,128]{3,2,1,0:T(8,128)(2,1)S(1)}, bf16[2,2,512,128]{3,2,1,0:T(8,128)(2,1)S(1)}, u32[]{:S(2)}, u32[]{:S(2)}) collective-permute-start(bf16[2,2,512,128]{3,2,1,0:T(8,128)(2,1)S(1)} %pad_maximum_fusion.1.refs_0_), channel_id=1, source_target_pairs={{0,4},{1,5},{2,6},{3,7},{4,0},{5,1},{6,2},{7,3},{8,12},{9,13},{10,... | collective-permute-start | bytes 1572872 | tf_op jit(solution)/shard_map/ppermute | solution.py:33
  73.5 26.1 %collective-permute-start.5 = (bf16[2,2,512,128]{3,2,1,0:T(8,128)(2,1)S(1)}, bf16[2,2,512,128]{3,2,1,0:T(8,128)(2,1)S(1)}, u32[]{:S(2)}, u32[]{:S(2)}) collective-permute-start(bf16[2,2,512,128]{3,2,1,0:T(8,128)(2,1)S(1)} %pad_maximum_fusion.1.refs_0_), channel_id=1, source_target_pairs={{0,1},{1,0},{2,3},{3,2},{4,5},{5,4},{6,7},{7,6},{8,9},{9,8},{10,11... | collective-permute-start | bytes 1572872 | tf_op jit(solution)/shard_map/ppermute | solution.py:28
  77.0 25.0 %collective-permute-start.13 = (bf16[4,64,1024]{2,1,0:T(8,128)(2,1)S(1)}, bf16[4,64,1024]{2,1,0:T(8,128)(2,1)S(1)}, u32[]{:S(2)}, u32[]{:S(2)}) collective-permute-start(bf16[4,64,1024]{2,1,0:T(8,128)(2,1)S(1)} %collective-permute-done.12.refs_10_), channel_id=1, source_target_pairs={{0,16},{16,0},{32,48},{48,32},{64,80},{80,64},{96,112},{112,96},{1... | collective-permute-start | bytes 1572872 | tf_op jit(solution)/shard_map/ppermute | solution.py:24
  82.1 28.6 %collective-permute-start.14 = (bf16[2,4,64,1024]{3,2,1,0:T(8,128)(2,1)S(1)}, bf16[2,4,64,1024]{3,2,1,0:T(8,128)(2,1)S(1)}, u32[]{:S(2)}, u32[]{:S(2)}) collective-permute-start(bf16[2,4,64,1024]{3,2,1,0:T(8,128)(2,1)S(1)} %pad_maximum_fusion), channel_id=1, source_target_pairs={{0,480},{16,496},{32,0},{48,16},{64,32},{80,48},{96,64},{112,80},{... | collective-permute-start | bytes 3145736 | tf_op jit(solution)/shard_map/ppermute | solution.py:15
  95.7 27.0 %collective-permute-start.15 = (bf16[2,4,64,1024]{3,2,1,0:T(8,128)(2,1)S(1)}, bf16[2,4,64,1024]{3,2,1,0:T(8,128)(2,1)S(1)}, u32[]{:S(2)}, u32[]{:S(2)}) collective-permute-start(bf16[2,4,64,1024]{3,2,1,0:T(8,128)(2,1)S(1)} %pad_maximum_fusion), channel_id=1, source_target_pairs={{0,32},{16,48},{32,64},{48,80},{64,96},{80,112},{96,128},{112,144}... | collective-permute-start | bytes 3145736 | tf_op jit(solution)/shard_map/ppermute | solution.py:15
  97.6 6.3 %collective-permute-start.6 = (bf16[2,2,512,128]{3,2,1,0:T(8,128)(2,1)S(1)}, bf16[2,2,512,128]{3,2,1,0:T(8,128)(2,1)S(1)}, u32[]{:S(2)}, u32[]{:S(2)}) collective-permute-start(bf16[2,2,512,128]{3,2,1,0:T(8,128)(2,1)S(1)} %collective-permute-done.2.refs_1_), channel_id=1, source_target_pairs={{0,1},{1,0},{2,3},{3,2},{4,5},{5,4},{6,7},{7,6},{8,9},{9,8},{10,11... | collective-permute-start | bytes 1572872 | tf_op jit(solution)/shard_map/ppermute | solution.py:28
  99.6 4.4 %collective-permute-start.7 = (bf16[2,2,512,128]{3,2,1,0:T(8,128)(2,1)S(1)}, bf16[2,2,512,128]{3,2,1,0:T(8,128)(2,1)S(1)}, u32[]{:S(2)}, u32[]{:S(2)}) collective-permute-start(bf16[2,2,512,128]{3,2,1,0:T(8,128)(2,1)S(1)} %collective-permute-done.3.refs_2_), channel_id=1, source_target_pairs={{0,1},{1,0},{2,3},{3,2},{4,5},{5,4},{6,7},{7,6},{8,9},{9,8},{10,11... | collective-permute-start | bytes 1572872 | tf_op jit(solution)/shard_map/ppermute | solution.py:28
  102.0 3.8 %collective-permute-start.8 = (bf16[2,2,512,128]{3,2,1,0:T(8,128)(2,1)S(1)}, bf16[2,2,512,128]{3,2,1,0:T(8,128)(2,1)S(1)}, u32[]{:S(2)}, u32[]{:S(2)}) collective-permute-start(bf16[2,2,512,128]{3,2,1,0:T(8,128)(2,1)S(1)} %collective-permute-done.4.refs_3_), channel_id=1, source_target_pairs={{0,1},{1,0},{2,3},{3,2},{4,5},{5,4},{6,7},{7,6},{8,9},{9,8},{10,11... | collective-permute-start | bytes 1572872 | tf_op jit(solution)/shard_map/ppermute | solution.py:28

commit v13 on v12

--- a/solution.py
+++ b/solution.py
@@ -137,7 +137,7 @@
     sent = masked.reshape(OI, 32, OI, depth).transpose(1, 2, 0, 3)
     got = lax.all_to_all(sent, "row", split_axis=0, concat_axis=0, tiled=True)
     swapped = got.transpose(1, 0, 2, 3).reshape(pairs, depth)
-    swapped, up4 = lax.optimization_barrier((swapped, up4))
+    swapped, up4, down4 = lax.optimization_barrier((swapped, up4, down4))
     block = gather_four(place, integrals, up4, down4, far)
 
     both = jnp.stack([masked, swapped])

time: 127 us -> 123 us (0.969)
  the two profiles are of different devices: /device:TPU:60 before, /device:TPU:1 now
where the time goes in v13:
time: 123 us; the launch traced here: 121 us
  starting transfers between devices  71.8 us (58%)
  waiting for transfers between devices  30.9 us (25%)
  Pallas kernels  12.7 us (10%)
  local copies, waits for them, and re-layouts  3.14 us (3%)
  other arithmetic  2.17 us (2%)
    all_to_all x1, starting transfers between devices, on_device(): got = lax.all_to_all(sent, 'row', split_axis=0, concat_axis=0, tiled=True)  17 us
    ppermute x4, starting transfers between devices, core_swap(): return lax.ppermute(x, 'col', [(c, c ^ 1) for c in range(16)])  16.8 us
    ppermute x4, waiting for transfers between devices, z_shift(): return lax.ppermute(x, 'row', [(r, (r + 2 * d) % 32) for r in range(32)])  16.8 us
    ppermute x4, starting transfers between devices, z_shift(): return lax.ppermute(x, 'row', [(r, (r + 2 * d) % 32) for r in range(32)])  14.7 us
    ppermute x4, starting transfers between devices, chip_shift(): lax.ppermute(x, 'col', [(c, (c // 8 ^ dx) * 8 + (c // 2 % 4 + dy) % 4 * 2...  14.5 us
    ppermute x1, waiting for transfers between devices, on_device(): lax.ppermute(jnp.where(core == 0, up4, down4), ('row', 'col'), split_shif...  7.91 us
    pallas_call x2, Pallas kernels, on_device(): pl.pallas_call(functools.partial(add_neighbour, shift), out_shape=jax.Sha...  5.85 us
    pallas_call x1, Pallas kernels, on_device(): pl.pallas_call(first_half, out_shape=(jax.ShapeDtypeStruct((pairs, cols),...  4.87 us
  transfers between devices with their start and end apart: 17, of which 7 were waited for; matrix products, arithmetic and copies ran while one was open for 2% of the time, Pallas kernels for 8%

profile of v13, /device:TPU:1, one launch (start us, length us, event | category | flops | bytes accessed | tf_op | source)
XLA Modules:
  0.0 121.1 jit_solution(5171821508090421424)
XLA Ops:
  0.0 1.0 copy.6
  1.0 0.7 convert_bitcast_fusion
  1.7 0.1 broadcast_bitcast_fusion
  1.8 0.1 broadcast_multiply_fusion
  1.9 0.8 copy.10
  2.7 17.0 %all-to-all-start = ((bf16[32,4,4,128]{3,2,1,0:T(4,128)(2,1)}), bf16[32,4,4,128]{3,2,1,0:T(4,128)(2,1)S(1)}, u32[]{:S(2)}, u32[]{:S(2)}) async-start(bf16[32,4,4,128]{3,2,1,0:T(4,128)(2,1)} %bitcast.25), calls=%async_computation | async-start | bytes 262144 | tf_op jit(solution)/shard_map/all_to_all | solution.py:138
  19.6 7.1 %collective-permute-start = (bf16[64,1024]{1,0:T(8,128)(2,1)}, bf16[64,1024]{1,0:T(8,128)(2,1)S(1)}, u32[]{:S(2)}, u32[]{:S(2)}) collective-permute-start(bf16[64,1024]{1,0:T(8,128)(2,1)} %here.1), channel_id=1, source_target_pairs={{0,128},{16,144},{32,160},{48,176},{64,192},{80,208},{96,224},{112... | collective-permute-start | bytes 393224 | tf_op jit(solution)/shard_map/ppermute | solution.py:15
  26.7 2.1 %collective-permute-start.1 = (bf16[64,1024]{1,0:T(8,128)(2,1)}, bf16[64,1024]{1,0:T(8,128)(2,1)S(1)}, u32[]{:S(2)}, u32[]{:S(2)}) collective-permute-start(bf16[64,1024]{1,0:T(8,128)(2,1)} %here.1), channel_id=1, source_target_pairs={{0,384},{16,400},{32,416},{48,432},{64,448},{80,464},{96,480},{112... | collective-permute-start | bytes 393224 | tf_op jit(solution)/shard_map/ppermute | solution.py:15
  28.9 0.1 fusion.1
  29.0 4.7 %all-to-all-done = bf16[32,4,4,128]{3,2,1,0:T(4,128)(2,1)S(1)} async-done(((bf16[32,4,4,128]{3,2,1,0:T(4,128)(2,1)}), bf16[32,4,4,128]{3,2,1,0:T(4,128)(2,1)S(1)}, u32[]{:S(2)}, u32[]{:S(2)}) %all-to-all-start) | async-done | bytes 131104 | tf_op jit(solution)/shard_map/all_to_all | solution.py:138
  33.7 5.6 %collective-permute-done.below = bf16[64,1024]{1,0:T(8,128)(2,1)S(1)} collective-permute-done((bf16[64,1024]{1,0:T(8,128)(2,1)}, bf16[64,1024]{1,0:T(8,128)(2,1)S(1)}, u32[]{:S(2)}, u32[]{:S(2)}) %collective-permute-start) | collective-permute-done | bytes 131104 | tf_op jit(solution)/shard_map/ppermute | solution.py:15
  39.4 0.0 copy-start.2
  39.4 6.4 %collective-permute-done.1.above = bf16[64,1024]{1,0:T(8,128)(2,1)S(1)} collective-permute-done((bf16[64,1024]{1,0:T(8,128)(2,1)}, bf16[64,1024]{1,0:T(8,128)(2,1)S(1)}, u32[]{:S(2)}, u32[]{:S(2)}) %collective-permute-start.1) | collective-permute-done | bytes 131104 | tf_op jit(solution)/shard_map/ppermute | solution.py:15
  45.8 0.0 copy-start.3
  45.8 4.4 %collective-permute-start.2 = (bf16[2,512,128]{2,1,0:T(8,128)(2,1)S(1)}, bf16[2,512,128]{2,1,0:T(8,128)(2,1)S(1)}, u32[]{:S(2)}, u32[]{:S(2)}) collective-permute-start(bf16[2,512,128]{2,1,0:T(8,128)(2,1)S(1)} %get-tuple-element.16), channel_id=1, source_target_pairs={{0,8},{1,9},{2,10},{3,11},{4,12},{5,13},{6,14},{7,15},{8,0},{9,1},... | collective-permute-start | bytes 786440 | tf_op jit(solution)/shard_map/ppermute | solution.py:33
  50.2 2.0 %collective-permute-start.10 = (bf16[64,1024]{1,0:T(8,128)(2,1)S(1)}, bf16[64,1024]{1,0:T(8,128)(2,1)S(1)}, u32[]{:S(2)}, u32[]{:S(2)}) collective-permute-start(bf16[64,1024]{1,0:T(8,128)(2,1)S(1)} %broadcast_select_fusion), channel_id=1, source_target_pairs={{0,128},{1,385},{2,130},{3,387},{4,132},{5,389},{6,134},{7,391},{8... | collective-permute-start | bytes 393224 | tf_op jit(solution)/shard_map/ppermute | solution.py:132
  52.3 0.6 stack.50.place
  52.9 0.0 copy-start.1
  52.9 7.9 %collective-permute-done.10.far = bf16[64,1024]{1,0:T(8,128)(2,1)S(1)} collective-permute-done((bf16[64,1024]{1,0:T(8,128)(2,1)S(1)}, bf16[64,1024]{1,0:T(8,128)(2,1)S(1)}, u32[]{:S(2)}, u32[]{:S(2)}) %collective-permute-start.10) | collective-permute-done | bytes 131104 | tf_op jit(solution)/shard_map/ppermute | solution.py:132
  60.8 0.0 copy-done.2
  60.8 0.0 copy-done.3
  60.8 0.0 copy-start.4
  60.8 0.7 copy-done.4
  61.5 1.9 %shard_map.37.refs_8_ = bf16[4,64,1024]{2,1,0:T(8,128)(2,1)} custom-call(s32[5]{0:T(128)} %stack.50.place, bf16[64,1024]{1,0:T(8,128)(2,1)} %here.1, bf16[64,1024]{1,0:T(8,128)(2,1)} %copy-done.2, bf16[64,1024]{1,0:T(8,128)(2,1)} %copy-done.3, bf16[64,1024]{1,0:T(8,128)(2,1)} %copy-done.4), custom_call_target="tpu_custom_call" | custom-call | tf_op jit(solution)/shard_map/pallas_call | solution.py:74
  63.4 0.0 copy-start
  63.4 2.0 %collective-permute-start.12 = (bf16[4,64,1024]{2,1,0:T(8,128)(2,1)}, bf16[4,64,1024]{2,1,0:T(8,128)(2,1)S(1)}, u32[]{:S(2)}, u32[]{:S(2)}) collective-permute-start(bf16[4,64,1024]{2,1,0:T(8,128)(2,1)} %shard_map.37.refs_8_), channel_id=1, source_target_pairs={{0,64},{1,449},{2,66},{3,451},{4,68},{5,453},{6,70},{7,455},{8,72}... | collective-permute-start | bytes 1572872 | tf_op jit(solution)/shard_map/ppermute | solution.py:148
  65.4 2.4 %collective-permute-start.11 = (bf16[4,64,1024]{2,1,0:T(8,128)(2,1)}, bf16[4,64,1024]{2,1,0:T(8,128)(2,1)S(1)}, u32[]{:S(2)}, u32[]{:S(2)}) collective-permute-start(bf16[4,64,1024]{2,1,0:T(8,128)(2,1)} %shard_map.37.refs_8_), channel_id=1, source_target_pairs={{0,16},{16,0},{32,48},{48,32},{64,80},{80,64},{96,112},{112,96},{1... | collective-permute-start | bytes 1572872 | tf_op jit(solution)/shard_map/ppermute | solution.py:24
  67.8 0.0 collective-permute-done.2
  67.8 0.1 pad_maximum_fusion.1.refs_0_
  67.9 3.2 %collective-permute-start.3 = (bf16[2,2,512,128]{3,2,1,0:T(8,128)(2,1)S(1)}, bf16[2,2,512,128]{3,2,1,0:T(8,128)(2,1)S(1)}, u32[]{:S(2)}, u32[]{:S(2)}) collective-permute-start(bf16[2,2,512,128]{3,2,1,0:T(8,128)(2,1)S(1)} %pad_maximum_fusion.1.refs_0_), channel_id=1, source_target_pairs={{0,2},{1,3},{2,4},{3,5},{4,6},{5,7},{6,0},{7,1},{8,10},{9,11},{10,... | collective-permute-start | bytes 1572872 | tf_op jit(solution)/shard_map/ppermute | solution.py:33
  71.1 3.4 %collective-permute-start.4 = (bf16[2,2,512,128]{3,2,1,0:T(8,128)(2,1)S(1)}, bf16[2,2,512,128]{3,2,1,0:T(8,128)(2,1)S(1)}, u32[]{:S(2)}, u32[]{:S(2)}) collective-permute-start(bf16[2,2,512,128]{3,2,1,0:T(8,128)(2,1)S(1)} %pad_maximum_fusion.1.refs_0_), channel_id=1, source_target_pairs={{0,6},{1,7},{2,0},{3,1},{4,2},{5,3},{6,4},{7,5},{8,14},{9,15},{10,... | collective-permute-start | bytes 1572872 | tf_op jit(solution)/shard_map/ppermute | solution.py:33
  74.5 3.5 %collective-permute-start.5 = (bf16[2,2,512,128]{3,2,1,0:T(8,128)(2,1)S(1)}, bf16[2,2,512,128]{3,2,1,0:T(8,128)(2,1)S(1)}, u32[]{:S(2)}, u32[]{:S(2)}) collective-permute-start(bf16[2,2,512,128]{3,2,1,0:T(8,128)(2,1)S(1)} %pad_maximum_fusion.1.refs_0_), channel_id=1, source_target_pairs={{0,4},{1,5},{2,6},{3,7},{4,0},{5,1},{6,2},{7,3},{8,12},{9,13},{10,... | collective-permute-start | bytes 1572872 | tf_op jit(solution)/shard_map/ppermute | solution.py:33
  78.0 0.0 collective-permute-done.12.refs_10_
  78.0 6.6 %collective-permute-start.6 = (bf16[2,2,512,128]{3,2,1,0:T(8,128)(2,1)S(1)}, bf16[2,2,512,128]{3,2,1,0:T(8,128)(2,1)S(1)}, u32[]{:S(2)}, u32[]{:S(2)}) collective-permute-start(bf16[2,2,512,128]{3,2,1,0:T(8,128)(2,1)S(1)} %pad_maximum_fusion.1.refs_0_), channel_id=1, source_target_pairs={{0,1},{1,0},{2,3},{3,2},{4,5},{5,4},{6,7},{7,6},{8,9},{9,8},{10,11... | collective-permute-start | bytes 1572872 | tf_op jit(solution)/shard_map/ppermute | solution.py:28
  84.7 0.0 collective-permute-done.11.refs_9_
  84.7 2.4 %collective-permute-start.13 = (bf16[4,64,1024]{2,1,0:T(8,128)(2,1)S(1)}, bf16[4,64,1024]{2,1,0:T(8,128)(2,1)S(1)}, u32[]{:S(2)}, u32[]{:S(2)}) collective-permute-start(bf16[4,64,1024]{2,1,0:T(8,128)(2,1)S(1)} %collective-permute-done.12.refs_10_), channel_id=1, source_target_pairs={{0,16},{16,0},{32,48},{48,32},{64,80},{80,64},{96,112},{112,96},{1... | collective-permute-start | bytes 1572872 | tf_op jit(solution)/shard_map/ppermute | solution.py:24
  87.1 1.1 pad_maximum_fusion
  88.3 0.0 collective-permute-done.3.refs_1_
  88.3 3.3 %collective-permute-start.14 = (bf16[2,4,64,1024]{3,2,1,0:T(8,128)(2,1)S(1)}, bf16[2,4,64,1024]{3,2,1,0:T(8,128)(2,1)S(1)}, u32[]{:S(2)}, u32[]{:S(2)}) collective-permute-start(bf16[2,4,64,1024]{3,2,1,0:T(8,128)(2,1)S(1)} %pad_maximum_fusion), channel_id=1, source_target_pairs={{0,480},{16,496},{32,0},{48,16},{64,32},{80,48},{96,64},{112,80},{... | collective-permute-start | bytes 3145736 | tf_op jit(solution)/shard_map/ppermute | solution.py:15
  91.6 0.0 collective-permute-done.4.refs_2_
  91.6 2.3 %collective-permute-start.15 = (bf16[2,4,64,1024]{3,2,1,0:T(8,128)(2,1)S(1)}, bf16[2,4,64,1024]{3,2,1,0:T(8,128)(2,1)S(1)}, u32[]{:S(2)}, u32[]{:S(2)}) collective-permute-start(bf16[2,4,64,1024]{3,2,1,0:T(8,128)(2,1)S(1)} %pad_maximum_fusion), channel_id=1, source_target_pairs={{0,32},{16,48},{32,64},{48,80},{64,96},{80,112},{96,128},{112,144}... | collective-permute-start | bytes 3145736 | tf_op jit(solution)/shard_map/ppermute | solution.py:15
  93.8 0.1 collective-permute-done.5.refs_3_
  93.9 5.8 %collective-permute-start.7 = (bf16[2,2,512,128]{3,2,1,0:T(8,128)(2,1)S(1)}, bf16[2,2,512,128]{3,2,1,0:T(8,128)(2,1)S(1)}, u32[]{:S(2)}, u32[]{:S(2)}) collective-permute-start(bf16[2,2,512,128]{3,2,1,0:T(8,128)(2,1)S(1)} %collective-permute-done.3.refs_1_), channel_id=1, source_target_pairs={{0,1},{1,0},{2,3},{3,2},{4,5},{5,4},{6,7},{7,6},{8,9},{9,8},{10,11... | collective-permute-start | bytes 1572872 | tf_op jit(solution)/shard_map/ppermute | solution.py:28
  99.7 0.0 collective-permute-done.6.refs_4_
  99.7 1.9 %collective-permute-start.8 = (bf16[2,2,512,128]{3,2,1,0:T(8,128)(2,1)S(1)}, bf16[2,2,512,128]{3,2,1,0:T(8,128)(2,1)S(1)}, u32[]{:S(2)}, u32[]{:S(2)}) collective-permute-start(bf16[2,2,512,128]{3,2,1,0:T(8,128)(2,1)S(1)} %collective-permute-done.4.refs_2_), channel_id=1, source_target_pairs={{0,1},{1,0},{2,3},{3,2},{4,5},{5,4},{6,7},{7,6},{8,9},{9,8},{10,11... | collective-permute-start | bytes 1572872 | tf_op jit(solution)/shard_map/ppermute | solution.py:28
  101.7 0.0 collective-permute-done.13.refs_11_
  101.7 2.4 %collective-permute-start.9 = (bf16[2,2,512,128]{3,2,1,0:T(8,128)(2,1)S(1)}, bf16[2,2,512,128]{3,2,1,0:T(8,128)(2,1)S(1)}, u32[]{:S(2)}, u32[]{:S(2)}) collective-permute-start(bf16[2,2,512,128]{3,2,1,0:T(8,128)(2,1)S(1)} %collective-permute-done.5.refs_3_), channel_id=1, source_target_pairs={{0,1},{1,0},{2,3},{3,2},{4,5},{5,4},{6,7},{7,6},{8,9},{9,8},{10,11... | collective-permute-start | bytes 1572872 | tf_op jit(solution)/shard_map/ppermute | solution.py:28
  104.1 0.0 collective-permute-done.7.refs_5_
  104.1 0.0 collective-permute-done.8.refs_6_
  104.1 1.5 %collective-permute-done.9.refs_7_ = bf16[2,2,512,128]{3,2,1,0:T(8,128)(2,1)S(1)} collective-permute-done((bf16[2,2,512,128]{3,2,1,0:T(8,128)(2,1)S(1)}, bf16[2,2,512,128]{3,2,1,0:T(8,128)(2,1)S(1)}, u32[]{:S(2)}, u32[]{:S(2)}) %collective-permute-start.9) | collective-permute-done | bytes 524320 | tf_op jit(solution)/shard_map/ppermute | solution.py:28
  105.6 0.0 copy-done.1
  105.6 0.0 copy-done
  105.6 4.9 %shard_map.38 = (f32[512,1024]{1,0:T(8,128)S(1)}, bf16[2,2,512,1024]{3,2,1,0:T(8,128)(2,1)S(1)}) custom-call(s32[5]{0:T(128)S(1)} %copy-done.1, bf16[2,2,512,128]{3,2,1,0:T(8,128)(2,1)S(1)} %pad_maximum_fusion.1.refs_0_, bf16[2,2,512,128]{3,2,1,0:T(8,128)(2,1)S(1)} %collective-permute-done.3.refs_1_, ...), custom_call_target="tpu_custom_call" | custom-call | flops 2147483648 | bytes 10485760 | tf_op jit(solution)/shard_map/pallas_call | solution.py:164
  110.5 4.7 %collective-permute-done.14.block = bf16[2,4,64,1024]{3,2,1,0:T(8,128)(2,1)S(1)} collective-permute-done((bf16[2,4,64,1024]{3,2,1,0:T(8,128)(2,1)S(1)}, bf16[2,4,64,1024]{3,2,1,0:T(8,128)(2,1)S(1)}, u32[]{:S(2)}, u32[]{:S(2)}) %collective-permute-start.14) | collective-permute-done | bytes 1048608 | tf_op jit(solution)/shard_map/ppermute | solution.py:15
  115.2 2.4 %shard_map.39.total = f32[512,1024]{1,0:T(8,128)S(1)} custom-call(s32[5]{0:T(128)S(1)} %copy-done.1, f32[512,1024]{1,0:T(8,128)S(1)} %get-tuple-element.13.total, bf16[2,2,512,1024]{3,2,1,0:T(8,128)(2,1)S(1)} %get-tuple-element.14.kept, bf16[2,4,64,1024]{3,2,1,0:T(8,128)(2,1)S(1)} %collective-permute-done.14.block), custom_call_target="tpu_custom_call" | custom-call | flops 2147483648 | bytes 10485760 | tf_op jit(solution)/shard_map/pallas_call | solution.py:177
  117.6 0.0 collective-permute-done.15.block
  117.7 3.4 %shard_map.40 = bf16[512,1024]{1,0:T(8,128)(2,1)} custom-call(s32[5]{0:T(128)S(1)} %copy-done.1, f32[512,1024]{1,0:T(8,128)S(1)} %shard_map.39.total, bf16[2,2,512,1024]{3,2,1,0:T(8,128)(2,1)S(1)} %get-tuple-element.14.kept, bf16[2,4,64,1024]{3,2,1,0:T(8,128)(2,1)S(1)} %collective-permute-done.15.block), custom_call_target="tpu_custom_call" | custom-call | flops 2147483648 | bytes 10485760 | tf_op jit(solution)/shard_map/pallas_call | solution.py:177
  (3 shorter events, 0.1 us)
Async XLA Ops:
  2.7 31.0 %all-to-all-start = ((bf16[32,4,4,128]{3,2,1,0:T(4,128)(2,1)}), bf16[32,4,4,128]{3,2,1,0:T(4,128)(2,1)S(1)}, u32[]{:S(2)}, u32[]{:S(2)}) async-start(bf16[32,4,4,128]{3,2,1,0:T(4,128)(2,1)} %bitcast.25), calls=%async_computation | async-start | bytes 262144 | tf_op jit(solution)/shard_map/all_to_all | solution.py:138
  19.6 19.7 %collective-permute-start = (bf16[64,1024]{1,0:T(8,128)(2,1)}, bf16[64,1024]{1,0:T(8,128)(2,1)S(1)}, u32[]{:S(2)}, u32[]{:S(2)}) collective-permute-start(bf16[64,1024]{1,0:T(8,128)(2,1)} %here.1), channel_id=1, source_target_pairs={{0,128},{16,144},{32,160},{48,176},{64,192},{80,208},{96,224},{112... | collective-permute-start | bytes 393224 | tf_op jit(solution)/shard_map/ppermute | solution.py:15
  26.7 19.1 %collective-permute-start.1 = (bf16[64,1024]{1,0:T(8,128)(2,1)}, bf16[64,1024]{1,0:T(8,128)(2,1)S(1)}, u32[]{:S(2)}, u32[]{:S(2)}) collective-permute-start(bf16[64,1024]{1,0:T(8,128)(2,1)} %here.1), channel_id=1, source_target_pairs={{0,384},{16,400},{32,416},{48,432},{64,448},{80,464},{96,480},{112... | collective-permute-start | bytes 393224 | tf_op jit(solution)/shard_map/ppermute | solution.py:15
  39.4 21.4 %copy-start.2 = (bf16[64,1024]{1,0:T(8,128)(2,1)}, bf16[64,1024]{1,0:T(8,128)(2,1)S(1)}, u32[]{:S(2)}) copy-start(bf16[64,1024]{1,0:T(8,128)(2,1)S(1)} %collective-permute-done.below) | copy-start | bytes 393220
  45.8 15.0 %copy-start.3 = (bf16[64,1024]{1,0:T(8,128)(2,1)}, bf16[64,1024]{1,0:T(8,128)(2,1)S(1)}, u32[]{:S(2)}) copy-start(bf16[64,1024]{1,0:T(8,128)(2,1)S(1)} %collective-permute-done.1.above) | copy-start | bytes 393220
  45.8 22.0 %collective-permute-start.2 = (bf16[2,512,128]{2,1,0:T(8,128)(2,1)S(1)}, bf16[2,512,128]{2,1,0:T(8,128)(2,1)S(1)}, u32[]{:S(2)}, u32[]{:S(2)}) collective-permute-start(bf16[2,512,128]{2,1,0:T(8,128)(2,1)S(1)} %get-tuple-element.16), channel_id=1, source_target_pairs={{0,8},{1,9},{2,10},{3,11},{4,12},{5,13},{6,14},{7,15},{8,0},{9,1},... | collective-permute-start | bytes 786440 | tf_op jit(solution)/shard_map/ppermute | solution.py:33
  50.2 10.6 %collective-permute-start.10 = (bf16[64,1024]{1,0:T(8,128)(2,1)S(1)}, bf16[64,1024]{1,0:T(8,128)(2,1)S(1)}, u32[]{:S(2)}, u32[]{:S(2)}) collective-permute-start(bf16[64,1024]{1,0:T(8,128)(2,1)S(1)} %broadcast_select_fusion), channel_id=1, source_target_pairs={{0,128},{1,385},{2,130},{3,387},{4,132},{5,389},{6,134},{7,391},{8... | collective-permute-start | bytes 393224 | tf_op jit(solution)/shard_map/ppermute | solution.py:132
  52.9 52.7 %copy-start.1 = (s32[5]{0:T(128)S(1)}, s32[5]{0:T(128)}, u32[]{:S(2)}) copy-start(s32[5]{0:T(128)} %stack.50.place) | copy-start | bytes 64
  60.8 0.7 copy-start.4
  63.4 42.2 %copy-start = (bf16[4,64,1024]{2,1,0:T(8,128)(2,1)S(1)}, bf16[4,64,1024]{2,1,0:T(8,128)(2,1)}, u32[]{:S(2)}) copy-start(bf16[4,64,1024]{2,1,0:T(8,128)(2,1)} %shard_map.37.refs_8_) | copy-start | bytes 1572868
  63.4 14.6 %collective-permute-start.12 = (bf16[4,64,1024]{2,1,0:T(8,128)(2,1)}, bf16[4,64,1024]{2,1,0:T(8,128)(2,1)S(1)}, u32[]{:S(2)}, u32[]{:S(2)}) collective-permute-start(bf16[4,64,1024]{2,1,0:T(8,128)(2,1)} %shard_map.37.refs_8_), channel_id=1, source_target_pairs={{0,64},{1,449},{2,66},{3,451},{4,68},{5,453},{6,70},{7,455},{8,72}... | collective-permute-start | bytes 1572872 | tf_op jit(solution)/shard_map/ppermute | solution.py:148
  65.4 19.2 %collective-permute-start.11 = (bf16[4,64,1024]{2,1,0:T(8,128)(2,1)}, bf16[4,64,1024]{2,1,0:T(8,128)(2,1)S(1)}, u32[]{:S(2)}, u32[]{:S(2)}) collective-permute-start(bf16[4,64,1024]{2,1,0:T(8,128)(2,1)} %shard_map.37.refs_8_), channel_id=1, source_target_pairs={{0,16},{16,0},{32,48},{48,32},{64,80},{80,64},{96,112},{112,96},{1... | collective-permute-start | bytes 1572872 | tf_op jit(solution)/shard_map/ppermute | solution.py:24
  67.9 20.4 %collective-permute-start.3 = (bf16[2,2,512,128]{3,2,1,0:T(8,128)(2,1)S(1)}, bf16[2,2,512,128]{3,2,1,0:T(8,128)(2,1)S(1)}, u32[]{:S(2)}, u32[]{:S(2)}) collective-permute-start(bf16[2,2,512,128]{3,2,1,0:T(8,128)(2,1)S(1)} %pad_maximum_fusion.1.refs_0_), channel_id=1, source_target_pairs={{0,2},{1,3},{2,4},{3,5},{4,6},{5,7},{6,0},{7,1},{8,10},{9,11},{10,... | collective-permute-start | bytes 1572872 | tf_op jit(solution)/shard_map/ppermute | solution.py:33
  71.1 20.4 %collective-permute-start.4 = (bf16[2,2,512,128]{3,2,1,0:T(8,128)(2,1)S(1)}, bf16[2,2,512,128]{3,2,1,0:T(8,128)(2,1)S(1)}, u32[]{:S(2)}, u32[]{:S(2)}) collective-permute-start(bf16[2,2,512,128]{3,2,1,0:T(8,128)(2,1)S(1)} %pad_maximum_fusion.1.refs_0_), channel_id=1, source_target_pairs={{0,6},{1,7},{2,0},{3,1},{4,2},{5,3},{6,4},{7,5},{8,14},{9,15},{10,... | collective-permute-start | bytes 1572872 | tf_op jit(solution)/shard_map/ppermute | solution.py:33
  74.5 19.4 %collective-permute-start.5 = (bf16[2,2,512,128]{3,2,1,0:T(8,128)(2,1)S(1)}, bf16[2,2,512,128]{3,2,1,0:T(8,128)(2,1)S(1)}, u32[]{:S(2)}, u32[]{:S(2)}) collective-permute-start(bf16[2,2,512,128]{3,2,1,0:T(8,128)(2,1)S(1)} %pad_maximum_fusion.1.refs_0_), channel_id=1, source_target_pairs={{0,4},{1,5},{2,6},{3,7},{4,0},{5,1},{6,2},{7,3},{8,12},{9,13},{10,... | collective-permute-start | bytes 1572872 | tf_op jit(solution)/shard_map/ppermute | solution.py:33
  78.0 21.7 %collective-permute-start.6 = (bf16[2,2,512,128]{3,2,1,0:T(8,128)(2,1)S(1)}, bf16[2,2,512,128]{3,2,1,0:T(8,128)(2,1)S(1)}, u32[]{:S(2)}, u32[]{:S(2)}) collective-permute-start(bf16[2,2,512,128]{3,2,1,0:T(8,128)(2,1)S(1)} %pad_maximum_fusion.1.refs_0_), channel_id=1, source_target_pairs={{0,1},{1,0},{2,3},{3,2},{4,5},{5,4},{6,7},{7,6},{8,9},{9,8},{10,11... | collective-permute-start | bytes 1572872 | tf_op jit(solution)/shard_map/ppermute | solution.py:28
  84.7 17.0 %collective-permute-start.13 = (bf16[4,64,1024]{2,1,0:T(8,128)(2,1)S(1)}, bf16[4,64,1024]{2,1,0:T(8,128)(2,1)S(1)}, u32[]{:S(2)}, u32[]{:S(2)}) collective-permute-start(bf16[4,64,1024]{2,1,0:T(8,128)(2,1)S(1)} %collective-permute-done.12.refs_10_), channel_id=1, source_target_pairs={{0,16},{16,0},{32,48},{48,32},{64,80},{80,64},{96,112},{112,96},{1... | collective-permute-start | bytes 1572872 | tf_op jit(solution)/shard_map/ppermute | solution.py:24
  88.3 26.9 %collective-permute-start.14 = (bf16[2,4,64,1024]{3,2,1,0:T(8,128)(2,1)S(1)}, bf16[2,4,64,1024]{3,2,1,0:T(8,128)(2,1)S(1)}, u32[]{:S(2)}, u32[]{:S(2)}) collective-permute-start(bf16[2,4,64,1024]{3,2,1,0:T(8,128)(2,1)S(1)} %pad_maximum_fusion), channel_id=1, source_target_pairs={{0,480},{16,496},{32,0},{48,16},{64,32},{80,48},{96,64},{112,80},{... | collective-permute-start | bytes 3145736 | tf_op jit(solution)/shard_map/ppermute | solution.py:15
  91.6 26.1 %collective-permute-start.15 = (bf16[2,4,64,1024]{3,2,1,0:T(8,128)(2,1)S(1)}, bf16[2,4,64,1024]{3,2,1,0:T(8,128)(2,1)S(1)}, u32[]{:S(2)}, u32[]{:S(2)}) collective-permute-start(bf16[2,4,64,1024]{3,2,1,0:T(8,128)(2,1)S(1)} %pad_maximum_fusion), channel_id=1, source_target_pairs={{0,32},{16,48},{32,64},{48,80},{64,96},{80,112},{96,128},{112,144}... | collective-permute-start | bytes 3145736 | tf_op jit(solution)/shard_map/ppermute | solution.py:15
  93.9 10.2 %collective-permute-start.7 = (bf16[2,2,512,128]{3,2,1,0:T(8,128)(2,1)S(1)}, bf16[2,2,512,128]{3,2,1,0:T(8,128)(2,1)S(1)}, u32[]{:S(2)}, u32[]{:S(2)}) collective-permute-start(bf16[2,2,512,128]{3,2,1,0:T(8,128)(2,1)S(1)} %collective-permute-done.3.refs_1_), channel_id=1, source_target_pairs={{0,1},{1,0},{2,3},{3,2},{4,5},{5,4},{6,7},{7,6},{8,9},{9,8},{10,11... | collective-permute-start | bytes 1572872 | tf_op jit(solution)/shard_map/ppermute | solution.py:28
  99.7 4.4 %collective-permute-start.8 = (bf16[2,2,512,128]{3,2,1,0:T(8,128)(2,1)S(1)}, bf16[2,2,512,128]{3,2,1,0:T(8,128)(2,1)S(1)}, u32[]{:S(2)}, u32[]{:S(2)}) collective-permute-start(bf16[2,2,512,128]{3,2,1,0:T(8,128)(2,1)S(1)} %collective-permute-done.4.refs_2_), channel_id=1, source_target_pairs={{0,1},{1,0},{2,3},{3,2},{4,5},{5,4},{6,7},{7,6},{8,9},{9,8},{10,11... | collective-permute-start | bytes 1572872 | tf_op jit(solution)/shard_map/ppermute | solution.py:28
  101.7 3.9 %collective-permute-start.9 = (bf16[2,2,512,128]{3,2,1,0:T(8,128)(2,1)S(1)}, bf16[2,2,512,128]{3,2,1,0:T(8,128)(2,1)S(1)}, u32[]{:S(2)}, u32[]{:S(2)}) collective-permute-start(bf16[2,2,512,128]{3,2,1,0:T(8,128)(2,1)S(1)} %collective-permute-done.5.refs_3_), channel_id=1, source_target_pairs={{0,1},{1,0},{2,3},{3,2},{4,5},{5,4},{6,7},{7,6},{8,9},{9,8},{10,11... | collective-permute-start | bytes 1572872 | tf_op jit(solution)/shard_map/ppermute | solution.py:28

commit v14 on v13

--- a/solution.py
+++ b/solution.py
@@ -8,7 +8,7 @@
 from jax.sharding import PartitionSpec as P
 
 OI = 4
-NTILE = 256
+NTILE = 512
 
 
 def z_shift(x, d):

time: 123 us -> 122 us (level)
  transfers between devices with their start and end apart: 17 -> 17, of which waited for: 7 -> 7; matrix products, arithmetic and copies ran while one was open for 2% -> 2% of each run, Pallas kernels for 8% -> 7%
where the time goes in v14:
time: 122 us; the launch traced here: 120 us
  starting transfers between devices  71.8 us (59%)
  waiting for transfers between devices  31.3 us (26%)
  Pallas kernels  11.6 us (10%)
  local copies, waits for them, and re-layouts  3.14 us (3%)
  other arithmetic  2.17 us (2%)
    ppermute x4, waiting for transfers between devices, z_shift(): return lax.ppermute(x, 'row', [(r, (r + 2 * d) % 32) for r in range(32)])  17.1 us
    all_to_all x1, starting transfers between devices, on_device(): got = lax.all_to_all(sent, 'row', split_axis=0, concat_axis=0, tiled=True)  17 us
    ppermute x4, starting transfers between devices, core_swap(): return lax.ppermute(x, 'col', [(c, c ^ 1) for c in range(16)])  16.8 us
    ppermute x4, starting transfers between devices, z_shift(): return lax.ppermute(x, 'row', [(r, (r + 2 * d) % 32) for r in range(32)])  14.7 us
    ppermute x4, starting transfers between devices, chip_shift(): lax.ppermute(x, 'col', [(c, (c // 8 ^ dx) * 8 + (c // 2 % 4 + dy) % 4 * 2...  14.5 us
    ppermute x1, waiting for transfers between devices, on_device(): lax.ppermute(jnp.where(core == 0, up4, down4), ('row', 'col'), split_shif...  7.91 us
    pallas_call x2, Pallas kernels, on_device(): pl.pallas_call(functools.partial(add_neighbour, shift), out_shape=jax.Sha...  5.1 us
    ppermute x2, starting transfers between devices, x_swap(): return lax.ppermute(x, 'row', [(r, r ^ 1) for r in range(32)])  4.83 us
  transfers between devices with their start and end apart: 17, of which 7 were waited for; matrix products, arithmetic and copies ran while one was open for 2% of the time, Pallas kernels for 7%

profile of v14, /device:TPU:1, one launch (start us, length us, event | category | flops | bytes accessed | tf_op | source)
XLA Modules:
  0.0 120.3 jit_solution(1811186623788095122)
XLA Ops:
  0.0 1.0 copy.6
  1.0 0.7 convert_bitcast_fusion
  1.7 0.1 broadcast_bitcast_fusion
  1.8 0.1 broadcast_multiply_fusion
  1.9 0.8 copy.10
  2.7 17.0 %all-to-all-start = ((bf16[32,4,4,128]{3,2,1,0:T(4,128)(2,1)}), bf16[32,4,4,128]{3,2,1,0:T(4,128)(2,1)S(1)}, u32[]{:S(2)}, u32[]{:S(2)}) async-start(bf16[32,4,4,128]{3,2,1,0:T(4,128)(2,1)} %bitcast.25), calls=%async_computation | async-start | bytes 262144 | tf_op jit(solution)/shard_map/all_to_all | solution.py:138
  19.6 7.1 %collective-permute-start = (bf16[64,1024]{1,0:T(8,128)(2,1)}, bf16[64,1024]{1,0:T(8,128)(2,1)S(1)}, u32[]{:S(2)}, u32[]{:S(2)}) collective-permute-start(bf16[64,1024]{1,0:T(8,128)(2,1)} %here.1), channel_id=1, source_target_pairs={{0,128},{16,144},{32,160},{48,176},{64,192},{80,208},{96,224},{112... | collective-permute-start | bytes 393224 | tf_op jit(solution)/shard_map/ppermute | solution.py:15
  26.7 2.1 %collective-permute-start.1 = (bf16[64,1024]{1,0:T(8,128)(2,1)}, bf16[64,1024]{1,0:T(8,128)(2,1)S(1)}, u32[]{:S(2)}, u32[]{:S(2)}) collective-permute-start(bf16[64,1024]{1,0:T(8,128)(2,1)} %here.1), channel_id=1, source_target_pairs={{0,384},{16,400},{32,416},{48,432},{64,448},{80,464},{96,480},{112... | collective-permute-start | bytes 393224 | tf_op jit(solution)/shard_map/ppermute | solution.py:15
  28.9 0.1 fusion.1
  29.0 4.7 %all-to-all-done = bf16[32,4,4,128]{3,2,1,0:T(4,128)(2,1)S(1)} async-done(((bf16[32,4,4,128]{3,2,1,0:T(4,128)(2,1)}), bf16[32,4,4,128]{3,2,1,0:T(4,128)(2,1)S(1)}, u32[]{:S(2)}, u32[]{:S(2)}) %all-to-all-start) | async-done | bytes 131104 | tf_op jit(solution)/shard_map/all_to_all | solution.py:138
  33.7 5.6 %collective-permute-done.below = bf16[64,1024]{1,0:T(8,128)(2,1)S(1)} collective-permute-done((bf16[64,1024]{1,0:T(8,128)(2,1)}, bf16[64,1024]{1,0:T(8,128)(2,1)S(1)}, u32[]{:S(2)}, u32[]{:S(2)}) %collective-permute-start) | collective-permute-done | bytes 131104 | tf_op jit(solution)/shard_map/ppermute | solution.py:15
  39.4 0.0 copy-start.2
  39.4 6.4 %collective-permute-done.1.above = bf16[64,1024]{1,0:T(8,128)(2,1)S(1)} collective-permute-done((bf16[64,1024]{1,0:T(8,128)(2,1)}, bf16[64,1024]{1,0:T(8,128)(2,1)S(1)}, u32[]{:S(2)}, u32[]{:S(2)}) %collective-permute-start.1) | collective-permute-done | bytes 131104 | tf_op jit(solution)/shard_map/ppermute | solution.py:15
  45.8 0.0 copy-start.3
  45.8 4.4 %collective-permute-start.2 = (bf16[2,512,128]{2,1,0:T(8,128)(2,1)S(1)}, bf16[2,512,128]{2,1,0:T(8,128)(2,1)S(1)}, u32[]{:S(2)}, u32[]{:S(2)}) collective-permute-start(bf16[2,512,128]{2,1,0:T(8,128)(2,1)S(1)} %get-tuple-element.16), channel_id=1, source_target_pairs={{0,8},{1,9},{2,10},{3,11},{4,12},{5,13},{6,14},{7,15},{8,0},{9,1},... | collective-permute-start | bytes 786440 | tf_op jit(solution)/shard_map/ppermute | solution.py:33
  50.2 2.0 %collective-permute-start.10 = (bf16[64,1024]{1,0:T(8,128)(2,1)S(1)}, bf16[64,1024]{1,0:T(8,128)(2,1)S(1)}, u32[]{:S(2)}, u32[]{:S(2)}) collective-permute-start(bf16[64,1024]{1,0:T(8,128)(2,1)S(1)} %broadcast_select_fusion), channel_id=1, source_target_pairs={{0,128},{1,385},{2,130},{3,387},{4,132},{5,389},{6,134},{7,391},{8... | collective-permute-start | bytes 393224 | tf_op jit(solution)/shard_map/ppermute | solution.py:132
  52.3 0.6 stack.50.place
  52.9 0.0 copy-start.1
  52.9 7.9 %collective-permute-done.10.far = bf16[64,1024]{1,0:T(8,128)(2,1)S(1)} collective-permute-done((bf16[64,1024]{1,0:T(8,128)(2,1)S(1)}, bf16[64,1024]{1,0:T(8,128)(2,1)S(1)}, u32[]{:S(2)}, u32[]{:S(2)}) %collective-permute-start.10) | collective-permute-done | bytes 131104 | tf_op jit(solution)/shard_map/ppermute | solution.py:132
  60.8 0.0 copy-done.2
  60.8 0.0 copy-done.3
  60.8 0.0 copy-start.4
  60.8 0.7 copy-done.4
  61.5 1.9 %shard_map.37.refs_8_ = bf16[4,64,1024]{2,1,0:T(8,128)(2,1)} custom-call(s32[5]{0:T(128)} %stack.50.place, bf16[64,1024]{1,0:T(8,128)(2,1)} %here.1, bf16[64,1024]{1,0:T(8,128)(2,1)} %copy-done.2, bf16[64,1024]{1,0:T(8,128)(2,1)} %copy-done.3, bf16[64,1024]{1,0:T(8,128)(2,1)} %copy-done.4), custom_call_target="tpu_custom_call" | custom-call | tf_op jit(solution)/shard_map/pallas_call | solution.py:74
  63.4 0.0 copy-start
  63.4 2.0 %collective-permute-start.12 = (bf16[4,64,1024]{2,1,0:T(8,128)(2,1)}, bf16[4,64,1024]{2,1,0:T(8,128)(2,1)S(1)}, u32[]{:S(2)}, u32[]{:S(2)}) collective-permute-start(bf16[4,64,1024]{2,1,0:T(8,128)(2,1)} %shard_map.37.refs_8_), channel_id=1, source_target_pairs={{0,64},{1,449},{2,66},{3,451},{4,68},{5,453},{6,70},{7,455},{8,72}... | collective-permute-start | bytes 1572872 | tf_op jit(solution)/shard_map/ppermute | solution.py:148
  65.4 2.4 %collective-permute-start.11 = (bf16[4,64,1024]{2,1,0:T(8,128)(2,1)}, bf16[4,64,1024]{2,1,0:T(8,128)(2,1)S(1)}, u32[]{:S(2)}, u32[]{:S(2)}) collective-permute-start(bf16[4,64,1024]{2,1,0:T(8,128)(2,1)} %shard_map.37.refs_8_), channel_id=1, source_target_pairs={{0,16},{16,0},{32,48},{48,32},{64,80},{80,64},{96,112},{112,96},{1... | collective-permute-start | bytes 1572872 | tf_op jit(solution)/shard_map/ppermute | solution.py:24
  67.8 0.0 collective-permute-done.2
  67.8 0.1 pad_maximum_fusion.1.refs_0_
  67.9 3.2 %collective-permute-start.3 = (bf16[2,2,512,128]{3,2,1,0:T(8,128)(2,1)S(1)}, bf16[2,2,512,128]{3,2,1,0:T(8,128)(2,1)S(1)}, u32[]{:S(2)}, u32[]{:S(2)}) collective-permute-start(bf16[2,2,512,128]{3,2,1,0:T(8,128)(2,1)S(1)} %pad_maximum_fusion.1.refs_0_), channel_id=1, source_target_pairs={{0,2},{1,3},{2,4},{3,5},{4,6},{5,7},{6,0},{7,1},{8,10},{9,11},{10,... | collective-permute-start | bytes 1572872 | tf_op jit(solution)/shard_map/ppermute | solution.py:33
  71.1 3.4 %collective-permute-start.4 = (bf16[2,2,512,128]{3,2,1,0:T(8,128)(2,1)S(1)}, bf16[2,2,512,128]{3,2,1,0:T(8,128)(2,1)S(1)}, u32[]{:S(2)}, u32[]{:S(2)}) collective-permute-start(bf16[2,2,512,128]{3,2,1,0:T(8,128)(2,1)S(1)} %pad_maximum_fusion.1.refs_0_), channel_id=1, source_target_pairs={{0,6},{1,7},{2,0},{3,1},{4,2},{5,3},{6,4},{7,5},{8,14},{9,15},{10,... | collective-permute-start | bytes 1572872 | tf_op jit(solution)/shard_map/ppermute | solution.py:33
  74.5 3.5 %collective-permute-start.5 = (bf16[2,2,512,128]{3,2,1,0:T(8,128)(2,1)S(1)}, bf16[2,2,512,128]{3,2,1,0:T(8,128)(2,1)S(1)}, u32[]{:S(2)}, u32[]{:S(2)}) collective-permute-start(bf16[2,2,512,128]{3,2,1,0:T(8,128)(2,1)S(1)} %pad_maximum_fusion.1.refs_0_), channel_id=1, source_target_pairs={{0,4},{1,5},{2,6},{3,7},{4,0},{5,1},{6,2},{7,3},{8,12},{9,13},{10,... | collective-permute-start | bytes 1572872 | tf_op jit(solution)/shard_map/ppermute | solution.py:33
  78.0 0.0 collective-permute-done.12.refs_10_
  78.0 6.6 %collective-permute-start.6 = (bf16[2,2,512,128]{3,2,1,0:T(8,128)(2,1)S(1)}, bf16[2,2,512,128]{3,2,1,0:T(8,128)(2,1)S(1)}, u32[]{:S(2)}, u32[]{:S(2)}) collective-permute-start(bf16[2,2,512,128]{3,2,1,0:T(8,128)(2,1)S(1)} %pad_maximum_fusion.1.refs_0_), channel_id=1, source_target_pairs={{0,1},{1,0},{2,3},{3,2},{4,5},{5,4},{6,7},{7,6},{8,9},{9,8},{10,11... | collective-permute-start | bytes 1572872 | tf_op jit(solution)/shard_map/ppermute | solution.py:28
  84.7 0.0 collective-permute-done.11.refs_9_
  84.7 2.4 %collective-permute-start.13 = (bf16[4,64,1024]{2,1,0:T(8,128)(2,1)S(1)}, bf16[4,64,1024]{2,1,0:T(8,128)(2,1)S(1)}, u32[]{:S(2)}, u32[]{:S(2)}) collective-permute-start(bf16[4,64,1024]{2,1,0:T(8,128)(2,1)S(1)} %collective-permute-done.12.refs_10_), channel_id=1, source_target_pairs={{0,16},{16,0},{32,48},{48,32},{64,80},{80,64},{96,112},{112,96},{1... | collective-permute-start | bytes 1572872 | tf_op jit(solution)/shard_map/ppermute | solution.py:24
  87.1 1.1 pad_maximum_fusion
  88.3 0.0 collective-permute-done.3.refs_1_
  88.3 3.3 %collective-permute-start.14 = (bf16[2,4,64,1024]{3,2,1,0:T(8,128)(2,1)S(1)}, bf16[2,4,64,1024]{3,2,1,0:T(8,128)(2,1)S(1)}, u32[]{:S(2)}, u32[]{:S(2)}) collective-permute-start(bf16[2,4,64,1024]{3,2,1,0:T(8,128)(2,1)S(1)} %pad_maximum_fusion), channel_id=1, source_target_pairs={{0,480},{16,496},{32,0},{48,16},{64,32},{80,48},{96,64},{112,80},{... | collective-permute-start | bytes 3145736 | tf_op jit(solution)/shard_map/ppermute | solution.py:15
  91.6 0.0 collective-permute-done.4.refs_2_
  91.6 2.3 %collective-permute-start.15 = (bf16[2,4,64,1024]{3,2,1,0:T(8,128)(2,1)S(1)}, bf16[2,4,64,1024]{3,2,1,0:T(8,128)(2,1)S(1)}, u32[]{:S(2)}, u32[]{:S(2)}) collective-permute-start(bf16[2,4,64,1024]{3,2,1,0:T(8,128)(2,1)S(1)} %pad_maximum_fusion), channel_id=1, source_target_pairs={{0,32},{16,48},{32,64},{48,80},{64,96},{80,112},{96,128},{112,144}... | collective-permute-start | bytes 3145736 | tf_op jit(solution)/shard_map/ppermute | solution.py:15
  93.8 0.1 collective-permute-done.5.refs_3_
  93.9 5.8 %collective-permute-start.7 = (bf16[2,2,512,128]{3,2,1,0:T(8,128)(2,1)S(1)}, bf16[2,2,512,128]{3,2,1,0:T(8,128)(2,1)S(1)}, u32[]{:S(2)}, u32[]{:S(2)}) collective-permute-start(bf16[2,2,512,128]{3,2,1,0:T(8,128)(2,1)S(1)} %collective-permute-done.3.refs_1_), channel_id=1, source_target_pairs={{0,1},{1,0},{2,3},{3,2},{4,5},{5,4},{6,7},{7,6},{8,9},{9,8},{10,11... | collective-permute-start | bytes 1572872 | tf_op jit(solution)/shard_map/ppermute | solution.py:28
  99.7 0.0 collective-permute-done.6.refs_4_
  99.7 1.9 %collective-permute-start.8 = (bf16[2,2,512,128]{3,2,1,0:T(8,128)(2,1)S(1)}, bf16[2,2,512,128]{3,2,1,0:T(8,128)(2,1)S(1)}, u32[]{:S(2)}, u32[]{:S(2)}) collective-permute-start(bf16[2,2,512,128]{3,2,1,0:T(8,128)(2,1)S(1)} %collective-permute-done.4.refs_2_), channel_id=1, source_target_pairs={{0,1},{1,0},{2,3},{3,2},{4,5},{5,4},{6,7},{7,6},{8,9},{9,8},{10,11... | collective-permute-start | bytes 1572872 | tf_op jit(solution)/shard_map/ppermute | solution.py:28
  101.7 0.0 collective-permute-done.13.refs_11_
  101.7 2.4 %collective-permute-start.9 = (bf16[2,2,512,128]{3,2,1,0:T(8,128)(2,1)S(1)}, bf16[2,2,512,128]{3,2,1,0:T(8,128)(2,1)S(1)}, u32[]{:S(2)}, u32[]{:S(2)}) collective-permute-start(bf16[2,2,512,128]{3,2,1,0:T(8,128)(2,1)S(1)} %collective-permute-done.5.refs_3_), channel_id=1, source_target_pairs={{0,1},{1,0},{2,3},{3,2},{4,5},{5,4},{6,7},{7,6},{8,9},{9,8},{10,11... | collective-permute-start | bytes 1572872 | tf_op jit(solution)/shard_map/ppermute | solution.py:28
  104.1 0.0 collective-permute-done.7.refs_5_
  104.1 0.0 collective-permute-done.8.refs_6_
  104.1 1.5 %collective-permute-done.9.refs_7_ = bf16[2,2,512,128]{3,2,1,0:T(8,128)(2,1)S(1)} collective-permute-done((bf16[2,2,512,128]{3,2,1,0:T(8,128)(2,1)S(1)}, bf16[2,2,512,128]{3,2,1,0:T(8,128)(2,1)S(1)}, u32[]{:S(2)}, u32[]{:S(2)}) %collective-permute-start.9) | collective-permute-done | bytes 524320 | tf_op jit(solution)/shard_map/ppermute | solution.py:28
  105.6 0.0 copy-done.1
  105.6 0.0 copy-done
  105.6 4.5 %shard_map.38 = (f32[512,1024]{1,0:T(8,128)S(1)}, bf16[2,2,512,1024]{3,2,1,0:T(8,128)(2,1)S(1)}) custom-call(s32[5]{0:T(128)S(1)} %copy-done.1, bf16[2,2,512,128]{3,2,1,0:T(8,128)(2,1)S(1)} %pad_maximum_fusion.1.refs_0_, bf16[2,2,512,128]{3,2,1,0:T(8,128)(2,1)S(1)} %collective-permute-done.3.refs_1_, ...), custom_call_target="tpu_custom_call" | custom-call | flops 2147483648 | bytes 10485760 | tf_op jit(solution)/shard_map/pallas_call | solution.py:164
  110.2 5.0 %collective-permute-done.14.block = bf16[2,4,64,1024]{3,2,1,0:T(8,128)(2,1)S(1)} collective-permute-done((bf16[2,4,64,1024]{3,2,1,0:T(8,128)(2,1)S(1)}, bf16[2,4,64,1024]{3,2,1,0:T(8,128)(2,1)S(1)}, u32[]{:S(2)}, u32[]{:S(2)}) %collective-permute-start.14) | collective-permute-done | bytes 1048608 | tf_op jit(solution)/shard_map/ppermute | solution.py:15
  115.2 2.1 %shard_map.39.total = f32[512,1024]{1,0:T(8,128)S(1)} custom-call(s32[5]{0:T(128)S(1)} %copy-done.1, f32[512,1024]{1,0:T(8,128)S(1)} %get-tuple-element.13.total, bf16[2,2,512,1024]{3,2,1,0:T(8,128)(2,1)S(1)} %get-tuple-element.14.kept, bf16[2,4,64,1024]{3,2,1,0:T(8,128)(2,1)S(1)} %collective-permute-done.14.block), custom_call_target="tpu_custom_call" | custom-call | flops 2147483648 | bytes 10485760 | tf_op jit(solution)/shard_map/pallas_call | solution.py:177
  117.3 0.0 collective-permute-done.15.block
  117.3 3.0 %shard_map.40 = bf16[512,1024]{1,0:T(8,128)(2,1)} custom-call(s32[5]{0:T(128)S(1)} %copy-done.1, f32[512,1024]{1,0:T(8,128)S(1)} %shard_map.39.total, bf16[2,2,512,1024]{3,2,1,0:T(8,128)(2,1)S(1)} %get-tuple-element.14.kept, bf16[2,4,64,1024]{3,2,1,0:T(8,128)(2,1)S(1)} %collective-permute-done.15.block), custom_call_target="tpu_custom_call" | custom-call | flops 2147483648 | bytes 10485760 | tf_op jit(solution)/shard_map/pallas_call | solution.py:177
  (3 shorter events, 0.1 us)
Async XLA Ops:
  2.7 31.0 %all-to-all-start = ((bf16[32,4,4,128]{3,2,1,0:T(4,128)(2,1)}), bf16[32,4,4,128]{3,2,1,0:T(4,128)(2,1)S(1)}, u32[]{:S(2)}, u32[]{:S(2)}) async-start(bf16[32,4,4,128]{3,2,1,0:T(4,128)(2,1)} %bitcast.25), calls=%async_computation | async-start | bytes 262144 | tf_op jit(solution)/shard_map/all_to_all | solution.py:138
  19.6 19.7 %collective-permute-start = (bf16[64,1024]{1,0:T(8,128)(2,1)}, bf16[64,1024]{1,0:T(8,128)(2,1)S(1)}, u32[]{:S(2)}, u32[]{:S(2)}) collective-permute-start(bf16[64,1024]{1,0:T(8,128)(2,1)} %here.1), channel_id=1, source_target_pairs={{0,128},{16,144},{32,160},{48,176},{64,192},{80,208},{96,224},{112... | collective-permute-start | bytes 393224 | tf_op jit(solution)/shard_map/ppermute | solution.py:15
  26.7 19.1 %collective-permute-start.1 = (bf16[64,1024]{1,0:T(8,128)(2,1)}, bf16[64,1024]{1,0:T(8,128)(2,1)S(1)}, u32[]{:S(2)}, u32[]{:S(2)}) collective-permute-start(bf16[64,1024]{1,0:T(8,128)(2,1)} %here.1), channel_id=1, source_target_pairs={{0,384},{16,400},{32,416},{48,432},{64,448},{80,464},{96,480},{112... | collective-permute-start | bytes 393224 | tf_op jit(solution)/shard_map/ppermute | solution.py:15
  39.4 21.4 %copy-start.2 = (bf16[64,1024]{1,0:T(8,128)(2,1)}, bf16[64,1024]{1,0:T(8,128)(2,1)S(1)}, u32[]{:S(2)}) copy-start(bf16[64,1024]{1,0:T(8,128)(2,1)S(1)} %collective-permute-done.below) | copy-start | bytes 393220
  45.8 15.0 %copy-start.3 = (bf16[64,1024]{1,0:T(8,128)(2,1)}, bf16[64,1024]{1,0:T(8,128)(2,1)S(1)}, u32[]{:S(2)}) copy-start(bf16[64,1024]{1,0:T(8,128)(2,1)S(1)} %collective-permute-done.1.above) | copy-start | bytes 393220
  45.8 22.0 %collective-permute-start.2 = (bf16[2,512,128]{2,1,0:T(8,128)(2,1)S(1)}, bf16[2,512,128]{2,1,0:T(8,128)(2,1)S(1)}, u32[]{:S(2)}, u32[]{:S(2)}) collective-permute-start(bf16[2,512,128]{2,1,0:T(8,128)(2,1)S(1)} %get-tuple-element.16), channel_id=1, source_target_pairs={{0,8},{1,9},{2,10},{3,11},{4,12},{5,13},{6,14},{7,15},{8,0},{9,1},... | collective-permute-start | bytes 786440 | tf_op jit(solution)/shard_map/ppermute | solution.py:33
  50.2 10.6 %collective-permute-start.10 = (bf16[64,1024]{1,0:T(8,128)(2,1)S(1)}, bf16[64,1024]{1,0:T(8,128)(2,1)S(1)}, u32[]{:S(2)}, u32[]{:S(2)}) collective-permute-start(bf16[64,1024]{1,0:T(8,128)(2,1)S(1)} %broadcast_select_fusion), channel_id=1, source_target_pairs={{0,128},{1,385},{2,130},{3,387},{4,132},{5,389},{6,134},{7,391},{8... | collective-permute-start | bytes 393224 | tf_op jit(solution)/shard_map/ppermute | solution.py:132
  52.9 52.7 %copy-start.1 = (s32[5]{0:T(128)S(1)}, s32[5]{0:T(128)}, u32[]{:S(2)}) copy-start(s32[5]{0:T(128)} %stack.50.place) | copy-start | bytes 64
  60.8 0.7 copy-start.4
  63.4 42.2 %copy-start = (bf16[4,64,1024]{2,1,0:T(8,128)(2,1)S(1)}, bf16[4,64,1024]{2,1,0:T(8,128)(2,1)}, u32[]{:S(2)}) copy-start(bf16[4,64,1024]{2,1,0:T(8,128)(2,1)} %shard_map.37.refs_8_) | copy-start | bytes 1572868
  63.4 14.6 %collective-permute-start.12 = (bf16[4,64,1024]{2,1,0:T(8,128)(2,1)}, bf16[4,64,1024]{2,1,0:T(8,128)(2,1)S(1)}, u32[]{:S(2)}, u32[]{:S(2)}) collective-permute-start(bf16[4,64,1024]{2,1,0:T(8,128)(2,1)} %shard_map.37.refs_8_), channel_id=1, source_target_pairs={{0,64},{1,449},{2,66},{3,451},{4,68},{5,453},{6,70},{7,455},{8,72}... | collective-permute-start | bytes 1572872 | tf_op jit(solution)/shard_map/ppermute | solution.py:148
  65.4 19.2 %collective-permute-start.11 = (bf16[4,64,1024]{2,1,0:T(8,128)(2,1)}, bf16[4,64,1024]{2,1,0:T(8,128)(2,1)S(1)}, u32[]{:S(2)}, u32[]{:S(2)}) collective-permute-start(bf16[4,64,1024]{2,1,0:T(8,128)(2,1)} %shard_map.37.refs_8_), channel_id=1, source_target_pairs={{0,16},{16,0},{32,48},{48,32},{64,80},{80,64},{96,112},{112,96},{1... | collective-permute-start | bytes 1572872 | tf_op jit(solution)/shard_map/ppermute | solution.py:24
  67.9 20.4 %collective-permute-start.3 = (bf16[2,2,512,128]{3,2,1,0:T(8,128)(2,1)S(1)}, bf16[2,2,512,128]{3,2,1,0:T(8,128)(2,1)S(1)}, u32[]{:S(2)}, u32[]{:S(2)}) collective-permute-start(bf16[2,2,512,128]{3,2,1,0:T(8,128)(2,1)S(1)} %pad_maximum_fusion.1.refs_0_), channel_id=1, source_target_pairs={{0,2},{1,3},{2,4},{3,5},{4,6},{5,7},{6,0},{7,1},{8,10},{9,11},{10,... | collective-permute-start | bytes 1572872 | tf_op jit(solution)/shard_map/ppermute | solution.py:33
  71.1 20.4 %collective-permute-start.4 = (bf16[2,2,512,128]{3,2,1,0:T(8,128)(2,1)S(1)}, bf16[2,2,512,128]{3,2,1,0:T(8,128)(2,1)S(1)}, u32[]{:S(2)}, u32[]{:S(2)}) collective-permute-start(bf16[2,2,512,128]{3,2,1,0:T(8,128)(2,1)S(1)} %pad_maximum_fusion.1.refs_0_), channel_id=1, source_target_pairs={{0,6},{1,7},{2,0},{3,1},{4,2},{5,3},{6,4},{7,5},{8,14},{9,15},{10,... | collective-permute-start | bytes 1572872 | tf_op jit(solution)/shard_map/ppermute | solution.py:33
  74.5 19.4 %collective-permute-start.5 = (bf16[2,2,512,128]{3,2,1,0:T(8,128)(2,1)S(1)}, bf16[2,2,512,128]{3,2,1,0:T(8,128)(2,1)S(1)}, u32[]{:S(2)}, u32[]{:S(2)}) collective-permute-start(bf16[2,2,512,128]{3,2,1,0:T(8,128)(2,1)S(1)} %pad_maximum_fusion.1.refs_0_), channel_id=1, source_target_pairs={{0,4},{1,5},{2,6},{3,7},{4,0},{5,1},{6,2},{7,3},{8,12},{9,13},{10,... | collective-permute-start | bytes 1572872 | tf_op jit(solution)/shard_map/ppermute | solution.py:33
  78.0 21.7 %collective-permute-start.6 = (bf16[2,2,512,128]{3,2,1,0:T(8,128)(2,1)S(1)}, bf16[2,2,512,128]{3,2,1,0:T(8,128)(2,1)S(1)}, u32[]{:S(2)}, u32[]{:S(2)}) collective-permute-start(bf16[2,2,512,128]{3,2,1,0:T(8,128)(2,1)S(1)} %pad_maximum_fusion.1.refs_0_), channel_id=1, source_target_pairs={{0,1},{1,0},{2,3},{3,2},{4,5},{5,4},{6,7},{7,6},{8,9},{9,8},{10,11... | collective-permute-start | bytes 1572872 | tf_op jit(solution)/shard_map/ppermute | solution.py:28
  84.7 17.0 %collective-permute-start.13 = (bf16[4,64,1024]{2,1,0:T(8,128)(2,1)S(1)}, bf16[4,64,1024]{2,1,0:T(8,128)(2,1)S(1)}, u32[]{:S(2)}, u32[]{:S(2)}) collective-permute-start(bf16[4,64,1024]{2,1,0:T(8,128)(2,1)S(1)} %collective-permute-done.12.refs_10_), channel_id=1, source_target_pairs={{0,16},{16,0},{32,48},{48,32},{64,80},{80,64},{96,112},{112,96},{1... | collective-permute-start | bytes 1572872 | tf_op jit(solution)/shard_map/ppermute | solution.py:24
  88.3 26.9 %collective-permute-start.14 = (bf16[2,4,64,1024]{3,2,1,0:T(8,128)(2,1)S(1)}, bf16[2,4,64,1024]{3,2,1,0:T(8,128)(2,1)S(1)}, u32[]{:S(2)}, u32[]{:S(2)}) collective-permute-start(bf16[2,4,64,1024]{3,2,1,0:T(8,128)(2,1)S(1)} %pad_maximum_fusion), channel_id=1, source_target_pairs={{0,480},{16,496},{32,0},{48,16},{64,32},{80,48},{96,64},{112,80},{... | collective-permute-start | bytes 3145736 | tf_op jit(solution)/shard_map/ppermute | solution.py:15
  91.6 25.7 %collective-permute-start.15 = (bf16[2,4,64,1024]{3,2,1,0:T(8,128)(2,1)S(1)}, bf16[2,4,64,1024]{3,2,1,0:T(8,128)(2,1)S(1)}, u32[]{:S(2)}, u32[]{:S(2)}) collective-permute-start(bf16[2,4,64,1024]{3,2,1,0:T(8,128)(2,1)S(1)} %pad_maximum_fusion), channel_id=1, source_target_pairs={{0,32},{16,48},{32,64},{48,80},{64,96},{80,112},{96,128},{112,144}... | collective-permute-start | bytes 3145736 | tf_op jit(solution)/shard_map/ppermute | solution.py:15
  93.9 10.2 %collective-permute-start.7 = (bf16[2,2,512,128]{3,2,1,0:T(8,128)(2,1)S(1)}, bf16[2,2,512,128]{3,2,1,0:T(8,128)(2,1)S(1)}, u32[]{:S(2)}, u32[]{:S(2)}) collective-permute-start(bf16[2,2,512,128]{3,2,1,0:T(8,128)(2,1)S(1)} %collective-permute-done.3.refs_1_), channel_id=1, source_target_pairs={{0,1},{1,0},{2,3},{3,2},{4,5},{5,4},{6,7},{7,6},{8,9},{9,8},{10,11... | collective-permute-start | bytes 1572872 | tf_op jit(solution)/shard_map/ppermute | solution.py:28
  99.7 4.4 %collective-permute-start.8 = (bf16[2,2,512,128]{3,2,1,0:T(8,128)(2,1)S(1)}, bf16[2,2,512,128]{3,2,1,0:T(8,128)(2,1)S(1)}, u32[]{:S(2)}, u32[]{:S(2)}) collective-permute-start(bf16[2,2,512,128]{3,2,1,0:T(8,128)(2,1)S(1)} %collective-permute-done.4.refs_2_), channel_id=1, source_target_pairs={{0,1},{1,0},{2,3},{3,2},{4,5},{5,4},{6,7},{7,6},{8,9},{9,8},{10,11... | collective-permute-start | bytes 1572872 | tf_op jit(solution)/shard_map/ppermute | solution.py:28
  101.7 3.9 %collective-permute-start.9 = (bf16[2,2,512,128]{3,2,1,0:T(8,128)(2,1)S(1)}, bf16[2,2,512,128]{3,2,1,0:T(8,128)(2,1)S(1)}, u32[]{:S(2)}, u32[]{:S(2)}) collective-permute-start(bf16[2,2,512,128]{3,2,1,0:T(8,128)(2,1)S(1)} %collective-permute-done.5.refs_3_), channel_id=1, source_target_pairs={{0,1},{1,0},{2,3},{3,2},{4,5},{5,4},{6,7},{7,6},{8,9},{9,8},{10,11... | collective-permute-start | bytes 1572872 | tf_op jit(solution)/shard_map/ppermute | solution.py:28
